TPU v7x, 32 devices: a whole 2x2x4 slice. The times are simulated.
32 devices in a mesh: dp: 16 (over z, y, x), rep: 2 (over core).
Axes of the slice: x: 2, y: 2, z: 4, core: 2. Of those that a mesh axis runs over, the one named last changes fastest.
Arguments:
- source: int32 [16384], P(('dp', 'rep')), may hold values from 0 to 8191
- target: int32 [16384], P(('dp', 'rep')), may hold values from 0 to 8191
- neighbours: int32 [16384, 2, 10], P(('dp', 'rep')), may hold values from 0 to 8191
- neighbour_ticks: int32 [16384, 2, 10], P(('dp', 'rep')), may hold values from 0 to 16383
- event_ticks: int32 [16384], P(('dp', 'rep')), may hold values from 0 to 16383, each once
- event_types: int32 [16384], P(('dp', 'rep')), may hold values 0 or 1
- labels: int32 [16384], P(('dp', 'rep')), may hold values 0 or 1
- edge_feats: bfloat16 [16384, 172], P(('dp', 'rep')), may hold values from -6 to 6
- weights: float32 [16384], P(('dp', 'rep')), may hold values from 0.25 to 10, as said below
- memory: float32 [8192, 172], replicated, may hold values from -6 to 6
- node_ticks: int32 [8192], replicated, may hold values from 0 to 16383
- gru_in: float32 [688, 516], replicated, may hold values from -0.21875 to 0.21875
- gru_hid: float32 [172, 516], replicated, may hold values from -0.4375 to 0.4375
- keys_values: float32 [344, 344], replicated, may hold values from -0.3125 to 0.3125
- tall_stack: float32 [3, 344, 172], replicated, may hold values from -0.3125 to 0.3125
- squares: float32 [2, 172, 172], replicated, may hold values from -0.625 to 0.625
- vectors: float32 [15, 172], replicated, may hold values from -2 to 2
- first_gru_in: float32 [688, 516], replicated, may hold values from -8.34465e-07 to 8.34465e-07
- first_gru_hid: float32 [172, 516], replicated, may hold values from -4.7683716e-07 to 4.7683716e-07
- first_keys_values: float32 [344, 344], replicated, may hold values from -3.8146973e-06 to 3.8146973e-06
- first_tall: float32 [3, 344, 172], replicated, may hold values from -3.8146973e-06 to 3.8146973e-06
- first_squares: float32 [2, 172, 172], replicated, may hold values from -3.8146973e-06 to 3.8146973e-06
- first_vectors: float32 [15, 172], replicated, may hold values from -1.9073486e-05 to 1.9073486e-05
- second_gru_in: float32 [688, 516], replicated, may hold values from 1.56491e-15 to 6.25964e-15
- second_gru_hid: float32 [172, 516], replicated, may hold values from 6.2596397e-16 to 2.5038559e-15
- second_keys_values: float32 [344, 344], replicated, may hold values from 3.12982e-14 to 1.251928e-13
- second_tall: float32 [3, 344, 172], replicated, may hold values from 3.12982e-14 to 1.251928e-13
- second_squares: float32 [2, 172, 172], replicated, may hold values from 3.12982e-14 to 1.251928e-13
- second_vectors: float32 [15, 172], replicated, may hold values from 7.82455e-13 to 3.12982e-12
Outputs:
- grad_norm: float32 [], replicated
- loss_sum: float32 [], replicated
- weight_sum: float32 [], replicated
- new_memory: float32 [8192, 172], replicated
- new_gru_in: float32 [688, 516], replicated
- new_gru_hid: float32 [172, 516], replicated
- new_keys_values: float32 [344, 344], replicated
- new_tall: float32 [3, 344, 172], replicated
- new_squares: float32 [2, 172, 172], replicated
- new_vectors: float32 [15, 172], replicated
- out_first_gru_in: float32 [688, 516], replicated
- out_first_gru_hid: float32 [172, 516], replicated
- out_first_keys_values: float32 [344, 344], replicated
- out_first_tall: float32 [3, 344, 172], replicated
- out_first_squares: float32 [2, 172, 172], replicated
- out_first_vectors: float32 [15, 172], replicated
- out_second_gru_in: float32 [688, 516], replicated
- out_second_gru_hid: float32 [172, 516], replicated
- out_second_keys_values: float32 [344, 344], replicated
- out_second_tall: float32 [3, 344, 172], replicated
- out_second_squares: float32 [2, 172, 172], replicated
- out_second_vectors: float32 [15, 172], replicated
Inputs may be any that keep to these rules, and one draw needn't show every extreme that they name: `event_ticks`: each tick 0 to 16383 appears once. `weights`: positive.
All inputs are finite; a program needn't handle non-finite values. No bound on the sum of `event_types` or of `labels` on one device may be relied on, other than what follows from the above.
Results may differ from a plain program's by a relative error of at most 0.0048.
Values sent between devices are 32-bit elements; how exact they have to be, the bound alone decides.
No kernel may reach another device: no remote copies, remote signals or barrier semaphores. Data moves between devices by JAX's collectives and lax.ppermute only.
A program may use at most 192 MiB of HBM per device.

v0:
```python
import math

import jax
import jax.numpy as jnp
from jax import lax
from jax.sharding import PartitionSpec as P

HEADS = 2
STEP = 10


HIGHEST = lax.Precision.HIGHEST
LEARN_RATE = 0.03
VECTOR_RATE = 0.3
BETA_ONE = 0.9
BETA_TWO = 0.999
ADAM_EPS = 1e-08
DECAY = 0.01
CLIP_AT = 0.005
TIME_RATE = 64.0
NORM_EPS = 1e-06


def time_code(time_gap, frequency, phase_row):
    return jnp.cos(time_gap[..., None] * frequency + phase_row)


def softplus(logit_in):
    return jnp.maximum(logit_in, 0.0) + jnp.log1p(jnp.exp(-jnp.abs(logit_in)))


def gru_cell(gates_in, gates_hid, own_rows, vector_rows):
    feat_width = own_rows.shape[-1]
    total_in = gates_in + vector_rows[2:5].reshape(-1)
    total_hid = gates_hid + vector_rows[5:8].reshape(-1)
    update = jax.nn.sigmoid(total_in[:, :feat_width] + total_hid[:, :feat_width])
    reset_gate = jax.nn.sigmoid(
        total_in[:, feat_width : 2 * feat_width] + total_hid[:, feat_width : 2 * feat_width]
    )
    candidate = jnp.tanh(
        total_in[:, 2 * feat_width :] + reset_gate * total_hid[:, 2 * feat_width :]
    )
    return (1.0 - update) * candidate + update * own_rows


def attend(query_rows, key_rows, value_rows):
    row_count, near_count, feat_width = key_rows.shape
    head_size = feat_width // HEADS
    heads_q = query_rows.reshape(row_count, HEADS, head_size)
    heads_k = key_rows.reshape(row_count, near_count, HEADS, head_size)
    heads_v = value_rows.reshape(row_count, near_count, HEADS, head_size)
    scores = jnp.einsum("rhd,rjhd->rhj", heads_q, heads_k, precision=HIGHEST) * head_size ** (-0.5)
    scores = scores - jnp.max(scores, axis=-1, keepdims=True)
    exponent = jnp.exp(scores)
    attn_weights = exponent / jnp.sum(exponent, axis=-1, keepdims=True)
    attended = jnp.einsum("rhj,rjhd->rhd", attn_weights, heads_v, precision=HIGHEST)
    return attended.reshape(row_count, feat_width)


def head_terms(pre_rows, out_row, label_wide, weights):
    logit = jnp.sum(jax.nn.gelu(pre_rows) * out_row, axis=-1)
    return weights * (softplus(logit) - label_wide * logit)


def adam_all(params, firsts, seconds, grads):
    squares_sum = jnp.zeros((), jnp.float32)
    for grad_item in grads:
        squares_sum = squares_sum + jnp.sum(grad_item * grad_item)
    grad_norm = jnp.sqrt(squares_sum)
    factor = jnp.minimum(1.0, CLIP_AT / (grad_norm + NORM_EPS))
    new_params, new_firsts, new_seconds = ([], [], [])
    for position in range(len(params)):
        clipped = grads[position] * factor
        moment_one = BETA_ONE * firsts[position] + (1.0 - BETA_ONE) * clipped
        moment_two = BETA_TWO * seconds[position] + (1.0 - BETA_TWO) * clipped * clipped
        step_dir = (
            moment_one
            / (1.0 - BETA_ONE**STEP)
            / (jnp.sqrt(moment_two / (1.0 - BETA_TWO**STEP)) + ADAM_EPS)
        )
        decay_rate = DECAY if position < len(params) - 1 else 0.0
        step_rate = LEARN_RATE if position < len(params) - 1 else VECTOR_RATE
        new_params.append(params[position] - step_rate * (step_dir + decay_rate * params[position]))
        new_firsts.append(moment_one)
        new_seconds.append(moment_two)
    return (grad_norm, new_params, new_firsts, new_seconds)


def fetch(mem_table, node_ids):
    row_total = node_ids.shape[0]
    block_rows = math.gcd(row_total, 512)
    columns = jnp.arange(mem_table.shape[0], dtype=jnp.int32)

    def one_block(id_block):
        one_hot = (id_block[:, None] == columns[None, :]).astype(jnp.bfloat16)
        return jnp.dot(one_hot, mem_table, preferred_element_type=jnp.float32).astype(jnp.bfloat16)

    fetched = lax.map(one_block, node_ids.reshape(-1, block_rows))
    return fetched.reshape(row_total, mem_table.shape[1])


def forward_dot(data_low, weight_low):
    return jnp.dot(data_low, weight_low, preferred_element_type=jnp.float32)


def outer_sum(left_op, right_op):
    return lax.dot_general(
        left_op, right_op, (((0,), (0,)), ((), ())), preferred_element_type=jnp.float32
    )


def against(grad_low, weight_low):
    return lax.dot_general(
        grad_low, weight_low, (((1,), (1,)), ((), ())), preferred_element_type=jnp.float32
    )


def body(
    source,
    target,
    neighbours,
    neighbour_ticks,
    event_ticks,
    event_types,
    labels,
    edge_feats,
    weights,
    memory,
    node_ticks,
    gru_in,
    gru_hid,
    keys_values,
    tall_stack,
    squares,
    vectors,
    first_gru_in,
    first_gru_hid,
    first_keys_values,
    first_tall,
    first_squares,
    first_vectors,
    second_gru_in,
    second_gru_hid,
    second_keys_values,
    second_tall,
    second_squares,
    second_vectors,
):
    bf_type = jnp.bfloat16
    events_here = event_ticks.shape[0]
    feat_width = memory.shape[1]
    node_count = memory.shape[0]
    device_count = lax.axis_size("dp") * lax.axis_size("rep")
    time_scale = TIME_RATE / (events_here * device_count)
    mem_low = memory.astype(bf_type)
    end_nodes = jnp.concatenate([source, target])
    near_ids = jnp.transpose(neighbours, (1, 0, 2)).reshape(-1)
    fetched = fetch(mem_low, jnp.concatenate([end_nodes, near_ids]))
    own_rows = fetched[: 2 * events_here]
    near_rows = fetched[2 * events_here :]
    partner = jnp.concatenate([own_rows[events_here:], own_rows[:events_here]])
    both_ticks = jnp.concatenate([event_ticks, event_ticks])
    gap_own = (both_ticks - node_ticks[end_nodes]).astype(jnp.float32) * time_scale
    gap_near = (
        both_ticks[:, None] - jnp.transpose(neighbour_ticks, (1, 0, 2)).reshape(2 * events_here, -1)
    ).astype(jnp.float32) * time_scale
    edge_rows = edge_feats * event_types.astype(bf_type)[:, None]
    edge_rows = jnp.concatenate([edge_rows, edge_rows])
    w_gin = gru_in.astype(bf_type)
    w_ghid = gru_hid.astype(bf_type)
    w_pairs = keys_values.astype(bf_type)
    tall_low = tall_stack.astype(bf_type)
    square_low = squares.astype(bf_type)
    code_own, code_own_back = jax.vjp(
        lambda frequency, phase_row: time_code(gap_own, frequency, phase_row),
        vectors[0],
        vectors[1],
    )
    message = jnp.concatenate([own_rows, partner, code_own.astype(bf_type), edge_rows], axis=1)
    gates_in = forward_dot(message, w_gin)
    gates_hid = forward_dot(own_rows, w_ghid)
    own_wide = own_rows.astype(jnp.float32)
    renewed, gru_back = jax.vjp(
        lambda pre_in, pre_hid, vector_rows: gru_cell(pre_in, pre_hid, own_wide, vector_rows),
        gates_in,
        gates_hid,
        vectors,
    )
    renewed_low = renewed.astype(bf_type)
    phase_code, phase_back = jax.vjp(jnp.cos, vectors[1])
    query_in = jnp.concatenate(
        [renewed_low, jnp.broadcast_to(phase_code.astype(bf_type), renewed_low.shape)], axis=1
    )
    queries = forward_dot(query_in, tall_low[0]) + vectors[8]
    code_near, near_back = jax.vjp(
        lambda frequency, phase_row: time_code(gap_near, frequency, phase_row),
        vectors[0],
        vectors[1],
    )
    near_in = jnp.concatenate(
        [near_rows, code_near.astype(bf_type).reshape(near_rows.shape)], axis=1
    )
    pair_rows = forward_dot(near_in, w_pairs).reshape(2 * events_here, -1, 2 * feat_width)
    attended, attend_back = jax.vjp(
        lambda query_rows, both_rows, value_bias: attend(
            query_rows, both_rows[..., :feat_width], both_rows[..., feat_width:] + value_bias
        ),
        queries,
        pair_rows,
        vectors[9],
    )
    attended_low = attended.astype(bf_type)
    projected = forward_dot(attended_low, square_low[0]) + vectors[10]
    mlp_in = jnp.concatenate([projected.astype(bf_type), renewed_low], axis=1)
    inner_pre = forward_dot(mlp_in, tall_low[1]) + vectors[11]
    activated, gelu_back = jax.vjp(jax.nn.gelu, inner_pre)
    activated_low = activated.astype(bf_type)
    embedding = forward_dot(activated_low, square_low[1]) + vectors[12]
    embedding_low = embedding.astype(bf_type)
    dec_in = jnp.concatenate([embedding_low[:events_here], embedding_low[events_here:]], axis=1)
    dec_pre = forward_dot(dec_in, tall_low[2]) + vectors[13]
    label_wide = labels.astype(jnp.float32)
    loss_terms, head_back = jax.vjp(
        lambda pre_rows, out_row: head_terms(pre_rows, out_row, label_wide, weights),
        dec_pre,
        vectors[14],
    )
    loss_sum, weight_sum = lax.psum((jnp.sum(loss_terms), jnp.sum(weights)), ("dp", "rep"))
    d_dec_pre, d_out_row = head_back(jnp.ones((events_here,), jnp.float32) / weight_sum)
    dec_grad_low = d_dec_pre.astype(bf_type)
    grad_dec = outer_sum(dec_in, dec_grad_low)
    d_dec_in = against(dec_grad_low, tall_low[2])
    d_embedding = jnp.concatenate([d_dec_in[:, :feat_width], d_dec_in[:, feat_width:]], axis=0)
    embed_grad_low = d_embedding.astype(bf_type)
    grad_two = outer_sum(activated_low, embed_grad_low)
    d_inner = gelu_back(against(embed_grad_low, square_low[1]))[0]
    inner_grad_low = d_inner.astype(bf_type)
    grad_one = outer_sum(mlp_in, inner_grad_low)
    d_mlp_in = against(inner_grad_low, tall_low[1])
    d_projected = d_mlp_in[:, :feat_width]
    proj_grad_low = d_projected.astype(bf_type)
    grad_out = outer_sum(attended_low, proj_grad_low)
    d_queries, d_pair_rows, d_value_bias = attend_back(against(proj_grad_low, square_low[0]))
    query_grad_low = d_queries.astype(bf_type)
    grad_query = outer_sum(query_in, query_grad_low)
    d_query_in = against(query_grad_low, tall_low[0])
    d_renewed = d_mlp_in[:, feat_width:] + d_query_in[:, :feat_width]
    d_phase_query = phase_back(jnp.sum(d_query_in[:, feat_width:], axis=0))[0]
    pair_grad_low = d_pair_rows.reshape(near_in.shape[0], -1).astype(bf_type)
    grad_pairs = outer_sum(near_in, pair_grad_low)
    d_code_near = against(pair_grad_low, w_pairs[feat_width:])
    d_freq_near, d_phase_near = near_back(d_code_near.reshape(code_near.shape))
    d_gates_in, d_gates_hid, d_gru_vectors = gru_back(d_renewed)
    gin_grad_low = d_gates_in.astype(bf_type)
    grad_gin = outer_sum(message, gin_grad_low)
    d_code_own = against(gin_grad_low, w_gin[2 * feat_width : 3 * feat_width])
    d_freq_own, d_phase_own = code_own_back(d_code_own)
    hid_grad_low = d_gates_hid.astype(bf_type)
    grad_ghid = outer_sum(own_rows, hid_grad_low)
    grad_vectors = jnp.concatenate(
        [
            jnp.stack([d_freq_own + d_freq_near, d_phase_own + d_phase_near + d_phase_query]),
            d_gru_vectors[2:8],
            jnp.stack(
                [
                    jnp.sum(d_queries, axis=0),
                    d_value_bias,
                    jnp.sum(d_projected, axis=0),
                    jnp.sum(d_inner, axis=0),
                    jnp.sum(d_embedding, axis=0),
                    jnp.sum(d_dec_pre, axis=0),
                    d_out_row,
                ]
            ),
        ],
        axis=0,
    )
    grad_tall = jnp.stack([grad_query, grad_one, grad_dec])
    grad_square = jnp.stack([grad_out, grad_two])
    grads = lax.psum(
        (grad_gin, grad_ghid, grad_pairs, grad_tall, grad_square, grad_vectors), ("dp", "rep")
    )
    params = (gru_in, gru_hid, keys_values, tall_stack, squares, vectors)
    firsts = (
        first_gru_in,
        first_gru_hid,
        first_keys_values,
        first_tall,
        first_squares,
        first_vectors,
    )
    seconds = (
        second_gru_in,
        second_gru_hid,
        second_keys_values,
        second_tall,
        second_squares,
        second_vectors,
    )
    grad_norm, new_params, new_firsts, new_seconds = adam_all(params, firsts, seconds, grads)
    update_order = jnp.concatenate([2 * event_ticks, 2 * event_ticks + 1])
    local_latest = jnp.full((node_count,), -1, jnp.int32).at[end_nodes].max(update_order)
    latest_order = lax.pmax(local_latest, ("dp", "rep"))
    winner = update_order == latest_order[end_nodes]
    local_rows = (
        jnp.zeros((node_count, feat_width), jnp.float32)
        .at[end_nodes]
        .add(jnp.where(winner[:, None], renewed, 0.0))
    )
    merged = lax.psum(local_rows, ("dp", "rep"))
    new_memory = jnp.where(latest_order[:, None] >= 0, merged, memory)
    return (
        grad_norm,
        loss_sum,
        weight_sum,
        new_memory,
        new_params[0],
        new_params[1],
        new_params[2],
        new_params[3],
        new_params[4],
        new_params[5],
        new_firsts[0],
        new_firsts[1],
        new_firsts[2],
        new_firsts[3],
        new_firsts[4],
        new_firsts[5],
        new_seconds[0],
        new_seconds[1],
        new_seconds[2],
        new_seconds[3],
        new_seconds[4],
        new_seconds[5],
    )


def solution(mesh):
    placed = (
        P(("dp", "rep")),
        P(("dp", "rep")),
        P(("dp", "rep"), None, None),
        P(("dp", "rep"), None, None),
        P(("dp", "rep")),
        P(("dp", "rep")),
        P(("dp", "rep")),
        P(("dp", "rep"), None),
        P(("dp", "rep")),
        P(),
        P(),
        P(),
        P(),
        P(),
        P(),
        P(),
        P(),
        P(),
        P(),
        P(),
        P(),
        P(),
        P(),
        P(),
        P(),
        P(),
        P(),
        P(),
        P(),
    )
    return jax.shard_map(
        body,
        mesh=mesh,
        in_specs=placed,
        out_specs=(
            P(),
            P(),
            P(),
            P(),
            P(),
            P(),
            P(),
            P(),
            P(),
            P(),
            P(),
            P(),
            P(),
            P(),
            P(),
            P(),
            P(),
            P(),
            P(),
            P(),
            P(),
            P(),
        ),
        check_vma=False,
    )
```

profile of v0, /device:TPU:0, one launch (start us, length us, event | category | flops | bytes accessed | tf_op | source)
XLA Modules:
  0.0 859.6 jit_solution(5818821651574302048)
XLA Ops:
  11.1 8.2 copy.103
  25.1 154.5 %while.11 = (s32[]{:T(128)}, bf16[22,512,172]{1,2,0:T(8,128)(2,1)}, s32[22,512]{1,0:T(8,128)S(1)}, bf16[8192,172]{1,0:T(8,128)(2,1)}, s32[]{:T(128)}) while((s32[]{:T(128)}, bf16[22,512,172]{1,2,0:T(8,128)(2,1)}, s32[22,512]{1,0:T(8,128)S(1)}, bf16[8192,172]{1,0:T(8,128)(2,1)}, s32[]{:T(128)}) %tuple.76), condition=%wide.region_1.2_spmd.clone, body=%wide.region_0.1_spmd.clone.sunk | while | flops 1447122944 | bytes 4380749 | solution.py:98
  195.2 42.4 %pmax.7 = s32[8192]{0:T(1024)S(1)} all-reduce(s32[8192]{0:T(1024)S(1)} %scatter_custom_fusion), channel_id=1, replica_groups=mesh['dp'=16,'rep'=2] {'dp','rep'}, use_global_device_ids=true, to_apply=%region_40.41 | all-reduce | flops 8192 | bytes 65536 | tf_op jit(solution)/shard_map/pmax | solution.py:303
  253.9 24.1 %cosine_convert_fusion = bf16[10240,172]{0,1:T(8,128)(2,1)S(1)} fusion(f32[172]{0:T(256)S(1)} %bitcast.165, f32[172]{0:T(256)S(1)} %bitcast.169, f32[10240]{0:T(1024)S(1)} %convert_multiply_fusion.3), kind=kLoop, calls=%fused_computation.21 | loop fusion | flops 5283840 | bytes 3564896 | tf_op jit(solution)/shard_map/convert_element_type | solution.py:201
  283.9 8.7 %fusion.9 = f32[10240,344]{1,0:T(8,128)} fusion(bf16[344,344]{1,0:T(8,128)(2,1)S(1)} %convert_element_type.123, bf16[10240,172]{0,1:T(8,128)(2,1)S(1)} %cosine_convert_fusion, bf16[10240,172]{0,1:T(8,128)(2,1)S(1)} %bitcast.143), kind=kOutput, calls=%fused_computation.25 | convolution fusion | flops 2437611520 | bytes 21372032 | tf_op jit(solution)/shard_map/dot_general | solution.py:103
  292.6 19.3 %reshape.348 = f32[1024,10,344]{2,1,0:T(8,128)} reshape(f32[10240,344]{1,0:T(8,128)} %fusion.9) | data formatting | bytes 28180480 | tf_op jit(solution)/shard_map/reshape | solution.py:203
  312.0 21.6 %fusion.110 = (f32[1024,10,172]{2,1,0:T(8,128)}, f32[1024,10,172]{2,1,0:T(8,128)}) fusion(f32[1024,10,344]{2,1,0:T(8,128)} %reshape.348), kind=kLoop, calls=%fused_computation.232 | loop fusion | bytes 28180480 | tf_op jit(solution)/shard_map/jvp()/slice | solution.py:206
  333.6 12.8 %copy.109 = f32[1024,10,172]{0,2,1:T(8,128)} copy(f32[1024,10,172]{2,1,0:T(8,128)} %get-tuple-element.204) | data formatting | bytes 14090240 | tf_op jit(solution)/shard_map/jvp()/slice | solution.py:206
  346.4 7.9 reshape.349
  367.8 12.8 %copy.146 = f32[1024,10,172]{0,2,1:T(8,128)} copy(f32[1024,10,172]{2,1,0:T(8,128)} %get-tuple-element.203) | data formatting | bytes 14090240
  410.5 40.7 %psum.63 = f32[]{:T(128)} all-reduce(f32[]{:T(128)} %get-tuple-element.161), channel_id=1, replica_groups=mesh['dp'=16,'rep'=2] {'dp','rep'}, use_global_device_ids=true, to_apply=%region_3.4 | all-reduce | flops 1 | bytes 8 | tf_op jit(solution)/shard_map/psum | solution.py:228
  462.8 8.1 multiply_bitcast_fusion.1
  489.1 7.8 reshape.352
  496.9 7.9 reshape.351
  504.8 8.9 %add_convert_fusion = bf16[1024,10,344]{0,2,1:T(8,128)(2,1)} fusion(f32[1024,10,172]{0,2,1:T(8,128)} %reshape.352, f32[1024,10,172]{0,2,1:T(8,128)} %reshape.351), kind=kLoop, calls=%fused_computation.12 | loop fusion | flops 7045120 | bytes 21135360 | tf_op jit(solution)/shard_map/convert_element_type | solution.py:249
  513.6 16.7 %copy.112 = bf16[1024,10,344]{2,1,0:T(8,128)(2,1)} copy(bf16[1024,10,344]{0,2,1:T(8,128)(2,1)} %add_convert_fusion) | data formatting | bytes 14090240 | tf_op jit(solution)/shard_map/convert_element_type | solution.py:249
  530.3 16.2 %convert_element_type.139 = bf16[10240,344]{1,0:T(8,128)(2,1)} reshape(bf16[1024,10,344]{2,1,0:T(8,128)(2,1)} %copy.112) | data formatting | bytes 14090240 | tf_op jit(solution)/shard_map/convert_element_type | solution.py:249
  546.5 10.0 %fusion.8 = f32[344,344]{1,0:T(8,128)} fusion(bf16[10240,344]{1,0:T(8,128)(2,1)} %convert_element_type.139, bf16[10240,172]{0,1:T(8,128)(2,1)} %copy-done.5, bf16[10240,172]{0,1:T(8,128)(2,1)} %bitcast.144), kind=kOutput, calls=%fused_computation.24 | convolution fusion | flops 2437611520 | bytes 14563584 | tf_op jit(solution)/shard_map/dot_general | solution.py:107
  557.7 9.9 %scatter_custom_fusion.1 = f32[8192,172]{1,0:T(8,128)} fusion(s32[1024]{0:T(1024)} %bitcast.162, f32[1024,172]{1,0:T(8,128)S(1)} %copy.113, f32[]{:T(128)} %constant.39.clone.1), kind=kCustom, calls=%fused_computation.27 | custom fusion | flops 176128 | bytes 5636608 | tf_op jit(solution)/shard_map/scatter-add | solution.py:308
  576.5 28.1 %fusion.7 = (f32[172]{0:T(256)S(1)}, f32[172]{0:T(256)S(1)}) fusion(f32[172]{0:T(256)S(1)} %bitcast.167, f32[172]{0:T(256)S(1)} %bitcast.171, f32[1024,10]{0,1:T(8,128)S(1)} %convert_multiply_fusion.2, bf16[1024,10,344]{0,2,1:T(8,128)(2,1)} %add_convert_fusion, bf16[344,344]{1,0:T(8,128)(2,1)S(1)} %copy-done.42), kind=kOutput, calls=%fused_computation.23 | convolution fusion | flops 1224089344 | bytes 7249248 | tf_op jit(solution)/shard_map/dot_general | solution.py:113
  605.5 41.9 %all-reduce.8 = (f32[15,172]{1,0:T(8,128)S(1)}, f32[]{:T(128)}) all-reduce(f32[15,172]{1,0:T(8,128)S(1)} %concatenate.85, f32[]{:T(128)} %get-tuple-element.160), channel_id=1, replica_groups=mesh['dp'=16,'rep'=2] {'dp','rep'}, use_global_device_ids=true, to_apply=%region_35.36 | all-reduce | flops 2581 | bytes 20648 | tf_op jit(solution)/shard_map/psum | solution.py:280
  648.0 156.3 %all-reduce.12.cloned.1.call-done = (f32[688,516]{0,1:T(8,128)}, f32[172,516]{1,0:T(8,128)}, f32[344,344]{1,0:T(8,128)}, f32[3,344,172]{1,2,0:T(8,128)}, f32[2,172,172]{2,1,0:T(8,128)}, /*index=5*/f32[8192,172]{1,0:T(8,128)}) async-done(((f32[688,516]{0,1:T(8,128)}, f32[172,516]{1,0:T(8,128)}, f32[344,344]{1,0:T(8,128)}, f32[3,344,172]{1,2,0:T(8,128)}, f32[2,172,172]{2,1,0:T(8,128)}, ...) | async-done | bytes 8831184 | tf_op jit(solution)/shard_map/psum | solution.py:280
  815.8 11.5 %broadcast_select_fusion = f32[8192,172]{1,0:T(8,128)} fusion(f32[8192,172]{1,0:T(8,128)} %get-tuple-element.177, f32[8192,172]{1,0:T(8,128)} %copy.103, pred[8192]{0:T(1024)(128)(4,1)S(1)} %broadcast_compare_fusion), kind=kLoop, calls=%fused_computation.29 | loop fusion | flops 1409024 | bytes 16916480 | tf_op jit(solution)/shard_map/jit(_where)/select_n | solution.py:311
  827.3 8.5 copy.119
  (377 shorter events, 307.8 us)
Async XLA Ops:
  7.2 230.3 %copy-start = (s32[8192]{0:T(1024)S(1)}, s32[8192]{0:T(1024)}, u32[]{:S(2)}) copy-start(s32[8192]{0:T(1024)} %param.41) | copy-start | bytes 98308
  7.2 797.1 %all-reduce.12.cloned.1.call-start = ((), (), s32[]{:S(2)}) async-start(), calls=%async_computation | async-start | bytes 24272896 | tf_op jit(solution)/shard_map/psum | solution.py:280
  9.0 244.9 %copy-start.85 = (f32[1,172]{1,0:T(1,128)}, f32[1,172]{1,0:T(1,128)S(1)}, u32[]{:S(2)}) copy-start(f32[1,172]{1,0:T(1,128)S(1)} %get-tuple-element.227) | copy-start | bytes 2068
  9.0 244.9 %copy-start.87 = (f32[1,172]{1,0:T(1,128)}, f32[1,172]{1,0:T(1,128)S(1)}, u32[]{:S(2)}) copy-start(f32[1,172]{1,0:T(1,128)S(1)} %get-tuple-element.228) | copy-start | bytes 2068
  182.3 172.6 %copy-start.66 = (bf16[512,172]{0,1:T(8,128)(2,1)}, bf16[512,172]{0,1:T(8,128)(2,1)S(1)}, u32[]{:S(2)}) copy-start(bf16[512,172]{0,1:T(8,128)(2,1)S(1)} %get-tuple-element.206) | copy-start | bytes 528388
  189.0 61.0 %copy-start.78 = (s32[1024]{0:T(1024)}, s32[1024]{0:T(1024)S(1)}, u32[]{:S(2)}) copy-start(s32[1024]{0:T(1024)S(1)} %get-tuple-element.231) | copy-start | bytes 12292
  189.0 60.8 %copy-start.84 = (s32[1024,1]{0,1:T(1,128)}, s32[1024,1]{0,1:T(1,128)S(1)}, u32[]{:S(2)}) copy-start(s32[1024,1]{0,1:T(1,128)S(1)} %compare_select_fusion) | copy-start | bytes 12292
  237.5 12.4 %copy-start.2 = (s32[8192]{0:T(1024)}, s32[8192]{0:T(1024)S(1)}, u32[]{:S(2)}) copy-start(s32[8192]{0:T(1024)S(1)} %pmax.7) | copy-start | bytes 98308
  250.0 32.2 %copy-start.41 = (bf16[344,344]{1,0:T(8,128)(2,1)}, bf16[344,344]{1,0:T(8,128)(2,1)S(1)}, u32[]{:S(2)}) copy-start(bf16[344,344]{1,0:T(8,128)(2,1)S(1)} %convert_element_type.123) | copy-start | bytes 710020
  250.0 28.0 %copy-start.80 = (f32[1024]{0:T(1024)}, f32[1024]{0:T(1024)S(1)}, u32[]{:S(2)}) copy-start(f32[1024]{0:T(1024)S(1)} %convert_multiply_fusion.4) | copy-start | bytes 12292
  251.2 26.8 %copy-start.4 = (bf16[20,512,172]{1,2,0:T(8,128)(2,1)S(1)}, bf16[20,512,172]{1,2,0:T(8,128)(2,1)}, u32[]{:S(2)}) copy-start(bf16[20,512,172]{1,2,0:T(8,128)(2,1)} %slice.157) | copy-start | bytes 10567684
  253.8 101.1 %copy-start.54 = (bf16[1024,172]{0,1:T(8,128)(2,1)}, bf16[1024,172]{0,1:T(8,128)(2,1)S(1)}, u32[]{:S(2)}) copy-start(bf16[1024,172]{0,1:T(8,128)(2,1)S(1)} %cosine_convert_fusion.1) | copy-start | bytes 1056772
  461.3 10.0 %slice-start = ((s8[7208960]{0:T(1024)(128)(4,1)}), s8[4194304]{0:T(1024)(128)(4,1)S(1)}, s32[]{:S(2)}) async-start(s8[7208960]{0:T(1024)(128)(4,1)} %bitcast.139), calls=%async_computation.1 | async-start | bytes 8388608
  462.8 8.5 slice-start.1
  546.5 10.1 %copy-start.24 = (f32[1024,172]{0,1:T(8,128)S(1)}, f32[1024,172]{0,1:T(8,128)}, u32[]{:S(2)}) copy-start(f32[1024,172]{0,1:T(8,128)} %get-tuple-element.196) | copy-start | bytes 2113540
  546.5 10.4 %copy-start.48 = (f32[1,172,172]{2,1,0:T(8,128)S(1)}, f32[1,172,172]{2,1,0:T(8,128)}, u32[]{:S(2)}) copy-start(f32[1,172,172]{2,1,0:T(8,128)} %convolution_bitcast_fusion.4) | copy-start | bytes 355012
  546.5 10.4 %copy-start.72 = (f32[1,172,172]{2,1,0:T(8,128)S(1)}, f32[1,172,172]{2,1,0:T(8,128)}, u32[]{:S(2)}) copy-start(f32[1,172,172]{2,1,0:T(8,128)} %convolution_bitcast_fusion.3) | copy-start | bytes 355012
  557.7 9.9 %copy-start.60 = (f32[1,344,172]{1,2,0:T(8,128)S(1)}, f32[1,344,172]{1,2,0:T(8,128)}, u32[]{:S(2)}) copy-start(f32[1,344,172]{1,2,0:T(8,128)} %convolution_bitcast_fusion) | copy-start | bytes 710020
  557.7 9.9 %copy-start.61 = (f32[1,344,172]{1,2,0:T(8,128)S(1)}, f32[1,344,172]{1,2,0:T(8,128)}, u32[]{:S(2)}) copy-start(f32[1,344,172]{1,2,0:T(8,128)} %convolution_bitcast_fusion.1) | copy-start | bytes 710020
  557.7 9.9 %copy-start.62 = (f32[1,344,172]{1,2,0:T(8,128)S(1)}, f32[1,344,172]{1,2,0:T(8,128)}, u32[]{:S(2)}) copy-start(f32[1,344,172]{1,2,0:T(8,128)} %convolution_bitcast_fusion.2) | copy-start | bytes 710020
  576.5 28.2 %copy-start.37 = (f32[512,344]{0,1:T(8,128)S(1)}, f32[512,344]{0,1:T(8,128)}, u32[]{:S(2)}) copy-start(f32[512,344]{0,1:T(8,128)} %copy-done.36) | copy-start | bytes 2113540
  576.5 28.4 %copy-start.53 = (f32[512,172]{0,1:T(8,128)S(1)}, f32[512,172]{0,1:T(8,128)}, u32[]{:S(2)}) copy-start(f32[512,172]{0,1:T(8,128)} %get-tuple-element.235) | copy-start | bytes 1056772
  576.5 28.9 %copy-start.77 = (f32[15,172]{1,0:T(8,128)S(1)}, f32[15,172]{1,0:T(8,128)}, u32[]{:S(2)}) copy-start(f32[15,172]{1,0:T(8,128)} %param.47) | copy-start | bytes 30964
  576.5 71.5 %copy-start.3 = (s32[8192]{0:T(1024)S(1)}, s32[8192]{0:T(1024)}, u32[]{:S(2)}) copy-start(s32[8192]{0:T(1024)} %copy-done.2) | copy-start | bytes 98308
  (78 other events, 283.8 us)
Sparse Core Ops, SparseCore 0:
  568.7 235.5 all-reduce.11
where the time goes:
time: 870 us; the launch traced here: 860 us
  matrix products  235 us (27%)
  local copies, waits for them, and re-layouts  193 us (22%)
  waiting for transfers between devices  156 us (18%)
  other arithmetic  129 us (15%)
  blocking collectives  125 us (14%)
  between operations  21.5 us (2%)
    psum x1, waiting for transfers between devices, body(): lax.psum((grad_gin, grad_ghid, grad_pairs, grad_tall, grad_square, grad_v...  156 us
    dot_general x22, matrix products, one_block(): jnp.dot(one_hot, mem_table, preferred_element_type=jnp.float32)  154 us
    unnamed x214, local copies, waits for them, and re-layouts  44.4 us
    pmax x1, blocking collectives, body(): latest_order = lax.pmax(local_latest, ('dp', 'rep'))  42.4 us
    psum x1, blocking collectives, body(): lax.psum((grad_gin, grad_ghid, grad_pairs, grad_tall, grad_square, grad_v...  41.9 us
    psum x1, blocking collectives, body(): lax.psum((jnp.sum(loss_terms), jnp.sum(weights)), ('dp', 'rep'))  40.7 us
    dot_general x7, matrix products, against(): lax.dot_general(grad_low, weight_low, (((1,), (1,)), ((), ())), preferred...  40 us
    convert_element_type x2, local copies, waits for them, and re-layouts, body(): pair_grad_low = d_pair_rows.reshape(near_in.shape[0], -1).astype(bf_type)  32.9 us
  transfers between devices with their start and end apart: 1, of which 1 were waited for; matrix products, arithmetic and copies ran while one was open for 4% of the time, Pallas kernels for 0%

commit v1 on v0

v1 whole, which is shorter than its diff:
```python
import math

import jax
import jax.numpy as jnp
from jax import lax
from jax.experimental import pallas as pl
from jax.experimental.pallas import tpu as pltpu
from jax.sharding import PartitionSpec as P

F32 = jnp.float32
BF = jnp.bfloat16
I32 = jnp.int32
NBR = 10
MEM = 172
PAD = 176
HALF = 86
HPAD = 88
STEP = 10
LEARN_RATE = 0.03
VECTOR_RATE = 0.3
BETA_ONE = 0.9
BETA_TWO = 0.999
ADAM_EPS = 1e-08
DECAY = 0.01
CLIP_AT = 0.005
TIME_RATE = 64.0
NORM_EPS = 1e-06
VMEM_CAP = 58 * 2**20


def params(limit=VMEM_CAP):
    return pltpu.CompilerParams(vmem_limit_bytes=limit)


def nn(a, b):
    return lax.dot_general(a, b, (((1,), (0,)), ((), ())), preferred_element_type=F32)


def nt(a, b):
    return lax.dot_general(a, b, (((1,), (1,)), ((), ())), preferred_element_type=F32)


def zeros(rows, cols):
    return jnp.zeros((rows, cols), F32)


def rows_to(x, total):
    return jnp.concatenate([x, zeros(total - x.shape[0], x.shape[1])], axis=0)


def cols_to(x, total):
    return jnp.concatenate([x, zeros(x.shape[0], total - x.shape[1])], axis=1)


def split_rows(x):
    gap = zeros(HPAD - HALF, x.shape[1])
    return jnp.concatenate([x[:HALF], gap, x[HALF:], gap], axis=0)


def prep_kernel(gin, ghid, kv, tall, sq, vec,
                wg, wgc, wh, kvm, kvct, kvc, t0t, t0, t1t, t1, t2t, t2, s0t, s0, s1t, s1, vb):
    full = gin[...]
    for gate in range(3):
        rows = full[gate * MEM : (gate + 1) * MEM]
        parts = [cols_to(rows[:, q * MEM : (q + 1) * MEM], PAD) for q in range(4)]
        wide = rows_to(jnp.concatenate(parts, axis=1), PAD)
        wg[pl.ds(gate * PAD, PAD), :] = wide.astype(BF)
        code = cols_to(rows_to(rows[:, 2 * MEM : 3 * MEM], PAD), 256)
        wgc[:, gate * PAD : (gate + 1) * PAD] = jnp.transpose(code)[:PAD].astype(BF)
    hid = ghid[...]
    for gate in range(3):
        part = cols_to(rows_to(hid[:, gate * MEM : (gate + 1) * MEM], PAD), 256)
        wh[pl.ds(gate * PAD, PAD), :] = jnp.transpose(part)[:PAD].astype(BF)
    pairs = kv[...]
    mem_t = jnp.transpose(cols_to(rows_to(pairs[:MEM], 256), 384))
    code_t = jnp.transpose(cols_to(rows_to(pairs[MEM:], 256), 384))
    kvm[...] = jnp.concatenate([split_rows(mem_t[:MEM]), split_rows(mem_t[MEM : 2 * MEM])], axis=0).astype(BF)
    code_rows = jnp.concatenate([split_rows(code_t[:MEM]), split_rows(code_t[MEM : 2 * MEM])], axis=0)
    kvct[...] = code_rows[:, :PAD].astype(BF)
    kvc[...] = jnp.transpose(rows_to(code_rows, 384))[:PAD, : 2 * PAD].astype(BF)
    query = tall[0]
    query_t = split_rows(query[:, :MEM])
    t0t[...] = cols_to(query_t, PAD).astype(BF)
    t0[...] = jnp.transpose(rows_to(cols_to(query_t, 256), 256))[:PAD, :PAD].astype(BF)
    for src, fwd, back in ((tall[1], t1t, t1), (tall[2], t2t, t2)):
        wide = jnp.concatenate([cols_to(src[:, :MEM], PAD), cols_to(src[:, MEM:], PAD)], axis=1)
        fwd[...] = rows_to(wide, PAD).astype(BF)
        back[...] = jnp.transpose(rows_to(cols_to(wide, 384), 256))[: 2 * PAD, :PAD].astype(BF)
    first = cols_to(split_rows(sq[0]), PAD)
    s0[...] = first.astype(BF)
    s0t[...] = jnp.transpose(rows_to(cols_to(first, 256), 256))[:PAD, :PAD].astype(BF)
    second = rows_to(cols_to(sq[1], PAD), PAD)
    s1[...] = second.astype(BF)
    s1t[...] = jnp.transpose(rows_to(cols_to(second, 256), 256))[:PAD, :PAD].astype(BF)
    cols = jnp.transpose(cols_to(rows_to(vec[...], 128), 256))
    phase_low = jnp.cos(cols[:PAD, 1:2]).astype(BF)
    wide_phase = jnp.broadcast_to(phase_low.astype(F32), (PAD, 128)).astype(BF)
    row_id = lax.broadcasted_iota(I32, (PAD, 128), 0)
    wide_phase = jnp.where(row_id < MEM, wide_phase.astype(F32), 0.0).astype(BF)
    steady = nn(cols_to(split_rows(query[:, MEM:]), PAD).astype(BF), wide_phase)
    for i in range(15):
        column = cols[:, i : i + 1]
        if i in (8, 9):
            column = split_rows(column[:MEM])
        wide = jnp.broadcast_to(column[:PAD], (PAD, 128))
        vb[i] = wide + steady if i == 8 else wide


def prep(gin, ghid, kv, tall, sq, vec):
    bf = lambda *s: jax.ShapeDtypeStruct(s, BF)
    outs = [bf(528, 704), bf(176, 528), bf(528, 176), bf(352, 256), bf(352, 176), bf(176, 352),
            bf(176, 176), bf(176, 176), bf(176, 352), bf(352, 176), bf(176, 352), bf(352, 176),
            bf(176, 176), bf(176, 176), bf(176, 176), bf(176, 176), jax.ShapeDtypeStruct((15, PAD, 128), F32)]
    return pl.pallas_call(
        prep_kernel, out_shape=outs, compiler_params=params(), name="prep",
    )(gin.T, ghid, kv, jnp.transpose(tall, (0, 2, 1)), sq, vec)


def table_kernel(steps, ids, mem, ticks, table, own, wide):
    step = pl.program_id(0)
    cols = mem.shape[1]

    @pl.when(step == 0)
    def _():
        wide[...] = jnp.zeros_like(wide)

    @pl.when(step < steps)
    def _():
        wide[0:MEM, :] = mem[...].astype(BF).astype(F32)
        wide[PAD : PAD + 1, :] = ticks[...].astype(F32)
        base = pl.multiple_of(step * cols, cols)
        for c in range(cols // 128):
            for h in range(2):
                table[pl.ds(base + 128 * c, 128), 128 * h : 128 * h + 128] = jnp.transpose(
                    wide[128 * h : 128 * h + 128, 128 * c : 128 * c + 128])

    @pl.when(step == steps)
    def _():
        def group(g, carry):
            for v in range(4):
                at = pl.multiple_of(g * 32 + v * 8, 8)
                rows = [table[pl.ds(ids[at + u], 1), :] for u in range(8)]
                own[pl.ds(at, 8), :] = jnp.concatenate(rows, axis=0)
            return carry

        lax.fori_loop(0, own.shape[0] // 32, group, 0)


def build_table(ids, mem_t, ticks):
    nodes = mem_t.shape[1]
    ends = ids.shape[0]
    cols = 1024
    steps = nodes // cols
    return pl.pallas_call(
        lambda *r: table_kernel(steps, *r),
        out_shape=[jax.ShapeDtypeStruct((nodes, 256), F32), jax.ShapeDtypeStruct((ends, 256), F32)],
        grid=(steps + 1,),
        in_specs=[pl.BlockSpec(memory_space=pltpu.SMEM),
                  pl.BlockSpec((MEM, cols), lambda i: (0, jnp.minimum(i, steps - 1))),
                  pl.BlockSpec((1, cols), lambda i: (0, jnp.minimum(i, steps - 1)))],
        out_specs=[pl.BlockSpec((nodes, 256), lambda i: (0, 0)), pl.BlockSpec((ends, 256), lambda i: (0, 0))],
        scratch_shapes=[pltpu.VMEM((256, cols), F32)],
        compiler_params=params(), name="table",
    )(ids, mem_t, ticks.reshape(1, nodes))


def near_kernel(chunk, ids, table, near):
    step = pl.program_id(0)
    base = step * chunk

    def group(g, carry):
        for v in range(2):
            at = pl.multiple_of(g * 32 + v * 16, 16)
            rows = [table[pl.ds(ids[base + at + u], 1), :] for u in range(16)]
            near[pl.ds(at, 16), :] = jnp.concatenate(rows, axis=0).astype(BF)
        return carry

    lax.fori_loop(0, chunk // 32, group, 0)


def gather_near(ids, table):
    chunk = 1024
    total = ids.shape[0]
    return pl.pallas_call(
        lambda *r: near_kernel(chunk, *r),
        out_shape=jax.ShapeDtypeStruct((total, 256), BF),
        grid=(total // chunk,),
        in_specs=[pl.BlockSpec(memory_space=pltpu.SMEM), pl.BlockSpec(table.shape, lambda i: (0, 0))],
        out_specs=pl.BlockSpec((chunk, 256), lambda i: (i, 0)),
        compiler_params=params(), name="near",
    )(ids, table)


PI_HI = 1.5703125
PI_MID = 4.8351287841796875e-04
PI_LO = 3.1385571319e-07
TURN = 12582912.0


def cos_sin(x):
    shifted = x * (2.0 / math.pi) + TURN
    n = shifted - TURN
    r = ((x - n * PI_HI) - n * PI_MID) - n * PI_LO
    z = r * r
    sin_r = r + r * (z * (-1.6666654611e-01 + z * (8.3321608736e-03 + z * -1.9515295891e-04)))
    cos_r = (1.0 - 0.5 * z) + (z * z) * (4.166664568298827e-02 + z * (-1.388731625493765e-03 + z * 2.443315711809948e-05))
    q = n.astype(I32)
    odd = (q & 1) == 1
    c = jnp.where(odd, sin_r, cos_r)
    s = jnp.where(odd, cos_r, sin_r)
    c = jnp.where(((q + 1) & 2) == 2, -c, c)
    s = jnp.where((q & 2) == 2, -s, s)
    return c, s


def sigmoid(x):
    return 0.5 * jnp.tanh(0.5 * x) + 0.5


def twice(x):
    return jnp.concatenate([x, x], axis=1)


def wide_rows(x, rows):
    return jnp.broadcast_to(x, (rows, x.shape[1]))


def gru_kernel(scale, own, ticks, edge, types, wg, wh, vb, msg, keep, ren, rows, gap_out):
    own_t = jnp.concatenate(
        [jnp.transpose(own[0:128, :]), jnp.transpose(own[128:256, :])], axis=1)
    gap = (twice(ticks[...].astype(F32)) - own_t[PAD : PAD + 1]) * scale
    row_id = lax.broadcasted_iota(I32, (PAD, 256), 0)
    own_x = jnp.where(row_id < MEM, own_t[:PAD], 0.0)
    msg[0:PAD, :] = own_x.astype(BF)
    msg[PAD : 2 * PAD, :] = jnp.concatenate([own_x[:, 128:], own_x[:, :128]], axis=1).astype(BF)
    edges = rows_to(edge[...].astype(F32) * types[...].astype(F32), PAD)
    msg[3 * PAD : 4 * PAD, :] = twice(edges).astype(BF)
    gap_out[...] = wide_rows(gap, 8)
    gap16 = wide_rows(gap, 16)
    for st in range(PAD // 16):
        at = 16 * st
        x = twice(vb[0, at : at + 16, :]) * gap16 + twice(vb[1, at : at + 16, :])
        c, s = cos_sin(x)
        msg[2 * PAD + at : 2 * PAD + at + 16, :] = c.astype(BF)
        keep[4, at : at + 16, :] = -s
    gates = nn(wg[...], msg[...])
    hidden = nn(wh[...], msg[0:PAD, :])
    for st in range(PAD // 8):
        at = 8 * st
        o = own_x[at : at + 8]
        pre = [gates[g * PAD + at : g * PAD + at + 8] + twice(vb[2 + g, at : at + 8, :]) for g in range(3)]
        hid = [hidden[g * PAD + at : g * PAD + at + 8] + twice(vb[5 + g, at : at + 8, :]) for g in range(3)]
        u = sigmoid(pre[0] + hid[0])
        r = sigmoid(pre[1] + hid[1])
        n = jnp.tanh(pre[2] + r * hid[2])
        keep[0, at : at + 8, :] = u
        keep[1, at : at + 8, :] = r
        keep[2, at : at + 8, :] = n
        keep[3, at : at + 8, :] = hid[2]
        ren[at : at + 8, :] = (1.0 - u) * n + u * o
    full = jnp.concatenate([ren[...], zeros(256 - PAD, 256)], axis=0)
    rows[0:128, :] = jnp.transpose(full[:, :128])
    rows[128:256, :] = jnp.transpose(full[:, 128:])


def gru(scale, own, ticks, edge_t, types, wg, wh, vb):
    ends = own.shape[0]
    blocks = ends // 256
    whole = lambda a: pl.BlockSpec(a.shape, lambda i: (0,) * len(a.shape))
    return pl.pallas_call(
        lambda *r: gru_kernel(scale, *r),
        out_shape=[jax.ShapeDtypeStruct((4 * PAD, ends), BF), jax.ShapeDtypeStruct((5, PAD, ends), F32),
                   jax.ShapeDtypeStruct((PAD, ends), F32), jax.ShapeDtypeStruct((ends, 256), F32),
                   jax.ShapeDtypeStruct((8, ends), F32)],
        grid=(blocks,),
        in_specs=[pl.BlockSpec((256, 256), lambda i: (i, 0)), pl.BlockSpec((1, 128), lambda i: (0, i)),
                  pl.BlockSpec((MEM, 128), lambda i: (0, i)), pl.BlockSpec((1, 128), lambda i: (0, i)),
                  whole(wg), whole(wh), whole(vb)],
        out_specs=[pl.BlockSpec((4 * PAD, 256), lambda i: (0, i)), pl.BlockSpec((5, PAD, 256), lambda i: (0, 0, i)),
                   pl.BlockSpec((PAD, 256), lambda i: (0, i)), pl.BlockSpec((256, 256), lambda i: (i, 0)),
                   pl.BlockSpec((8, 256), lambda i: (0, i))],
        compiler_params=params(), name="gru",
    )(own, ticks, edge_t, types, wg, wh, vb)


GELU_C = math.sqrt(2.0 / math.pi)


def gelu_parts(x):
    sq = x * x
    t = jnp.tanh(GELU_C * (x + 0.044715 * (sq * x)))
    half = 0.5 * (1.0 + t)
    slope = half + (0.5 * x) * (1.0 - t * t) * (GELU_C + (GELU_C * 3.0 * 0.044715) * sq)
    return x * half, slope


def fold(x):
    return x[:, :128] + x[:, 128:]


def main_kernel(scale, near, gaps_t, ticks, msg, keep, ren, gap_own, labels, weights, total,
                wgc, kvm, kvct, kvc, t0t, t0, t1t, t1, t2t, t2, s0t, s0, s1t, s1, vb,
                ga, gb, loss,
                pair, code, dcode, soft, back, grads, g_in, g_kv, g_one, g_dec, g_qo, g_th, vacc):
    step = pl.program_id(0)
    inv_size = HALF ** -0.5

    @pl.when(step == 0)
    def _():
        for ref in (g_in, g_kv, g_one, g_dec, g_qo, g_th, vacc, loss):
            ref[...] = jnp.zeros_like(ref)

    tick2 = twice(ticks[...].astype(F32))
    renewed = ren[...]
    ren_low = renewed.astype(BF)
    queries = nn(t0t[...], ren_low) + twice(vb[8])
    for j in range(NBR):
        gap16 = wide_rows((tick2 - gaps_t[j : j + 1, :].astype(F32)) * scale, 16)
        for st in range(PAD // 16):
            at = 16 * st
            x = twice(vb[0, at : at + 16, :]) * gap16 + twice(vb[1, at : at + 16, :])
            c, s = cos_sin(x)
            code[j, at : at + 16, :] = c.astype(BF)
            dcode[j, at : at + 16, :] = -s
        pair[j] = nt(kvm[...], near[j]) + nn(kvct[...], code[j])
        for h in range(2):
            acc = zeros(8, 256)
            for st in range(HPAD // 8):
                at = HPAD * h + 8 * st
                acc = acc + pair[j, at : at + 8, :] * queries[at : at + 8]
            soft[2 * j + h] = wide_rows(jnp.sum(acc, axis=0, keepdims=True) * inv_size, 8)
    for h in range(2):
        top = soft[h]
        for j in range(1, NBR):
            top = jnp.maximum(top, soft[2 * j + h])
        norm = zeros(8, 256)
        for j in range(NBR):
            e = jnp.exp(soft[2 * j + h] - top)
            soft[2 * j + h] = e
            norm = norm + e
        inv = 1.0 / norm
        for j in range(NBR):
            soft[2 * j + h] = soft[2 * j + h] * inv
    att = []
    for st in range(PAD // 8):
        at = 8 * st
        h = 0 if at < HPAD else 1
        acc = twice(vb[9, at : at + 8, :])
        for j in range(NBR):
            acc = acc + soft[2 * j + h] * pair[j, PAD + at : PAD + at + 8, :]
        att.append(acc)
    att_low = jnp.concatenate(att, axis=0).astype(BF)
    projected = nn(s0t[...], att_low) + twice(vb[10])
    mlp_in = jnp.concatenate([projected.astype(BF), ren_low], axis=0)
    inner = nn(t1t[...], mlp_in) + twice(vb[11])
    act, act_slope = gelu_parts(inner)
    act_low = act.astype(BF)
    emb_low = (nn(s1t[...], act_low) + twice(vb[12])).astype(BF)
    dec_in = jnp.concatenate([emb_low[:, :128], emb_low[:, 128:]], axis=0)
    dec_pre = nn(t2t[...], dec_in) + vb[13]
    dec_act, dec_slope = gelu_parts(dec_pre)
    logit = jnp.sum(dec_act * vb[14], axis=0, keepdims=True)
    label = labels[...].astype(F32)
    tail = jnp.exp(-jnp.abs(logit))
    plus = jnp.maximum(logit, 0.0) + jnp.log1p(tail)
    loss[...] += weights[...] * (plus - label * logit)
    d_logit = weights[...] / total[...] * (sigmoid(logit) - label)
    d_out = d_logit * dec_act
    d_dec = (d_logit * vb[14]) * dec_slope
    d_dec_low = d_dec.astype(BF)
    g_dec[...] += nt(d_dec_low, dec_in)
    d_dec_in = nn(t2[...], d_dec_low)
    d_emb = jnp.concatenate([d_dec_in[:PAD], d_dec_in[PAD:]], axis=1)
    d_emb_low = d_emb.astype(BF)
    g_th[:, 0:256] += jnp.concatenate([nt(act_low, d_emb_low), zeros(PAD, 256 - PAD)], axis=1)
    d_inner = nn(s1[...], d_emb_low) * act_slope
    d_inner_low = d_inner.astype(BF)
    g_one[...] += nt(d_inner_low, mlp_in)
    d_mlp = nn(t1[...], d_inner_low)
    d_proj = d_mlp[:PAD]
    d_proj_low = d_proj.astype(BF)
    g_qo[:, 256:512] += jnp.concatenate([nt(att_low, d_proj_low), zeros(PAD, 256 - PAD)], axis=1)
    d_att = nn(s0[...], d_proj_low)
    for h in range(2):
        mean = zeros(8, 256)
        for j in range(NBR):
            acc = zeros(8, 256)
            for st in range(HPAD // 8):
                at = HPAD * h + 8 * st
                acc = acc + pair[j, PAD + at : PAD + at + 8, :] * d_att[at : at + 8]
            wide = wide_rows(jnp.sum(acc, axis=0, keepdims=True), 8)
            back[2 * j + h] = wide
            mean = mean + wide * soft[2 * j + h]
        for j in range(NBR):
            back[2 * j + h] = (soft[2 * j + h] * inv_size) * (back[2 * j + h] - mean)
    d_q = []
    for st in range(PAD // 8):
        at = 8 * st
        h = 0 if at < HPAD else 1
        acc = zeros(8, 256)
        for j in range(NBR):
            acc = acc + back[2 * j + h] * pair[j, at : at + 8, :]
        d_q.append(acc)
    d_query = jnp.concatenate(d_q, axis=0)
    for j in range(NBR):
        for st in range(2 * PAD // 16):
            parts = []
            for half in range(2):
                at = 16 * st + 8 * half
                if at < PAD:
                    parts.append(back[2 * j + (at >= HPAD)] * queries[at : at + 8])
                else:
                    parts.append(soft[2 * j + (at - PAD >= HPAD)] * d_att[at - PAD : at - PAD + 8])
            grads[16 * st : 16 * st + 16, 256 * j : 256 * j + 256] = jnp.concatenate(parts, axis=0).astype(BF)
    d_codes = nn(kvc[...], grads[...])
    for st in range(PAD // 8):
        at = 8 * st
        f_acc = zeros(8, 256)
        p_acc = zeros(8, 256)
        for j in range(NBR):
            gap8 = wide_rows((tick2 - gaps_t[j : j + 1, :].astype(F32)) * scale, 8)
            d_arg = d_codes[at : at + 8, 256 * j : 256 * j + 256] * dcode[j, at : at + 8, :]
            f_acc = f_acc + d_arg * gap8
            p_acc = p_acc + d_arg
        vacc[0, at : at + 8, :] += fold(f_acc)
        vacc[1, at : at + 8, :] += fold(p_acc)
    mem_part = nn(grads[:, 0:256], near[0])
    code_part = nt(grads[:, 0:256], code[0])
    for j in range(1, NBR):
        mem_part = mem_part + nn(grads[:, 256 * j : 256 * j + 256], near[j])
        code_part = code_part + nt(grads[:, 256 * j : 256 * j + 256], code[j])
    g_kv[:, 0:256] += mem_part
    g_kv[:, 256:512] += jnp.concatenate([code_part, zeros(2 * PAD, 256 - PAD)], axis=1)
    d_q_low = d_query.astype(BF)
    g_qo[:, 0:256] += jnp.concatenate([nt(d_q_low, ren_low), zeros(PAD, 256 - PAD)], axis=1)
    d_ren = d_mlp[PAD:] + nn(t0[...], d_q_low)
    own_x = msg[0:PAD, :].astype(F32)
    u, r, n, hn = keep[0], keep[1], keep[2], keep[3]
    d_u = d_ren * (own_x - n) * (u * (1.0 - u))
    d_n = d_ren * (1.0 - u) * (1.0 - n * n)
    d_r = d_n * hn * (r * (1.0 - r))
    d_h = d_n * r
    gates = jnp.concatenate([d_u, d_r, d_n], axis=0).astype(BF)
    g_in[...] += nt(gates, msg[...])
    g_th[:, 256:512] += jnp.concatenate([nt(msg[0:PAD, :], d_h.astype(BF)), zeros(PAD, 256 - PAD)], axis=1)
    d_arg = nn(wgc[...], gates) * keep[4]
    vacc[0] += fold(d_arg * gap_own[0:1, :])
    vacc[1] += fold(d_arg)
    for i, item in ((2, d_u), (3, d_r), (4, d_n), (7, d_h), (8, d_query), (9, d_att), (10, d_proj), (11, d_inner),
                    (12, d_emb), (15, d_q_low.astype(F32))):
        vacc[i] += fold(item)
    vacc[13] += d_dec
    vacc[14] += d_out

    @pl.when(step == pl.num_programs(0) - 1)
    def _():
        wide = cols_to(g_in[...], 768)
        for c in range(6):
            gb[528 * c : 528 * c + 528, :] = wide[:, 128 * c : 128 * c + 128]
        lane = lax.broadcasted_iota(I32, (PAD, 128), 1)
        vecs = zeros(PAD, 128)
        for i in range(16):
            column = jnp.sum(vacc[i], axis=1, keepdims=True)
            vecs = jnp.where(lane == i, column, vecs)
        flat = jnp.transpose(jnp.concatenate([vecs, zeros(256 - PAD, 128)], axis=0))
        gb[3168:3184, :] = flat[0:16, 0:128]
        gb[3184:3200, :] = flat[0:16, 128:256]
        at = 0
        for left, right, rows in ((g_kv[:, 0:PAD], g_kv[:, 256 : 256 + PAD], 352),
                                  (g_one[:, 0:PAD], g_one[:, PAD : 2 * PAD], 176),
                                  (g_dec[:, 0:PAD], g_dec[:, PAD : 2 * PAD], 176),
                                  (g_qo[:, 0:PAD], g_qo[:, 256 : 256 + PAD], 176),
                                  (g_th[:, 0:PAD], g_th[:, 256 : 256 + PAD], 176)):
            wide = jnp.concatenate([left, right, zeros(rows, 32)], axis=1)
            for c in range(3):
                ga[at : at + rows, :] = wide[:, 128 * c : 128 * c + 128]
                at += rows
        ga[3168:3200, :] = zeros(32, 128)


def main(scale, near, near_ticks, ticks, msg, keep, ren, gap_own, labels, weights, total, w):
    ends = ren.shape[1]
    blocks = ends // 256
    whole = lambda a: pl.BlockSpec(a.shape, lambda i: (0,) * len(a.shape))
    lanes = lambda: pl.BlockSpec((1, 128), lambda i: (0, i))
    return pl.pallas_call(
        lambda *r: main_kernel(scale, *r),
        out_shape=[jax.ShapeDtypeStruct((3200, 128), F32), jax.ShapeDtypeStruct((3200, 128), F32),
                   jax.ShapeDtypeStruct((1, 128), F32)],
        grid=(blocks,),
        in_specs=[pl.BlockSpec((NBR, 256, 256), lambda i: (0, i, 0)), pl.BlockSpec((NBR, 256), lambda i: (0, i)), lanes(),
                  pl.BlockSpec((4 * PAD, 256), lambda i: (0, i)), pl.BlockSpec((5, PAD, 256), lambda i: (0, 0, i)),
                  pl.BlockSpec((PAD, 256), lambda i: (0, i)), pl.BlockSpec((8, 256), lambda i: (0, i)), lanes(), lanes(),
                  pl.BlockSpec((1, 128), lambda i: (0, 0))] + [whole(a) for a in w],
        out_specs=[pl.BlockSpec((3200, 128), lambda i: (0, 0)), pl.BlockSpec((3200, 128), lambda i: (0, 0)),
                   pl.BlockSpec((1, 128), lambda i: (0, 0))],
        scratch_shapes=[pltpu.VMEM((NBR, 352, 256), F32), pltpu.VMEM((NBR, PAD, 256), BF), pltpu.VMEM((NBR, PAD, 256), F32),
                        pltpu.VMEM((20, 8, 256), F32), pltpu.VMEM((20, 8, 256), F32), pltpu.VMEM((352, 2560), BF),
                        pltpu.VMEM((528, 704), F32), pltpu.VMEM((352, 512), F32), pltpu.VMEM((PAD, 352), F32),
                        pltpu.VMEM((PAD, 352), F32), pltpu.VMEM((PAD, 512), F32), pltpu.VMEM((PAD, 512), F32),
                        pltpu.VMEM((16, PAD, 128), F32)],
        compiler_params=params(), name="main",
    )(near.reshape(NBR, ends, 256), near_ticks, ticks, msg, keep, ren, gap_own, labels, weights, total, *w)


def panels(flat, at, rows, count):
    return jnp.concatenate([flat[at + c * rows : at + (c + 1) * rows] for c in range(count)], axis=1)


def unsplit(x, axis):
    take = lambda a, b: lax.slice_in_dim(x, a, b, axis=axis)
    return jnp.concatenate([take(0, HALF), take(HPAD, HPAD + HALF)], axis=axis)


def unpack(ga, gb, vec):
    wide = panels(gb, 0, 528, 6)[:, :704].reshape(3, PAD, 4, PAD)[:, :MEM, :, :MEM].reshape(3 * MEM, 4 * MEM)
    vecs = jnp.concatenate([gb[3168:3184], gb[3184:3200]], axis=1)[:, :PAD]
    kv = panels(ga, 0, 352, 3)
    kv_out = jnp.concatenate([unsplit(kv[:PAD], 0), unsplit(kv[PAD:], 0)], axis=0)
    kv_out = jnp.concatenate([kv_out[:, :MEM], kv_out[:, PAD : PAD + MEM]], axis=1).T
    pick = lambda x: jnp.concatenate([x[:MEM, :MEM], x[:MEM, PAD : PAD + MEM]], axis=1)
    one = pick(panels(ga, 1056, PAD, 3))
    dec = pick(panels(ga, 1584, PAD, 3))
    qo = panels(ga, 2112, PAD, 3)
    th = panels(ga, 2640, PAD, 3)
    query_t = unsplit(qo[:, :MEM], 0)
    out = unsplit(qo[:, PAD : PAD + MEM], 0)[:, :MEM]
    two = th[:MEM, :MEM]
    hid_n = th[:MEM, PAD : PAD + MEM]
    phase = vec[1]
    phase_low = jnp.cos(phase).astype(BF).astype(F32)
    sum_dq = unsplit(vecs[15], 0)
    query = jnp.concatenate([query_t.T, phase_low[:, None] * sum_dq[None, :]], axis=0)
    grad_in = wide.T
    hid = jnp.concatenate([grad_in[:MEM, : 2 * MEM], hid_n], axis=1)
    tall = jnp.stack([query, one.T, dec.T])
    rows = [vecs[0, :MEM], vecs[1, :MEM], vecs[2, :MEM], vecs[3, :MEM], vecs[4, :MEM], vecs[2, :MEM], vecs[3, :MEM],
            vecs[7, :MEM], unsplit(vecs[8], 0), unsplit(vecs[9], 0)] + [vecs[i, :MEM] for i in range(10, 15)]
    return grad_in, hid, kv_out, tall, jnp.stack([out, two]), jnp.stack(rows), sum_dq


def adam_all(params_in, firsts, seconds, grads):
    squares_sum = jnp.zeros((), F32)
    for item in grads:
        squares_sum = squares_sum + jnp.sum(item * item)
    grad_norm = jnp.sqrt(squares_sum)
    factor = jnp.minimum(1.0, CLIP_AT / (grad_norm + NORM_EPS))
    new_params, new_firsts, new_seconds = [], [], []
    for at in range(len(params_in)):
        clipped = grads[at] * factor
        one = BETA_ONE * firsts[at] + (1.0 - BETA_ONE) * clipped
        two = BETA_TWO * seconds[at] + (1.0 - BETA_TWO) * clipped * clipped
        move = one / (1.0 - BETA_ONE**STEP) / (jnp.sqrt(two / (1.0 - BETA_TWO**STEP)) + ADAM_EPS)
        last = at == len(params_in) - 1
        decay, rate = (0.0, VECTOR_RATE) if last else (DECAY, LEARN_RATE)
        new_params.append(params_in[at] - rate * (move + decay * params_in[at]))
        new_firsts.append(one)
        new_seconds.append(two)
    return grad_norm, new_params, new_firsts, new_seconds


AXES = ("dp", "rep")


def body(source, target, neighbours, neighbour_ticks, event_ticks, event_types, labels, edge_feats, weights, memory,
         node_ticks, gru_in, gru_hid, keys_values, tall_stack, squares, vectors, *moments):
    events = event_ticks.shape[0]
    nodes = memory.shape[0]
    devices = lax.axis_size("dp") * lax.axis_size("rep")
    scale = TIME_RATE / (events * devices)
    tiles = events // 128
    order = lambda x: jnp.transpose(x, (2, 1, 0)).reshape(NBR, 2, tiles, 128).transpose(0, 2, 1, 3).reshape(NBR, 2 * events)
    end_nodes = jnp.stack([source.reshape(tiles, 128), target.reshape(tiles, 128)], axis=1).reshape(-1)
    near_ids = order(neighbours).reshape(-1)
    near_ticks = order(neighbour_ticks)
    row = lambda x: x.reshape(1, events)
    mem_t = memory.T
    w = prep(gru_in, gru_hid, keys_values, tall_stack, squares, vectors)
    wg, wgc, wh = w[0], w[1], w[2]
    vb = w[-1]
    table, own = build_table(end_nodes, mem_t, node_ticks)
    msg, keep, ren, ren_rows, gap_own = gru(scale, own, row(event_ticks), edge_feats.T, row(event_types), wg, wh, vb)
    near = gather_near(near_ids, table)
    weight_sum = lax.psum(jnp.sum(weights), AXES)
    ga, gb, loss = main(scale, near, near_ticks, row(event_ticks), msg, keep, ren, gap_own, row(labels), row(weights),
                        jnp.full((1, 128), weight_sum, F32), [wgc] + list(w[3:]))
    ga, gb, loss_sum = lax.psum((ga, gb, jnp.sum(loss)), AXES)
    grad_in, hid, kv, tall, square, vec, sum_dq = unpack(ga, gb, vectors)
    phase_in = jnp.sum(tall_stack[0][MEM:].astype(BF).astype(F32) * sum_dq[None, :], axis=1)
    vec = vec.at[1].add(-jnp.sin(vectors[1]) * phase_in)
    grad_norm, new_p, new_f, new_s = adam_all(
        (gru_in, gru_hid, keys_values, tall_stack, squares, vectors), moments[:6], moments[6:],
        (grad_in, hid, kv, tall, square, vec))
    ticks2 = jnp.stack([2 * event_ticks.reshape(tiles, 128), 2 * event_ticks.reshape(tiles, 128) + 1], axis=1).reshape(-1)
    local = jnp.full((nodes,), -1, I32).at[end_nodes].max(ticks2)
    latest = lax.pmax(local, AXES)
    winner = ticks2 == latest[end_nodes]
    rows = jnp.zeros((nodes, MEM), F32).at[end_nodes].add(jnp.where(winner[:, None], ren_rows[:, :MEM], 0.0))
    merged = lax.psum(rows, AXES)
    new_memory = jnp.where(latest[:, None] >= 0, merged, memory)
    return (grad_norm, loss_sum, weight_sum, new_memory, *new_p, *new_f, *new_s)


def solution(mesh):
    split = P(AXES)
    placed = (split, split, P(AXES, None, None), P(AXES, None, None), split, split, split, P(AXES, None), split)
    return jax.shard_map(body, mesh=mesh, in_specs=placed + (P(),) * 20, out_specs=(P(),) * 22, check_vma=False)
```

time: 870 us -> 522 us (0.60); the launches traced: 860 us -> 520 us
  matrix products: 235 us -> 0 us
  local copies, waits for them, and re-layouts: 193 us -> 62.1 us
  Pallas kernels: 0 us -> 86.9 us
  other arithmetic: 129 us -> 59.6 us
  waiting for transfers between devices: 156 us -> 168 us
    dot_general x45 -> x0, matrix products: 235 us -> none  [the longest x22 154 us: one_block(): jnp.dot(one_hot, mem_table, preferred_element_type=jnp.float32)]
    pallas_call x0 -> x5, Pallas kernels: none -> 86.9 us  [the longest x1 35.6 us: main(): pl.pallas_call(lambda *r: main_kernel(scale, *r), out_shape=[jax.ShapeDty...]
    reshape x11 -> x3, local copies, waits for them, and re-layouts: 52.8 us -> 7.2 us  [the longest x2 5.75 us: unpack(): panels(gb, 0, 528, 6)[:, :704].reshape(3, PAD, 4, PAD)[:, :MEM, :, :MEM]]
    convert_element_type x10 -> x0, other arithmetic: 42.6 us -> none  [the longest x1 24.1 us: body(): code_near.astype(bf_type).reshape(near_rows.shape)]
    slice x13 -> x9, local copies, waits for them, and re-layouts: 45.6 us -> 5.33 us  [the longest x2 3.3 us: panels(): flat[at + c * rows:at + (c + 1) * rows]]
    convert_element_type x4 -> x0, local copies, waits for them, and re-layouts: 34.7 us -> none  [the longest x2 32.9 us: body(): pair_grad_low = d_pair_rows.reshape(near_in.shape[0], -1).astype(bf_type)]
    transpose x2 -> x0, other arithmetic: 12.2 us -> none  [the longest x1 8.06 us: attend(): jnp.einsum('rhj,rjhd->rhd', attn_weights, heads_v, precision=HIGHEST)]
    psum x1, waiting for transfers between devices: 156 us -> 168 us  [body(): ga, gb, loss_sum = lax.psum((ga, gb, jnp.sum(loss)), AXES)]
  transfers between devices with their start and end apart: 1 -> 1, of which waited for: 1 -> 1; matrix products, arithmetic and copies ran while one was open for 4% -> 3% of each run, Pallas kernels for 0% -> 0%
where the time goes in v1:
time: 522 us; the launch traced here: 520 us
  waiting for transfers between devices  168 us (32%)
  blocking collectives  124 us (24%)
  Pallas kernels  86.9 us (17%)
  local copies, waits for them, and re-layouts  62.1 us (12%)
  other arithmetic  59.6 us (11%)
  between operations  19.6 us (4%)
    psum x1, waiting for transfers between devices, body(): ga, gb, loss_sum = lax.psum((ga, gb, jnp.sum(loss)), AXES)  168 us
    psum x1, blocking collectives, body(): weight_sum = lax.psum(jnp.sum(weights), AXES)  42.2 us
    unnamed x75, local copies, waits for them, and re-layouts  41.9 us
    psum x1, blocking collectives, body(): ga, gb, loss_sum = lax.psum((ga, gb, jnp.sum(loss)), AXES)  41.6 us
    pmax x1, blocking collectives, body(): latest = lax.pmax(local, AXES)  40.5 us
    pallas_call x1, Pallas kernels, main(): pl.pallas_call(lambda *r: main_kernel(scale, *r), out_shape=[jax.ShapeDty...  35.6 us
    pallas_call x1, Pallas kernels, gather_near(): pl.pallas_call(lambda *r: near_kernel(chunk, *r), out_shape=jax.ShapeDtyp...  26.2 us
    sub x6, other arithmetic, adam_all(): new_params.append(params_in[at] - rate * (move + decay * params_in[at]))  15.8 us
  transfers between devices with their start and end apart: 1, of which 1 were waited for; matrix products, arithmetic and copies ran while one was open for 3% of the time, Pallas kernels for 0%

profile of v1, /device:TPU:0, one launch (start us, length us, event | category | flops | bytes accessed | tf_op | source)
XLA Modules:
  0.0 520.4 jit_solution(11419004817157417308)
XLA Ops:
  11.7 42.2 %psum.35 = f32[]{:T(128)} all-reduce(f32[]{:T(128)} %reduce_sum.83), channel_id=1, replica_groups=mesh['dp'=16,'rep'=2] {'dp','rep'}, use_global_device_ids=true, to_apply=%region_1.0 | all-reduce | flops 1 | bytes 8 | tf_op jit(solution)/shard_map/psum | solution.py:584
  55.3 6.1 %scatter_custom_fusion = s32[8192]{0:T(1024)S(1)} fusion(s32[1024]{0:T(1024)S(1)} %bitcast.97, s32[1024]{0:T(1024)S(1)} %bitcast.99, s32[]{:T(128)} %constant.41.clone.1), kind=kCustom, calls=%fused_computation.100 | custom fusion | flops 1024 | bytes 32772 | tf_op jit(solution)/shard_map/scatter-max | solution.py:595
  61.4 40.5 %pmax.7 = s32[8192]{0:T(1024)S(1)} all-reduce(s32[8192]{0:T(1024)S(1)} %scatter_custom_fusion), channel_id=1, replica_groups=mesh['dp'=16,'rep'=2] {'dp','rep'}, use_global_device_ids=true, to_apply=%region_14.0 | all-reduce | flops 8192 | bytes 65536 | tf_op jit(solution)/shard_map/pmax | solution.py:596
  101.9 6.2 %gather_fusion = s32[1024]{0:T(1024)S(1)} fusion(s32[8192]{0:T(1024)S(1)} %pmax.7, s32[1024]{0:T(1024)S(1)} %broadcast_clamp_fusion), kind=kCustom, calls=%fused_computation | custom fusion | bytes 12288 | tf_op jit(solution)/shard_map/gather | solution.py:597
  108.1 12.2 %table.1 = (f32[8192,256]{1,0:T(8,128)}, f32[1024,256]{1,0:T(8,128)}) custom-call(s32[1024]{0:T(1024)} %bitcast.90, f32[172,8192]{1,0:T(8,128)} %bitcast.80, s32[1,8192]{1,0:T(1,128)} %bitcast.91), custom_call_target="tpu_custom_call" | custom-call | tf_op jit(solution)/shard_map/table/pallas_call | solution.py:154
  120.3 26.2 %near.1 = bf16[10240,256]{1,0:T(8,128)(2,1)} custom-call(s32[10240]{0:T(1024)} %bitcast.87, f32[8192,256]{1,0:T(8,128)} %get-tuple-element.61.r_1_), custom_call_target="tpu_custom_call" | custom-call | tf_op jit(solution)/shard_map/near/pallas_call | solution.py:184
  146.5 6.1 %prep.1 = (bf16[528,704]{1,0:T(8,128)(2,1)}, bf16[176,528]{1,0:T(8,128)(2,1)}, bf16[528,176]{1,0:T(8,128)(2,1)}, bf16[352,256]{1,0:T(8,128)(2,1)}, bf16[352,176]...) custom-call(f32[516,688]{1,0:T(8,128)} %bitcast.83, ...), custom_call_target="tpu_custom_call" | custom-call | tf_op jit(solution)/shard_map/prep/pallas_call | solution.py:114
  152.6 6.8 %gru.1 = (bf16[704,1024]{1,0:T(8,128)(2,1)}, f32[5,176,1024]{2,1,0:T(8,128)}, f32[176,1024]{1,0:T(8,128)}, f32[1024,256]{1,0:T(8,128)}, f32[8,1024]{1,0:T(8,128)}) custom-call(f32[1024,256]{1,0:T(8,128)} %get-tuple-element.62.r_0_, s32[1,512]{1,0:T(1,128)} %bitcast.92, bf16[172,512]{1,0:T(8,128)(2,1)} %bitcast.86, s32[1,512]{1,0:T(1,128)} %bitcast.106, ...), custom_call_target="tpu_custom_call" | custom-call | tf_op jit(solution)/shard_map/gru/pallas_call | solution.py:270
  159.4 10.8 %scatter_custom_fusion.1 = f32[8192,172]{1,0:T(8,128)} fusion(s32[1024]{0:T(1024)S(1)} %bitcast.98, f32[]{:T(128)} %constant.38.clone.1, f32[1024,256]{1,0:T(8,128)} %get-tuple-element.87, pred[1024]{0:T(1024)(128)(4,1)S(1)} %eq.7), kind=kCustom, calls=%fused_computation.3 | custom fusion | flops 352256 | bytes 6686720 | tf_op jit(solution)/shard_map/scatter-add | solution.py:598
  171.4 35.6 %main.1 = (f32[3200,128]{1,0:T(8,128)}, f32[3200,128]{1,0:T(8,128)}, f32[1,128]{1,0:T(1,128)}) custom-call(bf16[10,1024,256]{2,1,0:T(8,128)(2,1)} %bitcast.81, s32[10,1024]{1,0:T(8,128)} %reshape.197.r_1_, s32[1,512]{1,0:T(1,128)} %bitcast.93, bf16[704,1024]{1,0:T(8,128)(2,1)} %get-tuple-element.66.r_3_, f32[5,176,1024]{2,1,0:T(8,128)} %get-tuple-element.67.r_4_, ...), custom_call_target="tpu_custom_call" | custom-call | tf_op jit(solution)/shard_map/main/pallas_call | solution.py:486
  208.3 41.6 %psum.38 = f32[]{:T(128)} all-reduce(f32[]{:T(128)} %reduce_sum.92), channel_id=1, replica_groups=mesh['dp'=16,'rep'=2] {'dp','rep'}, use_global_device_ids=true, to_apply=%region_12.0 | all-reduce | flops 1 | bytes 8 | tf_op jit(solution)/shard_map/psum | solution.py:587
  249.8 8.4 %copy.79 = f32[8192,172]{1,0:T(8,128)} copy(f32[8192,172]{0,1:T(8,128)} %param.40) | data formatting | bytes 11272192 | tf_op args[9]
  264.9 167.9 %all-reduce.3.cloned.1.call-done = (f32[3200,128]{1,0:T(8,128)}, f32[3200,128]{1,0:T(8,128)}, f32[8192,172]{1,0:T(8,128)}) async-done(((f32[3200,128]{1,0:T(8,128)}, f32[3200,128]{1,0:T(8,128)}, f32[8192,172]{1,0:T(8,128)}), (f32[3200,128]{1,0:T(8,128)}, f32[3200,128]{1,0:T(8,128)}, f32[8192,172]{1,0:T(8,128)})) %all-reduce.3.cloned.1.call-update) | async-done | bytes 8912912 | tf_op jit(solution)/shard_map/psum | solution.py:587
  432.8 2.2 fusion.46
  437.6 3.1 reshape.202
  442.4 2.7 reshape.203
  461.4 11.3 %broadcast_select_fusion = f32[8192,172]{1,0:T(8,128)} fusion(f32[8192,172]{1,0:T(8,128)} %get-tuple-element.134, f32[8192,172]{1,0:T(8,128)} %copy.79, pred[8192]{0:T(1024)(128)(4,1)} %broadcast_compare_fusion), kind=kLoop, calls=%fused_computation.5 | loop fusion | flops 1409024 | bytes 16916480 | tf_op jit(solution)/shard_map/jit(_where)/select_n | solution.py:600
  472.6 8.5 %copy.92 = f32[8192,172]{0,1:T(8,128)} copy(f32[8192,172]{1,0:T(8,128)} %broadcast_select_fusion) | data formatting | bytes 11272192
  481.2 2.8 multiply_subtract_fusion.2
  486.0 2.9 multiply_subtract_fusion.3
  488.9 2.1 copy.94
  491.0 2.5 multiply_subtract_fusion.4
  496.5 2.1 copy.98
  504.7 5.1 multiply_subtract_fusion
  (119 shorter events, 45.1 us)
Async XLA Ops:
  7.2 425.6 %all-reduce.3.cloned.1.call-start = ((), (), s32[]{:S(2)}) async-start(), calls=%async_computation | async-start | bytes 23330816 | tf_op jit(solution)/shard_map/psum | solution.py:587
  54.6 53.5 %copy-start.22 = (s32[4,2,128]{2,1,0:T(2,128)}, s32[4,2,128]{2,1,0:T(2,128)S(1)}, u32[]{:S(2)}) copy-start(s32[4,2,128]{2,1,0:T(2,128)S(1)} %pad_add_fusion) | copy-start | bytes 12292
  249.8 8.4 %copy-start.9 = (f32[172,516]{1,0:T(8,128)S(1)}, f32[172,516]{1,0:T(8,128)}, u32[]{:S(2)}) copy-start(f32[172,516]{1,0:T(8,128)} %ghid.1) | copy-start | bytes 1065028
  249.8 9.4 %copy-start.7 = (f32[344,344]{1,0:T(8,128)S(1)}, f32[344,344]{1,0:T(8,128)}, u32[]{:S(2)}) copy-start(f32[344,344]{1,0:T(8,128)} %kv.1) | copy-start | bytes 1420036
  258.2 2.0 copy-start.17
  258.2 3.0 copy-start.18
  259.3 3.0 copy-start.15
  260.3 3.0 copy-start.16
  432.8 3.3 copy-start.10
  446.9 4.0 copy-start.11
  450.3 4.1 copy-start.19
  451.7 3.7 copy-start.14
  456.8 15.8 %copy-start.2 = (f32[1,344,172]{1,2,0:T(8,128)}, f32[1,344,172]{1,2,0:T(8,128)S(1)}, u32[]{:S(2)}) copy-start(f32[1,344,172]{1,2,0:T(8,128)S(1)} %get-tuple-element.193) | copy-start | bytes 710020
  456.8 15.8 %copy-start.4 = (f32[1,344,172]{1,2,0:T(8,128)}, f32[1,344,172]{1,2,0:T(8,128)S(1)}, u32[]{:S(2)}) copy-start(f32[1,344,172]{1,2,0:T(8,128)S(1)} %get-tuple-element.194) | copy-start | bytes 710020
  491.0 4.5 copy-start.8
  496.5 8.2 %copy-start = (f32[688,516]{0,1:T(8,128)S(1)}, f32[688,516]{0,1:T(8,128)}, u32[]{:S(2)}) copy-start(f32[688,516]{0,1:T(8,128)} %param.42) | copy-start | bytes 4260100
  504.7 5.1 copy-start.1
  504.7 5.1 copy-start.3
  504.7 5.1 copy-start.5
  504.7 5.1 copy-start.12
  504.7 5.1 copy-start.13
  509.9 1.9 copy-start.20
  509.9 1.9 copy-start.21
  509.9 1.9 copy-start.23
  (3 other events, 3.7 us)
Sparse Core Ops, SparseCore 0:
  207.2 225.6 all-reduce.2

commit v2 on v1

--- a/solution.py
+++ b/solution.py
@@ -129,6 +129,7 @@
         wide[0:MEM, :] = mem[...].astype(BF).astype(F32)
         wide[PAD : PAD + 1, :] = ticks[...].astype(F32)
         base = pl.multiple_of(step * cols, cols)
+        wide[PAD + 1 : PAD + 2, :] = (lax.broadcasted_iota(I32, (1, cols), 1) + base).astype(F32)
         for c in range(cols // 128):
             for h in range(2):
                 table[pl.ds(base + 128 * c, 128), 128 * h : 128 * h + 128] = jnp.transpose(
@@ -258,7 +259,7 @@
         keep[2, at : at + 8, :] = n
         keep[3, at : at + 8, :] = hid[2]
         ren[at : at + 8, :] = (1.0 - u) * n + u * o
-    full = jnp.concatenate([ren[...], zeros(256 - PAD, 256)], axis=0)
+    full = jnp.concatenate([ren[0:MEM, :], own_t[PAD + 1 : PAD + 2], zeros(255 - MEM, 256)], axis=0)
     rows[0:128, :] = jnp.transpose(full[:, :128])
     rows[128:256, :] = jnp.transpose(full[:, 128:])
 
@@ -298,10 +299,10 @@
     return x[:, :128] + x[:, 128:]
 
 
-def main_kernel(scale, near, gaps_t, ticks, msg, keep, ren, gap_own, labels, weights, total,
+def main_kernel(scale, core, near, gaps_t, ticks, msg, keep, ren, gap_own, labels, weights, total,
                 wgc, kvm, kvct, kvc, t0t, t0, t1t, t1, t2t, t2, s0t, s0, s1t, s1, vb,
-                ga, gb, loss,
-                pair, code, dcode, soft, back, grads, g_in, g_kv, g_one, g_dec, g_qo, g_th, vacc):
+                mine, theirs,
+                loss, pair, code, dcode, soft, back, grads, g_in, g_kv, g_one, g_dec, g_qo, g_th, vacc):
     step = pl.program_id(0)
     inv_size = HALF ** -0.5
 
@@ -452,8 +453,7 @@
     vacc[13] += d_dec
     vacc[14] += d_out
 
-    @pl.when(step == pl.num_programs(0) - 1)
-    def _():
+    def finish(ga, gb):
         wide = cols_to(g_in[...], 768)
         for c in range(6):
             gb[528 * c : 528 * c + 528, :] = wide[:, 128 * c : 128 * c + 128]
@@ -475,36 +475,156 @@
             for c in range(3):
                 ga[at : at + rows, :] = wide[:, 128 * c : 128 * c + 128]
                 at += rows
-        ga[3168:3200, :] = zeros(32, 128)
-
-
-def main(scale, near, near_ticks, ticks, msg, keep, ren, gap_own, labels, weights, total, w):
+        ga[3168:3200, :] = rows_to(loss[...], 32)
+
+    @pl.when((step == pl.num_programs(0) - 1) & (core[0] == 0))
+    def _():
+        finish(mine, theirs)
+
+    @pl.when((step == pl.num_programs(0) - 1) & (core[0] != 0))
+    def _():
+        finish(theirs, mine)
+
+
+def main(scale, near, near_ticks, ticks, msg, keep, ren, gap_own, labels, weights, total, core, w):
     ends = ren.shape[1]
     blocks = ends // 256
     whole = lambda a: pl.BlockSpec(a.shape, lambda i: (0,) * len(a.shape))
     lanes = lambda: pl.BlockSpec((1, 128), lambda i: (0, i))
     return pl.pallas_call(
         lambda *r: main_kernel(scale, *r),
-        out_shape=[jax.ShapeDtypeStruct((3200, 128), F32), jax.ShapeDtypeStruct((3200, 128), F32),
-                   jax.ShapeDtypeStruct((1, 128), F32)],
+        out_shape=[jax.ShapeDtypeStruct((3200, 128), F32), jax.ShapeDtypeStruct((3200, 128), F32)],
         grid=(blocks,),
-        in_specs=[pl.BlockSpec((NBR, 256, 256), lambda i: (0, i, 0)), pl.BlockSpec((NBR, 256), lambda i: (0, i)), lanes(),
+        in_specs=[pl.BlockSpec(memory_space=pltpu.SMEM), pl.BlockSpec((NBR, 256, 256), lambda i: (0, i, 0)), pl.BlockSpec((NBR, 256), lambda i: (0, i)), lanes(),
                   pl.BlockSpec((4 * PAD, 256), lambda i: (0, i)), pl.BlockSpec((5, PAD, 256), lambda i: (0, 0, i)),
                   pl.BlockSpec((PAD, 256), lambda i: (0, i)), pl.BlockSpec((8, 256), lambda i: (0, i)), lanes(), lanes(),
                   pl.BlockSpec((1, 128), lambda i: (0, 0))] + [whole(a) for a in w],
-        out_specs=[pl.BlockSpec((3200, 128), lambda i: (0, 0)), pl.BlockSpec((3200, 128), lambda i: (0, 0)),
-                   pl.BlockSpec((1, 128), lambda i: (0, 0))],
-        scratch_shapes=[pltpu.VMEM((NBR, 352, 256), F32), pltpu.VMEM((NBR, PAD, 256), BF), pltpu.VMEM((NBR, PAD, 256), F32),
+        out_specs=[pl.BlockSpec((3200, 128), lambda i: (0, 0)), pl.BlockSpec((3200, 128), lambda i: (0, 0))],
+        scratch_shapes=[pltpu.VMEM((1, 128), F32), pltpu.VMEM((NBR, 352, 256), F32), pltpu.VMEM((NBR, PAD, 256), BF), pltpu.VMEM((NBR, PAD, 256), F32),
                         pltpu.VMEM((20, 8, 256), F32), pltpu.VMEM((20, 8, 256), F32), pltpu.VMEM((352, 2560), BF),
                         pltpu.VMEM((528, 704), F32), pltpu.VMEM((352, 512), F32), pltpu.VMEM((PAD, 352), F32),
                         pltpu.VMEM((PAD, 352), F32), pltpu.VMEM((PAD, 512), F32), pltpu.VMEM((PAD, 512), F32),
                         pltpu.VMEM((16, PAD, 128), F32)],
         compiler_params=params(), name="main",
-    )(near.reshape(NBR, ends, 256), near_ticks, ticks, msg, keep, ren, gap_own, labels, weights, total, *w)
-
-
-def panels(flat, at, rows, count):
-    return jnp.concatenate([flat[at + c * rows : at + (c + 1) * rows] for c in range(count)], axis=1)
+    )(core, near.reshape(NBR, ends, 256), near_ticks, ticks, msg, keep, ren, gap_own, labels, weights, total, *w)
+
+
+def room(nodes, devices):
+    return -(-(nodes * 9) // (devices * 8 * 16)) * 16
+
+
+def pack_kernel(cap, rounds, nodes, ticks, latest, rows, out, first, second):
+    second[...] = jnp.full_like(second, -1.0)
+
+    def chunk(b, count):
+        base = b * 128
+        ticks_at = lax.div(b, 2) * 128
+        role = lax.rem(b, 2)
+
+        def eight(g, count):
+            for v in range(8):
+                e = g * 8 + v
+                i = base + e
+                won = latest[nodes[i]] == 2 * ticks[ticks_at + e] + role
+                row = rows[pl.ds(i, 1), :]
+                first[pl.ds(count, 1), :] = row[:, 0:128]
+                second[pl.ds(count, 1), :] = row[:, 128:256]
+                count = count + won.astype(I32)
+            return count
+
+        return lax.fori_loop(0, 16, eight, count)
+
+    count = lax.fori_loop(0, nodes.shape[0] // 128, chunk, jnp.int32(0))
+    second[pl.ds(count, 1), :] = jnp.full((1, 128), -1.0, F32)
+    tail = cap // 2
+    for r in range(rounds):
+        at = r * cap
+        out[r, 0:cap, :] = first[at : at + cap, :]
+        out[r, cap : cap + tail, :] = jnp.concatenate(
+            [second[at : at + tail, 0:64], second[at + tail : at + cap, 0:64]], axis=1)
+
+
+def pack(cap, nodes, ticks, latest, rows):
+    ends = nodes.shape[0]
+    rounds = ends // cap + 1
+    smem = pl.BlockSpec(memory_space=pltpu.SMEM)
+    spare = rounds * cap + 8
+    return pl.pallas_call(
+        lambda *r: pack_kernel(cap, rounds, *r),
+        out_shape=jax.ShapeDtypeStruct((rounds, cap + cap // 2, 128), F32),
+        in_specs=[smem, smem, smem, pl.BlockSpec(memory_space=pltpu.VMEM)],
+        out_specs=pl.BlockSpec(memory_space=pltpu.VMEM),
+        scratch_shapes=[pltpu.VMEM((spare, 128), F32), pltpu.VMEM((spare, 128), F32)],
+        compiler_params=params(), name="pack",
+    )(nodes, ticks, latest, rows)
+
+
+def merge_kernel(cap, blocks, ids, counts, rows, mem, out, table, second):
+    step = pl.program_id(0)
+    tail = cap // 2
+
+    @pl.when(step == 0)
+    def _():
+        table[...] = jnp.full_like(table, -1.0)
+
+    @pl.when(step < blocks)
+    def _():
+        half = rows[0, cap : cap + tail, :]
+        second[0:tail, :] = half
+        second[tail:cap, :] = jnp.concatenate([half[:, 64:], half[:, :64]], axis=1)
+        base = step * cap
+
+        def eight(g, carry):
+            for v in range(8):
+                i = g * 8 + v
+                table[pl.ds(ids[base + i], 1), :] = jnp.concatenate(
+                    [rows[0, pl.ds(i, 1), :], second[pl.ds(i, 1), :]], axis=1)
+            return carry
+
+        lax.fori_loop(0, lax.div(counts[step] + 7, 8), eight, 0)
+
+    @pl.when(step >= blocks)
+    def _():
+        cols = mem.shape[1]
+        base = pl.multiple_of((step - blocks) * cols, cols)
+        for c in range(cols // 128):
+            at = base + 128 * c
+            top = jnp.transpose(table[pl.ds(at, 128), 0:128])
+            low = jnp.transpose(table[pl.ds(at, 128), 128:256])
+            fresh = low[MEM - 128 : MEM - 127] >= 0.0
+            out[0:128, 128 * c : 128 * c + 128] = jnp.where(fresh, top, mem[0:128, 128 * c : 128 * c + 128])
+            out[128:MEM, 128 * c : 128 * c + 128] = jnp.where(
+                fresh, low[: MEM - 128], mem[128:MEM, 128 * c : 128 * c + 128])
+
+
+def merge(cap, gathered, mem_t):
+    blocks, height, _ = gathered.shape
+    nodes = mem_t.shape[1]
+    cols = 1024
+    ids = jnp.concatenate([gathered[:, cap:, MEM - 128], gathered[:, cap:, MEM - 64]], axis=1)
+    counts = jnp.sum((ids >= 0.0).astype(I32), axis=1)
+    ids = jnp.where(ids >= 0.0, ids, float(nodes)).astype(I32).reshape(-1)
+    smem = pl.BlockSpec(memory_space=pltpu.SMEM)
+    part = lambda i: (0, jnp.maximum(i - blocks, 0))
+    new = pl.pallas_call(
+        lambda *r: merge_kernel(cap, blocks, *r),
+        out_shape=jax.ShapeDtypeStruct((MEM, nodes), F32),
+        grid=(blocks + nodes // cols,),
+        in_specs=[smem, smem, pl.BlockSpec((1, height, 128), lambda i: (jnp.minimum(i, blocks - 1), 0, 0)),
+                  pl.BlockSpec((MEM, cols), part)],
+        out_specs=pl.BlockSpec((MEM, cols), part),
+        scratch_shapes=[pltpu.VMEM((nodes + 8, 256), F32), pltpu.VMEM((cap, 128), F32)],
+        compiler_params=params(), name="merge",
+    )(ids, counts, gathered, mem_t)
+    return new, jnp.any(counts == cap)
+
+
+def move(param, one, two, grad, factor, rate, decay):
+    clipped = grad * factor
+    one = BETA_ONE * one + (1.0 - BETA_ONE) * clipped
+    two = BETA_TWO * two + (1.0 - BETA_TWO) * clipped * clipped
+    step = (one * (1.0 / (1.0 - BETA_ONE**STEP))) / (jnp.sqrt(two * (1.0 / (1.0 - BETA_TWO**STEP))) + ADAM_EPS)
+    return param - rate * (step + decay * param), one, two
 
 
 def unsplit(x, axis):
@@ -512,54 +632,189 @@
     return jnp.concatenate([take(0, HALF), take(HPAD, HPAD + HALF)], axis=axis)
 
 
-def unpack(ga, gb, vec):
-    wide = panels(gb, 0, 528, 6)[:, :704].reshape(3, PAD, 4, PAD)[:, :MEM, :, :MEM].reshape(3 * MEM, 4 * MEM)
-    vecs = jnp.concatenate([gb[3168:3184], gb[3184:3200]], axis=1)[:, :PAD]
-    kv = panels(ga, 0, 352, 3)
-    kv_out = jnp.concatenate([unsplit(kv[:PAD], 0), unsplit(kv[PAD:], 0)], axis=0)
-    kv_out = jnp.concatenate([kv_out[:, :MEM], kv_out[:, PAD : PAD + MEM]], axis=1).T
-    pick = lambda x: jnp.concatenate([x[:MEM, :MEM], x[:MEM, PAD : PAD + MEM]], axis=1)
-    one = pick(panels(ga, 1056, PAD, 3))
-    dec = pick(panels(ga, 1584, PAD, 3))
-    qo = panels(ga, 2112, PAD, 3)
-    th = panels(ga, 2640, PAD, 3)
-    query_t = unsplit(qo[:, :MEM], 0)
-    out = unsplit(qo[:, PAD : PAD + MEM], 0)[:, :MEM]
-    two = th[:MEM, :MEM]
-    hid_n = th[:MEM, PAD : PAD + MEM]
-    phase = vec[1]
+def adam_kernel(count, where, *refs):
+    mine, other = refs[:count], refs[count : 2 * count]
+    refs = refs[2 * count :]
+    state, news, (norm_out, loss_out) = refs[:18], refs[18:36], refs[36:38]
+    a, b, g_gin, g_hid, g_kv, g_tall, g_sq, g_vec = refs[38:]
+    core, place = where[0], where[1]
+    height = mine[0].shape[0]
+    for k in range(count):
+        at = pl.multiple_of((place ^ k) * height, 8)
+
+        @pl.when(core == 0)
+        def _():
+            a[pl.ds(at, height), :] = mine[k][...]
+            b[pl.ds(at, height), :] = other[k][...]
+
+        @pl.when(core != 0)
+        def _():
+            b[pl.ds(at, height), :] = mine[k][...]
+            a[pl.ds(at, height), :] = other[k][...]
+
+    def panels(ref, at, rows, n):
+        return jnp.concatenate([ref[at + c * rows : at + (c + 1) * rows, :] for c in range(n)], axis=1)
+
+    vec = state[5]
+    tall = state[3]
+    wide = panels(b, 0, 528, 6)
+    gates = []
+    for g in range(3):
+        rows = wide[PAD * g : PAD * g + MEM]
+        gates.append(jnp.concatenate([rows[:, PAD * q : PAD * q + MEM] for q in range(4)], axis=1))
+    g_gin[...] = jnp.concatenate(gates, axis=0)
+    vecs = jnp.concatenate([b[3168:3184, :], b[3184:3200, :]], axis=1)
+    kv = panels(a, 0, 352, 3)
+    kv = jnp.concatenate([unsplit(kv[:PAD], 0), unsplit(kv[PAD:], 0)], axis=0)
+    kv = jnp.concatenate([kv[:, :MEM], kv[:, PAD : PAD + MEM]], axis=1)
+    g_kv[...] = jnp.transpose(rows_to(cols_to(kv, 384), 384))[: 2 * MEM, : 2 * MEM]
+    for i, at in ((1, 1056), (2, 1584)):
+        x = panels(a, at, PAD, 3)[:MEM]
+        g_tall[i] = jnp.concatenate([x[:, :MEM], x[:, PAD : PAD + MEM]], axis=1)
+    both = unsplit(panels(a, 2112, PAD, 3), 0)
+    sum_dq = unsplit(jnp.transpose(rows_to(vecs, 128))[:PAD, 15:16], 0)
+    phase = vec[1:2, :]
     phase_low = jnp.cos(phase).astype(BF).astype(F32)
-    sum_dq = unsplit(vecs[15], 0)
-    query = jnp.concatenate([query_t.T, phase_low[:, None] * sum_dq[None, :]], axis=0)
-    grad_in = wide.T
-    hid = jnp.concatenate([grad_in[:MEM, : 2 * MEM], hid_n], axis=1)
-    tall = jnp.stack([query, one.T, dec.T])
-    rows = [vecs[0, :MEM], vecs[1, :MEM], vecs[2, :MEM], vecs[3, :MEM], vecs[4, :MEM], vecs[2, :MEM], vecs[3, :MEM],
-            vecs[7, :MEM], unsplit(vecs[8], 0), unsplit(vecs[9], 0)] + [vecs[i, :MEM] for i in range(10, 15)]
-    return grad_in, hid, kv_out, tall, jnp.stack([out, two]), jnp.stack(rows), sum_dq
-
-
-def adam_all(params_in, firsts, seconds, grads):
-    squares_sum = jnp.zeros((), F32)
-    for item in grads:
-        squares_sum = squares_sum + jnp.sum(item * item)
-    grad_norm = jnp.sqrt(squares_sum)
-    factor = jnp.minimum(1.0, CLIP_AT / (grad_norm + NORM_EPS))
-    new_params, new_firsts, new_seconds = [], [], []
-    for at in range(len(params_in)):
-        clipped = grads[at] * factor
-        one = BETA_ONE * firsts[at] + (1.0 - BETA_ONE) * clipped
-        two = BETA_TWO * seconds[at] + (1.0 - BETA_TWO) * clipped * clipped
-        move = one / (1.0 - BETA_ONE**STEP) / (jnp.sqrt(two / (1.0 - BETA_TWO**STEP)) + ADAM_EPS)
-        last = at == len(params_in) - 1
-        decay, rate = (0.0, VECTOR_RATE) if last else (DECAY, LEARN_RATE)
-        new_params.append(params_in[at] - rate * (move + decay * params_in[at]))
-        new_firsts.append(one)
-        new_seconds.append(two)
-    return grad_norm, new_params, new_firsts, new_seconds
+    g_tall[0] = jnp.concatenate([both[:, :MEM], sum_dq * phase_low], axis=1)
+    g_sq[0] = both[:, PAD : PAD + MEM]
+    last = panels(a, 2640, PAD, 3)[:MEM]
+    g_sq[1] = last[:, :MEM]
+    shared = jnp.transpose(rows_to(cols_to(g_gin[0 : 2 * MEM, 0:MEM], 256), 384))[:MEM, : 2 * MEM]
+    g_hid[...] = jnp.concatenate([shared, last[:, PAD : PAD + MEM]], axis=1)
+    query_low = tall[0][:, MEM:].astype(BF).astype(F32)
+    phase_in = jnp.sum(query_low * sum_dq, axis=0, keepdims=True)
+    row = lambda i: vecs[i : i + 1, :MEM]
+    g_vec[...] = jnp.concatenate(
+        [row(0), row(1) - jnp.sin(phase) * phase_in, row(2), row(3), row(4), row(2), row(3), row(7),
+         unsplit(vecs[8:9], 1), unsplit(vecs[9:10], 1)] + [row(i) for i in range(10, 15)], axis=0)
+    total = jnp.zeros((1, 1), F32)
+    for ref in (g_gin, g_hid, g_kv, g_vec):
+        total += jnp.sum(ref[...] * ref[...], keepdims=True)
+    for ref in (g_tall, g_sq):
+        for i in range(ref.shape[0]):
+            total += jnp.sum(ref[i] * ref[i], keepdims=True)
+    norm = jnp.sqrt(total)
+    factor = jnp.minimum(1.0, CLIP_AT / (norm + NORM_EPS))
+    norm_out[...] = norm
+    loss_out[...] = jnp.sum(a[3168:3169, :], keepdims=True)
+    for i, grad in enumerate((g_gin, g_hid, g_kv, g_tall, g_sq, g_vec)):
+        rate, decay = (VECTOR_RATE, 0.0) if i == 5 else (LEARN_RATE, DECAY)
+        param, one, two = state[i], state[6 + i], state[12 + i]
+        new = news[i], news[6 + i], news[12 + i]
+        if len(param.shape) == 3:
+            for j in range(param.shape[0]):
+                made = move(param[j], one[j], two[j], grad[j], factor, rate, decay)
+                for ref, value in zip(new, made):
+                    ref[j] = value
+        else:
+            rows = param.shape[0]
+            for at in range(0, rows, 16):
+                s = slice(at, min(at + 16, rows))
+                made = move(param[s], one[s], two[s], grad[s], factor, rate, decay)
+                for ref, value in zip(new, made):
+                    ref[s] = value
+
+
+def adam(where, mine, other, state):
+    swap = lambda x: jnp.transpose(x, (0, 2, 1))
+    def ready(group):
+        gin, hid, kv, tall, sq, vec = group
+        return [gin.T, hid, kv, swap(tall), sq, vec]
+    state = ready(state[0:6]) + ready(state[6:12]) + ready(state[12:18])
+    count = len(mine)
+    shapes = [x.shape for x in state[:6]]
+    vm = pl.BlockSpec(memory_space=pltpu.VMEM)
+    outs = [jax.ShapeDtypeStruct(x.shape, F32) for x in state] + [jax.ShapeDtypeStruct((1, 1), F32)] * 2
+    out = pl.pallas_call(
+        lambda *r: adam_kernel(count, *r),
+        out_shape=outs,
+        in_specs=[pl.BlockSpec(memory_space=pltpu.SMEM)] + [vm] * (2 * count + 18),
+        out_specs=[vm] * 20,
+        scratch_shapes=[pltpu.VMEM((3200, 128), F32), pltpu.VMEM((3200, 128), F32)] + [pltpu.VMEM(s, F32) for s in shapes],
+        compiler_params=params(), name="adam",
+    )(where, *mine, *other, *state)
+    back = lambda group: [group[0].T, group[1], group[2], swap(group[3]), group[4], group[5]]
+    return out[18].reshape(()), out[19].reshape(()), back(out[0:6]) + back(out[6:12]) + back(out[12:18])
 
 
 AXES = ("dp", "rep")
+
+
+def levels(size):
+    found, stride = [], 1
+    while size > 1:
+        n = size if size <= 8 else 4
+        found.append((stride, n))
+        stride, size = stride * n, size // n
+    return found
+
+
+def peers(stride, k):
+    dp, rep = lax.axis_size("dp"), lax.axis_size("rep")
+    return [(d * rep + r, (d ^ (k * stride)) * rep + r) for d in range(dp) for r in range(rep)]
+
+
+def twin():
+    dp, rep = lax.axis_size("dp"), lax.axis_size("rep")
+    return [(d * rep + r, d * rep + (rep - 1 - r)) for d in range(dp) for r in range(rep)]
+
+
+def send(x, pairs):
+    return lax.ppermute(x, AXES, pairs)
+
+
+def tree(items, join):
+    while len(items) > 1:
+        items = [join(items[i], items[i + 1]) for i in range(0, len(items), 2)]
+    return items[0]
+
+
+def place(d, stride, n):
+    return lax.rem(lax.div(d, stride), n)
+
+
+def reduce_level(x, d, stride, n):
+    c = place(d, stride, n)
+    rows = x.shape[0] // n
+    piece = lambda k: lax.dynamic_slice_in_dim(x, (c ^ k) * rows, rows, 0)
+    got = [send(piece(k), peers(stride, k)) for k in range(1, n)]
+    return tree([piece(0)] + got, jnp.add)
+
+
+def gather_level(x, d, stride, n):
+    return [x] + [send(x, peers(stride, k)) for k in range(1, n)]
+
+
+def in_order(pieces, d, stride, n):
+    c = place(d, stride, n)
+    lines = []
+    for i in range(n):
+        line = pieces[i]
+        for k in range(n):
+            if k != i:
+                line = jnp.where((c ^ k) == i, pieces[k], line)
+        lines.append(line)
+    return jnp.concatenate(lines, axis=0)
+
+
+def spread_latest(x, d):
+    nodes = lax.broadcasted_iota(I32, x.shape, 0) < x.shape[0] - 1
+    join = lambda p, q: jnp.where(nodes, jnp.maximum(p, q), p + q)
+    x = join(x, send(x, twin()))
+    for stride, n in levels(lax.axis_size("dp")):
+        x = tree(gather_level(x, d, stride, n), join)
+    return x
+
+
+def sum_grads(mine, theirs, d):
+    steps = levels(lax.axis_size("dp"))
+    x = mine + send(theirs, twin())
+    for stride, n in steps:
+        x = reduce_level(x, d, stride, n)
+    for stride, n in reversed(steps[1:]):
+        x = in_order(gather_level(x, d, stride, n), d, stride, n)
+    mine = gather_level(x, d, *steps[0])
+    return mine, [send(x, twin()) for x in mine]
 
 
 def body(source, target, neighbours, neighbour_ticks, event_ticks, event_types, labels, edge_feats, weights, memory,
@@ -567,38 +822,46 @@
     events = event_ticks.shape[0]
     nodes = memory.shape[0]
     devices = lax.axis_size("dp") * lax.axis_size("rep")
+    d, core = lax.axis_index("dp"), lax.axis_index("rep")
     scale = TIME_RATE / (events * devices)
     tiles = events // 128
     order = lambda x: jnp.transpose(x, (2, 1, 0)).reshape(NBR, 2, tiles, 128).transpose(0, 2, 1, 3).reshape(NBR, 2 * events)
-    end_nodes = jnp.stack([source.reshape(tiles, 128), target.reshape(tiles, 128)], axis=1).reshape(-1)
+    pair = lambda x, y: jnp.stack([x.reshape(tiles, 128), y.reshape(tiles, 128)], axis=1).reshape(-1)
+    end_nodes = pair(source, target)
     near_ids = order(neighbours).reshape(-1)
     near_ticks = order(neighbour_ticks)
     row = lambda x: x.reshape(1, events)
     mem_t = memory.T
+    local = jnp.full((nodes,), -1, I32).at[end_nodes].max(pair(2 * event_ticks, 2 * event_ticks + 1))
+    spread = jnp.concatenate([local.astype(F32).reshape(-1, 128), jnp.full((1, 128), jnp.sum(weights), F32)], axis=0)
+    spread = spread_latest(spread, d)
+    latest = spread[:-1].reshape(-1).astype(I32)
+    weight_sum = spread[-1, 0]
     w = prep(gru_in, gru_hid, keys_values, tall_stack, squares, vectors)
     wg, wgc, wh = w[0], w[1], w[2]
     vb = w[-1]
     table, own = build_table(end_nodes, mem_t, node_ticks)
     msg, keep, ren, ren_rows, gap_own = gru(scale, own, row(event_ticks), edge_feats.T, row(event_types), wg, wh, vb)
+    cap = room(nodes, devices)
+    packed = pack(cap, end_nodes, event_ticks, latest, ren_rows)
+    gathered = lax.all_gather(packed[0], AXES)
     near = gather_near(near_ids, table)
-    weight_sum = lax.psum(jnp.sum(weights), AXES)
-    ga, gb, loss = main(scale, near, near_ticks, row(event_ticks), msg, keep, ren, gap_own, row(labels), row(weights),
-                        jnp.full((1, 128), weight_sum, F32), [wgc] + list(w[3:]))
-    ga, gb, loss_sum = lax.psum((ga, gb, jnp.sum(loss)), AXES)
-    grad_in, hid, kv, tall, square, vec, sum_dq = unpack(ga, gb, vectors)
-    phase_in = jnp.sum(tall_stack[0][MEM:].astype(BF).astype(F32) * sum_dq[None, :], axis=1)
-    vec = vec.at[1].add(-jnp.sin(vectors[1]) * phase_in)
-    grad_norm, new_p, new_f, new_s = adam_all(
-        (gru_in, gru_hid, keys_values, tall_stack, squares, vectors), moments[:6], moments[6:],
-        (grad_in, hid, kv, tall, square, vec))
-    ticks2 = jnp.stack([2 * event_ticks.reshape(tiles, 128), 2 * event_ticks.reshape(tiles, 128) + 1], axis=1).reshape(-1)
-    local = jnp.full((nodes,), -1, I32).at[end_nodes].max(ticks2)
-    latest = lax.pmax(local, AXES)
-    winner = ticks2 == latest[end_nodes]
-    rows = jnp.zeros((nodes, MEM), F32).at[end_nodes].add(jnp.where(winner[:, None], ren_rows[:, :MEM], 0.0))
-    merged = lax.psum(rows, AXES)
-    new_memory = jnp.where(latest[:, None] >= 0, merged, memory)
-    return (grad_norm, loss_sum, weight_sum, new_memory, *new_p, *new_f, *new_s)
+    mine, theirs = main(scale, near, near_ticks, row(event_ticks), msg, keep, ren, gap_own, row(labels), row(weights),
+                        jnp.full((1, 128), weight_sum, F32), core.reshape(1), [wgc] + list(w[3:]))
+    mine, other = sum_grads(mine, theirs, d)
+    where = jnp.stack([core, place(d, *levels(lax.axis_size("dp"))[0])])
+    grad_norm, loss_sum, news = adam(
+        where, mine, other, (gru_in, gru_hid, keys_values, tall_stack, squares, vectors) + moments)
+    new_mem, more = merge(cap, gathered, mem_t)
+
+    def again(carry):
+        r, _, mem_now = carry
+        mem_now, more = merge(cap, lax.all_gather(lax.dynamic_index_in_dim(packed, r, 0, False), AXES), mem_now)
+        return r + 1, more & (r + 1 < packed.shape[0]), mem_now
+
+    if packed.shape[0] > 1:
+        new_mem = lax.while_loop(lambda c: c[1], again, (jnp.int32(1), more, new_mem))[2]
+    return (grad_norm, loss_sum, weight_sum, new_mem.T, *news)
 
 
 def solution(mesh):

time: 522 us -> 287 us (0.55)
  blocking collectives: 124 us -> 0 us
  waiting for transfers between devices: 168 us -> 56.1 us
  Pallas kernels: 86.9 us -> 146 us
  other arithmetic: 59.6 us -> 16 us
  local copies, waits for them, and re-layouts: 62.1 us -> 27 us
  starting transfers between devices: 0.04 us -> 24.9 us
    psum x1 -> x0, waiting for transfers between devices: 168 us -> none  [body(): ga, gb, loss_sum = lax.psum((ga, gb, jnp.sum(loss)), AXES)]
    psum x2 -> x0, blocking collectives: 83.8 us -> none  [the longest x1 42.2 us: body(): weight_sum = lax.psum(jnp.sum(weights), AXES)]
    pallas_call x0 -> x3, Pallas kernels: none -> 59 us  [the longest x1 37.1 us: merge(): pl.pallas_call(lambda *r: merge_kernel(cap, blocks, *r), out_shape=jax.Sh...]
    ppermute x0 -> x24, waiting for transfers between devices: none -> 56.1 us  [send(): return lax.ppermute(x, AXES, pairs)]
    pmax x1 -> x0, blocking collectives: 40.5 us -> none  [body(): latest = lax.pmax(local, AXES)]
    ppermute x0 -> x24, starting transfers between devices: none -> 24.8 us  [send(): return lax.ppermute(x, AXES, pairs)]
    unnamed x75 -> x26, local copies, waits for them, and re-layouts: 41.9 us -> 17.2 us
    sub x6 -> x0, other arithmetic: 15.8 us -> none  [adam_all(): new_params.append(params_in[at] - rate * (move + decay * params_in[at]))]
  transfers between devices with their start and end apart: 1 -> 25, of which waited for: 1 -> 16; matrix products, arithmetic and copies ran while one was open for 3% -> 7% of each run, Pallas kernels for 0% -> 36%
where the time goes in v2:
time: 287 us; the launch traced here: 285 us
  Pallas kernels  146 us (51%)
  waiting for transfers between devices  56.1 us (20%)
  local copies, waits for them, and re-layouts  27 us (9%)
  starting transfers between devices  24.9 us (9%)
  other arithmetic  16 us (6%)
  between operations  14.4 us (5%)
    ppermute x24, waiting for transfers between devices, send(): return lax.ppermute(x, AXES, pairs)  56.1 us
    pallas_call x1, Pallas kernels, merge(): pl.pallas_call(lambda *r: merge_kernel(cap, blocks, *r), out_shape=jax.Sh...  37.1 us
    pallas_call x1, Pallas kernels, main(): pl.pallas_call(lambda *r: main_kernel(scale, *r), out_shape=[jax.ShapeDty...  35.8 us
    pallas_call x1, Pallas kernels, gather_near(): pl.pallas_call(lambda *r: near_kernel(chunk, *r), out_shape=jax.ShapeDtyp...  26.2 us
    ppermute x24, starting transfers between devices, send(): return lax.ppermute(x, AXES, pairs)  24.8 us
    unnamed x26, local copies, waits for them, and re-layouts  17.2 us
    pallas_call x1, Pallas kernels, adam(): pl.pallas_call(lambda *r: adam_kernel(count, *r), out_shape=outs, in_spec...  14.6 us
    pallas_call x1, Pallas kernels, build_table(): pl.pallas_call(lambda *r: table_kernel(steps, *r), out_shape=[jax.ShapeDt...  12.2 us
  transfers between devices with their start and end apart: 25, of which 16 were waited for; matrix products, arithmetic and copies ran while one was open for 7% of the time, Pallas kernels for 36%

profile of v2, /device:TPU:0, one launch (start us, length us, event | category | flops | bytes accessed | tf_op | source)
XLA Modules:
  0.0 285.0 jit_solution(617401710075110470)
XLA Ops:
  8.7 6.1 %scatter_custom_fusion = s32[8192]{0:T(1024)S(1)} fusion(s32[1024]{0:T(1024)S(1)} %bitcast.86, s32[1024]{0:T(1024)S(1)} %bitcast.87, s32[]{:T(128)} %constant.16.clone.1), kind=kCustom, calls=%fused_computation.25 | custom fusion | flops 1024 | bytes 32772 | tf_op jit(solution)/shard_map/scatter-max | solution.py:835
  18.8 2.9 %collective-permute-start.2 = (f32[65,128]{1,0:T(8,128)S(1)}, f32[65,128]{1,0:T(8,128)S(1)}, u32[]{:S(2)}, u32[]{:S(2)}) collective-permute-start(f32[65,128]{1,0:T(8,128)S(1)} %add_select_fusion.2), channel_id=1, source_target_pairs={{0,4},{1,5},{2,6},{3,7},{4,0},{5,1},{6,2},{7,3},{8,12},{9,13},{10,... | collective-permute-start | bytes 99848 | tf_op jit(solution)/shard_map/ppermute | solution.py:763
  23.7 3.2 %collective-permute-done.3 = f32[65,128]{1,0:T(8,128)S(1)} collective-permute-done((f32[65,128]{1,0:T(8,128)S(1)}, f32[65,128]{1,0:T(8,128)S(1)}, u32[]{:S(2)}, u32[]{:S(2)}) %collective-permute-start.3) | collective-permute-done | bytes 33312 | tf_op jit(solution)/shard_map/ppermute | solution.py:763
  27.2 2.7 collective-permute-start.5
  33.2 12.2 %table.1 = (f32[8192,256]{1,0:T(8,128)}, f32[1024,256]{1,0:T(8,128)}) custom-call(s32[1024]{0:T(1024)} %bitcast.76, f32[172,8192]{1,0:T(8,128)} %bitcast.59, s32[1,8192]{1,0:T(1,128)} %bitcast.80), custom_call_target="tpu_custom_call" | custom-call | tf_op jit(solution)/shard_map/table/pallas_call | solution.py:155
  45.4 6.1 %prep.1 = (bf16[528,704]{1,0:T(8,128)(2,1)}, bf16[176,528]{1,0:T(8,128)(2,1)}, bf16[528,176]{1,0:T(8,128)(2,1)}, bf16[352,256]{1,0:T(8,128)(2,1)}, bf16[352,176]...) custom-call(f32[516,688]{1,0:T(8,128)} %bitcast.62, ...), custom_call_target="tpu_custom_call" | custom-call | tf_op jit(solution)/shard_map/prep/pallas_call | solution.py:114
  51.4 6.8 %gru.1 = (bf16[704,1024]{1,0:T(8,128)(2,1)}, f32[5,176,1024]{2,1,0:T(8,128)}, f32[176,1024]{1,0:T(8,128)}, f32[1024,256]{1,0:T(8,128)}, f32[8,1024]{1,0:T(8,128)}) custom-call(f32[1024,256]{1,0:T(8,128)} %get-tuple-element.90.r_0_, s32[1,512]{1,0:T(1,128)} %bitcast.81, bf16[172,512]{1,0:T(8,128)(2,1)} %bitcast.72, s32[1,512]{1,0:T(1,128)} %bitcast.88, ...), custom_call_target="tpu_custom_call" | custom-call | tf_op jit(solution)/shard_map/gru/pallas_call | solution.py:271
  59.0 7.3 %pack.1 = f32[4,432,128]{2,1,0:T(8,128)S(1)} custom-call(s32[1024]{0:T(1024)} %bitcast.77, s32[512]{0:T(512)} %r_1_.1, s32[8192]{0:T(1024)} %fusion.2.r_2_, f32[1024,256]{1,0:T(8,128)} %get-tuple-element.116.r_3_), custom_call_target="tpu_custom_call" | custom-call | tf_op jit(solution)/shard_map/pack/pallas_call | solution.py:552
  67.7 26.2 %near.1 = bf16[10240,256]{1,0:T(8,128)(2,1)} custom-call(s32[10240]{0:T(1024)} %bitcast.78, f32[8192,256]{1,0:T(8,128)} %get-tuple-element.89.r_1_), custom_call_target="tpu_custom_call" | custom-call | tf_op jit(solution)/shard_map/near/pallas_call | solution.py:185
  95.6 35.8 %main.1 = (f32[3200,128]{1,0:T(8,128)}, f32[3200,128]{1,0:T(8,128)}) custom-call(s32[1]{0:T(128)} %bitcast.2.r_0_, bf16[10,1024,256]{2,1,0:T(8,128)(2,1)} %bitcast.61, s32[10,1024]{1,0:T(8,128)} %reshape.129.r_2_, s32[1,512]{1,0:T(1,128)} %bitcast.82, bf16[704,1024]{1,0:T(8,128)(2,1)} %get-tuple-element.94.r_4_, f32[5,176,1024]{2,1,0:T(8,128)} %get-tuple-element.95.r_5_, ...), custom_call_target="tpu_custom_call" | custom-call | tf_op jit(solution)/shard_map/main/pallas_call | solution.py:494
  131.5 4.7 %collective-permute-done.7 = f32[3200,128]{1,0:T(8,128)S(1)} collective-permute-done((f32[3200,128]{1,0:T(8,128)}, f32[3200,128]{1,0:T(8,128)S(1)}, u32[]{:S(2)}, u32[]{:S(2)}) %collective-permute-start.7) | collective-permute-done | bytes 1638432 | tf_op jit(solution)/shard_map/ppermute | solution.py:763
  140.6 3.0 %collective-permute-start.10 = (f32[800,128]{1,0:T(8,128)}, f32[800,128]{1,0:T(8,128)}, u32[]{:S(2)}, u32[]{:S(2)}) collective-permute-start(f32[800,128]{1,0:T(8,128)} %get-tuple-element.241), channel_id=1, source_target_pairs={{0,6},{1,7},{2,4},{3,5},{4,2},{5,3},{6,0},{7,1},{8,14},{9,15},{10,... | collective-permute-start | bytes 1228808 | tf_op jit(solution)/shard_map/ppermute | solution.py:763
  144.0 9.2 %collective-permute-done.8 = f32[800,128]{1,0:T(8,128)} collective-permute-done((f32[800,128]{1,0:T(8,128)}, f32[800,128]{1,0:T(8,128)}, u32[]{:S(2)}, u32[]{:S(2)}) %collective-permute-start.8) | collective-permute-done | bytes 409632 | tf_op jit(solution)/shard_map/ppermute | solution.py:763
  153.2 9.0 %collective-permute-done.10 = f32[800,128]{1,0:T(8,128)} collective-permute-done((f32[800,128]{1,0:T(8,128)}, f32[800,128]{1,0:T(8,128)}, u32[]{:S(2)}, u32[]{:S(2)}) %collective-permute-start.10) | collective-permute-done | bytes 409632 | tf_op jit(solution)/shard_map/ppermute | solution.py:763
  168.2 2.4 collective-permute-done.11
  172.5 3.1 %collective-permute-done.12 = f32[200,128]{1,0:T(8,128)S(1)} collective-permute-done((f32[200,128]{1,0:T(8,128)S(1)}, f32[200,128]{1,0:T(8,128)S(1)}, u32[]{:S(2)}, u32[]{:S(2)}) %collective-permute-start.12) | collective-permute-done | bytes 102432 | tf_op jit(solution)/shard_map/ppermute | solution.py:763
  175.7 3.2 %collective-permute-start.15 = (f32[200,128]{1,0:T(8,128)S(1)}, f32[200,128]{1,0:T(8,128)S(1)}, u32[]{:S(2)}, u32[]{:S(2)}) collective-permute-start(f32[200,128]{1,0:T(8,128)S(1)} %add_add_fusion.1), channel_id=1, source_target_pairs={{0,16},{1,17},{2,18},{3,19},{4,20},{5,21},{6,22},{7,23},{8,24},{9,... | collective-permute-start | bytes 307208 | tf_op jit(solution)/shard_map/ppermute | solution.py:763
  180.4 3.9 %collective-permute-done.15 = f32[200,128]{1,0:T(8,128)S(1)} collective-permute-done((f32[200,128]{1,0:T(8,128)S(1)}, f32[200,128]{1,0:T(8,128)S(1)}, u32[]{:S(2)}, u32[]{:S(2)}) %collective-permute-start.15) | collective-permute-done | bytes 102432 | tf_op jit(solution)/shard_map/ppermute | solution.py:763
  189.1 9.8 %collective-permute-done.19.r_4_ = f32[800,128]{1,0:T(8,128)S(1)} collective-permute-done((f32[800,128]{1,0:T(8,128)S(1)}, f32[800,128]{1,0:T(8,128)S(1)}, u32[]{:S(2)}, u32[]{:S(2)}) %collective-permute-start.19) | collective-permute-done | bytes 409632 | tf_op jit(solution)/shard_map/ppermute | solution.py:763
  199.0 4.8 %collective-permute-done.18.r_3_ = f32[800,128]{1,0:T(8,128)S(1)} collective-permute-done((f32[800,128]{1,0:T(8,128)S(1)}, f32[800,128]{1,0:T(8,128)S(1)}, u32[]{:S(2)}, u32[]{:S(2)}) %collective-permute-start.18) | collective-permute-done | bytes 409632 | tf_op jit(solution)/shard_map/ppermute | solution.py:763
  209.1 14.6 %adam.1 = (f32[516,688]{1,0:T(8,128)}, f32[172,516]{1,0:T(8,128)}, f32[344,344]{1,0:T(8,128)}, f32[3,172,344]{2,1,0:T(8,128)}, f32[2,172,172]{2,1,0:T(8,128)}, /...) custom-call(s32[2]{0:T(128)} %pad_add_fusion.2.r_0_, ...), custom_call_target="tpu_custom_call" | custom-call | tf_op jit(solution)/shard_map/adam/pallas_call | solution.py:728
  229.7 5.1 %fusion.6 = (f32[32,144,1]{2,1,0:T(8,128)}, f32[32,144,1]{2,1,0:T(8,128)S(1)}) fusion(f32[32,432,128]{2,1,0:T(8,128)} %all-gather.3.cloned.1.call-done.r_2_), kind=kLoop, calls=%fused_computation.41 | loop fusion | bytes 73728 | tf_op jit(solution)/shard_map/slice | solution.py:604
  234.7 2.9 %copy.94 = f32[32,144,1]{1,0,2:T(8,128)S(1)} copy(f32[32,144,1]{2,1,0:T(8,128)} %get-tuple-element.238) | data formatting | bytes 36864
  240.4 37.1 %merge.2 = f32[172,8192]{1,0:T(8,128)} custom-call(s32[9216]{0:T(1024)} %fusion.1.r_0_, s32[32]{0:T(128)} %copy-done.9, f32[32,432,128]{2,1,0:T(8,128)} %all-gather.3.cloned.1.call-done.r_2_, f32[172,8192]{1,0:T(8,128)} %bitcast.60), custom_call_target="tpu_custom_call" | custom-call | tf_op jit(solution)/shard_map/merge/pallas_call | solution.py:609
  (92 shorter events, 48.8 us)
Async XLA Ops:
  7.2 222.5 %all-gather.3.cloned.1.call-start = ((), (), s32[]{:S(2)}) async-start(), calls=%async_computation | async-start | bytes 7299072 | tf_op jit(solution)/shard_map/all_gather | solution.py:847
  18.8 4.9 %collective-permute-start.2 = (f32[65,128]{1,0:T(8,128)S(1)}, f32[65,128]{1,0:T(8,128)S(1)}, u32[]{:S(2)}, u32[]{:S(2)}) collective-permute-start(f32[65,128]{1,0:T(8,128)S(1)} %add_select_fusion.2), channel_id=1, source_target_pairs={{0,4},{1,5},{2,6},{3,7},{4,0},{5,1},{6,2},{7,3},{8,12},{9,13},{10,... | collective-permute-start | bytes 99848 | tf_op jit(solution)/shard_map/ppermute | solution.py:763
  21.7 5.1 %collective-permute-start.3 = (f32[65,128]{1,0:T(8,128)S(1)}, f32[65,128]{1,0:T(8,128)S(1)}, u32[]{:S(2)}, u32[]{:S(2)}) collective-permute-start(f32[65,128]{1,0:T(8,128)S(1)} %add_select_fusion.2), channel_id=1, source_target_pairs={{0,6},{1,7},{2,4},{3,5},{4,2},{5,3},{6,0},{7,1},{8,14},{9,15},{10,... | collective-permute-start | bytes 99848 | tf_op jit(solution)/shard_map/ppermute | solution.py:763
  23.2 4.0 %collective-permute-start.1 = (f32[65,128]{1,0:T(8,128)S(1)}, f32[65,128]{1,0:T(8,128)S(1)}, u32[]{:S(2)}, u32[]{:S(2)}) collective-permute-start(f32[65,128]{1,0:T(8,128)S(1)} %add_select_fusion.2), channel_id=1, source_target_pairs={{0,2},{1,3},{2,0},{3,1},{4,6},{5,7},{6,4},{7,5},{8,10},{9,11},{10,... | collective-permute-start | bytes 99848 | tf_op jit(solution)/shard_map/ppermute | solution.py:763
  27.2 31.1 %collective-permute-start.5 = (f32[65,128]{1,0:T(8,128)S(1)}, f32[65,128]{1,0:T(8,128)S(1)}, u32[]{:S(2)}, u32[]{:S(2)}) collective-permute-start(f32[65,128]{1,0:T(8,128)S(1)} %add_select_fusion.1), channel_id=1, source_target_pairs={{0,16},{1,17},{2,18},{3,19},{4,20},{5,21},{6,22},{7,23},{8,24},{9,... | collective-permute-start | bytes 99848 | tf_op jit(solution)/shard_map/ppermute | solution.py:763
  29.9 28.4 %collective-permute-start.6 = (f32[65,128]{1,0:T(8,128)S(1)}, f32[65,128]{1,0:T(8,128)S(1)}, u32[]{:S(2)}, u32[]{:S(2)}) collective-permute-start(f32[65,128]{1,0:T(8,128)S(1)} %add_select_fusion.1), channel_id=1, source_target_pairs={{0,24},{1,25},{2,26},{3,27},{4,28},{5,29},{6,30},{7,31},{8,16},{9,... | collective-permute-start | bytes 99848 | tf_op jit(solution)/shard_map/ppermute | solution.py:763
  31.2 27.1 %collective-permute-start.4 = (f32[65,128]{1,0:T(8,128)S(1)}, f32[65,128]{1,0:T(8,128)S(1)}, u32[]{:S(2)}, u32[]{:S(2)}) collective-permute-start(f32[65,128]{1,0:T(8,128)S(1)} %add_select_fusion.1), channel_id=1, source_target_pairs={{0,8},{1,9},{2,10},{3,11},{4,12},{5,13},{6,14},{7,15},{8,0},{9,1},... | collective-permute-start | bytes 99848 | tf_op jit(solution)/shard_map/ppermute | solution.py:763
  131.4 4.8 %collective-permute-start.7 = (f32[3200,128]{1,0:T(8,128)}, f32[3200,128]{1,0:T(8,128)S(1)}, u32[]{:S(2)}, u32[]{:S(2)}) collective-permute-start(f32[3200,128]{1,0:T(8,128)} %get-tuple-element.113), channel_id=1, source_target_pairs={{0,1},{1,0},{2,3},{3,2},{4,5},{5,4},{6,7},{7,6},{8,9},{9,8},{10,11... | collective-permute-start | bytes 4915208 | tf_op jit(solution)/shard_map/ppermute | solution.py:763
  140.6 12.6 %collective-permute-start.8 = (f32[800,128]{1,0:T(8,128)}, f32[800,128]{1,0:T(8,128)}, u32[]{:S(2)}, u32[]{:S(2)}) collective-permute-start(f32[800,128]{1,0:T(8,128)} %get-tuple-element.240), channel_id=1, source_target_pairs={{0,2},{1,3},{2,0},{3,1},{4,6},{5,7},{6,4},{7,5},{8,10},{9,11},{10,... | collective-permute-start | bytes 1228808 | tf_op jit(solution)/shard_map/ppermute | solution.py:763
  140.6 21.5 %collective-permute-start.10 = (f32[800,128]{1,0:T(8,128)}, f32[800,128]{1,0:T(8,128)}, u32[]{:S(2)}, u32[]{:S(2)}) collective-permute-start(f32[800,128]{1,0:T(8,128)} %get-tuple-element.241), channel_id=1, source_target_pairs={{0,6},{1,7},{2,4},{3,5},{4,2},{5,3},{6,0},{7,1},{8,14},{9,15},{10,... | collective-permute-start | bytes 1228808 | tf_op jit(solution)/shard_map/ppermute | solution.py:763
  143.6 19.7 %collective-permute-start.9 = (f32[800,128]{1,0:T(8,128)S(1)}, f32[800,128]{1,0:T(8,128)}, u32[]{:S(2)}, u32[]{:S(2)}) collective-permute-start(f32[800,128]{1,0:T(8,128)S(1)} %get-tuple-element.242), channel_id=1, source_target_pairs={{0,4},{1,5},{2,6},{3,7},{4,0},{5,1},{6,2},{7,3},{8,12},{9,13},{10,... | collective-permute-start | bytes 1228808 | tf_op jit(solution)/shard_map/ppermute | solution.py:763
  164.7 6.0 %collective-permute-start.11 = (f32[200,128]{1,0:T(8,128)S(1)}, f32[200,128]{1,0:T(8,128)S(1)}, u32[]{:S(2)}, u32[]{:S(2)}) collective-permute-start(f32[200,128]{1,0:T(8,128)S(1)} %get-tuple-element.247), channel_id=1, source_target_pairs={{0,8},{1,9},{2,10},{3,11},{4,12},{5,13},{6,14},{7,15},{8,0},{9,1},... | collective-permute-start | bytes 307208 | tf_op jit(solution)/shard_map/ppermute | solution.py:763
  165.7 6.8 %collective-permute-start.13 = (f32[200,128]{1,0:T(8,128)S(1)}, f32[200,128]{1,0:T(8,128)S(1)}, u32[]{:S(2)}, u32[]{:S(2)}) collective-permute-start(f32[200,128]{1,0:T(8,128)S(1)} %get-tuple-element.248), channel_id=1, source_target_pairs={{0,24},{1,25},{2,26},{3,27},{4,28},{5,29},{6,30},{7,31},{8,16},{9,... | collective-permute-start | bytes 307208 | tf_op jit(solution)/shard_map/ppermute | solution.py:763
  167.9 7.7 %collective-permute-start.12 = (f32[200,128]{1,0:T(8,128)S(1)}, f32[200,128]{1,0:T(8,128)S(1)}, u32[]{:S(2)}, u32[]{:S(2)}) collective-permute-start(f32[200,128]{1,0:T(8,128)S(1)} %get-tuple-element.249), channel_id=1, source_target_pairs={{0,16},{1,17},{2,18},{3,19},{4,20},{5,21},{6,22},{7,23},{8,24},{9,... | collective-permute-start | bytes 307208 | tf_op jit(solution)/shard_map/ppermute | solution.py:763
  175.6 4.7 %collective-permute-start.16 = (f32[200,128]{1,0:T(8,128)S(1)}, f32[200,128]{1,0:T(8,128)S(1)}, u32[]{:S(2)}, u32[]{:S(2)}) collective-permute-start(f32[200,128]{1,0:T(8,128)S(1)} %add_add_fusion.1), channel_id=1, source_target_pairs={{0,8},{1,9},{2,10},{3,11},{4,12},{5,13},{6,14},{7,15},{8,0},{9,1},... | collective-permute-start | bytes 307208 | tf_op jit(solution)/shard_map/ppermute | solution.py:763
  175.7 8.6 %collective-permute-start.15 = (f32[200,128]{1,0:T(8,128)S(1)}, f32[200,128]{1,0:T(8,128)S(1)}, u32[]{:S(2)}, u32[]{:S(2)}) collective-permute-start(f32[200,128]{1,0:T(8,128)S(1)} %add_add_fusion.1), channel_id=1, source_target_pairs={{0,16},{1,17},{2,18},{3,19},{4,20},{5,21},{6,22},{7,23},{8,24},{9,... | collective-permute-start | bytes 307208 | tf_op jit(solution)/shard_map/ppermute | solution.py:763
  178.9 6.6 %collective-permute-start.14 = (f32[200,128]{1,0:T(8,128)S(1)}, f32[200,128]{1,0:T(8,128)S(1)}, u32[]{:S(2)}, u32[]{:S(2)}) collective-permute-start(f32[200,128]{1,0:T(8,128)S(1)} %add_add_fusion.1), channel_id=1, source_target_pairs={{0,24},{1,25},{2,26},{3,27},{4,28},{5,29},{6,30},{7,31},{8,16},{9,... | collective-permute-start | bytes 307208 | tf_op jit(solution)/shard_map/ppermute | solution.py:763
  185.6 13.4 %collective-permute-start.19 = (f32[800,128]{1,0:T(8,128)S(1)}, f32[800,128]{1,0:T(8,128)S(1)}, u32[]{:S(2)}, u32[]{:S(2)}) collective-permute-start(f32[800,128]{1,0:T(8,128)S(1)} %pad_maximum_fusion.1.r_1_), channel_id=1, source_target_pairs={{0,6},{1,7},{2,4},{3,5},{4,2},{5,3},{6,0},{7,1},{8,14},{9,15},{10,... | collective-permute-start | bytes 1228808 | tf_op jit(solution)/shard_map/ppermute | solution.py:763
  187.1 16.7 %collective-permute-start.18 = (f32[800,128]{1,0:T(8,128)S(1)}, f32[800,128]{1,0:T(8,128)S(1)}, u32[]{:S(2)}, u32[]{:S(2)}) collective-permute-start(f32[800,128]{1,0:T(8,128)S(1)} %pad_maximum_fusion.1.r_1_), channel_id=1, source_target_pairs={{0,4},{1,5},{2,6},{3,7},{4,0},{5,1},{6,2},{7,3},{8,12},{9,13},{10,... | collective-permute-start | bytes 1228808 | tf_op jit(solution)/shard_map/ppermute | solution.py:763
  187.7 16.1 %collective-permute-start.17 = (f32[800,128]{1,0:T(8,128)S(1)}, f32[800,128]{1,0:T(8,128)S(1)}, u32[]{:S(2)}, u32[]{:S(2)}) collective-permute-start(f32[800,128]{1,0:T(8,128)S(1)} %pad_maximum_fusion.1.r_1_), channel_id=1, source_target_pairs={{0,2},{1,3},{2,0},{3,1},{4,6},{5,7},{6,4},{7,5},{8,10},{9,11},{10,... | collective-permute-start | bytes 1228808 | tf_op jit(solution)/shard_map/ppermute | solution.py:763
  189.1 19.2 %collective-permute-start.20 = (f32[800,128]{1,0:T(8,128)S(1)}, f32[800,128]{1,0:T(8,128)S(1)}, u32[]{:S(2)}, u32[]{:S(2)}) collective-permute-start(f32[800,128]{1,0:T(8,128)S(1)} %pad_maximum_fusion.1.r_1_), channel_id=1, source_target_pairs={{0,1},{1,0},{2,3},{3,2},{4,5},{5,4},{6,7},{7,6},{8,9},{9,8},{10,11... | collective-permute-start | bytes 1228808 | tf_op jit(solution)/shard_map/ppermute | solution.py:763
  199.0 9.4 %collective-permute-start.23 = (f32[800,128]{1,0:T(8,128)S(1)}, f32[800,128]{1,0:T(8,128)}, u32[]{:S(2)}, u32[]{:S(2)}) collective-permute-start(f32[800,128]{1,0:T(8,128)S(1)} %collective-permute-done.19.r_4_), channel_id=1, source_target_pairs={{0,1},{1,0},{2,3},{3,2},{4,5},{5,4},{6,7},{7,6},{8,9},{9,8},{10,11... | collective-permute-start | bytes 1228808 | tf_op jit(solution)/shard_map/ppermute | solution.py:763
  203.8 4.6 %collective-permute-start.22 = (f32[800,128]{1,0:T(8,128)S(1)}, f32[800,128]{1,0:T(8,128)}, u32[]{:S(2)}, u32[]{:S(2)}) collective-permute-start(f32[800,128]{1,0:T(8,128)S(1)} %collective-permute-done.18.r_3_), channel_id=1, source_target_pairs={{0,1},{1,0},{2,3},{3,2},{4,5},{5,4},{6,7},{7,6},{8,9},{9,8},{10,11... | collective-permute-start | bytes 1228808 | tf_op jit(solution)/shard_map/ppermute | solution.py:763
  203.8 4.6 %collective-permute-start.21 = (f32[800,128]{1,0:T(8,128)S(1)}, f32[800,128]{1,0:T(8,128)}, u32[]{:S(2)}, u32[]{:S(2)}) collective-permute-start(f32[800,128]{1,0:T(8,128)S(1)} %collective-permute-done.17.r_2_), channel_id=1, source_target_pairs={{0,1},{1,0},{2,3},{3,2},{4,5},{5,4},{6,7},{7,6},{8,9},{9,8},{10,11... | collective-permute-start | bytes 1228808 | tf_op jit(solution)/shard_map/ppermute | solution.py:763
  (10 other events, 80.3 us)
Sparse Core Ops, SparseCore 0:
  67.2 72.1 all-gather.2

commit v3 on v2

v3 whole, which is shorter than its diff:
```python
import math

import jax
import jax.numpy as jnp
from jax import lax
from jax.experimental import pallas as pl
from jax.experimental.pallas import tpu as pltpu
from jax.sharding import PartitionSpec as P

F32 = jnp.float32
BF = jnp.bfloat16
I32 = jnp.int32
NBR = 10
MEM = 172
PAD = 176
HALF = 86
HPAD = 88
STEP = 10
LEARN_RATE = 0.03
VECTOR_RATE = 0.3
BETA_ONE = 0.9
BETA_TWO = 0.999
ADAM_EPS = 1e-08
DECAY = 0.01
CLIP_AT = 0.005
TIME_RATE = 64.0
NORM_EPS = 1e-06
VMEM_CAP = 58 * 2**20


def params(limit=VMEM_CAP):
    return pltpu.CompilerParams(vmem_limit_bytes=limit)


def cost(us):
    return pl.CostEstimate(flops=int(us * 1e9), bytes_accessed=int(us * 3e6), transcendentals=0)


def nn(a, b):
    return lax.dot_general(a, b, (((1,), (0,)), ((), ())), preferred_element_type=F32)


def nt(a, b):
    return lax.dot_general(a, b, (((1,), (1,)), ((), ())), preferred_element_type=F32)


def zeros(rows, cols):
    return jnp.zeros((rows, cols), F32)


def rows_to(x, total):
    return jnp.concatenate([x, zeros(total - x.shape[0], x.shape[1])], axis=0)


def cols_to(x, total):
    return jnp.concatenate([x, zeros(x.shape[0], total - x.shape[1])], axis=1)


def split_rows(x):
    gap = zeros(HPAD - HALF, x.shape[1])
    return jnp.concatenate([x[:HALF], gap, x[HALF:], gap], axis=0)


def eye(n):
    return (lax.broadcasted_iota(I32, (n, n), 0) == lax.broadcasted_iota(I32, (n, n), 1)).astype(BF)


def turned(x):
    return nt(eye(x.shape[1]), x.astype(BF))


def prep_kernel(gin, ghid, kv, tall, sq, vec,
                wg, wgc, wh, kvm, kvct, kvc, t0t, t0, t1t, t1, t2t, t2, s0t, s0, s1t, s1, vb):
    full = gin[...]
    for gate in range(3):
        rows = full[gate * MEM : (gate + 1) * MEM]
        parts = [cols_to(rows[:, q * MEM : (q + 1) * MEM], PAD) for q in range(4)]
        wide = rows_to(jnp.concatenate(parts, axis=1), PAD)
        wg[pl.ds(gate * PAD, PAD), :] = wide.astype(BF)
        code = cols_to(rows_to(rows[:, 2 * MEM : 3 * MEM], PAD), 256)
        wgc[:, gate * PAD : (gate + 1) * PAD] = turned(code)[:PAD].astype(BF)
    hid = ghid[...]
    for gate in range(3):
        part = cols_to(rows_to(hid[:, gate * MEM : (gate + 1) * MEM], PAD), 256)
        wh[pl.ds(gate * PAD, PAD), :] = turned(part)[:PAD].astype(BF)
    pairs = kv[...]
    both = turned(cols_to(pairs, 384))
    halves = jnp.concatenate([split_rows(both[:MEM]), split_rows(both[MEM : 2 * MEM])], axis=0)
    kvm[...] = cols_to(halves[:, :MEM], 256).astype(BF)
    code_rows = cols_to(halves[:, MEM:], 256)
    kvct[...] = code_rows[:, :PAD].astype(BF)
    kvc[...] = turned(code_rows)[:PAD].astype(BF)
    query = tall[0]
    query_t = cols_to(split_rows(query[:, :MEM]), 256)
    t0t[...] = query_t[:, :PAD].astype(BF)
    t0[...] = turned(query_t)[:PAD].astype(BF)
    for src, fwd, back in ((tall[1], t1t, t1), (tall[2], t2t, t2)):
        wide = rows_to(jnp.concatenate([cols_to(src[:, :MEM], PAD), cols_to(src[:, MEM:], PAD)], axis=1), PAD)
        fwd[...] = wide.astype(BF)
        back[...] = turned(cols_to(wide, 384))[: 2 * PAD].astype(BF)
    first = cols_to(split_rows(sq[:, 0, :]), 256)
    s0[...] = first[:, :PAD].astype(BF)
    s0t[...] = turned(first)[:PAD].astype(BF)
    second = cols_to(rows_to(sq[:, 1, :], PAD), 256)
    s1[...] = second[:, :PAD].astype(BF)
    s1t[...] = turned(second)[:PAD].astype(BF)
    cols = jnp.transpose(cols_to(rows_to(vec[...], 128), 256))
    phase_low = jnp.cos(cols[:PAD, 1:2]).astype(BF).astype(F32)
    row_id = lax.broadcasted_iota(I32, (PAD, 128), 0)
    wide_phase = jnp.where(row_id < MEM, jnp.broadcast_to(phase_low, (PAD, 128)), 0.0).astype(BF)
    steady = nn(cols_to(split_rows(query[:, MEM:]), PAD).astype(BF), wide_phase)
    for i in range(15):
        column = cols[:, i : i + 1]
        if i in (8, 9):
            column = split_rows(column[:MEM])
        wide = jnp.broadcast_to(column[:PAD], (PAD, 128))
        vb[i] = wide + steady if i == 8 else (wide * (0.5 / math.pi) if i < 2 else wide)


def prep(gin, ghid, kv, tall, sq, vec):
    bf = lambda *s: jax.ShapeDtypeStruct(s, BF)
    outs = [bf(528, 704), bf(176, 528), bf(528, 176), bf(352, 256), bf(352, 176), bf(176, 352),
            bf(176, 176), bf(176, 176), bf(176, 352), bf(352, 176), bf(176, 352), bf(352, 176),
            bf(176, 176), bf(176, 176), bf(176, 176), bf(176, 176), jax.ShapeDtypeStruct((15, PAD, 128), F32)]
    return pl.pallas_call(
        prep_kernel, out_shape=outs, compiler_params=params(), name="prep", cost_estimate=cost(6),
    )(gin.T, ghid, kv, jnp.transpose(tall, (0, 2, 1)), jnp.transpose(sq, (1, 0, 2)), vec)


def first_kernel(source, target, ticks, weights, out):
    tiles = source.shape[0]
    heights = out.shape[0] - 1
    nodes, orders = [], []
    for b in range(tiles):
        nodes += [source[b : b + 1, :], target[b : b + 1, :]]
        orders += [2 * ticks[b : b + 1, :], 2 * ticks[b : b + 1, :] + 1]
    count = 2 * tiles
    stack = jnp.concatenate([x.astype(F32) for x in nodes + orders], axis=0)
    cols = jnp.transpose(rows_to(stack, 128))
    lane = lax.broadcasted_iota(I32, (128, 128), 1)
    line = lax.broadcasted_iota(I32, (heights, 128), 0)
    total = zeros(heights, 384)
    for c in range(count):
        node = jnp.broadcast_to(cols[:, c : c + 1], (128, 128)).astype(I32)
        order = jnp.broadcast_to(cols[:, count + c : count + c + 1], (128, 128)).astype(I32)
        beaten = zeros(128, 128)
        for e in range(count):
            beaten = jnp.where((node == nodes[e]) & (orders[e] > order), 1.0, beaten)
        beaten = jnp.max(beaten, axis=1, keepdims=True)
        value = jnp.where(beaten > 0.0, 0, order + 1)
        here = (node & 127) == lane
        pick = lambda v: jnp.where(here, v, 0).astype(F32).astype(BF)
        right = jnp.concatenate([pick(value & 127), pick((value >> 7) & 127), pick(value >> 14)], axis=1)
        left = (jnp.broadcast_to(nodes[c] >> 7, (heights, 128)) == line).astype(BF)
        total = total + nn(left, right)
    out[0:heights, :] = total[:, :128] + 128.0 * total[:, 128:256] + 16384.0 * total[:, 256:] - 1.0
    out[heights : heights + 1, :] = jnp.broadcast_to(jnp.sum(weights[...], keepdims=True), (1, 128))


def first_latest(nodes, source, target, ticks, weights):
    return pl.pallas_call(
        first_kernel, out_shape=jax.ShapeDtypeStruct((nodes // 128 + 1, 128), F32),
        compiler_params=params(), name="latest", cost_estimate=cost(2),
    )(source, target, ticks, weights)


def fetch_kernel(steps, chunk, source, target, near_ids, mem, ticks, own, near, wide, left, right):
    step = pl.program_id(0)
    cols = mem.shape[1]

    @pl.when(step == 0)
    def _():
        wide[...] = jnp.zeros_like(wide)

    @pl.when(step < steps)
    def _():
        base = pl.multiple_of(step * cols, cols)
        wide[0:MEM, :] = mem[...].astype(BF).astype(F32)
        tick = ticks[...]
        for at, part in ((PAD, tick & 127), (PAD + 1, (tick >> 7) & 127), (PAD + 2, tick >> 14)):
            wide[at : at + 1, :] = part.astype(F32)
        unit = eye(256)
        for c in range(cols // 256):
            rows = nt(unit, wide[:, 256 * c : 256 * c + 256].astype(BF))
            left[pl.ds(base + 256 * c, 256), :] = rows[:, :128]
            right[pl.ds(base + 256 * c, 256), :] = rows[:, 128:]

    def move(out, at, ids):
        for h, table in enumerate((left, right)):
            rows = jnp.concatenate([table[pl.ds(i, 1), :] for i in ids], axis=0)
            out[pl.ds(at, 16), 128 * h : 128 * h + 128] = rows.astype(BF)

    @pl.when(step == steps)
    def _():
        def group(b, carry):
            for role, ids in enumerate((source, target)):
                def some(g, carry):
                    for v in range(2):
                        e = g * 32 + v * 16
                        at = pl.multiple_of(b * 256 + role * 128 + e, 16)
                        move(own, at, [ids[b * 128 + e + u] for u in range(16)])
                    return carry

                lax.fori_loop(0, 4, some, 0)
            return carry

        lax.fori_loop(0, own.shape[0] // 256, group, 0)

    @pl.when(step > steps)
    def _():
        base = (step - steps - 1) * chunk

        def group(g, carry):
            for v in range(4):
                at = pl.multiple_of(g * 64 + v * 16, 16)
                move(near, at, [near_ids[base + at + u] for u in range(16)])
            return carry

        lax.fori_loop(0, chunk // 64, group, 0)


def fetch(source, target, near_ids, mem_t, ticks):
    nodes = mem_t.shape[1]
    ends, nears = 2 * source.shape[0], near_ids.shape[0]
    cols, chunk = 4096, 5120
    steps = nodes // cols
    smem = pl.BlockSpec(memory_space=pltpu.SMEM)
    part = lambda i: (0, jnp.minimum(i, steps - 1))
    return pl.pallas_call(
        lambda *r: fetch_kernel(steps, chunk, *r),
        out_shape=[jax.ShapeDtypeStruct((ends, 256), BF), jax.ShapeDtypeStruct((nears, 256), BF)],
        grid=(steps + 1 + nears // chunk,),
        in_specs=[smem, smem, smem, pl.BlockSpec((MEM, cols), part), pl.BlockSpec((1, cols), part)],
        out_specs=[pl.BlockSpec((ends, 256), lambda i: (0, 0)),
                   pl.BlockSpec((chunk, 256), lambda i: (jnp.maximum(i - steps - 1, 0), 0))],
        scratch_shapes=[pltpu.VMEM((256, cols), F32), pltpu.VMEM((nodes, 128), F32), pltpu.VMEM((nodes, 128), F32)],
        compiler_params=params(), name="fetch", cost_estimate=cost(18),
    )(source, target, near_ids, mem_t, ticks.reshape(1, nodes))


ROUND = 12582912.0
SIN = (6.283185005187988, -41.34165573120117, 81.60100555419922, -76.5497817993164, 39.536705017089844)
COS = (0.9999999403953552, -19.739171981811523, 64.9345932006836, -85.2403335571289, 56.24237823486328)


def cos_sin(turns):
    e = turns - ((turns + ROUND) - ROUND)
    w = 0.25 - jnp.abs(e)
    z = w * w
    c = w * (SIN[0] + z * (SIN[1] + z * (SIN[2] + z * (SIN[3] + z * SIN[4]))))
    s = COS[0] + z * (COS[1] + z * (COS[2] + z * (COS[3] + z * COS[4])))
    return c, jnp.where(e > 0.0, -s, s)


def sigmoid(x):
    return 0.5 * jnp.tanh(0.5 * x) + 0.5


BLOCK = 512
TILES = BLOCK // 256


def across(x):
    return jnp.concatenate([x] * (2 * TILES), axis=1)


def chunks(x, width=128):
    return [x[:, at : at + width] for at in range(0, x.shape[1], width)]


def both(x):
    return jnp.concatenate([c for c in chunks(x) for _ in range(2)], axis=1)


def mix(x, y):
    return jnp.concatenate([c for pair in zip(chunks(x), chunks(y)) for c in pair], axis=1)


def sources_of(x):
    return jnp.concatenate(chunks(x)[0::2], axis=1)


def targets_of(x):
    return jnp.concatenate(chunks(x)[1::2], axis=1)


def wide_rows(x, rows):
    return jnp.broadcast_to(x, (rows, x.shape[1]))


def gru_kernel(scale, cap, rounds, sources, targets, ticks_at, latest, own, source, target, ticks, edge, types, wg, wh, vb,
               msg, keep, ren, gap_out, packed, left, right, first, second):
    step = pl.program_id(0)
    own_t = nt(eye(256), own[...])
    seen = own_t[PAD : PAD + 1] + 128.0 * own_t[PAD + 1 : PAD + 2] + 16384.0 * own_t[PAD + 2 : PAD + 3]
    gap = (both(ticks[...].astype(F32)) - seen) * scale
    row_id = lax.broadcasted_iota(I32, (PAD, BLOCK), 0)
    own_x = jnp.where(row_id < MEM, own_t[:PAD], 0.0)
    msg[0:PAD, :] = own_x.astype(BF)
    msg[PAD : 2 * PAD, :] = mix(targets_of(own_x), sources_of(own_x)).astype(BF)
    edges = rows_to(edge[...].astype(F32) * types[...].astype(F32), PAD)
    msg[3 * PAD : 4 * PAD, :] = both(edges).astype(BF)
    gap_out[...] = wide_rows(gap, 8)
    gap16 = wide_rows(gap, 16)
    for st in range(PAD // 16):
        at = 16 * st
        for m in range(TILES):
            q = slice(256 * m, 256 * m + 256)
            rate, phase = vb[0, at : at + 16, :], vb[1, at : at + 16, :]
            x = jnp.concatenate([rate, rate], axis=1) * gap16[:, q] + jnp.concatenate([phase, phase], axis=1)
            c, s = cos_sin(x)
            msg[2 * PAD + at : 2 * PAD + at + 16, q] = c.astype(BF)
            keep[4, at : at + 16, q] = s
    gates = nn(wg[...], msg[...])
    hidden = nn(wh[...], msg[0:PAD, :])
    for st in range(PAD // 8):
        at = 8 * st
        o = own_x[at : at + 8]
        pre = [gates[g * PAD + at : g * PAD + at + 8] + across(vb[2 + g, at : at + 8, :]) for g in range(3)]
        hid = [hidden[g * PAD + at : g * PAD + at + 8] + across(vb[5 + g, at : at + 8, :]) for g in range(3)]
        u = sigmoid(pre[0] + hid[0])
        r = sigmoid(pre[1] + hid[1])
        n = jnp.tanh(pre[2] + r * hid[2])
        keep[0, at : at + 8, :] = u
        keep[1, at : at + 8, :] = r
        keep[2, at : at + 8, :] = n
        keep[3, at : at + 8, :] = hid[2]
        ren[at : at + 8, :] = (1.0 - u) * n + u * o
    numbers = mix(source[...], target[...]).astype(F32)
    low = jnp.concatenate([ren[128:MEM, :], numbers, zeros(255 - MEM, BLOCK)], axis=0)
    for role in range(2 * TILES):
        at = pl.multiple_of(step * BLOCK + 128 * role, 128)
        left[pl.ds(at, 128), :] = jnp.transpose(ren[0:128, 128 * role : 128 * role + 128])
        right[pl.ds(at, 128), :] = jnp.transpose(low[:, 128 * role : 128 * role + 128])

    @pl.when(step == pl.num_programs(0) - 1)
    def _():
        pack_rows(cap, rounds, sources, targets, ticks_at, latest, left, right, packed, first, second)


def pack_rows(cap, rounds, sources, targets, ticks, latest, left, right, out, first, second):
    second[...] = jnp.full_like(second, -1.0)

    def chunk(b, count):
        for role, ids in enumerate((sources, targets)):
            def some(g, count):
                for v in range(32):
                    e = b * 128 + g * 32 + v
                    i = b * 256 + role * 128 + g * 32 + v
                    won = latest[ids[e]] == 2 * ticks[e] + role
                    first[pl.ds(count, 1), :] = left[pl.ds(i, 1), :]
                    second[pl.ds(count, 1), :] = right[pl.ds(i, 1), :]
                    count = count + won.astype(I32)
                return count

            count = lax.fori_loop(0, 4, some, count)
        return count

    count = lax.fori_loop(0, sources.shape[0] // 128, chunk, jnp.int32(0))
    second[pl.ds(count, 1), :] = jnp.full((1, 128), -1.0, F32)
    tail = cap // 2
    lane = lax.broadcasted_iota(I32, (1, 128), 1)
    for r in range(rounds):
        at = r * cap
        out[r, 0:cap, :] = first[at : at + cap, :]
        out[r, cap : cap + tail, :] = jnp.concatenate(
            [second[at : at + tail, 0:64], second[at + tail : at + cap, 0:64]], axis=1)
        lines = []
        for q in range(-(-cap // 128)):
            numbers = jnp.transpose(second[at + 128 * q : at + 128 * q + 128, :])[MEM - 128 : MEM - 127]
            lines.append(jnp.where(lane + 128 * q < cap, numbers, -1.0))
        out[r, cap + tail :, :] = jnp.concatenate(lines + [zeros(1, 128)] * (8 - len(lines)), axis=0)


def gru(scale, cap, sources, targets, ticks, latest, own, edge_t, types, wg, wh, vb):
    ends = own.shape[0]
    blocks = ends // BLOCK
    rounds = ends // cap + 1
    spare = rounds * cap + 128
    whole = lambda a: pl.BlockSpec(a.shape, lambda i: (0,) * len(a.shape))
    lanes = lambda: pl.BlockSpec((1, BLOCK // 2), lambda i: (0, i))
    smem = pl.BlockSpec(memory_space=pltpu.SMEM)
    row = lambda x: x.reshape(1, -1)
    packed = jax.ShapeDtypeStruct((rounds, cap + cap // 2 + 8, 128), F32)
    return pl.pallas_call(
        lambda *r: gru_kernel(scale, cap, rounds, *r),
        out_shape=[jax.ShapeDtypeStruct((4 * PAD, ends), BF), jax.ShapeDtypeStruct((5, PAD, ends), F32),
                   jax.ShapeDtypeStruct((PAD, ends), F32), jax.ShapeDtypeStruct((8, ends), F32), packed],
        grid=(blocks,),
        in_specs=[smem] * 4 + [pl.BlockSpec((BLOCK, 256), lambda i: (i, 0)), lanes(), lanes(), lanes(),
                  pl.BlockSpec((MEM, BLOCK // 2), lambda i: (0, i)), lanes(), whole(wg), whole(wh), whole(vb)],
        out_specs=[pl.BlockSpec((4 * PAD, BLOCK), lambda i: (0, i)), pl.BlockSpec((5, PAD, BLOCK), lambda i: (0, 0, i)),
                   pl.BlockSpec((PAD, BLOCK), lambda i: (0, i)), pl.BlockSpec((8, BLOCK), lambda i: (0, i)), whole(packed)],
        scratch_shapes=[pltpu.VMEM((ends, 128), F32), pltpu.VMEM((ends, 128), F32),
                        pltpu.VMEM((spare, 128), F32), pltpu.VMEM((spare, 128), F32)],
        compiler_params=params(), name="gru", cost_estimate=cost(10),
    )(sources, targets, ticks, latest, own, row(sources), row(targets), row(ticks), edge_t, types, wg, wh, vb)


UNROLL = 5
GELU_C = math.sqrt(2.0 / math.pi)


def gelu_parts(x):
    sq = x * x
    t = jnp.tanh(GELU_C * (x + 0.044715 * (sq * x)))
    half = 0.5 * (1.0 + t)
    slope = half + (0.5 * x) * (1.0 - t * t) * (GELU_C + (GELU_C * 3.0 * 0.044715) * sq)
    return x * half, slope


def fold(x):
    total, *others = chunks(x)
    for other in others:
        total = total + other
    return total


def main_kernel(scale, core, near, gaps_t, ticks, msg, keep, ren, gap_own, labels, weights, total,
                wgc, kvm, kvct, kvc, t0t, t0, t1t, t1, t2t, t2, s0t, s0, s1t, s1, vb,
                mine, theirs,
                loss, pair, code, dcode, soft, back, mean, d_query_at, grads, g_in, g_kv, g_one, g_dec, g_qo, g_th, vacc):
    step = pl.program_id(0)
    inv_size = HALF ** -0.5

    @pl.when(step == 0)
    def _():
        for ref in (g_in, g_kv, g_one, g_dec, g_qo, g_th, vacc, loss):
            ref[...] = jnp.zeros_like(ref)

    tick2 = both(ticks[...].astype(F32))
    renewed = ren[...]
    ren_low = renewed.astype(BF)
    queries = nn(t0t[...], ren_low) + across(vb[8])
    def each(one):
        def some(g, carry):
            for v in range(UNROLL):
                one(g * UNROLL + v)
            return carry

        lax.fori_loop(0, NBR // UNROLL, some, 0)

    def look(j):
        gap16 = wide_rows((tick2 - gaps_t[pl.ds(j, 1), :].astype(F32)) * scale, 16)
        for st in range(PAD // 16):
            at = 16 * st
            for m in range(TILES):
                q = slice(256 * m, 256 * m + 256)
                rate, phase = vb[0, at : at + 16, :], vb[1, at : at + 16, :]
                x = jnp.concatenate([rate, rate], axis=1) * gap16[:, q] + jnp.concatenate([phase, phase], axis=1)
                c, s = cos_sin(x)
                code[j, at : at + 16, q] = c.astype(BF)
                dcode[j, at : at + 16, q] = s
        pair[j] = nt(kvm[...], near[j]) + nn(kvct[...], code[j])
        for h in range(2):
            acc = zeros(8, BLOCK)
            for st in range(HPAD // 8):
                at = HPAD * h + 8 * st
                acc = acc + pair[j, at : at + 8, :] * queries[at : at + 8]
            soft[2 * j + h] = wide_rows(jnp.sum(acc, axis=0, keepdims=True) * inv_size, 8)

    each(look)
    for h in range(2):
        top = soft[h]
        for j in range(1, NBR):
            top = jnp.maximum(top, soft[2 * j + h])
        norm = zeros(8, BLOCK)
        for j in range(NBR):
            e = jnp.exp(soft[2 * j + h] - top)
            soft[2 * j + h] = e
            norm = norm + e
        inv = 1.0 / norm
        for j in range(NBR):
            soft[2 * j + h] = soft[2 * j + h] * inv
    att = []
    for st in range(PAD // 8):
        at = 8 * st
        h = 0 if at < HPAD else 1
        acc = across(vb[9, at : at + 8, :])
        for j in range(NBR):
            acc = acc + soft[2 * j + h] * pair[j, PAD + at : PAD + at + 8, :]
        att.append(acc)
    att_low = jnp.concatenate(att, axis=0).astype(BF)
    projected = nn(s0t[...], att_low) + across(vb[10])
    mlp_in = jnp.concatenate([projected.astype(BF), ren_low], axis=0)
    inner = nn(t1t[...], mlp_in) + across(vb[11])
    act, act_slope = gelu_parts(inner)
    act_low = act.astype(BF)
    emb_low = (nn(s1t[...], act_low) + across(vb[12])).astype(BF)
    dec_in = jnp.concatenate([sources_of(emb_low), targets_of(emb_low)], axis=0)
    out_row = jnp.concatenate([vb[14]] * TILES, axis=1)
    dec_pre = nn(t2t[...], dec_in) + jnp.concatenate([vb[13]] * TILES, axis=1)
    dec_act, dec_slope = gelu_parts(dec_pre)
    logit = jnp.sum(dec_act * out_row, axis=0, keepdims=True)
    label = labels[...].astype(F32)
    tail = jnp.exp(-jnp.abs(logit))
    plus = jnp.maximum(logit, 0.0) + jnp.log1p(tail)
    loss[...] += fold(weights[...] * (plus - label * logit))
    d_logit = weights[...] / total[:, 0:1] * (sigmoid(logit) - label)
    d_out = d_logit * dec_act
    d_dec = (d_logit * out_row) * dec_slope
    d_dec_low = d_dec.astype(BF)
    g_dec[...] += nt(d_dec_low, dec_in)
    d_dec_in = nn(t2[...], d_dec_low)
    d_emb = mix(d_dec_in[:PAD], d_dec_in[PAD:])
    d_emb_low = d_emb.astype(BF)
    g_th[:, 0:256] += jnp.concatenate([nt(act_low, d_emb_low), zeros(PAD, 256 - PAD)], axis=1)
    d_inner = nn(s1[...], d_emb_low) * act_slope
    d_inner_low = d_inner.astype(BF)
    g_one[...] += nt(d_inner_low, mlp_in)
    d_mlp = nn(t1[...], d_inner_low)
    d_proj = d_mlp[:PAD]
    d_proj_low = d_proj.astype(BF)
    g_qo[:, 256:512] += jnp.concatenate([nt(att_low, d_proj_low), zeros(PAD, 256 - PAD)], axis=1)
    d_att = nn(s0[...], d_proj_low)
    d_query_at[...] = jnp.zeros_like(d_query_at)
    mean[...] = jnp.zeros_like(mean)

    def weigh(j):
        for h in range(2):
            acc = zeros(8, BLOCK)
            for st in range(HPAD // 8):
                at = HPAD * h + 8 * st
                acc = acc + pair[j, PAD + at : PAD + at + 8, :] * d_att[at : at + 8]
            wide = wide_rows(jnp.sum(acc, axis=0, keepdims=True), 8)
            back[2 * j + h] = wide
            mean[h] += wide * soft[2 * j + h]

    def learn(j):
        share = [soft[2 * j + h] for h in range(2)]
        slope = [(share[h] * inv_size) * (back[2 * j + h] - mean[h]) for h in range(2)]
        for st in range(PAD // 8):
            at = 8 * st
            d_query_at[at : at + 8, :] += slope[at >= HPAD] * pair[j, at : at + 8, :]
        for st in range(2 * PAD // 16):
            parts = []
            for half in range(2):
                at = 16 * st + 8 * half
                if at < PAD:
                    parts.append(slope[at >= HPAD] * queries[at : at + 8])
                else:
                    parts.append(share[at - PAD >= HPAD] * d_att[at - PAD : at - PAD + 8])
            grads[j, 16 * st : 16 * st + 16, :] = jnp.concatenate(parts, axis=0).astype(BF)
        d_code = nn(kvc[...], grads[j])
        gap8 = wide_rows((tick2 - gaps_t[pl.ds(j, 1), :].astype(F32)) * scale, 8)
        for st in range(PAD // 8):
            at = 8 * st
            d_arg = d_code[at : at + 8] * dcode[j, at : at + 8, :]
            vacc[0, at : at + 8, :] += fold(d_arg * gap8)
            vacc[1, at : at + 8, :] += fold(d_arg)
        g_kv[:, 0:256] += nn(grads[j], near[j])
        g_kv[:, 256 : 256 + PAD] += nt(grads[j], code[j])

    each(weigh)
    each(learn)
    d_query = d_query_at[...]
    d_q_low = d_query.astype(BF)
    g_qo[:, 0:256] += jnp.concatenate([nt(d_q_low, ren_low), zeros(PAD, 256 - PAD)], axis=1)
    d_ren = d_mlp[PAD:] + nn(t0[...], d_q_low)
    own_x = msg[0:PAD, :].astype(F32)
    u, r, n, hn = keep[0], keep[1], keep[2], keep[3]
    d_u = d_ren * (own_x - n) * (u * (1.0 - u))
    d_n = d_ren * (1.0 - u) * (1.0 - n * n)
    d_r = d_n * hn * (r * (1.0 - r))
    d_h = d_n * r
    gates = jnp.concatenate([d_u, d_r, d_n], axis=0).astype(BF)
    g_in[...] += nt(gates, msg[...])
    g_th[:, 256:512] += jnp.concatenate([nt(msg[0:PAD, :], d_h.astype(BF)), zeros(PAD, 256 - PAD)], axis=1)
    d_arg = nn(wgc[...], gates) * keep[4]
    vacc[0] += fold(d_arg * gap_own[0:1, :])
    vacc[1] += fold(d_arg)
    for i, item in ((2, d_u), (3, d_r), (4, d_n), (7, d_h), (8, d_query), (9, d_att), (10, d_proj), (11, d_inner),
                    (12, d_emb), (15, d_q_low.astype(F32))):
        vacc[i] += fold(item)
    vacc[13] += fold(d_dec)
    vacc[14] += fold(d_out)

    def finish(ga, gb):
        wide = cols_to(g_in[...], 768)
        for c in range(6):
            gb[528 * c : 528 * c + 528, :] = wide[:, 128 * c : 128 * c + 128]
        lane = lax.broadcasted_iota(I32, (PAD, 128), 1)
        vecs = zeros(PAD, 128)
        for i in range(16):
            column = jnp.sum(vacc[i], axis=1, keepdims=True)
            vecs = jnp.where(lane == i, column, vecs)
        flat = jnp.transpose(jnp.concatenate([vecs, zeros(256 - PAD, 128)], axis=0))
        gb[3168:3184, :] = flat[0:16, 0:128]
        gb[3184:3200, :] = flat[0:16, 128:256]
        at = 0
        for left, right, rows in ((g_kv[:, 0:PAD], g_kv[:, 256 : 256 + PAD], 352),
                                  (g_one[:, 0:PAD], g_one[:, PAD : 2 * PAD], 176),
                                  (g_dec[:, 0:PAD], g_dec[:, PAD : 2 * PAD], 176),
                                  (g_qo[:, 0:PAD], g_qo[:, 256 : 256 + PAD], 176),
                                  (g_th[:, 0:PAD], g_th[:, 256 : 256 + PAD], 176)):
            wide = jnp.concatenate([left, right, zeros(rows, 32)], axis=1)
            for c in range(3):
                ga[at : at + rows, :] = wide[:, 128 * c : 128 * c + 128]
                at += rows
        ga[3168:3200, :] = rows_to(loss[...], 32)

    @pl.when((step == pl.num_programs(0) - 1) & (core[0] == 0))
    def _():
        finish(mine, theirs)

    @pl.when((step == pl.num_programs(0) - 1) & (core[0] != 0))
    def _():
        finish(theirs, mine)


def main(scale, near, near_ticks, ticks, msg, keep, ren, gap_own, labels, weights, total, core, w):
    ends = ren.shape[1]
    blocks = ends // BLOCK
    whole = lambda a: pl.BlockSpec(a.shape, lambda i: (0,) * len(a.shape))
    lanes = lambda: pl.BlockSpec((1, BLOCK // 2), lambda i: (0, i))
    return pl.pallas_call(
        lambda *r: main_kernel(scale, *r),
        out_shape=[jax.ShapeDtypeStruct((3200, 128), F32), jax.ShapeDtypeStruct((3200, 128), F32)],
        grid=(blocks,),
        in_specs=[pl.BlockSpec(memory_space=pltpu.SMEM), pl.BlockSpec((NBR, BLOCK, 256), lambda i: (0, i, 0)), pl.BlockSpec((NBR, BLOCK), lambda i: (0, i)), lanes(),
                  pl.BlockSpec((4 * PAD, BLOCK), lambda i: (0, i)), pl.BlockSpec((5, PAD, BLOCK), lambda i: (0, 0, i)),
                  pl.BlockSpec((PAD, BLOCK), lambda i: (0, i)), pl.BlockSpec((8, BLOCK), lambda i: (0, i)), lanes(), lanes(),
                  pl.BlockSpec((1, 128), lambda i: (0, 0))] + [whole(a) for a in w],
        out_specs=[pl.BlockSpec((3200, 128), lambda i: (0, 0)), pl.BlockSpec((3200, 128), lambda i: (0, 0))],
        scratch_shapes=[pltpu.VMEM((1, 128), F32), pltpu.VMEM((NBR, 352, BLOCK), F32), pltpu.VMEM((NBR, PAD, BLOCK), BF), pltpu.VMEM((NBR, PAD, BLOCK), F32),
                        pltpu.VMEM((20, 8, BLOCK), F32), pltpu.VMEM((20, 8, BLOCK), F32), pltpu.VMEM((2, 8, BLOCK), F32),
                        pltpu.VMEM((PAD, BLOCK), F32), pltpu.VMEM((NBR, 352, BLOCK), BF),
                        pltpu.VMEM((528, 704), F32), pltpu.VMEM((352, 512), F32), pltpu.VMEM((PAD, 352), F32),
                        pltpu.VMEM((PAD, 352), F32), pltpu.VMEM((PAD, 512), F32), pltpu.VMEM((PAD, 512), F32),
                        pltpu.VMEM((16, PAD, 128), F32)],
        compiler_params=params(), name="main", cost_estimate=cost(35),
    )(core, near.reshape(NBR, ends, 256), near_ticks, ticks, msg, keep, ren, gap_own, labels, weights, total, *w)


def room(nodes, devices):
    return -(-(nodes * 9) // (devices * 8 * 16)) * 16


def turned_exactly(x):
    high = x.astype(BF)
    rest = x - high.astype(F32)
    middle = rest.astype(BF)
    low = (rest - middle.astype(F32)).astype(BF)
    unit = eye(x.shape[1])
    return (nt(unit, high) + nt(unit, middle)) + nt(unit, low)


def merge_kernel(cap, group, steps, ids, counts, rows, mem, out, left, right, second):
    step = pl.program_id(0)
    tail = cap // 2
    width = -(-cap // 128) * 128

    @pl.when(step == 0)
    def _():
        left[...] = jnp.zeros_like(left)
        right[...] = jnp.full_like(right, -1.0)

    @pl.when(step < steps)
    def _():
        for q in range(group):
            half = rows[q, cap : cap + tail, :]
            second[q, 0:tail, :] = half
            second[q, tail:cap, :] = jnp.concatenate([half[:, 64:], half[:, :64]], axis=1)
        for q in range(group):
            base = (step * group + q) * width

            def some(g, carry):
                for v in range(16):
                    i = g * 16 + v
                    node = ids[base + i]
                    left[pl.ds(node, 1), :] = rows[q, pl.ds(i, 1), :]
                    right[pl.ds(node, 1), :] = second[q, pl.ds(i, 1), :]
                return carry

            lax.fori_loop(0, lax.div(counts[step * group + q] + 15, 16), some, 0)

    @pl.when(step >= steps)
    def _():
        cols = mem.shape[1]
        base = pl.multiple_of((step - steps) * cols, cols)
        for c in range(cols // 256):
            at = base + 256 * c
            s = slice(256 * c, 256 * c + 256)
            top = turned_exactly(left[pl.ds(at, 256), :])
            low = turned_exactly(right[pl.ds(at, 256), :])
            fresh = low[MEM - 128 : MEM - 127] >= 0.0
            out[0:128, s] = jnp.where(fresh, top, mem[0:128, s])
            out[128:MEM, s] = jnp.where(fresh, low[: MEM - 128], mem[128:MEM, s])


def merge(cap, gathered, mem_t):
    blocks, height, _ = gathered.shape
    nodes = mem_t.shape[1]
    cols, group = 4096, 8
    steps = blocks // group
    numbers = gathered[:, height - 8 : height - 8 + -(-cap // 128), :].reshape(blocks, -1)
    counts = jnp.sum((numbers >= 0.0).astype(I32), axis=1)
    ids = jnp.where(numbers >= 0.0, numbers, float(nodes)).astype(I32).reshape(-1)
    smem = pl.BlockSpec(memory_space=pltpu.SMEM)
    part = lambda i: (0, jnp.maximum(i - steps, 0))
    new = pl.pallas_call(
        lambda *r: merge_kernel(cap, group, steps, *r),
        out_shape=jax.ShapeDtypeStruct((MEM, nodes), F32),
        grid=(steps + nodes // cols,),
        in_specs=[smem, smem, pl.BlockSpec((group, height, 128), lambda i: (jnp.minimum(i, steps - 1), 0, 0)),
                  pl.BlockSpec((MEM, cols), part)],
        out_specs=pl.BlockSpec((MEM, cols), part),
        scratch_shapes=[pltpu.VMEM((nodes + 8, 128), F32), pltpu.VMEM((nodes + 8, 128), F32), pltpu.VMEM((group, cap, 128), F32)],
        compiler_params=params(), name="merge", cost_estimate=cost(20),
    )(ids, counts, gathered, mem_t)
    return new, jnp.any(counts == cap)


def move(param, one, two, grad, factor, rate, decay):
    clipped = grad * factor
    one = BETA_ONE * one + (1.0 - BETA_ONE) * clipped
    two = BETA_TWO * two + (1.0 - BETA_TWO) * clipped * clipped
    step = (one * (1.0 / (1.0 - BETA_ONE**STEP))) / (jnp.sqrt(two * (1.0 / (1.0 - BETA_TWO**STEP))) + ADAM_EPS)
    return param - rate * (step + decay * param), one, two


def unsplit(x, axis):
    take = lambda a, b: lax.slice_in_dim(x, a, b, axis=axis)
    return jnp.concatenate([take(0, HALF), take(HPAD, HPAD + HALF)], axis=axis)


def adam_kernel(parts, where, *refs):
    count = sum(n for _, n in parts)
    mine, other = refs[:count], refs[count : 2 * count]
    refs = refs[2 * count :]
    state, news, (norm_out, loss_out) = refs[:18], refs[18:36], refs[36:38]
    a, b, g_gin, g_hid, g_kv, g_tall, g_sq, g_vec = refs[38:]
    core = where[0]
    at_block = 0
    for p, (first, n) in enumerate(parts):
        height = mine[at_block].shape[0]
        for k in range(n):
            at = pl.multiple_of(first + (where[1 + p] ^ k) * height, 8)
            one, two = mine[at_block], other[at_block]
            at_block += 1

            @pl.when(core == 0)
            def _():
                a[pl.ds(at, height), :] = one[...]
                b[pl.ds(at, height), :] = two[...]

            @pl.when(core != 0)
            def _():
                b[pl.ds(at, height), :] = one[...]
                a[pl.ds(at, height), :] = two[...]

    def panels(ref, at, rows, n):
        return jnp.concatenate([ref[at + c * rows : at + (c + 1) * rows, :] for c in range(n)], axis=1)

    vec = state[5]
    tall = state[3]
    wide = panels(b, 0, 528, 6)
    gates = []
    for g in range(3):
        rows = wide[PAD * g : PAD * g + MEM]
        gates.append(jnp.concatenate([rows[:, PAD * q : PAD * q + MEM] for q in range(4)], axis=1))
    g_gin[...] = jnp.concatenate(gates, axis=0)
    vecs = jnp.concatenate([b[3168:3184, :], b[3184:3200, :]], axis=1)
    kv = panels(a, 0, 352, 3)
    kv = jnp.concatenate([unsplit(kv[:PAD], 0), unsplit(kv[PAD:], 0)], axis=0)
    kv = jnp.concatenate([kv[:, :MEM], kv[:, PAD : PAD + MEM]], axis=1)
    g_kv[...] = jnp.transpose(rows_to(cols_to(kv, 384), 384))[: 2 * MEM, : 2 * MEM]
    for i, at in ((1, 1056), (2, 1584)):
        x = panels(a, at, PAD, 3)[:MEM]
        g_tall[i] = jnp.concatenate([x[:, :MEM], x[:, PAD : PAD + MEM]], axis=1)
    both = unsplit(panels(a, 2112, PAD, 3), 0)
    sum_dq = unsplit(jnp.transpose(rows_to(vecs, 128))[:PAD, 15:16], 0)
    phase = vec[1:2, :]
    phase_low = jnp.cos(phase).astype(BF).astype(F32)
    g_tall[0] = jnp.concatenate([both[:, :MEM], sum_dq * phase_low], axis=1)
    g_sq[0] = both[:, PAD : PAD + MEM]
    last = panels(a, 2640, PAD, 3)[:MEM]
    g_sq[1] = last[:, :MEM]
    shared = jnp.transpose(rows_to(cols_to(g_gin[0 : 2 * MEM, 0:MEM], 256), 384))[:MEM, : 2 * MEM]
    g_hid[...] = jnp.concatenate([shared, last[:, PAD : PAD + MEM]], axis=1)
    query_low = tall[0][:, MEM:].astype(BF).astype(F32)
    phase_in = jnp.sum(query_low * sum_dq, axis=0, keepdims=True)
    row = lambda i: vecs[i : i + 1, :MEM]
    g_vec[...] = jnp.concatenate(
        [row(0), row(1) - jnp.sin(phase) * phase_in, row(2), row(3), row(4), row(2), row(3), row(7),
         unsplit(vecs[8:9], 1), unsplit(vecs[9:10], 1)] + [row(i) for i in range(10, 15)], axis=0)
    total = jnp.zeros((1, 1), F32)
    for ref in (g_gin, g_hid, g_kv, g_vec):
        total += jnp.sum(ref[...] * ref[...], keepdims=True)
    for ref in (g_tall, g_sq):
        for i in range(ref.shape[0]):
            total += jnp.sum(ref[i] * ref[i], keepdims=True)
    norm = jnp.sqrt(total)
    factor = jnp.minimum(1.0, CLIP_AT / (norm + NORM_EPS))
    norm_out[...] = norm
    loss_out[...] = jnp.sum(a[3168:3169, :], keepdims=True)
    for i, grad in enumerate((g_gin, g_hid, g_kv, g_tall, g_sq, g_vec)):
        rate, decay = (VECTOR_RATE, 0.0) if i == 5 else (LEARN_RATE, DECAY)
        param, one, two = state[i], state[6 + i], state[12 + i]
        new = news[i], news[6 + i], news[12 + i]
        if i == 4:
            for j in range(2):
                made = move(param[:, j, :], one[:, j, :], two[:, j, :], grad[j], factor, rate, decay)
                for ref, value in zip(new, made):
                    ref[:, j, :] = value
        elif len(param.shape) == 3:
            for j in range(param.shape[0]):
                made = move(param[j], one[j], two[j], grad[j], factor, rate, decay)
                for ref, value in zip(new, made):
                    ref[j] = value
        else:
            rows = param.shape[0]
            for at in range(0, rows, 16):
                s = slice(at, min(at + 16, rows))
                made = move(param[s], one[s], two[s], grad[s], factor, rate, decay)
                for ref, value in zip(new, made):
                    ref[s] = value


def adam(where, parts, mine, other, state):
    swap = lambda x: jnp.transpose(x, (0, 2, 1))
    def ready(group):
        gin, hid, kv, tall, sq, vec = group
        return [gin.T, hid, kv, swap(tall), jnp.transpose(sq, (1, 0, 2)), vec]
    state = ready(state[0:6]) + ready(state[6:12]) + ready(state[12:18])
    count = len(mine)
    shapes = [x.shape for x in state[:6]]
    shapes[4] = (2, MEM, MEM)
    vm = pl.BlockSpec(memory_space=pltpu.VMEM)
    outs = [jax.ShapeDtypeStruct(x.shape, F32) for x in state] + [jax.ShapeDtypeStruct((1, 1), F32)] * 2
    out = pl.pallas_call(
        lambda *r: adam_kernel(parts, *r),
        out_shape=outs,
        in_specs=[pl.BlockSpec(memory_space=pltpu.SMEM)] + [vm] * (2 * count + 18),
        out_specs=[vm] * 20,
        scratch_shapes=[pltpu.VMEM((3200, 128), F32), pltpu.VMEM((3200, 128), F32)] + [pltpu.VMEM(s, F32) for s in shapes],
        compiler_params=params(), name="adam", cost_estimate=cost(14),
    )(where, *mine, *other, *state)
    back = lambda group: [group[0].T, group[1], group[2], swap(group[3]), jnp.transpose(group[4], (1, 0, 2)), group[5]]
    return out[18].reshape(()), out[19].reshape(()), back(out[0:6]) + back(out[6:12]) + back(out[12:18])


AXES = ("dp", "rep")


def levels(size):
    found, stride = [], 1
    while size > 1:
        n = size if size <= 8 else 4
        found.append((stride, n))
        stride, size = stride * n, size // n
    return found


def peers(stride, k):
    dp, rep = lax.axis_size("dp"), lax.axis_size("rep")
    return [(d * rep + r, (d ^ (k * stride)) * rep + r) for d in range(dp) for r in range(rep)]


def twin():
    dp, rep = lax.axis_size("dp"), lax.axis_size("rep")
    return [(d * rep + r, d * rep + (rep - 1 - r)) for d in range(dp) for r in range(rep)]


def send(x, pairs):
    return lax.ppermute(x, AXES, pairs)


def tree(items, join):
    while len(items) > 1:
        items = [join(items[i], items[i + 1]) for i in range(0, len(items), 2)]
    return items[0]


def place(d, stride, n):
    return lax.rem(lax.div(d, stride), n)


def reduce_level(items, d, stride, n):
    c = place(d, stride, n)
    rows = items[0].shape[0] // n
    piece = lambda k: tree([lax.dynamic_slice_in_dim(x, (c ^ k) * rows, rows, 0) for x in items], jnp.add)
    return [piece(0)] + [send(piece(k), peers(stride, k)) for k in range(1, n)]


def gather_level(x, d, stride, n):
    return [x] + [send(x, peers(stride, k)) for k in range(1, n)]


def in_order(pieces, d, stride, n):
    c = place(d, stride, n)
    lines = []
    for i in range(n):
        line = pieces[i]
        for k in range(n):
            if k != i:
                line = jnp.where((c ^ k) == i, pieces[k], line)
        lines.append(line)
    return jnp.concatenate(lines, axis=0)


def spread_latest(x, d):
    nodes = lax.broadcasted_iota(I32, x.shape, 0) < x.shape[0] - 1
    join = lambda p, q: jnp.where(nodes, jnp.maximum(p, q), p + q)
    x = join(x, send(x, twin()))
    for stride, n in levels(lax.axis_size("dp")):
        x = tree(gather_level(x, d, stride, n), join)
    return x


def sum_grads(mine, theirs, d):
    steps = levels(lax.axis_size("dp"))
    items = [mine, send(theirs, twin())]
    for level in steps:
        items = reduce_level(items, d, *level)
    x = tree(items, jnp.add)
    for level in steps[:0:-1]:
        x = in_order(gather_level(x, d, *level), d, *level)
    return x, steps[0]


def body(source, target, neighbours, neighbour_ticks, event_ticks, event_types, labels, edge_feats, weights, memory,
         node_ticks, gru_in, gru_hid, keys_values, tall_stack, squares, vectors, *moments):
    events = event_ticks.shape[0]
    nodes = memory.shape[0]
    devices = lax.axis_size("dp") * lax.axis_size("rep")
    d, core = lax.axis_index("dp"), lax.axis_index("rep")
    scale = TIME_RATE / (events * devices)
    tiles = events // 128
    order = lambda x: jnp.transpose(x, (2, 1, 0)).reshape(NBR, 2, tiles, 128).transpose(0, 2, 1, 3).reshape(NBR, 2 * events)
    near_ids = order(neighbours).reshape(-1)
    near_ticks = order(neighbour_ticks)
    row = lambda x: x.reshape(1, events)
    lines = lambda x: x.reshape(tiles, 128)
    mem_t = memory.T
    spread = first_latest(nodes, lines(source), lines(target), lines(event_ticks), lines(weights))
    spread = spread_latest(spread, d)
    latest = spread[:-1].reshape(-1).astype(I32)
    w = prep(gru_in, gru_hid, keys_values, tall_stack, squares, vectors)
    wg, wgc, wh = w[0], w[1], w[2]
    vb = w[-1]
    own, near = fetch(source, target, near_ids, mem_t, node_ticks)
    cap = room(nodes, devices)
    msg, keep, ren, gap_own, packed = gru(
        scale, cap, source, target, event_ticks, latest, own, edge_feats.T, row(event_types), wg, wh, vb)
    gathered = lax.all_gather(packed[0], AXES)
    mine, theirs = main(scale, near, near_ticks, row(event_ticks), msg, keep, ren, gap_own, row(labels), row(weights),
                        spread[-1:], core.reshape(1), [wgc] + list(w[3:]))
    piece, level = sum_grads(mine, theirs, d)
    piece, gathered = lax.optimization_barrier((piece, gathered))
    blocks = gather_level(piece, d, *level)
    new_mem, more = merge(cap, gathered, mem_t)
    *blocks, new_mem = lax.optimization_barrier((*blocks, new_mem))
    other = [send(x, twin()) for x in blocks]
    grad_norm, loss_sum, news = adam(
        jnp.stack([core, place(d, *level)]), [(0, len(blocks))], blocks, other,
        (gru_in, gru_hid, keys_values, tall_stack, squares, vectors) + moments)
    weight_sum = spread[-1, 0]

    def again(carry):
        r, _, mem_now = carry
        mem_now, more = merge(cap, lax.all_gather(lax.dynamic_index_in_dim(packed, r, 0, False), AXES), mem_now)
        return r + 1, more & (r + 1 < packed.shape[0]), mem_now

    if packed.shape[0] > 1:
        new_mem = lax.while_loop(lambda c: c[1], again, (jnp.int32(1), more, new_mem))[2]
    return (grad_norm, loss_sum, weight_sum, new_mem.T, *news)


def solution(mesh):
    split = P(AXES)
    placed = (split, split, P(AXES, None, None), P(AXES, None, None), split, split, split, P(AXES, None), split)
    return jax.shard_map(body, mesh=mesh, in_specs=placed + (P(),) * 20, out_specs=(P(),) * 22, check_vma=False)
```

time: 287 us -> 221 us (0.77)
  Pallas kernels: 146 us -> 112 us
  local copies, waits for them, and re-layouts: 27 us -> 3.37 us
  other arithmetic: 16 us -> 8.31 us
    pallas_call x6 -> x5, Pallas kernels: 104 us -> 74.4 us  [the longest x1 23.1 us: fetch(): pl.pallas_call(lambda *r: fetch_kernel(steps, chunk, *r), out_shape=[jax....]
    unnamed x26 -> x16, local copies, waits for them, and re-layouts: 17.2 us -> 0.05 us
    another operation x4 -> x1, other arithmetic: 7.37 us -> 0.56 us  [body(): jnp.stack([core, place(d, *level)])]
    pallas_call x1, Pallas kernels: 35.8 us -> 31.3 us  [main(): pl.pallas_call(lambda *r: main_kernel(scale, *r), out_shape=[jax.ShapeDty...]
    slice x1 -> x2, local copies, waits for them, and re-layouts: 5.05 us -> 1.42 us  [the longest x1 0.91 us: merge(): gathered[:, height - 8:height - 8 + -(-cap // 128), :].reshape(blocks, -1)]
  transfers between devices with their start and end apart: 25 -> 25, of which waited for: 16 -> 13; matrix products, arithmetic and copies ran while one was open for 7% -> 3% of each run, Pallas kernels for 36% -> 37%
where the time goes in v3:
time: 221 us; the launch traced here: 220 us
  Pallas kernels  112 us (51%)
  waiting for transfers between devices  54.6 us (25%)
  starting transfers between devices  27.1 us (12%)
  between operations  14.3 us (6%)
  other arithmetic  8.31 us (4%)
  local copies, waits for them, and re-layouts  3.37 us (2%)
    ppermute x24, waiting for transfers between devices, send(): return lax.ppermute(x, AXES, pairs)  54.5 us
    pallas_call x1, Pallas kernels, main(): pl.pallas_call(lambda *r: main_kernel(scale, *r), out_shape=[jax.ShapeDty...  31.3 us
    ppermute x24, starting transfers between devices, send(): return lax.ppermute(x, AXES, pairs)  27 us
    pallas_call x1, Pallas kernels, fetch(): pl.pallas_call(lambda *r: fetch_kernel(steps, chunk, *r), out_shape=[jax....  23.1 us
    pallas_call x1, Pallas kernels, merge(): pl.pallas_call(lambda *r: merge_kernel(cap, group, steps, *r), out_shape=...  22 us
    pallas_call x1, Pallas kernels, adam(): pl.pallas_call(lambda *r: adam_kernel(parts, *r), out_shape=outs, in_spec...  15.8 us
    pallas_call x1, Pallas kernels, gru(): pl.pallas_call(lambda *r: gru_kernel(scale, cap, rounds, *r), out_shape=[...  10.7 us
    pallas_call x1, Pallas kernels, prep(): pl.pallas_call(prep_kernel, out_shape=outs, compiler_params=params(), nam...  6.11 us
  transfers between devices with their start and end apart: 25, of which 13 were waited for; matrix products, arithmetic and copies ran while one was open for 3% of the time, Pallas kernels for 37%

profile of v3, /device:TPU:0, one launch (start us, length us, event | category | flops | bytes accessed | tf_op | source)
XLA Modules:
  0.0 220.2 jit_solution(3600753260778621700)
XLA Ops:
  7.2 2.8 %latest.1 = f32[65,128]{1,0:T(8,128)} custom-call(s32[4,128]{1,0:T(4,128)} %bitcast.71, s32[4,128]{1,0:T(4,128)} %bitcast.73, s32[4,128]{1,0:T(4,128)} %bitcast.76, f32[4,128]{1,0:T(4,128)} %bitcast.79), custom_call_target="tpu_custom_call" | custom-call | flops 2000000000 | bytes 6000000 | tf_op jit(solution)/shard_map/latest/pallas_call | solution.py:161
  12.4 2.9 %collective-permute-start.2 = (f32[65,128]{1,0:T(8,128)S(1)}, f32[65,128]{1,0:T(8,128)S(1)}, u32[]{:S(2)}, u32[]{:S(2)}) collective-permute-start(f32[65,128]{1,0:T(8,128)S(1)} %add_select_fusion.2), channel_id=1, source_target_pairs={{0,4},{1,5},{2,6},{3,7},{4,0},{5,1},{6,2},{7,3},{8,12},{9,13},{10,... | collective-permute-start | bytes 99848 | tf_op jit(solution)/shard_map/ppermute | solution.py:866
  16.9 23.1 %fetch.1 = (bf16[1024,256]{1,0:T(8,128)(2,1)}, bf16[10240,256]{1,0:T(8,128)(2,1)}) custom-call(s32[512]{0:T(512)} %r_0_.3, s32[512]{0:T(512)} %r_1_.3, s32[10240]{0:T(1024)} %bitcast.69, f32[172,8192]{1,0:T(8,128)} %bitcast.54, s32[1,8192]{1,0:T(1,128)} %bitcast.70), custom_call_target="tpu_custom_call" | custom-call | flops 17999998976 | bytes 54000000 | tf_op jit(solution)/shard_map/fetch/pallas_call | solution.py:229
  40.1 3.1 %collective-permute-start.5 = (f32[65,128]{1,0:T(8,128)S(1)}, f32[65,128]{1,0:T(8,128)S(1)}, u32[]{:S(2)}, u32[]{:S(2)}) collective-permute-start(f32[65,128]{1,0:T(8,128)S(1)} %add_select_fusion.1), channel_id=1, source_target_pairs={{0,16},{1,17},{2,18},{3,19},{4,20},{5,21},{6,22},{7,23},{8,24},{9,... | collective-permute-start | bytes 99848 | tf_op jit(solution)/shard_map/ppermute | solution.py:866
  44.8 6.1 %prep.1 = (bf16[528,704]{1,0:T(8,128)(2,1)}, bf16[176,528]{1,0:T(8,128)(2,1)}, bf16[528,176]{1,0:T(8,128)(2,1)}, bf16[352,256]{1,0:T(8,128)(2,1)}, bf16[352,176]...) custom-call(f32[516,688]{1,0:T(8,128)} %bitcast.56, ...), custom_call_target="tpu_custom_call" | custom-call | flops 6000000000 | bytes 18000000 | tf_op jit(solution)/shard_map/prep/pallas_call | solution.py:125
  51.6 10.7 %gru.1 = (bf16[704,1024]{1,0:T(8,128)(2,1)}, f32[5,176,1024]{2,1,0:T(8,128)}, f32[176,1024]{1,0:T(8,128)}, f32[8,1024]{1,0:T(8,128)}, f32[4,440,128]{2,1,0:T(8,128)S(1)}) custom-call(s32[512]{0:T(512)} %r_0_.3, s32[512]{0:T(512)} %r_1_.3, s32[512]{0:T(512)} %r_2_.1, s32[8192]{0:T(1024)} %fusion.2.r_3_, bf16[1024,256]{1,0:T(8,128)(2,1)} %get-tuple-element.97.r_4_, ...), custom_call_target="tpu_custom_call" | custom-call | flops 10000000000 | bytes 30000000 | tf_op jit(solution)/shard_map/gru/pallas_call | solution.py:385
  64.3 31.3 %main.1 = (f32[3200,128]{1,0:T(8,128)}, f32[3200,128]{1,0:T(8,128)}) custom-call(s32[1]{0:T(128)} %bitcast.r_0_, bf16[10,1024,256]{2,1,0:T(8,128)(2,1)} %bitcast.82, s32[10,1024]{1,0:T(8,128)} %reshape.113.r_2_, s32[1,512]{1,0:T(1,128)} %bitcast.78, bf16[704,1024]{1,0:T(8,128)(2,1)} %get-tuple-element.101.r_4_, f32[5,176,1024]{2,1,0:T(8,128)} %get-tuple-element.102.r_5_, ...), custom_call_target="tpu_custom_call" | custom-call | flops 35000000512 | bytes 105000000 | tf_op jit(solution)/shard_map/main/pallas_call | solution.py:616
  95.6 3.7 %collective-permute-done.7 = f32[3200,128]{1,0:T(8,128)S(1)} collective-permute-done((f32[3200,128]{1,0:T(8,128)}, f32[3200,128]{1,0:T(8,128)S(1)}, u32[]{:S(2)}, u32[]{:S(2)}) %collective-permute-start.7) | collective-permute-done | bytes 1638432 | tf_op jit(solution)/shard_map/ppermute | solution.py:866
  99.3 2.4 %dynamic-slice_add_fusion.3 = (f32[800,128]{1,0:T(8,128)S(1)}, f32[800,128]{1,0:T(8,128)}, f32[800,128]{1,0:T(8,128)}, f32[800,128]{1,0:T(8,128)S(1)}) fusion(f32[3200,128]{1,0:T(8,128)S(1)} %collective-permute-done.7, s32[]{:T(128)S(6)} %select_n.158, f32[3200,128]{1,0:T(8,128)} %get-tuple-element.119, s32[]{:T(128)S(6)} %select_n.162, s32[]{:T(128)S(6)} %select_n.161, ...), kind=kLoop, calls=%fused_computation.9 | loop fusion | flops 409600 | bytes 4915216 | tf_op jit(solution)/shard_map/add | solution.py:871
  101.7 2.5 %collective-permute-start.10 = (f32[800,128]{1,0:T(8,128)}, f32[800,128]{1,0:T(8,128)S(1)}, u32[]{:S(2)}, u32[]{:S(2)}) collective-permute-start(f32[800,128]{1,0:T(8,128)} %get-tuple-element.159), channel_id=1, source_target_pairs={{0,6},{1,7},{2,4},{3,5},{4,2},{5,3},{6,0},{7,1},{8,14},{9,15},{10,... | collective-permute-start | bytes 1228808 | tf_op jit(solution)/shard_map/ppermute | solution.py:866
  105.2 13.4 %collective-permute-done.10 = f32[800,128]{1,0:T(8,128)S(1)} collective-permute-done((f32[800,128]{1,0:T(8,128)}, f32[800,128]{1,0:T(8,128)S(1)}, u32[]{:S(2)}, u32[]{:S(2)}) %collective-permute-start.10) | collective-permute-done | bytes 409632 | tf_op jit(solution)/shard_map/ppermute | solution.py:866
  118.6 13.3 %collective-permute-done.9 = f32[800,128]{1,0:T(8,128)S(1)} collective-permute-done((f32[800,128]{1,0:T(8,128)}, f32[800,128]{1,0:T(8,128)S(1)}, u32[]{:S(2)}, u32[]{:S(2)}) %collective-permute-start.9) | collective-permute-done | bytes 409632 | tf_op jit(solution)/shard_map/ppermute | solution.py:866
  131.9 3.2 %collective-permute-done.8 = f32[800,128]{1,0:T(8,128)S(1)} collective-permute-done((f32[800,128]{1,0:T(8,128)S(1)}, f32[800,128]{1,0:T(8,128)S(1)}, u32[]{:S(2)}, u32[]{:S(2)}) %collective-permute-start.8) | collective-permute-done | bytes 409632 | tf_op jit(solution)/shard_map/ppermute | solution.py:866
  135.2 2.2 collective-permute-start.11
  137.3 2.6 %collective-permute-start.13 = (f32[200,128]{1,0:T(8,128)S(1)}, f32[200,128]{1,0:T(8,128)S(1)}, u32[]{:S(2)}, u32[]{:S(2)}) collective-permute-start(f32[200,128]{1,0:T(8,128)S(1)} %get-tuple-element.163), channel_id=1, source_target_pairs={{0,24},{1,25},{2,26},{3,27},{4,28},{5,29},{6,30},{7,31},{8,16},{9,... | collective-permute-start | bytes 307208 | tf_op jit(solution)/shard_map/ppermute | solution.py:866
  139.9 3.9 %collective-permute-done.11 = f32[200,128]{1,0:T(8,128)S(1)} collective-permute-done((f32[200,128]{1,0:T(8,128)S(1)}, f32[200,128]{1,0:T(8,128)S(1)}, u32[]{:S(2)}, u32[]{:S(2)}) %collective-permute-start.11) | collective-permute-done | bytes 102432 | tf_op jit(solution)/shard_map/ppermute | solution.py:866
  143.8 5.0 %collective-permute-done.13 = f32[200,128]{1,0:T(8,128)S(1)} collective-permute-done((f32[200,128]{1,0:T(8,128)S(1)}, f32[200,128]{1,0:T(8,128)S(1)}, u32[]{:S(2)}, u32[]{:S(2)}) %collective-permute-start.13) | collective-permute-done | bytes 102432 | tf_op jit(solution)/shard_map/ppermute | solution.py:866
  148.8 5.2 %collective-permute-done.12 = f32[200,128]{1,0:T(8,128)S(1)} collective-permute-done((f32[200,128]{1,0:T(8,128)S(1)}, f32[200,128]{1,0:T(8,128)S(1)}, u32[]{:S(2)}, u32[]{:S(2)}) %collective-permute-start.12) | collective-permute-done | bytes 102432 | tf_op jit(solution)/shard_map/ppermute | solution.py:866
  154.1 2.1 collective-permute-start.15
  156.2 2.3 %collective-permute-start.14 = (f32[200,128]{1,0:T(8,128)S(1)}, f32[200,128]{1,0:T(8,128)S(1)}, u32[]{:S(2)}, u32[]{:S(2)}) collective-permute-start(f32[200,128]{1,0:T(8,128)S(1)} %add_add_fusion), channel_id=1, source_target_pairs={{0,24},{1,25},{2,26},{3,27},{4,28},{5,29},{6,30},{7,31},{8,16},{9,... | collective-permute-start | bytes 307208 | tf_op jit(solution)/shard_map/ppermute | solution.py:866
  158.7 4.7 %collective-permute-done.15 = f32[200,128]{1,0:T(8,128)S(1)} collective-permute-done((f32[200,128]{1,0:T(8,128)S(1)}, f32[200,128]{1,0:T(8,128)S(1)}, u32[]{:S(2)}, u32[]{:S(2)}) %collective-permute-start.15) | collective-permute-done | bytes 102432 | tf_op jit(solution)/shard_map/ppermute | solution.py:866
  163.6 2.2 %convert_reduce_fusion.1.r_1_ = s32[32]{0:T(128)} fusion(f32[32,440,128]{2,1,0:T(8,128)} %all-gather.3.cloned.1.call-done.r_2_), kind=kLoop, calls=%fused_computation.19 | loop fusion | flops 36832 | bytes 49280 | tf_op jit(solution)/shard_map/reduce_sum | solution.py:697
  171.0 22.0 %merge.2 = f32[172,8192]{1,0:T(8,128)} custom-call(s32[12288]{0:T(1024)} %fusion.1.r_0_, s32[32]{0:T(128)} %convert_reduce_fusion.1.r_1_, f32[32,440,128]{2,1,0:T(8,128)} %all-gather.3.cloned.1.call-done.r_2_, f32[172,8192]{1,0:T(8,128)} %bitcast.55), custom_call_target="tpu_custom_call" | custom-call | flops 20000000000 | bytes 60000000 | tf_op jit(solution)/shard_map/merge/pallas_call | solution.py:701
  196.7 15.8 %adam.1 = (f32[516,688]{1,0:T(8,128)}, f32[172,516]{1,0:T(8,128)}, f32[344,344]{1,0:T(8,128)}, f32[3,172,344]{2,1,0:T(8,128)}, f32[172,2,172]{2,1,0:T(2,128)}, /...) custom-call(s32[2]{0:T(128)} %pad_add_fusion.r_0_, ...), custom_call_target="tpu_custom_call" | custom-call | flops 14000000000 | bytes 42000000 | tf_op jit(solution)/shard_map/adam/pallas_call | solution.py:831
  (71 shorter events, 19.7 us)
Async XLA Ops:
  7.2 156.4 %all-gather.3.cloned.1.call-start = ((), (), s32[]{:S(2)}) async-start(), calls=%async_computation | async-start | bytes 7434240 | tf_op jit(solution)/shard_map/all_gather | solution.py:946
  12.4 27.6 %collective-permute-start.2 = (f32[65,128]{1,0:T(8,128)S(1)}, f32[65,128]{1,0:T(8,128)S(1)}, u32[]{:S(2)}, u32[]{:S(2)}) collective-permute-start(f32[65,128]{1,0:T(8,128)S(1)} %add_select_fusion.2), channel_id=1, source_target_pairs={{0,4},{1,5},{2,6},{3,7},{4,0},{5,1},{6,2},{7,3},{8,12},{9,13},{10,... | collective-permute-start | bytes 99848 | tf_op jit(solution)/shard_map/ppermute | solution.py:866
  15.4 24.7 %collective-permute-start.3 = (f32[65,128]{1,0:T(8,128)S(1)}, f32[65,128]{1,0:T(8,128)S(1)}, u32[]{:S(2)}, u32[]{:S(2)}) collective-permute-start(f32[65,128]{1,0:T(8,128)S(1)} %add_select_fusion.2), channel_id=1, source_target_pairs={{0,6},{1,7},{2,4},{3,5},{4,2},{5,3},{6,0},{7,1},{8,14},{9,15},{10,... | collective-permute-start | bytes 99848 | tf_op jit(solution)/shard_map/ppermute | solution.py:866
  16.8 23.2 %collective-permute-start.1 = (f32[65,128]{1,0:T(8,128)S(1)}, f32[65,128]{1,0:T(8,128)S(1)}, u32[]{:S(2)}, u32[]{:S(2)}) collective-permute-start(f32[65,128]{1,0:T(8,128)S(1)} %add_select_fusion.2), channel_id=1, source_target_pairs={{0,2},{1,3},{2,0},{3,1},{4,6},{5,7},{6,4},{7,5},{8,10},{9,11},{10,... | collective-permute-start | bytes 99848 | tf_op jit(solution)/shard_map/ppermute | solution.py:866
  40.1 10.8 %collective-permute-start.5 = (f32[65,128]{1,0:T(8,128)S(1)}, f32[65,128]{1,0:T(8,128)S(1)}, u32[]{:S(2)}, u32[]{:S(2)}) collective-permute-start(f32[65,128]{1,0:T(8,128)S(1)} %add_select_fusion.1), channel_id=1, source_target_pairs={{0,16},{1,17},{2,18},{3,19},{4,20},{5,21},{6,22},{7,23},{8,24},{9,... | collective-permute-start | bytes 99848 | tf_op jit(solution)/shard_map/ppermute | solution.py:866
  43.2 7.7 %collective-permute-start.6 = (f32[65,128]{1,0:T(8,128)S(1)}, f32[65,128]{1,0:T(8,128)S(1)}, u32[]{:S(2)}, u32[]{:S(2)}) collective-permute-start(f32[65,128]{1,0:T(8,128)S(1)} %add_select_fusion.1), channel_id=1, source_target_pairs={{0,24},{1,25},{2,26},{3,27},{4,28},{5,29},{6,30},{7,31},{8,16},{9,... | collective-permute-start | bytes 99848 | tf_op jit(solution)/shard_map/ppermute | solution.py:866
  44.6 6.4 %collective-permute-start.4 = (f32[65,128]{1,0:T(8,128)S(1)}, f32[65,128]{1,0:T(8,128)S(1)}, u32[]{:S(2)}, u32[]{:S(2)}) collective-permute-start(f32[65,128]{1,0:T(8,128)S(1)} %add_select_fusion.1), channel_id=1, source_target_pairs={{0,8},{1,9},{2,10},{3,11},{4,12},{5,13},{6,14},{7,15},{8,0},{9,1},... | collective-permute-start | bytes 99848 | tf_op jit(solution)/shard_map/ppermute | solution.py:866
  95.5 3.8 %collective-permute-start.7 = (f32[3200,128]{1,0:T(8,128)}, f32[3200,128]{1,0:T(8,128)S(1)}, u32[]{:S(2)}, u32[]{:S(2)}) collective-permute-start(f32[3200,128]{1,0:T(8,128)} %get-tuple-element.120), channel_id=1, source_target_pairs={{0,1},{1,0},{2,3},{3,2},{4,5},{5,4},{6,7},{7,6},{8,9},{9,8},{10,11... | collective-permute-start | bytes 4915208 | tf_op jit(solution)/shard_map/ppermute | solution.py:866
  101.7 16.9 %collective-permute-start.10 = (f32[800,128]{1,0:T(8,128)}, f32[800,128]{1,0:T(8,128)S(1)}, u32[]{:S(2)}, u32[]{:S(2)}) collective-permute-start(f32[800,128]{1,0:T(8,128)} %get-tuple-element.159), channel_id=1, source_target_pairs={{0,6},{1,7},{2,4},{3,5},{4,2},{5,3},{6,0},{7,1},{8,14},{9,15},{10,... | collective-permute-start | bytes 1228808 | tf_op jit(solution)/shard_map/ppermute | solution.py:866
  104.2 27.7 %collective-permute-start.9 = (f32[800,128]{1,0:T(8,128)}, f32[800,128]{1,0:T(8,128)S(1)}, u32[]{:S(2)}, u32[]{:S(2)}) collective-permute-start(f32[800,128]{1,0:T(8,128)} %get-tuple-element.160), channel_id=1, source_target_pairs={{0,4},{1,5},{2,6},{3,7},{4,0},{5,1},{6,2},{7,3},{8,12},{9,13},{10,... | collective-permute-start | bytes 1228808 | tf_op jit(solution)/shard_map/ppermute | solution.py:866
  104.7 30.4 %collective-permute-start.8 = (f32[800,128]{1,0:T(8,128)S(1)}, f32[800,128]{1,0:T(8,128)S(1)}, u32[]{:S(2)}, u32[]{:S(2)}) collective-permute-start(f32[800,128]{1,0:T(8,128)S(1)} %get-tuple-element.161), channel_id=1, source_target_pairs={{0,2},{1,3},{2,0},{3,1},{4,6},{5,7},{6,4},{7,5},{8,10},{9,11},{10,... | collective-permute-start | bytes 1228808 | tf_op jit(solution)/shard_map/ppermute | solution.py:866
  135.2 8.7 %collective-permute-start.11 = (f32[200,128]{1,0:T(8,128)S(1)}, f32[200,128]{1,0:T(8,128)S(1)}, u32[]{:S(2)}, u32[]{:S(2)}) collective-permute-start(f32[200,128]{1,0:T(8,128)S(1)} %get-tuple-element.162), channel_id=1, source_target_pairs={{0,8},{1,9},{2,10},{3,11},{4,12},{5,13},{6,14},{7,15},{8,0},{9,1},... | collective-permute-start | bytes 307208 | tf_op jit(solution)/shard_map/ppermute | solution.py:866
  137.3 11.5 %collective-permute-start.13 = (f32[200,128]{1,0:T(8,128)S(1)}, f32[200,128]{1,0:T(8,128)S(1)}, u32[]{:S(2)}, u32[]{:S(2)}) collective-permute-start(f32[200,128]{1,0:T(8,128)S(1)} %get-tuple-element.163), channel_id=1, source_target_pairs={{0,24},{1,25},{2,26},{3,27},{4,28},{5,29},{6,30},{7,31},{8,16},{9,... | collective-permute-start | bytes 307208 | tf_op jit(solution)/shard_map/ppermute | solution.py:866
  139.9 14.0 %collective-permute-start.12 = (f32[200,128]{1,0:T(8,128)S(1)}, f32[200,128]{1,0:T(8,128)S(1)}, u32[]{:S(2)}, u32[]{:S(2)}) collective-permute-start(f32[200,128]{1,0:T(8,128)S(1)} %get-tuple-element.164), channel_id=1, source_target_pairs={{0,16},{1,17},{2,18},{3,19},{4,20},{5,21},{6,22},{7,23},{8,24},{9,... | collective-permute-start | bytes 307208 | tf_op jit(solution)/shard_map/ppermute | solution.py:866
  154.0 4.7 %collective-permute-start.16 = (f32[200,128]{1,0:T(8,128)S(1)}, f32[200,128]{1,0:T(8,128)S(1)}, u32[]{:S(2)}, u32[]{:S(2)}) collective-permute-start(f32[200,128]{1,0:T(8,128)S(1)} %add_add_fusion), channel_id=1, source_target_pairs={{0,8},{1,9},{2,10},{3,11},{4,12},{5,13},{6,14},{7,15},{8,0},{9,1},... | collective-permute-start | bytes 307208 | tf_op jit(solution)/shard_map/ppermute | solution.py:866
  154.1 9.3 %collective-permute-start.15 = (f32[200,128]{1,0:T(8,128)S(1)}, f32[200,128]{1,0:T(8,128)S(1)}, u32[]{:S(2)}, u32[]{:S(2)}) collective-permute-start(f32[200,128]{1,0:T(8,128)S(1)} %add_add_fusion), channel_id=1, source_target_pairs={{0,16},{1,17},{2,18},{3,19},{4,20},{5,21},{6,22},{7,23},{8,24},{9,... | collective-permute-start | bytes 307208 | tf_op jit(solution)/shard_map/ppermute | solution.py:866
  156.2 7.2 %collective-permute-start.14 = (f32[200,128]{1,0:T(8,128)S(1)}, f32[200,128]{1,0:T(8,128)S(1)}, u32[]{:S(2)}, u32[]{:S(2)}) collective-permute-start(f32[200,128]{1,0:T(8,128)S(1)} %add_add_fusion), channel_id=1, source_target_pairs={{0,24},{1,25},{2,26},{3,27},{4,28},{5,29},{6,30},{7,31},{8,16},{9,... | collective-permute-start | bytes 307208 | tf_op jit(solution)/shard_map/ppermute | solution.py:866
  166.7 26.2 %collective-permute-start.19 = (f32[800,128]{1,0:T(8,128)S(1)}, f32[800,128]{1,0:T(8,128)S(1)}, u32[]{:S(2)}, u32[]{:S(2)}) collective-permute-start(f32[800,128]{1,0:T(8,128)S(1)} %pad_maximum_fusion.r_1_), channel_id=1, source_target_pairs={{0,6},{1,7},{2,4},{3,5},{4,2},{5,3},{6,0},{7,1},{8,14},{9,15},{10,... | collective-permute-start | bytes 1228808 | tf_op jit(solution)/shard_map/ppermute | solution.py:866
  168.5 24.4 %collective-permute-start.18 = (f32[800,128]{1,0:T(8,128)S(1)}, f32[800,128]{1,0:T(8,128)S(1)}, u32[]{:S(2)}, u32[]{:S(2)}) collective-permute-start(f32[800,128]{1,0:T(8,128)S(1)} %pad_maximum_fusion.r_1_), channel_id=1, source_target_pairs={{0,4},{1,5},{2,6},{3,7},{4,0},{5,1},{6,2},{7,3},{8,12},{9,13},{10,... | collective-permute-start | bytes 1228808 | tf_op jit(solution)/shard_map/ppermute | solution.py:866
  170.3 22.6 %collective-permute-start.17 = (f32[800,128]{1,0:T(8,128)S(1)}, f32[800,128]{1,0:T(8,128)S(1)}, u32[]{:S(2)}, u32[]{:S(2)}) collective-permute-start(f32[800,128]{1,0:T(8,128)S(1)} %pad_maximum_fusion.r_1_), channel_id=1, source_target_pairs={{0,2},{1,3},{2,0},{3,1},{4,6},{5,7},{6,4},{7,5},{8,10},{9,11},{10,... | collective-permute-start | bytes 1228808 | tf_op jit(solution)/shard_map/ppermute | solution.py:866
  193.0 2.8 %collective-permute-start.20 = (f32[800,128]{1,0:T(8,128)S(1)}, f32[800,128]{1,0:T(8,128)S(1)}, u32[]{:S(2)}, u32[]{:S(2)}) collective-permute-start(f32[800,128]{1,0:T(8,128)S(1)} %pad_maximum_fusion.r_1_), channel_id=1, source_target_pairs={{0,1},{1,0},{2,3},{3,2},{4,5},{5,4},{6,7},{7,6},{8,9},{9,8},{10,11... | collective-permute-start | bytes 1228808 | tf_op jit(solution)/shard_map/ppermute | solution.py:866
  193.1 2.9 %collective-permute-start.21 = (f32[800,128]{1,0:T(8,128)S(1)}, f32[800,128]{1,0:T(8,128)S(1)}, u32[]{:S(2)}, u32[]{:S(2)}) collective-permute-start(f32[800,128]{1,0:T(8,128)S(1)} %collective-permute-done.17.r_2_), channel_id=1, source_target_pairs={{0,1},{1,0},{2,3},{3,2},{4,5},{5,4},{6,7},{7,6},{8,9},{9,8},{10,11... | collective-permute-start | bytes 1228808 | tf_op jit(solution)/shard_map/ppermute | solution.py:866
  193.6 2.5 %collective-permute-start.22 = (f32[800,128]{1,0:T(8,128)S(1)}, f32[800,128]{1,0:T(8,128)}, u32[]{:S(2)}, u32[]{:S(2)}) collective-permute-start(f32[800,128]{1,0:T(8,128)S(1)} %collective-permute-done.18.r_3_), channel_id=1, source_target_pairs={{0,1},{1,0},{2,3},{3,2},{4,5},{5,4},{6,7},{7,6},{8,9},{9,8},{10,11... | collective-permute-start | bytes 1228808 | tf_op jit(solution)/shard_map/ppermute | solution.py:866
  193.6 3.0 %collective-permute-start.23 = (f32[800,128]{1,0:T(8,128)S(1)}, f32[800,128]{1,0:T(8,128)}, u32[]{:S(2)}, u32[]{:S(2)}) collective-permute-start(f32[800,128]{1,0:T(8,128)S(1)} %collective-permute-done.19.r_4_), channel_id=1, source_target_pairs={{0,1},{1,0},{2,3},{3,2},{4,5},{5,4},{6,7},{7,6},{8,9},{9,8},{10,11... | collective-permute-start | bytes 1228808 | tf_op jit(solution)/shard_map/ppermute | solution.py:866
  (9 other events, 79.5 us)
Sparse Core Ops, SparseCore 0:
  63.2 92.1 all-gather.2

commit v4 on v3

--- a/solution.py
+++ b/solution.py
@@ -69,20 +69,37 @@
     return nt(eye(x.shape[1]), x.astype(BF))
 
 
-def prep_kernel(gin, ghid, kv, tall, sq, vec,
-                wg, wgc, wh, kvm, kvct, kvc, t0t, t0, t1t, t1, t2t, t2, s0t, s0, s1t, s1, vb):
+def gate_weights_kernel(gin, ghid, vec, wg, wh, vb):
     full = gin[...]
     for gate in range(3):
         rows = full[gate * MEM : (gate + 1) * MEM]
         parts = [cols_to(rows[:, q * MEM : (q + 1) * MEM], PAD) for q in range(4)]
-        wide = rows_to(jnp.concatenate(parts, axis=1), PAD)
-        wg[pl.ds(gate * PAD, PAD), :] = wide.astype(BF)
-        code = cols_to(rows_to(rows[:, 2 * MEM : 3 * MEM], PAD), 256)
-        wgc[:, gate * PAD : (gate + 1) * PAD] = turned(code)[:PAD].astype(BF)
+        wg[pl.ds(gate * PAD, PAD), :] = rows_to(jnp.concatenate(parts, axis=1), PAD).astype(BF)
     hid = ghid[...]
     for gate in range(3):
         part = cols_to(rows_to(hid[:, gate * MEM : (gate + 1) * MEM], PAD), 256)
         wh[pl.ds(gate * PAD, PAD), :] = turned(part)[:PAD].astype(BF)
+    cols = jnp.transpose(cols_to(rows_to(vec[...], 128), 256))
+    for i in range(15):
+        column = cols[:, i : i + 1]
+        if i in (8, 9):
+            column = split_rows(column[:MEM])
+        wide = jnp.broadcast_to(column[:PAD], (PAD, 128))
+        vb[i] = wide * (0.5 / math.pi) if i < 2 else wide
+
+
+def gate_weights(gin, ghid, vec):
+    outs = [jax.ShapeDtypeStruct((528, 704), BF), jax.ShapeDtypeStruct((528, 176), BF),
+            jax.ShapeDtypeStruct((15, PAD, 128), F32)]
+    return pl.pallas_call(
+        gate_weights_kernel, out_shape=outs, compiler_params=params(), name="gate_weights", cost_estimate=cost(4),
+    )(gin.T, ghid, vec)
+
+
+def main_weights_kernel(gin, kv, tall, sq, vec, wgc, kvm, kvct, kvc, t0t, t0, t1t, t1, t2t, t2, s0t, s0, s1t, s1, steady):
+    for gate in range(3):
+        code = cols_to(rows_to(gin[gate * MEM : (gate + 1) * MEM, 2 * MEM : 3 * MEM], PAD), 256)
+        wgc[:, gate * PAD : (gate + 1) * PAD] = turned(code)[:PAD].astype(BF)
     pairs = kv[...]
     both = turned(cols_to(pairs, 384))
     halves = jnp.concatenate([split_rows(both[:MEM]), split_rows(both[MEM : 2 * MEM])], axis=0)
@@ -104,27 +121,20 @@
     second = cols_to(rows_to(sq[:, 1, :], PAD), 256)
     s1[...] = second[:, :PAD].astype(BF)
     s1t[...] = turned(second)[:PAD].astype(BF)
-    cols = jnp.transpose(cols_to(rows_to(vec[...], 128), 256))
-    phase_low = jnp.cos(cols[:PAD, 1:2]).astype(BF).astype(F32)
+    phase_low = jnp.cos(jnp.transpose(cols_to(rows_to(vec[...], 128), 256))[:PAD, 1:2]).astype(BF).astype(F32)
     row_id = lax.broadcasted_iota(I32, (PAD, 128), 0)
     wide_phase = jnp.where(row_id < MEM, jnp.broadcast_to(phase_low, (PAD, 128)), 0.0).astype(BF)
-    steady = nn(cols_to(split_rows(query[:, MEM:]), PAD).astype(BF), wide_phase)
-    for i in range(15):
-        column = cols[:, i : i + 1]
-        if i in (8, 9):
-            column = split_rows(column[:MEM])
-        wide = jnp.broadcast_to(column[:PAD], (PAD, 128))
-        vb[i] = wide + steady if i == 8 else (wide * (0.5 / math.pi) if i < 2 else wide)
-
-
-def prep(gin, ghid, kv, tall, sq, vec):
+    steady[...] = nn(cols_to(split_rows(query[:, MEM:]), PAD).astype(BF), wide_phase)
+
+
+def main_weights(gin, kv, tall, sq, vec):
     bf = lambda *s: jax.ShapeDtypeStruct(s, BF)
-    outs = [bf(528, 704), bf(176, 528), bf(528, 176), bf(352, 256), bf(352, 176), bf(176, 352),
+    outs = [bf(176, 528), bf(352, 256), bf(352, 176), bf(176, 352),
             bf(176, 176), bf(176, 176), bf(176, 352), bf(352, 176), bf(176, 352), bf(352, 176),
-            bf(176, 176), bf(176, 176), bf(176, 176), bf(176, 176), jax.ShapeDtypeStruct((15, PAD, 128), F32)]
+            bf(176, 176), bf(176, 176), bf(176, 176), bf(176, 176), jax.ShapeDtypeStruct((PAD, 128), F32)]
     return pl.pallas_call(
-        prep_kernel, out_shape=outs, compiler_params=params(), name="prep", cost_estimate=cost(6),
-    )(gin.T, ghid, kv, jnp.transpose(tall, (0, 2, 1)), jnp.transpose(sq, (1, 0, 2)), vec)
+        main_weights_kernel, out_shape=outs, compiler_params=params(), name="main_weights", cost_estimate=cost(5),
+    )(gin.T, kv, jnp.transpose(tall, (0, 2, 1)), jnp.transpose(sq, (1, 0, 2)), vec)
 
 
 def first_kernel(source, target, ticks, weights, out):
@@ -164,7 +174,13 @@
     )(source, target, ticks, weights)
 
 
-def fetch_kernel(steps, chunk, source, target, near_ids, mem, ticks, own, near, wide, left, right):
+def copy_rows(out, at, tables, ids):
+    for h, table in enumerate(tables):
+        rows = jnp.concatenate([table[pl.ds(i, 1), :] for i in ids], axis=0)
+        out[pl.ds(at, 16), 128 * h : 128 * h + 128] = rows.astype(BF)
+
+
+def table_kernel(source, target, mem, ticks, left, right, own, wide):
     step = pl.program_id(0)
     cols = mem.shape[1]
 
@@ -172,25 +188,18 @@
     def _():
         wide[...] = jnp.zeros_like(wide)
 
-    @pl.when(step < steps)
-    def _():
-        base = pl.multiple_of(step * cols, cols)
-        wide[0:MEM, :] = mem[...].astype(BF).astype(F32)
-        tick = ticks[...]
-        for at, part in ((PAD, tick & 127), (PAD + 1, (tick >> 7) & 127), (PAD + 2, tick >> 14)):
-            wide[at : at + 1, :] = part.astype(F32)
-        unit = eye(256)
-        for c in range(cols // 256):
-            rows = nt(unit, wide[:, 256 * c : 256 * c + 256].astype(BF))
-            left[pl.ds(base + 256 * c, 256), :] = rows[:, :128]
-            right[pl.ds(base + 256 * c, 256), :] = rows[:, 128:]
-
-    def move(out, at, ids):
-        for h, table in enumerate((left, right)):
-            rows = jnp.concatenate([table[pl.ds(i, 1), :] for i in ids], axis=0)
-            out[pl.ds(at, 16), 128 * h : 128 * h + 128] = rows.astype(BF)
-
-    @pl.when(step == steps)
+    base = pl.multiple_of(step * cols, cols)
+    wide[0:MEM, :] = mem[...].astype(BF).astype(F32)
+    tick = ticks[...]
+    for at, part in ((PAD, tick & 127), (PAD + 1, (tick >> 7) & 127), (PAD + 2, tick >> 14)):
+        wide[at : at + 1, :] = part.astype(F32)
+    unit = eye(256)
+    for c in range(cols // 256):
+        rows = nt(unit, wide[:, 256 * c : 256 * c + 256].astype(BF))
+        left[pl.ds(base + 256 * c, 256), :] = rows[:, :128]
+        right[pl.ds(base + 256 * c, 256), :] = rows[:, 128:]
+
+    @pl.when(step == pl.num_programs(0) - 1)
     def _():
         def group(b, carry):
             for role, ids in enumerate((source, target)):
@@ -198,7 +207,7 @@
                     for v in range(2):
                         e = g * 32 + v * 16
                         at = pl.multiple_of(b * 256 + role * 128 + e, 16)
-                        move(own, at, [ids[b * 128 + e + u] for u in range(16)])
+                        copy_rows(own, at, (left, right), [ids[b * 128 + e + u] for u in range(16)])
                     return carry
 
                 lax.fori_loop(0, 4, some, 0)
@@ -206,36 +215,48 @@
 
         lax.fori_loop(0, own.shape[0] // 256, group, 0)
 
-    @pl.when(step > steps)
-    def _():
-        base = (step - steps - 1) * chunk
-
-        def group(g, carry):
-            for v in range(4):
-                at = pl.multiple_of(g * 64 + v * 16, 16)
-                move(near, at, [near_ids[base + at + u] for u in range(16)])
-            return carry
-
-        lax.fori_loop(0, chunk // 64, group, 0)
-
-
-def fetch(source, target, near_ids, mem_t, ticks):
+
+def build_table(source, target, mem_t, ticks):
     nodes = mem_t.shape[1]
-    ends, nears = 2 * source.shape[0], near_ids.shape[0]
-    cols, chunk = 4096, 5120
-    steps = nodes // cols
+    ends = 2 * source.shape[0]
+    cols = 2048
     smem = pl.BlockSpec(memory_space=pltpu.SMEM)
-    part = lambda i: (0, jnp.minimum(i, steps - 1))
+    half = jax.ShapeDtypeStruct((nodes, 128), F32)
+    fixed = lambda i: (0, 0)
     return pl.pallas_call(
-        lambda *r: fetch_kernel(steps, chunk, *r),
-        out_shape=[jax.ShapeDtypeStruct((ends, 256), BF), jax.ShapeDtypeStruct((nears, 256), BF)],
-        grid=(steps + 1 + nears // chunk,),
-        in_specs=[smem, smem, smem, pl.BlockSpec((MEM, cols), part), pl.BlockSpec((1, cols), part)],
-        out_specs=[pl.BlockSpec((ends, 256), lambda i: (0, 0)),
-                   pl.BlockSpec((chunk, 256), lambda i: (jnp.maximum(i - steps - 1, 0), 0))],
-        scratch_shapes=[pltpu.VMEM((256, cols), F32), pltpu.VMEM((nodes, 128), F32), pltpu.VMEM((nodes, 128), F32)],
-        compiler_params=params(), name="fetch", cost_estimate=cost(18),
-    )(source, target, near_ids, mem_t, ticks.reshape(1, nodes))
+        table_kernel,
+        out_shape=[half, half, jax.ShapeDtypeStruct((ends, 256), BF)],
+        grid=(nodes // cols,),
+        in_specs=[smem, smem, pl.BlockSpec((MEM, cols), lambda i: (0, i)), pl.BlockSpec((1, cols), lambda i: (0, i))],
+        out_specs=[pl.BlockSpec((nodes, 128), fixed), pl.BlockSpec((nodes, 128), fixed), pl.BlockSpec((ends, 256), fixed)],
+        scratch_shapes=[pltpu.VMEM((256, cols), F32)],
+        compiler_params=params(), name="table", cost_estimate=cost(9),
+    )(source, target, mem_t, ticks.reshape(1, nodes))
+
+
+def near_kernel(chunk, ids, left, right, near):
+    base = pl.program_id(0) * chunk
+
+    def group(g, carry):
+        for v in range(4):
+            at = pl.multiple_of(g * 64 + v * 16, 16)
+            copy_rows(near, at, (left, right), [ids[base + at + u] for u in range(16)])
+        return carry
+
+    lax.fori_loop(0, chunk // 64, group, 0)
+
+
+def gather_near(ids, left, right):
+    nears, chunk = ids.shape[0], ids.shape[0]
+    whole = lambda a: pl.BlockSpec(a.shape, lambda i: (0, 0))
+    return pl.pallas_call(
+        lambda *r: near_kernel(chunk, *r),
+        out_shape=jax.ShapeDtypeStruct((nears, 256), BF),
+        grid=(nears // chunk,),
+        in_specs=[pl.BlockSpec(memory_space=pltpu.SMEM), whole(left), whole(right)],
+        out_specs=pl.BlockSpec((chunk, 256), lambda i: (i, 0)),
+        compiler_params=params(), name="near", cost_estimate=cost(16),
+    )(ids, left, right)
 
 
 ROUND = 12582912.0
@@ -288,7 +309,7 @@
     return jnp.broadcast_to(x, (rows, x.shape[1]))
 
 
-def gru_kernel(scale, cap, rounds, sources, targets, ticks_at, latest, own, source, target, ticks, edge, types, wg, wh, vb,
+def gru_kernel(scale, cap, rounds, nodes, sources, targets, ticks_at, latest, own, source, target, ticks, edge, types, wg, wh, vb,
                msg, keep, ren, gap_out, packed, left, right, first, second):
     step = pl.program_id(0)
     own_t = nt(eye(256), own[...])
@@ -335,12 +356,10 @@
 
     @pl.when(step == pl.num_programs(0) - 1)
     def _():
-        pack_rows(cap, rounds, sources, targets, ticks_at, latest, left, right, packed, first, second)
-
-
-def pack_rows(cap, rounds, sources, targets, ticks, latest, left, right, out, first, second):
-    second[...] = jnp.full_like(second, -1.0)
-
+        pack_rows(cap, rounds, nodes, sources, targets, ticks_at, latest, left, right, packed, first, second)
+
+
+def pack_rows(cap, rounds, nodes, sources, targets, ticks, latest, left, right, out, first, second):
     def chunk(b, count):
         for role, ids in enumerate((sources, targets)):
             def some(g, count):
@@ -357,7 +376,6 @@
         return count
 
     count = lax.fori_loop(0, sources.shape[0] // 128, chunk, jnp.int32(0))
-    second[pl.ds(count, 1), :] = jnp.full((1, 128), -1.0, F32)
     tail = cap // 2
     lane = lax.broadcasted_iota(I32, (1, 128), 1)
     for r in range(rounds):
@@ -365,15 +383,18 @@
         out[r, 0:cap, :] = first[at : at + cap, :]
         out[r, cap : cap + tail, :] = jnp.concatenate(
             [second[at : at + tail, 0:64], second[at + tail : at + cap, 0:64]], axis=1)
+        here = jnp.clip(count - at, 0, cap)
         lines = []
         for q in range(-(-cap // 128)):
             numbers = jnp.transpose(second[at + 128 * q : at + 128 * q + 128, :])[MEM - 128 : MEM - 127]
-            lines.append(jnp.where(lane + 128 * q < cap, numbers, -1.0))
-        out[r, cap + tail :, :] = jnp.concatenate(lines + [zeros(1, 128)] * (8 - len(lines)), axis=0)
+            lines.append(jnp.where(lane + 128 * q < here, numbers, float(nodes)))
+        lines.append(jnp.full((1, 128), here, I32).astype(F32))
+        lines += [zeros(1, 128)] * (8 - len(lines))
+        out[r, cap + tail :, :] = jnp.concatenate(lines, axis=0)
 
 
 def gru(scale, cap, sources, targets, ticks, latest, own, edge_t, types, wg, wh, vb):
-    ends = own.shape[0]
+    ends, nodes = own.shape[0], latest.shape[0]
     blocks = ends // BLOCK
     rounds = ends // cap + 1
     spare = rounds * cap + 128
@@ -383,7 +404,7 @@
     row = lambda x: x.reshape(1, -1)
     packed = jax.ShapeDtypeStruct((rounds, cap + cap // 2 + 8, 128), F32)
     return pl.pallas_call(
-        lambda *r: gru_kernel(scale, cap, rounds, *r),
+        lambda *r: gru_kernel(scale, cap, rounds, nodes, *r),
         out_shape=[jax.ShapeDtypeStruct((4 * PAD, ends), BF), jax.ShapeDtypeStruct((5, PAD, ends), F32),
                    jax.ShapeDtypeStruct((PAD, ends), F32), jax.ShapeDtypeStruct((8, ends), F32), packed],
         grid=(blocks,),
@@ -417,7 +438,7 @@
 
 
 def main_kernel(scale, core, near, gaps_t, ticks, msg, keep, ren, gap_own, labels, weights, total,
-                wgc, kvm, kvct, kvc, t0t, t0, t1t, t1, t2t, t2, s0t, s0, s1t, s1, vb,
+                wgc, kvm, kvct, kvc, t0t, t0, t1t, t1, t2t, t2, s0t, s0, s1t, s1, steady, vb,
                 mine, theirs,
                 loss, pair, code, dcode, soft, back, mean, d_query_at, grads, g_in, g_kv, g_one, g_dec, g_qo, g_th, vacc):
     step = pl.program_id(0)
@@ -431,7 +452,7 @@
     tick2 = both(ticks[...].astype(F32))
     renewed = ren[...]
     ren_low = renewed.astype(BF)
-    queries = nn(t0t[...], ren_low) + across(vb[8])
+    queries = nn(t0t[...], ren_low) + across(vb[8] + steady[...])
     def each(one):
         def some(g, carry):
             for v in range(UNROLL):
@@ -645,70 +666,113 @@
     return (nt(unit, high) + nt(unit, middle)) + nt(unit, low)
 
 
-def merge_kernel(cap, group, steps, ids, counts, rows, mem, out, left, right, second):
-    step = pl.program_id(0)
+def lay_rows(cap, number, rows, left, right, second):
     tail = cap // 2
     width = -(-cap // 128) * 128
 
+    def block(q, most):
+        half = rows[q, cap : cap + tail, :]
+        second[0:tail, :] = half
+        second[tail:cap, :] = jnp.concatenate([half[:, 64:], half[:, :64]], axis=1)
+        here = number(q, width)
+
+        def some(g, carry):
+            for v in range(16):
+                i = g * 16 + v
+                node = number(q, i)
+                left[pl.ds(node, 1), :] = rows[q, pl.ds(i, 1), :]
+                right[pl.ds(node, 1), :] = second[pl.ds(i, 1), :]
+            return carry
+
+        lax.fori_loop(0, lax.div(here + 15, 16), some, 0)
+        return jnp.maximum(most, here)
+
+    return lax.fori_loop(0, rows.shape[0], block, jnp.int32(0))
+
+
+def lay_kernel(cap, count, *refs):
+    arrays, (left, right, most, joined, second, sems), rest = refs[:count], refs[count : count + 6], refs[count + 6 :]
+    wholes, lists = rest[:count], rest[count:]
+    lines = cap + cap // 2
+    copies = []
+    for a, (rows, whole) in enumerate(zip(arrays, wholes)):
+        whole[...] = rows[:, lines:, :].astype(I32)
+        copies.append(pltpu.make_async_copy(whole, lists[a], sems.at[a]))
+        copies[a].start()
+    right[...] = jnp.full_like(right, -1.0)
+    for a, rows in enumerate(arrays):
+        blocks = rows.shape[0]
+        joined[a * blocks : (a + 1) * blocks] = rows[...]
+    largest = jnp.int32(0)
+    for a, rows in enumerate(arrays):
+        copies[a].wait()
+        number = lambda q, i: lists[a][q, lax.shift_right_logical(i, 7), i & 127]
+        largest = jnp.maximum(largest, lay_rows(cap, number, rows, left, right, second))
+    most[0] = largest
+
+
+def row_numbers(cap, x):
+    first, height = cap + cap // 2, -(-cap // 128) + 1
+    return x[:, first : first + height, :].astype(I32).reshape(-1)
+
+
+def lay(cap, nodes, arrays):
+    vm, smem = pl.BlockSpec(memory_space=pltpu.VMEM), pl.BlockSpec(memory_space=pltpu.SMEM)
+    table = jax.ShapeDtypeStruct((nodes + 8, 128), F32)
+    count = len(arrays)
+    blocks, height, _ = arrays[0].shape
+    return pl.pallas_call(
+        lambda *r: lay_kernel(cap, count, *r),
+        out_shape=[table, table, jax.ShapeDtypeStruct((1,), I32), jax.ShapeDtypeStruct((count * blocks, height, 128), F32)],
+        in_specs=[vm] * count, out_specs=[vm, vm, smem, vm],
+        scratch_shapes=[pltpu.VMEM((cap, 128), F32), pltpu.SemaphoreType.DMA((count,))]
+        + [kind((blocks, 8, 128), I32) for kind in (pltpu.VMEM, pltpu.SMEM) for _ in arrays],
+        compiler_params=params(), name="lay", cost_estimate=cost(14),
+    )(*arrays)
+
+
+def merge_kernel(cap, numbers, rows, far_left, far_right, before, mem, out, full, left, right, second, sems):
+    step = pl.program_id(0)
+
     @pl.when(step == 0)
     def _():
-        left[...] = jnp.zeros_like(left)
-        right[...] = jnp.full_like(right, -1.0)
-
-    @pl.when(step < steps)
-    def _():
-        for q in range(group):
-            half = rows[q, cap : cap + tail, :]
-            second[q, 0:tail, :] = half
-            second[q, tail:cap, :] = jnp.concatenate([half[:, 64:], half[:, :64]], axis=1)
-        for q in range(group):
-            base = (step * group + q) * width
-
-            def some(g, carry):
-                for v in range(16):
-                    i = g * 16 + v
-                    node = ids[base + i]
-                    left[pl.ds(node, 1), :] = rows[q, pl.ds(i, 1), :]
-                    right[pl.ds(node, 1), :] = second[q, pl.ds(i, 1), :]
-                return carry
-
-            lax.fori_loop(0, lax.div(counts[step * group + q] + 15, 16), some, 0)
-
-    @pl.when(step >= steps)
-    def _():
-        cols = mem.shape[1]
-        base = pl.multiple_of((step - steps) * cols, cols)
-        for c in range(cols // 256):
-            at = base + 256 * c
-            s = slice(256 * c, 256 * c + 256)
-            top = turned_exactly(left[pl.ds(at, 256), :])
-            low = turned_exactly(right[pl.ds(at, 256), :])
-            fresh = low[MEM - 128 : MEM - 127] >= 0.0
-            out[0:128, s] = jnp.where(fresh, top, mem[0:128, s])
-            out[128:MEM, s] = jnp.where(fresh, low[: MEM - 128], mem[128:MEM, s])
-
-
-def merge(cap, gathered, mem_t):
-    blocks, height, _ = gathered.shape
+        copies = [pltpu.make_async_copy(far_left, left, sems.at[0]), pltpu.make_async_copy(far_right, right, sems.at[1])]
+        for copy in copies:
+            copy.start()
+        for copy in copies:
+            copy.wait()
+        width = -(-cap // 128) * 128 + 128
+        most = lay_rows(cap, lambda q, i: numbers[q * width + i], rows, left, right, second)
+        full[0] = (jnp.maximum(most, before[0]) == cap).astype(I32)
+
+    cols = mem.shape[1]
+    base = pl.multiple_of(step * cols, cols)
+    for c in range(cols // 256):
+        at = base + 256 * c
+        s = slice(256 * c, 256 * c + 256)
+        top = turned_exactly(left[pl.ds(at, 256), :])
+        low = turned_exactly(right[pl.ds(at, 256), :])
+        fresh = low[MEM - 128 : MEM - 127] >= 0.0
+        out[0:128, s] = jnp.where(fresh, top, mem[0:128, s])
+        out[128:MEM, s] = jnp.where(fresh, low[: MEM - 128], mem[128:MEM, s])
+
+
+def merge(cap, laid, rows, mem_t):
     nodes = mem_t.shape[1]
-    cols, group = 4096, 8
-    steps = blocks // group
-    numbers = gathered[:, height - 8 : height - 8 + -(-cap // 128), :].reshape(blocks, -1)
-    counts = jnp.sum((numbers >= 0.0).astype(I32), axis=1)
-    ids = jnp.where(numbers >= 0.0, numbers, float(nodes)).astype(I32).reshape(-1)
-    smem = pl.BlockSpec(memory_space=pltpu.SMEM)
-    part = lambda i: (0, jnp.maximum(i - steps, 0))
-    new = pl.pallas_call(
-        lambda *r: merge_kernel(cap, group, steps, *r),
-        out_shape=jax.ShapeDtypeStruct((MEM, nodes), F32),
-        grid=(steps + nodes // cols,),
-        in_specs=[smem, smem, pl.BlockSpec((group, height, 128), lambda i: (jnp.minimum(i, steps - 1), 0, 0)),
-                  pl.BlockSpec((MEM, cols), part)],
-        out_specs=pl.BlockSpec((MEM, cols), part),
-        scratch_shapes=[pltpu.VMEM((nodes + 8, 128), F32), pltpu.VMEM((nodes + 8, 128), F32), pltpu.VMEM((group, cap, 128), F32)],
-        compiler_params=params(), name="merge", cost_estimate=cost(20),
-    )(ids, counts, gathered, mem_t)
-    return new, jnp.any(counts == cap)
+    cols = 2048
+    part = pl.BlockSpec((MEM, cols), lambda i: (0, i))
+    smem, far = pl.BlockSpec(memory_space=pltpu.SMEM), pl.BlockSpec(memory_space=pl.ANY)
+    new, full = pl.pallas_call(
+        lambda *r: merge_kernel(cap, *r),
+        out_shape=[jax.ShapeDtypeStruct((MEM, nodes), F32), jax.ShapeDtypeStruct((1,), I32)],
+        grid=(nodes // cols,),
+        in_specs=[smem, pl.BlockSpec(rows.shape, lambda i: (0, 0, 0)), far, far, smem, part],
+        out_specs=[part, smem],
+        scratch_shapes=[pltpu.VMEM((nodes + 8, 128), F32), pltpu.VMEM((nodes + 8, 128), F32), pltpu.VMEM((cap, 128), F32),
+                        pltpu.SemaphoreType.DMA((2,))],
+        compiler_params=params(), name="merge", cost_estimate=cost(18),
+    )(row_numbers(cap, rows), rows, *laid, mem_t)
+    return new, full[0] > 0
 
 
 def move(param, one, two, grad, factor, rate, decay):
@@ -728,8 +792,13 @@
     count = sum(n for _, n in parts)
     mine, other = refs[:count], refs[count : 2 * count]
     refs = refs[2 * count :]
-    state, news, (norm_out, loss_out) = refs[:18], refs[18:36], refs[36:38]
-    a, b, g_gin, g_hid, g_kv, g_tall, g_sq, g_vec = refs[38:]
+    far, out, (norm_out, loss_out) = refs[:18], refs[18:36], refs[36:38]
+    a, b, g_gin, g_hid, g_kv, g_tall, g_sq, g_vec = refs[38:46]
+    state, sems_in, sems_out = refs[46:64], refs[64], refs[65]
+    fetches = [pltpu.make_async_copy(far[i], state[i], sems_in.at[i]) for i in range(18)]
+    stores = [pltpu.make_async_copy(state[i], out[i], sems_out.at[i]) for i in range(18)]
+    for i in (5, 3, 0, 6, 12, 1, 7, 13, 2, 8, 14, 9, 15, 4, 10, 16, 11, 17):
+        fetches[i].start()
     core = where[0]
     at_block = 0
     for p, (first, n) in enumerate(parts):
@@ -752,8 +821,7 @@
     def panels(ref, at, rows, n):
         return jnp.concatenate([ref[at + c * rows : at + (c + 1) * rows, :] for c in range(n)], axis=1)
 
-    vec = state[5]
-    tall = state[3]
+    vec, tall = state[5], state[3]
     wide = panels(b, 0, 528, 6)
     gates = []
     for g in range(3):
@@ -770,6 +838,8 @@
         g_tall[i] = jnp.concatenate([x[:, :MEM], x[:, PAD : PAD + MEM]], axis=1)
     both = unsplit(panels(a, 2112, PAD, 3), 0)
     sum_dq = unsplit(jnp.transpose(rows_to(vecs, 128))[:PAD, 15:16], 0)
+    fetches[5].wait()
+    fetches[3].wait()
     phase = vec[1:2, :]
     phase_low = jnp.cos(phase).astype(BF).astype(F32)
     g_tall[0] = jnp.concatenate([both[:, :MEM], sum_dq * phase_low], axis=1)
@@ -796,8 +866,10 @@
     loss_out[...] = jnp.sum(a[3168:3169, :], keepdims=True)
     for i, grad in enumerate((g_gin, g_hid, g_kv, g_tall, g_sq, g_vec)):
         rate, decay = (VECTOR_RATE, 0.0) if i == 5 else (LEARN_RATE, DECAY)
-        param, one, two = state[i], state[6 + i], state[12 + i]
-        new = news[i], news[6 + i], news[12 + i]
+        new = param, one, two = state[i], state[6 + i], state[12 + i]
+        for at in (i, 6 + i, 12 + i):
+            if at not in (3, 5):
+                fetches[at].wait()
         if i == 4:
             for j in range(2):
                 made = move(param[:, j, :], one[:, j, :], two[:, j, :], grad[j], factor, rate, decay)
@@ -815,6 +887,10 @@
                 made = move(param[s], one[s], two[s], grad[s], factor, rate, decay)
                 for ref, value in zip(new, made):
                     ref[s] = value
+        for at in (i, 6 + i, 12 + i):
+            stores[at].start()
+    for store in stores:
+        store.wait()
 
 
 def adam(where, parts, mine, other, state):
@@ -826,14 +902,15 @@
     count = len(mine)
     shapes = [x.shape for x in state[:6]]
     shapes[4] = (2, MEM, MEM)
-    vm = pl.BlockSpec(memory_space=pltpu.VMEM)
+    vm, far = pl.BlockSpec(memory_space=pltpu.VMEM), pl.BlockSpec(memory_space=pl.ANY)
     outs = [jax.ShapeDtypeStruct(x.shape, F32) for x in state] + [jax.ShapeDtypeStruct((1, 1), F32)] * 2
     out = pl.pallas_call(
         lambda *r: adam_kernel(parts, *r),
         out_shape=outs,
-        in_specs=[pl.BlockSpec(memory_space=pltpu.SMEM)] + [vm] * (2 * count + 18),
-        out_specs=[vm] * 20,
-        scratch_shapes=[pltpu.VMEM((3200, 128), F32), pltpu.VMEM((3200, 128), F32)] + [pltpu.VMEM(s, F32) for s in shapes],
+        in_specs=[pl.BlockSpec(memory_space=pltpu.SMEM)] + [vm] * (2 * count) + [far] * 18,
+        out_specs=[far] * 18 + [vm] * 2,
+        scratch_shapes=[pltpu.VMEM((3200, 128), F32), pltpu.VMEM((3200, 128), F32)] + [pltpu.VMEM(s, F32) for s in shapes]
+        + [pltpu.VMEM(x.shape, F32) for x in state] + [pltpu.SemaphoreType.DMA((18,))] * 2,
         compiler_params=params(), name="adam", cost_estimate=cost(14),
     )(where, *mine, *other, *state)
     back = lambda group: [group[0].T, group[1], group[2], swap(group[3]), jnp.transpose(group[4], (1, 0, 2)), group[5]]
@@ -908,15 +985,14 @@
     return x
 
 
-def sum_grads(mine, theirs, d):
-    steps = levels(lax.axis_size("dp"))
-    items = [mine, send(theirs, twin())]
-    for level in steps:
-        items = reduce_level(items, d, *level)
-    x = tree(items, jnp.add)
-    for level in steps[:0:-1]:
-        x = in_order(gather_level(x, d, *level), d, *level)
-    return x, steps[0]
+def spread_upper(x, d):
+    for level in levels(lax.axis_size("dp"))[:0:-1]:
+        x = jnp.concatenate(gather_level(x, d, *level), axis=0)
+    return x
+
+
+def tie(*xs):
+    return lax.optimization_barrier(xs)
 
 
 def body(source, target, neighbours, neighbour_ticks, event_ticks, event_types, labels, edge_feats, weights, memory,
@@ -936,30 +1012,52 @@
     spread = first_latest(nodes, lines(source), lines(target), lines(event_ticks), lines(weights))
     spread = spread_latest(spread, d)
     latest = spread[:-1].reshape(-1).astype(I32)
-    w = prep(gru_in, gru_hid, keys_values, tall_stack, squares, vectors)
-    wg, wgc, wh = w[0], w[1], w[2]
-    vb = w[-1]
-    own, near = fetch(source, target, near_ids, mem_t, node_ticks)
+    wg, wh, vb = gate_weights(gru_in, gru_hid, vectors)
+    left, right, own = build_table(source, target, mem_t, node_ticks)
     cap = room(nodes, devices)
     msg, keep, ren, gap_own, packed = gru(
         scale, cap, source, target, event_ticks, latest, own, edge_feats.T, row(event_types), wg, wh, vb)
-    gathered = lax.all_gather(packed[0], AXES)
+    height = packed.shape[1]
+    low, *upper = levels(lax.axis_size("dp"))
+    first_round, left, right = tie(packed[0], left, right)
+    rows = spread_upper(first_round, d)
+    near = gather_near(near_ids, left, right)
+    rows, near, vec_late = tie(rows, near, vectors)
+    w = main_weights(gru_in, keys_values, tall_stack, squares, vec_late)
+    held = gather_level(rows, d, *low)
     mine, theirs = main(scale, near, near_ticks, row(event_ticks), msg, keep, ren, gap_own, row(labels), row(weights),
-                        spread[-1:], core.reshape(1), [wgc] + list(w[3:]))
-    piece, level = sum_grads(mine, theirs, d)
-    piece, gathered = lax.optimization_barrier((piece, gathered))
-    blocks = gather_level(piece, d, *level)
-    new_mem, more = merge(cap, gathered, mem_t)
-    *blocks, new_mem = lax.optimization_barrier((*blocks, new_mem))
+                        spread[-1:], core.reshape(1), list(w) + [vb])
+    mine, theirs, *held = tie(mine, theirs, *held)
+    got = send(theirs, twin())
+    items = reduce_level([mine, got], d, *low)
+    as_rows = lambda x: x.reshape(-1, height, 128)
+    items[0], *held = tie(items[0], *held)
+    laid = lay(cap, nodes, [as_rows(x) for x in held])
+    joined = tie(*items, *laid)
+    items, laid, joined = list(joined[: len(items)]), joined[len(items) : -1], joined[-1]
+    swapped = send(joined, twin())
+    for level in upper:
+        items = reduce_level(items, d, *level)
+    *items, swapped = tie(*items, swapped)
+    piece = tree(items, jnp.add)
+    for level in upper[::-1]:
+        piece = in_order(gather_level(piece, d, *level), d, *level)
+    piece, swapped = tie(piece, swapped)
+    blocks = gather_level(piece, d, *low)
+    new_mem, more = merge(cap, laid, swapped, mem_t)
+    *blocks, new_mem = tie(*blocks, new_mem)
     other = [send(x, twin()) for x in blocks]
     grad_norm, loss_sum, news = adam(
-        jnp.stack([core, place(d, *level)]), [(0, len(blocks))], blocks, other,
+        jnp.stack([core, place(d, *low)]), [(0, len(blocks))], blocks, other,
         (gru_in, gru_hid, keys_values, tall_stack, squares, vectors) + moments)
     weight_sum = spread[-1, 0]
 
     def again(carry):
         r, _, mem_now = carry
-        mem_now, more = merge(cap, lax.all_gather(lax.dynamic_index_in_dim(packed, r, 0, False), AXES), mem_now)
+        rows = spread_upper(lax.dynamic_index_in_dim(packed, r, 0, False), d)
+        held = gather_level(rows, d, *low)
+        *laid, joined = lay(cap, nodes, [as_rows(x) for x in held])
+        mem_now, more = merge(cap, laid, send(joined, twin()), mem_now)
         return r + 1, more & (r + 1 < packed.shape[0]), mem_now
 
     if packed.shape[0] > 1:

time: 221 us -> 201 us (0.910)
  waiting for transfers between devices: 54.6 us -> 20.1 us
  Pallas kernels: 112 us -> 135 us
  between operations: 14.3 us -> 1.85 us
  starting transfers between devices: 27.1 us -> 34.7 us
  other arithmetic: 8.31 us -> 5.61 us
    ppermute x24 -> x31, waiting for transfers between devices: 54.5 us -> 20.1 us  [send(): return lax.ppermute(x, AXES, pairs)]
    pallas_call x4 -> x7, Pallas kernels: 61.9 us -> 88.7 us  [the longest x1 20.7 us: lay(): pl.pallas_call(lambda *r: lay_kernel(cap, count, *r), out_shape=[table, t...]
    ppermute x24 -> x31, starting transfers between devices: 27 us -> 34.7 us  [send(): return lax.ppermute(x, AXES, pairs)]
    pallas_call x1, Pallas kernels: 15.8 us -> 10.9 us  [adam(): pl.pallas_call(lambda *r: adam_kernel(parts, *r), out_shape=outs, in_spec...]
    reduce_sum x1 -> x0, other arithmetic: 2.21 us -> none  [merge(): counts = jnp.sum((numbers >= 0.0).astype(I32), axis=1)]
  transfers between devices with their start and end apart: 25 -> 31, of which waited for: 13 -> 9; matrix products, arithmetic and copies ran while one was open for 3% -> 2% of each run, Pallas kernels for 37% -> 55%
where the time goes in v4:
time: 201 us; the launch traced here: 200 us
  Pallas kernels  135 us (67%)
  starting transfers between devices  34.7 us (17%)
  waiting for transfers between devices  20.1 us (10%)
  other arithmetic  5.61 us (3%)
  local copies, waits for them, and re-layouts  3.21 us (2%)
    ppermute x31, starting transfers between devices, send(): return lax.ppermute(x, AXES, pairs)  34.7 us
    pallas_call x1, Pallas kernels, main(): pl.pallas_call(lambda *r: main_kernel(scale, *r), out_shape=[jax.ShapeDty...  32.4 us
    pallas_call x1, Pallas kernels, lay(): pl.pallas_call(lambda *r: lay_kernel(cap, count, *r), out_shape=[table, t...  20.7 us
    pallas_call x1, Pallas kernels, merge(): pl.pallas_call(lambda *r: merge_kernel(cap, *r), out_shape=[jax.ShapeDtyp...  20.6 us
    ppermute x31, waiting for transfers between devices, send(): return lax.ppermute(x, AXES, pairs)  20.1 us
    pallas_call x1, Pallas kernels, gather_near(): pl.pallas_call(lambda *r: near_kernel(chunk, *r), out_shape=jax.ShapeDtyp...  19.1 us
    pallas_call x1, Pallas kernels, adam(): pl.pallas_call(lambda *r: adam_kernel(parts, *r), out_shape=outs, in_spec...  10.9 us
    pallas_call x1, Pallas kernels, gru(): pl.pallas_call(lambda *r: gru_kernel(scale, cap, rounds, nodes, *r), out_...  10.7 us
  transfers between devices with their start and end apart: 31, of which 9 were waited for; matrix products, arithmetic and copies ran while one was open for 2% of the time, Pallas kernels for 55%

profile of v4, /device:TPU:0, one launch (start us, length us, event | category | flops | bytes accessed | tf_op | source)
XLA Modules:
  0.0 200.3 jit_solution(9667811817013402019)
XLA Ops:
  0.7 2.8 %latest.1 = f32[65,128]{1,0:T(8,128)} custom-call(s32[4,128]{1,0:T(4,128)} %bitcast.112, s32[4,128]{1,0:T(4,128)} %bitcast.114, s32[4,128]{1,0:T(4,128)} %bitcast.117, f32[4,128]{1,0:T(4,128)} %bitcast.120), custom_call_target="tpu_custom_call" | custom-call | flops 2000000000 | bytes 6000000 | tf_op jit(solution)/shard_map/latest/pallas_call | solution.py:171
  5.9 2.9 %collective-permute-start.9 = (f32[65,128]{1,0:T(8,128)S(1)}, f32[65,128]{1,0:T(8,128)S(1)}, u32[]{:S(2)}, u32[]{:S(2)}) collective-permute-start(f32[65,128]{1,0:T(8,128)S(1)} %add_select_fusion.2), channel_id=1, source_target_pairs={{0,4},{1,5},{2,6},{3,7},{4,0},{5,1},{6,2},{7,3},{8,12},{9,13},{10,... | collective-permute-start | bytes 99848 | tf_op jit(solution)/shard_map/ppermute | solution.py:943
  10.3 9.4 %table.1 = (f32[8192,128]{1,0:T(8,128)}, f32[8192,128]{1,0:T(8,128)}, bf16[1024,256]{1,0:T(8,128)(2,1)}) custom-call(s32[512]{0:T(512)} %r_0_.1, s32[512]{0:T(512)} %r_1_.1, f32[172,8192]{1,0:T(8,128)} %bitcast.88, s32[1,8192]{1,0:T(1,128)} %bitcast.111), custom_call_target="tpu_custom_call" | custom-call | flops 8999999488 | bytes 27000000 | tf_op jit(solution)/shard_map/table/pallas_call | solution.py:226
  19.9 3.1 %collective-permute-start.12 = (f32[65,128]{1,0:T(8,128)S(1)}, f32[65,128]{1,0:T(8,128)S(1)}, u32[]{:S(2)}, u32[]{:S(2)}) collective-permute-start(f32[65,128]{1,0:T(8,128)S(1)} %add_select_fusion.1), channel_id=1, source_target_pairs={{0,16},{1,17},{2,18},{3,19},{4,20},{5,21},{6,22},{7,23},{8,24},{9,... | collective-permute-start | bytes 99848 | tf_op jit(solution)/shard_map/ppermute | solution.py:943
  24.5 3.7 %gate_weights.1 = (bf16[528,704]{1,0:T(8,128)(2,1)}, bf16[528,176]{1,0:T(8,128)(2,1)}, f32[15,176,128]{2,1,0:T(8,128)}) custom-call(f32[516,688]{1,0:T(8,128)} %bitcast.90, f32[172,516]{1,0:T(8,128)} %r_10_.1, f32[15,172]{1,0:T(8,128)} %r_14_.1), custom_call_target="tpu_custom_call" | custom-call | flops 4000000000 | bytes 12000000 | tf_op jit(solution)/shard_map/gate_weights/pallas_call | solution.py:94
  29.6 10.7 %gru.1 = (bf16[704,1024]{1,0:T(8,128)(2,1)}, f32[5,176,1024]{2,1,0:T(8,128)}, f32[176,1024]{1,0:T(8,128)}, f32[8,1024]{1,0:T(8,128)}, f32[4,440,128]{2,1,0:T(8,128)S(1)}) custom-call(s32[512]{0:T(512)} %r_0_.1, s32[512]{0:T(512)} %r_1_.1, s32[512]{0:T(512)} %r_2_.1, s32[8192]{0:T(1024)} %fusion.r_3_, bf16[1024,256]{1,0:T(8,128)(2,1)} %get-tuple-element.140.r_4_, ...), custom_call_target="tpu_custom_call" | custom-call | flops 10000000000 | bytes 30000000 | tf_op jit(solution)/shard_map/gru/pallas_call | solution.py:406
  40.3 3.0 %collective-permute-start.16 = (f32[440,128]{1,0:T(8,128)S(1)}, f32[440,128]{1,0:T(8,128)S(1)}, u32[]{:S(2)}, u32[]{:S(2)}) collective-permute-start(f32[440,128]{1,0:T(8,128)S(1)} %slice_bitcast_fusion), channel_id=1, source_target_pairs={{0,24},{1,25},{2,26},{3,27},{4,28},{5,29},{6,30},{7,31},{8,16},{9,... | collective-permute-start | bytes 675848 | tf_op jit(solution)/shard_map/ppermute | solution.py:943
  44.8 19.1 %near.1 = bf16[10240,256]{1,0:T(8,128)(2,1)} custom-call(s32[10240]{0:T(1024)} %bitcast.110, f32[8192,128]{1,0:T(8,128)} %get-tuple-element.148.r_1_, f32[8192,128]{1,0:T(8,128)} %get-tuple-element.149.r_2_), custom_call_target="tpu_custom_call" | custom-call | flops 16000000000 | bytes 48000000 | tf_op jit(solution)/shard_map/near/pallas_call | solution.py:252
  64.5 2.5 %collective-permute-start.19 = (f32[1760,128]{1,0:T(8,128)S(1)}, f32[1760,128]{1,0:T(8,128)S(1)}, u32[]{:S(2)}, u32[]{:S(2)}) collective-permute-start(f32[1760,128]{1,0:T(8,128)S(1)} %pad_maximum_fusion.1), channel_id=1, source_target_pairs={{0,6},{1,7},{2,4},{3,5},{4,2},{5,3},{6,0},{7,1},{8,14},{9,15},{10,... | collective-permute-start | bytes 2703368 | tf_op jit(solution)/shard_map/ppermute | solution.py:943
  68.0 4.4 %main_weights.1 = (bf16[176,528]{1,0:T(8,128)(2,1)}, bf16[352,256]{1,0:T(8,128)(2,1)}, bf16[352,176]{1,0:T(8,128)(2,1)}, bf16[176,352]{1,0:T(8,128)(2,1)}, bf16[...) custom-call(f32[516,688]{1,0:T(8,128)} %bitcast.91, ...), custom_call_target="tpu_custom_call" | custom-call | flops 5000000000 | bytes 15000000 | tf_op jit(solution)/shard_map/main_weights/pallas_call | solution.py:135
  72.5 32.4 %main.1 = (f32[3200,128]{1,0:T(8,128)}, f32[3200,128]{1,0:T(8,128)}) custom-call(s32[1]{0:T(128)} %bitcast.7.r_0_, bf16[10,1024,256]{2,1,0:T(8,128)(2,1)} %bitcast.123, s32[10,1024]{1,0:T(8,128)} %reshape.145.r_2_, s32[1,512]{1,0:T(1,128)} %bitcast.119, bf16[704,1024]{1,0:T(8,128)(2,1)} %get-tuple-element.151.r_4_, f32[5,176,1024]{2,1,0:T(8,128)} %get-tuple-element.152.r_5_, ...), custom_call_target="tpu_custom_call" | custom-call | flops 35000000512 | bytes 105000000 | tf_op jit(solution)/shard_map/main/pallas_call | solution.py:637
  106.3 3.7 %collective-permute-done.20 = f32[3200,128]{1,0:T(8,128)S(1)} collective-permute-done((f32[3200,128]{1,0:T(8,128)}, f32[3200,128]{1,0:T(8,128)S(1)}, u32[]{:S(2)}, u32[]{:S(2)}) %collective-permute-start.20) | collective-permute-done | bytes 1638432 | tf_op jit(solution)/shard_map/ppermute | solution.py:943
  110.1 1.7 dynamic-slice_add_fusion
  111.7 2.5 %collective-permute-start.23 = (f32[800,128]{1,0:T(8,128)S(1)}, f32[800,128]{1,0:T(8,128)S(1)}, u32[]{:S(2)}, u32[]{:S(2)}) collective-permute-start(f32[800,128]{1,0:T(8,128)S(1)} %get-tuple-element.240), channel_id=1, source_target_pairs={{0,6},{1,7},{2,4},{3,5},{4,2},{5,3},{6,0},{7,1},{8,14},{9,15},{10,... | collective-permute-start | bytes 1228808 | tf_op jit(solution)/shard_map/ppermute | solution.py:943
  115.3 20.7 %lay.2 = (f32[8200,128]{1,0:T(8,128)}, f32[8200,128]{1,0:T(8,128)}, s32[1]{0:T(128)}, f32[16,440,128]{2,1,0:T(8,128)}) custom-call(f32[4,440,128]{2,1,0:T(8,128)} %bitcast.84, f32[4,440,128]{2,1,0:T(8,128)} %bitcast.97, f32[4,440,128]{2,1,0:T(8,128)} %bitcast.96, f32[4,440,128]{2,1,0:T(8,128)} %bitcast.95), custom_call_target="tpu_custom_call" | custom-call | flops 14000000000 | bytes 42000000 | tf_op jit(solution)/shard_map/lay/pallas_call | solution.py:724
  136.3 3.0 %collective-permute-start.26 = (f32[200,128]{1,0:T(8,128)S(1)}, f32[200,128]{1,0:T(8,128)S(1)}, u32[]{:S(2)}, u32[]{:S(2)}) collective-permute-start(f32[200,128]{1,0:T(8,128)S(1)} %get-tuple-element.244), channel_id=1, source_target_pairs={{0,24},{1,25},{2,26},{3,27},{4,28},{5,29},{6,30},{7,31},{8,16},{9,... | collective-permute-start | bytes 307208 | tf_op jit(solution)/shard_map/ppermute | solution.py:943
  140.8 3.2 %collective-permute-done.26 = f32[200,128]{1,0:T(8,128)S(1)} collective-permute-done((f32[200,128]{1,0:T(8,128)S(1)}, f32[200,128]{1,0:T(8,128)S(1)}, u32[]{:S(2)}, u32[]{:S(2)}) %collective-permute-start.26) | collective-permute-done | bytes 102432 | tf_op jit(solution)/shard_map/ppermute | solution.py:943
  143.9 4.6 %collective-permute-done.25 = f32[200,128]{1,0:T(8,128)S(1)} collective-permute-done((f32[200,128]{1,0:T(8,128)S(1)}, f32[200,128]{1,0:T(8,128)S(1)}, u32[]{:S(2)}, u32[]{:S(2)}) %collective-permute-start.25) | collective-permute-done | bytes 102432 | tf_op jit(solution)/shard_map/ppermute | solution.py:943
  149.1 2.6 %collective-permute-start.29 = (f32[200,128]{1,0:T(8,128)S(1)}, f32[200,128]{1,0:T(8,128)S(1)}, u32[]{:S(2)}, u32[]{:S(2)}) collective-permute-start(f32[200,128]{1,0:T(8,128)S(1)} %add_add_fusion), channel_id=1, source_target_pairs={{0,16},{1,17},{2,18},{3,19},{4,20},{5,21},{6,22},{7,23},{8,24},{9,... | collective-permute-start | bytes 307208 | tf_op jit(solution)/shard_map/ppermute | solution.py:943
  154.4 5.2 %collective-permute-done.29 = f32[200,128]{1,0:T(8,128)S(1)} collective-permute-done((f32[200,128]{1,0:T(8,128)S(1)}, f32[200,128]{1,0:T(8,128)S(1)}, u32[]{:S(2)}, u32[]{:S(2)}) %collective-permute-start.29) | collective-permute-done | bytes 102432 | tf_op jit(solution)/shard_map/ppermute | solution.py:943
  159.8 2.5 %collective-permute-start.33 = (f32[800,128]{1,0:T(8,128)S(1)}, f32[800,128]{1,0:T(8,128)S(1)}, u32[]{:S(2)}, u32[]{:S(2)}) collective-permute-start(f32[800,128]{1,0:T(8,128)S(1)} %pad_maximum_fusion.2.r_1_), channel_id=1, source_target_pairs={{0,6},{1,7},{2,4},{3,5},{4,2},{5,3},{6,0},{7,1},{8,14},{9,15},{10,... | collective-permute-start | bytes 1228808 | tf_op jit(solution)/shard_map/ppermute | solution.py:943
  163.3 1.5 slice_convert_fusion.2
  164.8 20.6 %merge.2 = (f32[172,8192]{1,0:T(8,128)}, s32[1]{0:T(128)}) custom-call(s32[8192]{0:T(1024)} %bitcast.87, f32[16,440,128]{2,1,0:T(8,128)} %collective-permute-done.27.r_1_, f32[8200,128]{1,0:T(8,128)} %get-tuple-element.201.r_2_, f32[8200,128]{1,0:T(8,128)} %get-tuple-element.202.r_3_, s32[1]{0:T(128)} %get-tuple-element.203.r_4_, f32[172,8192]{1,0:T(8,128)} %bitcast.89), custom_call_target="tpu_custom_call" | custom-call | flops 17999998976 | bytes 54000000 | tf_op jit(solution)/shard_map/merge/pallas_call | solution.py:765
  189.2 10.9 %adam.1 = (f32[516,688]{1,0:T(8,128)}, f32[172,516]{1,0:T(8,128)}, f32[344,344]{1,0:T(8,128)}, f32[3,172,344]{2,1,0:T(8,128)}, f32[172,2,172]{2,1,0:T(2,128)}, /...) custom-call(s32[2]{0:T(128)} %pad_add_fusion.r_0_, ...), custom_call_target="tpu_custom_call" | custom-call | flops 14000000000 | bytes 42000000 | tf_op jit(solution)/shard_map/adam/pallas_call | solution.py:907
  (88 shorter events, 21.7 us)
Async XLA Ops:
  5.9 13.9 %collective-permute-start.9 = (f32[65,128]{1,0:T(8,128)S(1)}, f32[65,128]{1,0:T(8,128)S(1)}, u32[]{:S(2)}, u32[]{:S(2)}) collective-permute-start(f32[65,128]{1,0:T(8,128)S(1)} %add_select_fusion.2), channel_id=1, source_target_pairs={{0,4},{1,5},{2,6},{3,7},{4,0},{5,1},{6,2},{7,3},{8,12},{9,13},{10,... | collective-permute-start | bytes 99848 | tf_op jit(solution)/shard_map/ppermute | solution.py:943
  8.8 11.0 %collective-permute-start.10 = (f32[65,128]{1,0:T(8,128)S(1)}, f32[65,128]{1,0:T(8,128)S(1)}, u32[]{:S(2)}, u32[]{:S(2)}) collective-permute-start(f32[65,128]{1,0:T(8,128)S(1)} %add_select_fusion.2), channel_id=1, source_target_pairs={{0,6},{1,7},{2,4},{3,5},{4,2},{5,3},{6,0},{7,1},{8,14},{9,15},{10,... | collective-permute-start | bytes 99848 | tf_op jit(solution)/shard_map/ppermute | solution.py:943
  10.2 9.5 %collective-permute-start.8 = (f32[65,128]{1,0:T(8,128)S(1)}, f32[65,128]{1,0:T(8,128)S(1)}, u32[]{:S(2)}, u32[]{:S(2)}) collective-permute-start(f32[65,128]{1,0:T(8,128)S(1)} %add_select_fusion.2), channel_id=1, source_target_pairs={{0,2},{1,3},{2,0},{3,1},{4,6},{5,7},{6,4},{7,5},{8,10},{9,11},{10,... | collective-permute-start | bytes 99848 | tf_op jit(solution)/shard_map/ppermute | solution.py:943
  19.9 9.1 %collective-permute-start.12 = (f32[65,128]{1,0:T(8,128)S(1)}, f32[65,128]{1,0:T(8,128)S(1)}, u32[]{:S(2)}, u32[]{:S(2)}) collective-permute-start(f32[65,128]{1,0:T(8,128)S(1)} %add_select_fusion.1), channel_id=1, source_target_pairs={{0,16},{1,17},{2,18},{3,19},{4,20},{5,21},{6,22},{7,23},{8,24},{9,... | collective-permute-start | bytes 99848 | tf_op jit(solution)/shard_map/ppermute | solution.py:943
  22.9 6.0 %collective-permute-start.13 = (f32[65,128]{1,0:T(8,128)S(1)}, f32[65,128]{1,0:T(8,128)S(1)}, u32[]{:S(2)}, u32[]{:S(2)}) collective-permute-start(f32[65,128]{1,0:T(8,128)S(1)} %add_select_fusion.1), channel_id=1, source_target_pairs={{0,24},{1,25},{2,26},{3,27},{4,28},{5,29},{6,30},{7,31},{8,16},{9,... | collective-permute-start | bytes 99848 | tf_op jit(solution)/shard_map/ppermute | solution.py:943
  40.3 24.0 %collective-permute-start.16 = (f32[440,128]{1,0:T(8,128)S(1)}, f32[440,128]{1,0:T(8,128)S(1)}, u32[]{:S(2)}, u32[]{:S(2)}) collective-permute-start(f32[440,128]{1,0:T(8,128)S(1)} %slice_bitcast_fusion), channel_id=1, source_target_pairs={{0,24},{1,25},{2,26},{3,27},{4,28},{5,29},{6,30},{7,31},{8,16},{9,... | collective-permute-start | bytes 675848 | tf_op jit(solution)/shard_map/ppermute | solution.py:943
  43.3 21.0 %collective-permute-start.15 = (f32[440,128]{1,0:T(8,128)S(1)}, f32[440,128]{1,0:T(8,128)S(1)}, u32[]{:S(2)}, u32[]{:S(2)}) collective-permute-start(f32[440,128]{1,0:T(8,128)S(1)} %slice_bitcast_fusion), channel_id=1, source_target_pairs={{0,16},{1,17},{2,18},{3,19},{4,20},{5,21},{6,22},{7,23},{8,24},{9,... | collective-permute-start | bytes 675848 | tf_op jit(solution)/shard_map/ppermute | solution.py:943
  43.7 20.7 %collective-permute-start.14 = (f32[440,128]{1,0:T(8,128)S(1)}, f32[440,128]{1,0:T(8,128)S(1)}, u32[]{:S(2)}, u32[]{:S(2)}) collective-permute-start(f32[440,128]{1,0:T(8,128)S(1)} %slice_bitcast_fusion), channel_id=1, source_target_pairs={{0,8},{1,9},{2,10},{3,11},{4,12},{5,13},{6,14},{7,15},{8,0},{9,1},... | collective-permute-start | bytes 675848 | tf_op jit(solution)/shard_map/ppermute | solution.py:943
  64.5 40.4 %collective-permute-start.19 = (f32[1760,128]{1,0:T(8,128)S(1)}, f32[1760,128]{1,0:T(8,128)S(1)}, u32[]{:S(2)}, u32[]{:S(2)}) collective-permute-start(f32[1760,128]{1,0:T(8,128)S(1)} %pad_maximum_fusion.1), channel_id=1, source_target_pairs={{0,6},{1,7},{2,4},{3,5},{4,2},{5,3},{6,0},{7,1},{8,14},{9,15},{10,... | collective-permute-start | bytes 2703368 | tf_op jit(solution)/shard_map/ppermute | solution.py:943
  67.0 37.9 %collective-permute-start.18 = (f32[1760,128]{1,0:T(8,128)S(1)}, f32[1760,128]{1,0:T(8,128)S(1)}, u32[]{:S(2)}, u32[]{:S(2)}) collective-permute-start(f32[1760,128]{1,0:T(8,128)S(1)} %pad_maximum_fusion.1), channel_id=1, source_target_pairs={{0,4},{1,5},{2,6},{3,7},{4,0},{5,1},{6,2},{7,3},{8,12},{9,13},{10,... | collective-permute-start | bytes 2703368 | tf_op jit(solution)/shard_map/ppermute | solution.py:943
  67.5 37.4 %collective-permute-start.17 = (f32[1760,128]{1,0:T(8,128)S(1)}, f32[1760,128]{1,0:T(8,128)S(1)}, u32[]{:S(2)}, u32[]{:S(2)}) collective-permute-start(f32[1760,128]{1,0:T(8,128)S(1)} %pad_maximum_fusion.1), channel_id=1, source_target_pairs={{0,2},{1,3},{2,0},{3,1},{4,6},{5,7},{6,4},{7,5},{8,10},{9,11},{10,... | collective-permute-start | bytes 2703368 | tf_op jit(solution)/shard_map/ppermute | solution.py:943
  111.7 24.3 %collective-permute-start.23 = (f32[800,128]{1,0:T(8,128)S(1)}, f32[800,128]{1,0:T(8,128)S(1)}, u32[]{:S(2)}, u32[]{:S(2)}) collective-permute-start(f32[800,128]{1,0:T(8,128)S(1)} %get-tuple-element.240), channel_id=1, source_target_pairs={{0,6},{1,7},{2,4},{3,5},{4,2},{5,3},{6,0},{7,1},{8,14},{9,15},{10,... | collective-permute-start | bytes 1228808 | tf_op jit(solution)/shard_map/ppermute | solution.py:943
  114.3 21.8 %collective-permute-start.22 = (f32[800,128]{1,0:T(8,128)S(1)}, f32[800,128]{1,0:T(8,128)S(1)}, u32[]{:S(2)}, u32[]{:S(2)}) collective-permute-start(f32[800,128]{1,0:T(8,128)S(1)} %get-tuple-element.241), channel_id=1, source_target_pairs={{0,4},{1,5},{2,6},{3,7},{4,0},{5,1},{6,2},{7,3},{8,12},{9,13},{10,... | collective-permute-start | bytes 1228808 | tf_op jit(solution)/shard_map/ppermute | solution.py:943
  114.8 21.3 %collective-permute-start.21 = (f32[800,128]{1,0:T(8,128)S(1)}, f32[800,128]{1,0:T(8,128)S(1)}, u32[]{:S(2)}, u32[]{:S(2)}) collective-permute-start(f32[800,128]{1,0:T(8,128)S(1)} %get-tuple-element.242), channel_id=1, source_target_pairs={{0,2},{1,3},{2,0},{3,1},{4,6},{5,7},{6,4},{7,5},{8,10},{9,11},{10,... | collective-permute-start | bytes 1228808 | tf_op jit(solution)/shard_map/ppermute | solution.py:943
  136.1 12.5 %collective-permute-start.27 = (f32[16,440,128]{2,1,0:T(8,128)}, f32[16,440,128]{2,1,0:T(8,128)}, u32[]{:S(2)}, u32[]{:S(2)}) collective-permute-start(f32[16,440,128]{2,1,0:T(8,128)} %get-tuple-element.193), channel_id=1, source_target_pairs={{0,1},{1,0},{2,3},{3,2},{4,5},{5,4},{6,7},{7,6},{8,9},{9,8},{10,11... | collective-permute-start | bytes 10813448 | tf_op jit(solution)/shard_map/ppermute | solution.py:943
  136.3 7.6 %collective-permute-start.26 = (f32[200,128]{1,0:T(8,128)S(1)}, f32[200,128]{1,0:T(8,128)S(1)}, u32[]{:S(2)}, u32[]{:S(2)}) collective-permute-start(f32[200,128]{1,0:T(8,128)S(1)} %get-tuple-element.244), channel_id=1, source_target_pairs={{0,24},{1,25},{2,26},{3,27},{4,28},{5,29},{6,30},{7,31},{8,16},{9,... | collective-permute-start | bytes 307208 | tf_op jit(solution)/shard_map/ppermute | solution.py:943
  139.3 9.2 %collective-permute-start.25 = (f32[200,128]{1,0:T(8,128)S(1)}, f32[200,128]{1,0:T(8,128)S(1)}, u32[]{:S(2)}, u32[]{:S(2)}) collective-permute-start(f32[200,128]{1,0:T(8,128)S(1)} %get-tuple-element.245), channel_id=1, source_target_pairs={{0,16},{1,17},{2,18},{3,19},{4,20},{5,21},{6,22},{7,23},{8,24},{9,... | collective-permute-start | bytes 307208 | tf_op jit(solution)/shard_map/ppermute | solution.py:943
  139.3 9.2 %collective-permute-start.24 = (f32[200,128]{1,0:T(8,128)S(1)}, f32[200,128]{1,0:T(8,128)S(1)}, u32[]{:S(2)}, u32[]{:S(2)}) collective-permute-start(f32[200,128]{1,0:T(8,128)S(1)} %get-tuple-element.246), channel_id=1, source_target_pairs={{0,8},{1,9},{2,10},{3,11},{4,12},{5,13},{6,14},{7,15},{8,0},{9,1},... | collective-permute-start | bytes 307208 | tf_op jit(solution)/shard_map/ppermute | solution.py:943
  148.6 5.8 %collective-permute-start.30 = (f32[200,128]{1,0:T(8,128)S(1)}, f32[200,128]{1,0:T(8,128)S(1)}, u32[]{:S(2)}, u32[]{:S(2)}) collective-permute-start(f32[200,128]{1,0:T(8,128)S(1)} %add_add_fusion), channel_id=1, source_target_pairs={{0,8},{1,9},{2,10},{3,11},{4,12},{5,13},{6,14},{7,15},{8,0},{9,1},... | collective-permute-start | bytes 307208 | tf_op jit(solution)/shard_map/ppermute | solution.py:943
  149.1 10.6 %collective-permute-start.29 = (f32[200,128]{1,0:T(8,128)S(1)}, f32[200,128]{1,0:T(8,128)S(1)}, u32[]{:S(2)}, u32[]{:S(2)}) collective-permute-start(f32[200,128]{1,0:T(8,128)S(1)} %add_add_fusion), channel_id=1, source_target_pairs={{0,16},{1,17},{2,18},{3,19},{4,20},{5,21},{6,22},{7,23},{8,24},{9,... | collective-permute-start | bytes 307208 | tf_op jit(solution)/shard_map/ppermute | solution.py:943
  151.6 8.0 %collective-permute-start.28 = (f32[200,128]{1,0:T(8,128)S(1)}, f32[200,128]{1,0:T(8,128)S(1)}, u32[]{:S(2)}, u32[]{:S(2)}) collective-permute-start(f32[200,128]{1,0:T(8,128)S(1)} %add_add_fusion), channel_id=1, source_target_pairs={{0,24},{1,25},{2,26},{3,27},{4,28},{5,29},{6,30},{7,31},{8,16},{9,... | collective-permute-start | bytes 307208 | tf_op jit(solution)/shard_map/ppermute | solution.py:943
  159.8 25.7 %collective-permute-start.33 = (f32[800,128]{1,0:T(8,128)S(1)}, f32[800,128]{1,0:T(8,128)S(1)}, u32[]{:S(2)}, u32[]{:S(2)}) collective-permute-start(f32[800,128]{1,0:T(8,128)S(1)} %pad_maximum_fusion.2.r_1_), channel_id=1, source_target_pairs={{0,6},{1,7},{2,4},{3,5},{4,2},{5,3},{6,0},{7,1},{8,14},{9,15},{10,... | collective-permute-start | bytes 1228808 | tf_op jit(solution)/shard_map/ppermute | solution.py:943
  162.3 23.2 %collective-permute-start.32 = (f32[800,128]{1,0:T(8,128)S(1)}, f32[800,128]{1,0:T(8,128)S(1)}, u32[]{:S(2)}, u32[]{:S(2)}) collective-permute-start(f32[800,128]{1,0:T(8,128)S(1)} %pad_maximum_fusion.2.r_1_), channel_id=1, source_target_pairs={{0,4},{1,5},{2,6},{3,7},{4,0},{5,1},{6,2},{7,3},{8,12},{9,13},{10,... | collective-permute-start | bytes 1228808 | tf_op jit(solution)/shard_map/ppermute | solution.py:943
  162.8 22.7 %collective-permute-start.31 = (f32[800,128]{1,0:T(8,128)S(1)}, f32[800,128]{1,0:T(8,128)S(1)}, u32[]{:S(2)}, u32[]{:S(2)}) collective-permute-start(f32[800,128]{1,0:T(8,128)S(1)} %pad_maximum_fusion.2.r_1_), channel_id=1, source_target_pairs={{0,2},{1,3},{2,0},{3,1},{4,6},{5,7},{6,4},{7,5},{8,10},{9,11},{10,... | collective-permute-start | bytes 1228808 | tf_op jit(solution)/shard_map/ppermute | solution.py:943
  (18 other events, 75.5 us)

commit v5 on v4

--- a/solution.py
+++ b/solution.py
@@ -180,9 +180,15 @@
         out[pl.ds(at, 16), 128 * h : 128 * h + 128] = rows.astype(BF)
 
 
-def table_kernel(source, target, mem, ticks, left, right, own, wide):
+def table_kernel(source, target, mem, ticks, far_left, far_right, own, wide, left, right, sems):
     step = pl.program_id(0)
     cols = mem.shape[1]
+    steps = far_left.shape[0] // cols
+
+    def copies(at):
+        part = pl.ds(pl.multiple_of(at * cols, cols), cols)
+        return [pltpu.make_async_copy(near.at[part], far.at[part], sems.at[h, at])
+                for h, (near, far) in enumerate(((left, far_left), (right, far_right)))]
 
     @pl.when(step == 0)
     def _():
@@ -198,8 +204,10 @@
         rows = nt(unit, wide[:, 256 * c : 256 * c + 256].astype(BF))
         left[pl.ds(base + 256 * c, 256), :] = rows[:, :128]
         right[pl.ds(base + 256 * c, 256), :] = rows[:, 128:]
-
-    @pl.when(step == pl.num_programs(0) - 1)
+    for copy in copies(step):
+        copy.start()
+
+    @pl.when(step == steps - 1)
     def _():
         def group(b, carry):
             for role, ids in enumerate((source, target)):
@@ -214,6 +222,9 @@
             return carry
 
         lax.fori_loop(0, own.shape[0] // 256, group, 0)
+        for at in range(steps):
+            for copy in copies(at):
+                copy.wait()
 
 
 def build_table(source, target, mem_t, ticks):
@@ -228,8 +239,9 @@
         out_shape=[half, half, jax.ShapeDtypeStruct((ends, 256), BF)],
         grid=(nodes // cols,),
         in_specs=[smem, smem, pl.BlockSpec((MEM, cols), lambda i: (0, i)), pl.BlockSpec((1, cols), lambda i: (0, i))],
-        out_specs=[pl.BlockSpec((nodes, 128), fixed), pl.BlockSpec((nodes, 128), fixed), pl.BlockSpec((ends, 256), fixed)],
-        scratch_shapes=[pltpu.VMEM((256, cols), F32)],
+        out_specs=[pl.BlockSpec(memory_space=pl.ANY), pl.BlockSpec(memory_space=pl.ANY), pl.BlockSpec((ends, 256), fixed)],
+        scratch_shapes=[pltpu.VMEM((256, cols), F32), pltpu.VMEM((nodes, 128), F32), pltpu.VMEM((nodes, 128), F32),
+                        pltpu.SemaphoreType.DMA((2, nodes // cols))],
         compiler_params=params(), name="table", cost_estimate=cost(9),
     )(source, target, mem_t, ticks.reshape(1, nodes))
 
@@ -418,7 +430,9 @@
     )(sources, targets, ticks, latest, own, row(sources), row(targets), row(ticks), edge_t, types, wg, wh, vb)
 
 
-UNROLL = 5
+UNROLL = 10
+ROWS = 2944
+VECTORS = 2904
 GELU_C = math.sqrt(2.0 / math.pi)
 
 
@@ -597,28 +611,29 @@
     vacc[14] += fold(d_out)
 
     def finish(ga, gb):
-        wide = cols_to(g_in[...], 768)
-        for c in range(6):
-            gb[528 * c : 528 * c + 528, :] = wide[:, 128 * c : 128 * c + 128]
+        def panels(out, x):
+            rows, lanes = x.shape
+            whole = lanes // 128
+            for c in range(whole):
+                out[rows * c : rows * c + rows, :] = x[:, 128 * c : 128 * c + 128]
+            last = x[:, 128 * whole :]
+            out[rows * whole : rows * whole + rows // 2, :] = jnp.concatenate([last[: rows // 2], last[rows // 2 :]], axis=1)
+
+        panels(gb, g_in[...])
         lane = lax.broadcasted_iota(I32, (PAD, 128), 1)
         vecs = zeros(PAD, 128)
         for i in range(16):
             column = jnp.sum(vacc[i], axis=1, keepdims=True)
             vecs = jnp.where(lane == i, column, vecs)
         flat = jnp.transpose(jnp.concatenate([vecs, zeros(256 - PAD, 128)], axis=0))
-        gb[3168:3184, :] = flat[0:16, 0:128]
-        gb[3184:3200, :] = flat[0:16, 128:256]
-        at = 0
-        for left, right, rows in ((g_kv[:, 0:PAD], g_kv[:, 256 : 256 + PAD], 352),
-                                  (g_one[:, 0:PAD], g_one[:, PAD : 2 * PAD], 176),
-                                  (g_dec[:, 0:PAD], g_dec[:, PAD : 2 * PAD], 176),
-                                  (g_qo[:, 0:PAD], g_qo[:, 256 : 256 + PAD], 176),
-                                  (g_th[:, 0:PAD], g_th[:, 256 : 256 + PAD], 176)):
-            wide = jnp.concatenate([left, right, zeros(rows, 32)], axis=1)
-            for c in range(3):
-                ga[at : at + rows, :] = wide[:, 128 * c : 128 * c + 128]
-                at += rows
-        ga[3168:3200, :] = rows_to(loss[...], 32)
+        gb[VECTORS : VECTORS + 16, :] = flat[0:16, 0:128]
+        gb[VECTORS + 16 : VECTORS + 32, :] = flat[0:16, 128:256]
+        gb[VECTORS + 32 :, :] = zeros(ROWS - VECTORS - 32, 128)
+        units = [g_kv[at : at + PAD, c : c + PAD] for at in (0, PAD) for c in (0, 256)]
+        units += [g_one[...], g_dec[...]]
+        units += [ref[:, c : c + PAD] for ref in (g_qo, g_th) for c in (0, 256)]
+        panels(ga, jnp.concatenate(units, axis=1))
+        ga[VECTORS:, :] = rows_to(loss[...], ROWS - VECTORS)
 
     @pl.when((step == pl.num_programs(0) - 1) & (core[0] == 0))
     def _():
@@ -636,13 +651,13 @@
     lanes = lambda: pl.BlockSpec((1, BLOCK // 2), lambda i: (0, i))
     return pl.pallas_call(
         lambda *r: main_kernel(scale, *r),
-        out_shape=[jax.ShapeDtypeStruct((3200, 128), F32), jax.ShapeDtypeStruct((3200, 128), F32)],
+        out_shape=[jax.ShapeDtypeStruct((ROWS, 128), F32), jax.ShapeDtypeStruct((ROWS, 128), F32)],
         grid=(blocks,),
         in_specs=[pl.BlockSpec(memory_space=pltpu.SMEM), pl.BlockSpec((NBR, BLOCK, 256), lambda i: (0, i, 0)), pl.BlockSpec((NBR, BLOCK), lambda i: (0, i)), lanes(),
                   pl.BlockSpec((4 * PAD, BLOCK), lambda i: (0, i)), pl.BlockSpec((5, PAD, BLOCK), lambda i: (0, 0, i)),
                   pl.BlockSpec((PAD, BLOCK), lambda i: (0, i)), pl.BlockSpec((8, BLOCK), lambda i: (0, i)), lanes(), lanes(),
                   pl.BlockSpec((1, 128), lambda i: (0, 0))] + [whole(a) for a in w],
-        out_specs=[pl.BlockSpec((3200, 128), lambda i: (0, 0)), pl.BlockSpec((3200, 128), lambda i: (0, 0))],
+        out_specs=[pl.BlockSpec((ROWS, 128), lambda i: (0, 0)), pl.BlockSpec((ROWS, 128), lambda i: (0, 0))],
         scratch_shapes=[pltpu.VMEM((1, 128), F32), pltpu.VMEM((NBR, 352, BLOCK), F32), pltpu.VMEM((NBR, PAD, BLOCK), BF), pltpu.VMEM((NBR, PAD, BLOCK), F32),
                         pltpu.VMEM((20, 8, BLOCK), F32), pltpu.VMEM((20, 8, BLOCK), F32), pltpu.VMEM((2, 8, BLOCK), F32),
                         pltpu.VMEM((PAD, BLOCK), F32), pltpu.VMEM((NBR, 352, BLOCK), BF),
@@ -666,20 +681,27 @@
     return (nt(unit, high) + nt(unit, middle)) + nt(unit, low)
 
 
-def lay_rows(cap, number, rows, left, right, second):
+def fetch_numbers(cap, rows, whole, numbers, sem):
+    whole[...] = rows[:, cap + cap // 2 :, :].astype(I32)
+    copy = pltpu.make_async_copy(whole, numbers, sem)
+    copy.start()
+    return copy
+
+
+def lay_rows(cap, rows, numbers, left, right, second):
     tail = cap // 2
-    width = -(-cap // 128) * 128
 
     def block(q, most):
         half = rows[q, cap : cap + tail, :]
         second[0:tail, :] = half
         second[tail:cap, :] = jnp.concatenate([half[:, 64:], half[:, :64]], axis=1)
-        here = number(q, width)
+        here = numbers[q, -(-cap // 128), 0]
 
         def some(g, carry):
+            few = numbers.at[q, lax.shift_right_logical(g, 3), pl.ds((g & 7) * 16, 16)]
             for v in range(16):
                 i = g * 16 + v
-                node = number(q, i)
+                node = few[v]
                 left[pl.ds(node, 1), :] = rows[q, pl.ds(i, 1), :]
                 right[pl.ds(node, 1), :] = second[pl.ds(i, 1), :]
             return carry
@@ -693,12 +715,7 @@
 def lay_kernel(cap, count, *refs):
     arrays, (left, right, most, joined, second, sems), rest = refs[:count], refs[count : count + 6], refs[count + 6 :]
     wholes, lists = rest[:count], rest[count:]
-    lines = cap + cap // 2
-    copies = []
-    for a, (rows, whole) in enumerate(zip(arrays, wholes)):
-        whole[...] = rows[:, lines:, :].astype(I32)
-        copies.append(pltpu.make_async_copy(whole, lists[a], sems.at[a]))
-        copies[a].start()
+    copies = [fetch_numbers(cap, arrays[a], wholes[a], lists[a], sems.at[a]) for a in range(count)]
     right[...] = jnp.full_like(right, -1.0)
     for a, rows in enumerate(arrays):
         blocks = rows.shape[0]
@@ -706,14 +723,8 @@
     largest = jnp.int32(0)
     for a, rows in enumerate(arrays):
         copies[a].wait()
-        number = lambda q, i: lists[a][q, lax.shift_right_logical(i, 7), i & 127]
-        largest = jnp.maximum(largest, lay_rows(cap, number, rows, left, right, second))
+        largest = jnp.maximum(largest, lay_rows(cap, rows, lists[a], left, right, second))
     most[0] = largest
-
-
-def row_numbers(cap, x):
-    first, height = cap + cap // 2, -(-cap // 128) + 1
-    return x[:, first : first + height, :].astype(I32).reshape(-1)
 
 
 def lay(cap, nodes, arrays):
@@ -731,7 +742,7 @@
     )(*arrays)
 
 
-def merge_kernel(cap, numbers, rows, far_left, far_right, before, mem, out, full, left, right, second, sems):
+def merge_kernel(cap, rows, far_left, far_right, before, mem, out, full, left, right, second, sems, whole, numbers):
     step = pl.program_id(0)
 
     @pl.when(step == 0)
@@ -739,10 +750,10 @@
         copies = [pltpu.make_async_copy(far_left, left, sems.at[0]), pltpu.make_async_copy(far_right, right, sems.at[1])]
         for copy in copies:
             copy.start()
+        copies.append(fetch_numbers(cap, rows, whole, numbers, sems.at[2]))
         for copy in copies:
             copy.wait()
-        width = -(-cap // 128) * 128 + 128
-        most = lay_rows(cap, lambda q, i: numbers[q * width + i], rows, left, right, second)
+        most = lay_rows(cap, rows, numbers, left, right, second)
         full[0] = (jnp.maximum(most, before[0]) == cap).astype(I32)
 
     cols = mem.shape[1]
@@ -766,12 +777,12 @@
         lambda *r: merge_kernel(cap, *r),
         out_shape=[jax.ShapeDtypeStruct((MEM, nodes), F32), jax.ShapeDtypeStruct((1,), I32)],
         grid=(nodes // cols,),
-        in_specs=[smem, pl.BlockSpec(rows.shape, lambda i: (0, 0, 0)), far, far, smem, part],
+        in_specs=[pl.BlockSpec(rows.shape, lambda i: (0, 0, 0)), far, far, smem, part],
         out_specs=[part, smem],
         scratch_shapes=[pltpu.VMEM((nodes + 8, 128), F32), pltpu.VMEM((nodes + 8, 128), F32), pltpu.VMEM((cap, 128), F32),
-                        pltpu.SemaphoreType.DMA((2,))],
+                        pltpu.SemaphoreType.DMA((3,))] + [kind((rows.shape[0], 8, 128), I32) for kind in (pltpu.VMEM, pltpu.SMEM)],
         compiler_params=params(), name="merge", cost_estimate=cost(18),
-    )(row_numbers(cap, rows), rows, *laid, mem_t)
+    )(rows, *laid, mem_t)
     return new, full[0] > 0
 
 
@@ -818,36 +829,36 @@
                 b[pl.ds(at, height), :] = one[...]
                 a[pl.ds(at, height), :] = two[...]
 
-    def panels(ref, at, rows, n):
-        return jnp.concatenate([ref[at + c * rows : at + (c + 1) * rows, :] for c in range(n)], axis=1)
+    def panels(ref, rows, lanes):
+        whole = lanes // 128
+        parts = [ref[c * rows : (c + 1) * rows, :] for c in range(whole)]
+        last = ref[whole * rows : whole * rows + rows // 2, :]
+        return jnp.concatenate(parts + [jnp.concatenate([last[:, :64], last[:, 64:]], axis=0)], axis=1)
 
     vec, tall = state[5], state[3]
-    wide = panels(b, 0, 528, 6)
+    wide = panels(b, 528, 704)
     gates = []
     for g in range(3):
         rows = wide[PAD * g : PAD * g + MEM]
         gates.append(jnp.concatenate([rows[:, PAD * q : PAD * q + MEM] for q in range(4)], axis=1))
     g_gin[...] = jnp.concatenate(gates, axis=0)
-    vecs = jnp.concatenate([b[3168:3184, :], b[3184:3200, :]], axis=1)
-    kv = panels(a, 0, 352, 3)
-    kv = jnp.concatenate([unsplit(kv[:PAD], 0), unsplit(kv[PAD:], 0)], axis=0)
-    kv = jnp.concatenate([kv[:, :MEM], kv[:, PAD : PAD + MEM]], axis=1)
+    vecs = jnp.concatenate([b[VECTORS : VECTORS + 16, :], b[VECTORS + 16 : VECTORS + 32, :]], axis=1)
+    units = panels(a, PAD, 12 * PAD)
+    unit = lambda i: units[:, PAD * i : PAD * i + MEM]
+    kv = jnp.concatenate([jnp.concatenate([unsplit(unit(2 * i), 0), unsplit(unit(2 * i + 1), 0)], axis=1) for i in range(2)], axis=0)
     g_kv[...] = jnp.transpose(rows_to(cols_to(kv, 384), 384))[: 2 * MEM, : 2 * MEM]
-    for i, at in ((1, 1056), (2, 1584)):
-        x = panels(a, at, PAD, 3)[:MEM]
-        g_tall[i] = jnp.concatenate([x[:, :MEM], x[:, PAD : PAD + MEM]], axis=1)
-    both = unsplit(panels(a, 2112, PAD, 3), 0)
+    for i in (1, 2):
+        g_tall[i] = jnp.concatenate([unit(2 + 2 * i)[:MEM], unit(3 + 2 * i)[:MEM]], axis=1)
     sum_dq = unsplit(jnp.transpose(rows_to(vecs, 128))[:PAD, 15:16], 0)
     fetches[5].wait()
     fetches[3].wait()
     phase = vec[1:2, :]
     phase_low = jnp.cos(phase).astype(BF).astype(F32)
-    g_tall[0] = jnp.concatenate([both[:, :MEM], sum_dq * phase_low], axis=1)
-    g_sq[0] = both[:, PAD : PAD + MEM]
-    last = panels(a, 2640, PAD, 3)[:MEM]
-    g_sq[1] = last[:, :MEM]
+    g_tall[0] = jnp.concatenate([unsplit(unit(8), 0), sum_dq * phase_low], axis=1)
+    g_sq[0] = unsplit(unit(9), 0)
+    g_sq[1] = unit(10)[:MEM]
     shared = jnp.transpose(rows_to(cols_to(g_gin[0 : 2 * MEM, 0:MEM], 256), 384))[:MEM, : 2 * MEM]
-    g_hid[...] = jnp.concatenate([shared, last[:, PAD : PAD + MEM]], axis=1)
+    g_hid[...] = jnp.concatenate([shared, unit(11)[:MEM]], axis=1)
     query_low = tall[0][:, MEM:].astype(BF).astype(F32)
     phase_in = jnp.sum(query_low * sum_dq, axis=0, keepdims=True)
     row = lambda i: vecs[i : i + 1, :MEM]
@@ -863,7 +874,7 @@
     norm = jnp.sqrt(total)
     factor = jnp.minimum(1.0, CLIP_AT / (norm + NORM_EPS))
     norm_out[...] = norm
-    loss_out[...] = jnp.sum(a[3168:3169, :], keepdims=True)
+    loss_out[...] = jnp.sum(a[VECTORS : VECTORS + 1, :], keepdims=True)
     for i, grad in enumerate((g_gin, g_hid, g_kv, g_tall, g_sq, g_vec)):
         rate, decay = (VECTOR_RATE, 0.0) if i == 5 else (LEARN_RATE, DECAY)
         new = param, one, two = state[i], state[6 + i], state[12 + i]
@@ -909,7 +920,7 @@
         out_shape=outs,
         in_specs=[pl.BlockSpec(memory_space=pltpu.SMEM)] + [vm] * (2 * count) + [far] * 18,
         out_specs=[far] * 18 + [vm] * 2,
-        scratch_shapes=[pltpu.VMEM((3200, 128), F32), pltpu.VMEM((3200, 128), F32)] + [pltpu.VMEM(s, F32) for s in shapes]
+        scratch_shapes=[pltpu.VMEM((ROWS, 128), F32)] * 2 + [pltpu.VMEM(s, F32) for s in shapes]
         + [pltpu.VMEM(x.shape, F32) for x in state] + [pltpu.SemaphoreType.DMA((18,))] * 2,
         compiler_params=params(), name="adam", cost_estimate=cost(14),
     )(where, *mine, *other, *state)

time: 201 us -> 192 us (0.955)
  Pallas kernels: 135 us -> 123 us
  waiting for transfers between devices: 20.1 us -> 24.6 us
    pallas_call x1, Pallas kernels: 20.7 us -> 15 us  [lay(): pl.pallas_call(lambda *r: lay_kernel(cap, count, *r), out_shape=[table, t...]
    pallas_call x1, Pallas kernels: 32.4 us -> 27.7 us  [main(): pl.pallas_call(lambda *r: main_kernel(scale, *r), out_shape=[jax.ShapeDty...]
    ppermute x31, waiting for transfers between devices: 20.1 us -> 24.6 us  [send(): return lax.ppermute(x, AXES, pairs)]
  transfers between devices with their start and end apart: 31 -> 31, of which waited for: 9 -> 12; matrix products, arithmetic and copies ran while one was open for 2% -> 1% of each run, Pallas kernels for 55% -> 52%
where the time goes in v5:
time: 192 us; the launch traced here: 191 us
  Pallas kernels  123 us (64%)
  starting transfers between devices  34.7 us (18%)
  waiting for transfers between devices  24.6 us (13%)
  other arithmetic  4.13 us (2%)
  local copies, waits for them, and re-layouts  3.06 us (2%)
    ppermute x31, starting transfers between devices, send(): return lax.ppermute(x, AXES, pairs)  34.7 us
    pallas_call x1, Pallas kernels, main(): pl.pallas_call(lambda *r: main_kernel(scale, *r), out_shape=[jax.ShapeDty...  27.7 us
    ppermute x31, waiting for transfers between devices, send(): return lax.ppermute(x, AXES, pairs)  24.6 us
    pallas_call x1, Pallas kernels, merge(): pl.pallas_call(lambda *r: merge_kernel(cap, *r), out_shape=[jax.ShapeDtyp...  20.5 us
    pallas_call x1, Pallas kernels, gather_near(): pl.pallas_call(lambda *r: near_kernel(chunk, *r), out_shape=jax.ShapeDtyp...  19.1 us
    pallas_call x1, Pallas kernels, lay(): pl.pallas_call(lambda *r: lay_kernel(cap, count, *r), out_shape=[table, t...  15 us
    pallas_call x1, Pallas kernels, gru(): pl.pallas_call(lambda *r: gru_kernel(scale, cap, rounds, nodes, *r), out_...  10.7 us
    pallas_call x1, Pallas kernels, adam(): pl.pallas_call(lambda *r: adam_kernel(parts, *r), out_shape=outs, in_spec...  10.7 us
  transfers between devices with their start and end apart: 31, of which 12 were waited for; matrix products, arithmetic and copies ran while one was open for 1% of the time, Pallas kernels for 52%

profile of v5, /device:TPU:0, one launch (start us, length us, event | category | flops | bytes accessed | tf_op | source)
XLA Modules:
  0.0 191.0 jit_solution(9297944716625286746)
XLA Ops:
  0.7 2.8 %latest.1 = f32[65,128]{1,0:T(8,128)} custom-call(s32[4,128]{1,0:T(4,128)} %bitcast.106, s32[4,128]{1,0:T(4,128)} %bitcast.108, s32[4,128]{1,0:T(4,128)} %bitcast.111, f32[4,128]{1,0:T(4,128)} %bitcast.114), custom_call_target="tpu_custom_call" | custom-call | flops 2000000000 | bytes 6000000 | tf_op jit(solution)/shard_map/latest/pallas_call | solution.py:171
  5.9 2.9 %collective-permute-start.9 = (f32[65,128]{1,0:T(8,128)S(1)}, f32[65,128]{1,0:T(8,128)S(1)}, u32[]{:S(2)}, u32[]{:S(2)}) collective-permute-start(f32[65,128]{1,0:T(8,128)S(1)} %add_select_fusion.2), channel_id=1, source_target_pairs={{0,4},{1,5},{2,6},{3,7},{4,0},{5,1},{6,2},{7,3},{8,12},{9,13},{10,... | collective-permute-start | bytes 99848 | tf_op jit(solution)/shard_map/ppermute | solution.py:954
  10.3 8.2 %table.1 = (f32[8192,128]{1,0:T(8,128)}, f32[8192,128]{1,0:T(8,128)}, bf16[1024,256]{1,0:T(8,128)(2,1)}) custom-call(s32[512]{0:T(512)} %r_0_.1, s32[512]{0:T(512)} %r_1_.1, f32[172,8192]{1,0:T(8,128)} %bitcast.82, s32[1,8192]{1,0:T(1,128)} %bitcast.105), custom_call_target="tpu_custom_call" | custom-call | flops 8999999488 | bytes 27000000 | tf_op jit(solution)/shard_map/table/pallas_call | solution.py:237
  18.6 3.1 %collective-permute-start.12 = (f32[65,128]{1,0:T(8,128)S(1)}, f32[65,128]{1,0:T(8,128)S(1)}, u32[]{:S(2)}, u32[]{:S(2)}) collective-permute-start(f32[65,128]{1,0:T(8,128)S(1)} %add_select_fusion.1), channel_id=1, source_target_pairs={{0,16},{1,17},{2,18},{3,19},{4,20},{5,21},{6,22},{7,23},{8,24},{9,... | collective-permute-start | bytes 99848 | tf_op jit(solution)/shard_map/ppermute | solution.py:954
  23.3 3.8 %gate_weights.1 = (bf16[528,704]{1,0:T(8,128)(2,1)}, bf16[528,176]{1,0:T(8,128)(2,1)}, f32[15,176,128]{2,1,0:T(8,128)}) custom-call(f32[516,688]{1,0:T(8,128)} %bitcast.84, f32[172,516]{1,0:T(8,128)} %r_10_.1, f32[15,172]{1,0:T(8,128)} %r_14_.1), custom_call_target="tpu_custom_call" | custom-call | flops 4000000000 | bytes 12000000 | tf_op jit(solution)/shard_map/gate_weights/pallas_call | solution.py:94
  28.4 10.7 %gru.1 = (bf16[704,1024]{1,0:T(8,128)(2,1)}, f32[5,176,1024]{2,1,0:T(8,128)}, f32[176,1024]{1,0:T(8,128)}, f32[8,1024]{1,0:T(8,128)}, f32[4,440,128]{2,1,0:T(8,128)S(1)}) custom-call(s32[512]{0:T(512)} %r_0_.1, s32[512]{0:T(512)} %r_1_.1, s32[512]{0:T(512)} %r_2_.1, s32[8192]{0:T(1024)} %fusion.r_3_, bf16[1024,256]{1,0:T(8,128)(2,1)} %get-tuple-element.140.r_4_, ...), custom_call_target="tpu_custom_call" | custom-call | flops 10000000000 | bytes 30000000 | tf_op jit(solution)/shard_map/gru/pallas_call | solution.py:418
  39.1 3.0 %collective-permute-start.16 = (f32[440,128]{1,0:T(8,128)S(1)}, f32[440,128]{1,0:T(8,128)S(1)}, u32[]{:S(2)}, u32[]{:S(2)}) collective-permute-start(f32[440,128]{1,0:T(8,128)S(1)} %slice_bitcast_fusion), channel_id=1, source_target_pairs={{0,24},{1,25},{2,26},{3,27},{4,28},{5,29},{6,30},{7,31},{8,16},{9,... | collective-permute-start | bytes 675848 | tf_op jit(solution)/shard_map/ppermute | solution.py:954
  43.6 19.1 %near.1 = bf16[10240,256]{1,0:T(8,128)(2,1)} custom-call(s32[10240]{0:T(1024)} %bitcast.104, f32[8192,128]{1,0:T(8,128)} %get-tuple-element.148.r_1_, f32[8192,128]{1,0:T(8,128)} %get-tuple-element.149.r_2_), custom_call_target="tpu_custom_call" | custom-call | flops 16000000000 | bytes 48000000 | tf_op jit(solution)/shard_map/near/pallas_call | solution.py:264
  63.3 2.5 %collective-permute-start.19 = (f32[1760,128]{1,0:T(8,128)S(1)}, f32[1760,128]{1,0:T(8,128)S(1)}, u32[]{:S(2)}, u32[]{:S(2)}) collective-permute-start(f32[1760,128]{1,0:T(8,128)S(1)} %pad_maximum_fusion.1), channel_id=1, source_target_pairs={{0,6},{1,7},{2,4},{3,5},{4,2},{5,3},{6,0},{7,1},{8,14},{9,15},{10,... | collective-permute-start | bytes 2703368 | tf_op jit(solution)/shard_map/ppermute | solution.py:954
  66.8 4.4 %main_weights.1 = (bf16[176,528]{1,0:T(8,128)(2,1)}, bf16[352,256]{1,0:T(8,128)(2,1)}, bf16[352,176]{1,0:T(8,128)(2,1)}, bf16[176,352]{1,0:T(8,128)(2,1)}, bf16[...) custom-call(f32[516,688]{1,0:T(8,128)} %bitcast.85, ...), custom_call_target="tpu_custom_call" | custom-call | flops 5000000000 | bytes 15000000 | tf_op jit(solution)/shard_map/main_weights/pallas_call | solution.py:135
  71.3 27.7 %main.1 = (f32[2944,128]{1,0:T(8,128)}, f32[2944,128]{1,0:T(8,128)}) custom-call(s32[1]{0:T(128)} %bitcast.6.r_0_, bf16[10,1024,256]{2,1,0:T(8,128)(2,1)} %bitcast.117, s32[10,1024]{1,0:T(8,128)} %reshape.139.r_2_, s32[1,512]{1,0:T(1,128)} %bitcast.113, bf16[704,1024]{1,0:T(8,128)(2,1)} %get-tuple-element.151.r_4_, f32[5,176,1024]{2,1,0:T(8,128)} %get-tuple-element.152.r_5_, ...), custom_call_target="tpu_custom_call" | custom-call | flops 35000000512 | bytes 105000000 | tf_op jit(solution)/shard_map/main/pallas_call | solution.py:652
  98.9 4.4 %collective-permute-done.18 = f32[1760,128]{1,0:T(8,128)S(1)} collective-permute-done((f32[1760,128]{1,0:T(8,128)S(1)}, f32[1760,128]{1,0:T(8,128)S(1)}, u32[]{:S(2)}, u32[]{:S(2)}) %collective-permute-start.18) | collective-permute-done | bytes 901152 | tf_op jit(solution)/shard_map/ppermute | solution.py:954
  104.6 3.5 %collective-permute-done.20 = f32[2944,128]{1,0:T(8,128)S(1)} collective-permute-done((f32[2944,128]{1,0:T(8,128)}, f32[2944,128]{1,0:T(8,128)S(1)}, u32[]{:S(2)}, u32[]{:S(2)}) %collective-permute-start.20) | collective-permute-done | bytes 1507360 | tf_op jit(solution)/shard_map/ppermute | solution.py:954
  109.7 1.8 collective-permute-start.23
  113.3 15.0 %lay.2 = (f32[8200,128]{1,0:T(8,128)}, f32[8200,128]{1,0:T(8,128)}, s32[1]{0:T(128)}, f32[16,440,128]{2,1,0:T(8,128)}) custom-call(f32[4,440,128]{2,1,0:T(8,128)} %bitcast.80, f32[4,440,128]{2,1,0:T(8,128)} %bitcast.91, f32[4,440,128]{2,1,0:T(8,128)} %bitcast.90, f32[4,440,128]{2,1,0:T(8,128)} %bitcast.89), custom_call_target="tpu_custom_call" | custom-call | flops 14000000000 | bytes 42000000 | tf_op jit(solution)/shard_map/lay/pallas_call | solution.py:735
  129.8 2.7 %collective-permute-start.26 = (f32[184,128]{1,0:T(8,128)S(1)}, f32[184,128]{1,0:T(8,128)S(1)}, u32[]{:S(2)}, u32[]{:S(2)}) collective-permute-start(f32[184,128]{1,0:T(8,128)S(1)} %get-tuple-element.244), channel_id=1, source_target_pairs={{0,24},{1,25},{2,26},{3,27},{4,28},{5,29},{6,30},{7,31},{8,16},{9,... | collective-permute-start | bytes 282632 | tf_op jit(solution)/shard_map/ppermute | solution.py:954
  132.5 1.8 collective-permute-start.24
  134.3 3.0 %collective-permute-done.26 = f32[184,128]{1,0:T(8,128)S(1)} collective-permute-done((f32[184,128]{1,0:T(8,128)S(1)}, f32[184,128]{1,0:T(8,128)S(1)}, u32[]{:S(2)}, u32[]{:S(2)}) %collective-permute-start.26) | collective-permute-done | bytes 94240 | tf_op jit(solution)/shard_map/ppermute | solution.py:954
  137.3 3.8 %collective-permute-done.25 = f32[184,128]{1,0:T(8,128)S(1)} collective-permute-done((f32[184,128]{1,0:T(8,128)S(1)}, f32[184,128]{1,0:T(8,128)S(1)}, u32[]{:S(2)}, u32[]{:S(2)}) %collective-permute-start.25) | collective-permute-done | bytes 94240 | tf_op jit(solution)/shard_map/ppermute | solution.py:954
  141.8 2.5 %collective-permute-start.29 = (f32[184,128]{1,0:T(8,128)S(1)}, f32[184,128]{1,0:T(8,128)S(1)}, u32[]{:S(2)}, u32[]{:S(2)}) collective-permute-start(f32[184,128]{1,0:T(8,128)S(1)} %add_add_fusion), channel_id=1, source_target_pairs={{0,16},{1,17},{2,18},{3,19},{4,20},{5,21},{6,22},{7,23},{8,24},{9,... | collective-permute-start | bytes 282632 | tf_op jit(solution)/shard_map/ppermute | solution.py:954
  147.0 5.1 %collective-permute-done.29 = f32[184,128]{1,0:T(8,128)S(1)} collective-permute-done((f32[184,128]{1,0:T(8,128)S(1)}, f32[184,128]{1,0:T(8,128)S(1)}, u32[]{:S(2)}, u32[]{:S(2)}) %collective-permute-start.29) | collective-permute-done | bytes 94240 | tf_op jit(solution)/shard_map/ppermute | solution.py:954
  152.2 1.7 collective-permute-start.33
  155.8 20.5 %merge.2 = (f32[172,8192]{1,0:T(8,128)}, s32[1]{0:T(128)}) custom-call(f32[16,440,128]{2,1,0:T(8,128)} %collective-permute-done.27.r_0_, f32[8200,128]{1,0:T(8,128)} %get-tuple-element.201.r_1_, f32[8200,128]{1,0:T(8,128)} %get-tuple-element.202.r_2_, s32[1]{0:T(128)} %get-tuple-element.203.r_3_, f32[172,8192]{1,0:T(8,128)} %bitcast.83), custom_call_target="tpu_custom_call" | custom-call | flops 17999998976 | bytes 54000000 | tf_op jit(solution)/shard_map/merge/pallas_call | solution.py:776
  180.1 10.7 %adam.1 = (f32[516,688]{1,0:T(8,128)}, f32[172,516]{1,0:T(8,128)}, f32[344,344]{1,0:T(8,128)}, f32[3,172,344]{2,1,0:T(8,128)}, f32[172,2,172]{2,1,0:T(2,128)}, /...) custom-call(s32[2]{0:T(128)} %pad_add_fusion.r_0_, ...), custom_call_target="tpu_custom_call" | custom-call | flops 14000000000 | bytes 42000000 | tf_op jit(solution)/shard_map/adam/pallas_call | solution.py:918
  (87 shorter events, 24.6 us)
Async XLA Ops:
  5.9 12.7 %collective-permute-start.9 = (f32[65,128]{1,0:T(8,128)S(1)}, f32[65,128]{1,0:T(8,128)S(1)}, u32[]{:S(2)}, u32[]{:S(2)}) collective-permute-start(f32[65,128]{1,0:T(8,128)S(1)} %add_select_fusion.2), channel_id=1, source_target_pairs={{0,4},{1,5},{2,6},{3,7},{4,0},{5,1},{6,2},{7,3},{8,12},{9,13},{10,... | collective-permute-start | bytes 99848 | tf_op jit(solution)/shard_map/ppermute | solution.py:954
  8.8 9.7 %collective-permute-start.10 = (f32[65,128]{1,0:T(8,128)S(1)}, f32[65,128]{1,0:T(8,128)S(1)}, u32[]{:S(2)}, u32[]{:S(2)}) collective-permute-start(f32[65,128]{1,0:T(8,128)S(1)} %add_select_fusion.2), channel_id=1, source_target_pairs={{0,6},{1,7},{2,4},{3,5},{4,2},{5,3},{6,0},{7,1},{8,14},{9,15},{10,... | collective-permute-start | bytes 99848 | tf_op jit(solution)/shard_map/ppermute | solution.py:954
  10.2 8.3 %collective-permute-start.8 = (f32[65,128]{1,0:T(8,128)S(1)}, f32[65,128]{1,0:T(8,128)S(1)}, u32[]{:S(2)}, u32[]{:S(2)}) collective-permute-start(f32[65,128]{1,0:T(8,128)S(1)} %add_select_fusion.2), channel_id=1, source_target_pairs={{0,2},{1,3},{2,0},{3,1},{4,6},{5,7},{6,4},{7,5},{8,10},{9,11},{10,... | collective-permute-start | bytes 99848 | tf_op jit(solution)/shard_map/ppermute | solution.py:954
  18.6 9.1 %collective-permute-start.12 = (f32[65,128]{1,0:T(8,128)S(1)}, f32[65,128]{1,0:T(8,128)S(1)}, u32[]{:S(2)}, u32[]{:S(2)}) collective-permute-start(f32[65,128]{1,0:T(8,128)S(1)} %add_select_fusion.1), channel_id=1, source_target_pairs={{0,16},{1,17},{2,18},{3,19},{4,20},{5,21},{6,22},{7,23},{8,24},{9,... | collective-permute-start | bytes 99848 | tf_op jit(solution)/shard_map/ppermute | solution.py:954
  21.7 6.0 %collective-permute-start.13 = (f32[65,128]{1,0:T(8,128)S(1)}, f32[65,128]{1,0:T(8,128)S(1)}, u32[]{:S(2)}, u32[]{:S(2)}) collective-permute-start(f32[65,128]{1,0:T(8,128)S(1)} %add_select_fusion.1), channel_id=1, source_target_pairs={{0,24},{1,25},{2,26},{3,27},{4,28},{5,29},{6,30},{7,31},{8,16},{9,... | collective-permute-start | bytes 99848 | tf_op jit(solution)/shard_map/ppermute | solution.py:954
  39.1 24.0 %collective-permute-start.16 = (f32[440,128]{1,0:T(8,128)S(1)}, f32[440,128]{1,0:T(8,128)S(1)}, u32[]{:S(2)}, u32[]{:S(2)}) collective-permute-start(f32[440,128]{1,0:T(8,128)S(1)} %slice_bitcast_fusion), channel_id=1, source_target_pairs={{0,24},{1,25},{2,26},{3,27},{4,28},{5,29},{6,30},{7,31},{8,16},{9,... | collective-permute-start | bytes 675848 | tf_op jit(solution)/shard_map/ppermute | solution.py:954
  42.1 21.0 %collective-permute-start.15 = (f32[440,128]{1,0:T(8,128)S(1)}, f32[440,128]{1,0:T(8,128)S(1)}, u32[]{:S(2)}, u32[]{:S(2)}) collective-permute-start(f32[440,128]{1,0:T(8,128)S(1)} %slice_bitcast_fusion), channel_id=1, source_target_pairs={{0,16},{1,17},{2,18},{3,19},{4,20},{5,21},{6,22},{7,23},{8,24},{9,... | collective-permute-start | bytes 675848 | tf_op jit(solution)/shard_map/ppermute | solution.py:954
  42.5 20.7 %collective-permute-start.14 = (f32[440,128]{1,0:T(8,128)S(1)}, f32[440,128]{1,0:T(8,128)S(1)}, u32[]{:S(2)}, u32[]{:S(2)}) collective-permute-start(f32[440,128]{1,0:T(8,128)S(1)} %slice_bitcast_fusion), channel_id=1, source_target_pairs={{0,8},{1,9},{2,10},{3,11},{4,12},{5,13},{6,14},{7,15},{8,0},{9,1},... | collective-permute-start | bytes 675848 | tf_op jit(solution)/shard_map/ppermute | solution.py:954
  63.3 35.7 %collective-permute-start.19 = (f32[1760,128]{1,0:T(8,128)S(1)}, f32[1760,128]{1,0:T(8,128)S(1)}, u32[]{:S(2)}, u32[]{:S(2)}) collective-permute-start(f32[1760,128]{1,0:T(8,128)S(1)} %pad_maximum_fusion.1), channel_id=1, source_target_pairs={{0,6},{1,7},{2,4},{3,5},{4,2},{5,3},{6,0},{7,1},{8,14},{9,15},{10,... | collective-permute-start | bytes 2703368 | tf_op jit(solution)/shard_map/ppermute | solution.py:954
  65.8 37.6 %collective-permute-start.18 = (f32[1760,128]{1,0:T(8,128)S(1)}, f32[1760,128]{1,0:T(8,128)S(1)}, u32[]{:S(2)}, u32[]{:S(2)}) collective-permute-start(f32[1760,128]{1,0:T(8,128)S(1)} %pad_maximum_fusion.1), channel_id=1, source_target_pairs={{0,4},{1,5},{2,6},{3,7},{4,0},{5,1},{6,2},{7,3},{8,12},{9,13},{10,... | collective-permute-start | bytes 2703368 | tf_op jit(solution)/shard_map/ppermute | solution.py:954
  66.3 37.2 %collective-permute-start.17 = (f32[1760,128]{1,0:T(8,128)S(1)}, f32[1760,128]{1,0:T(8,128)S(1)}, u32[]{:S(2)}, u32[]{:S(2)}) collective-permute-start(f32[1760,128]{1,0:T(8,128)S(1)} %pad_maximum_fusion.1), channel_id=1, source_target_pairs={{0,2},{1,3},{2,0},{3,1},{4,6},{5,7},{6,4},{7,5},{8,10},{9,11},{10,... | collective-permute-start | bytes 2703368 | tf_op jit(solution)/shard_map/ppermute | solution.py:954
  109.7 18.5 %collective-permute-start.23 = (f32[736,128]{1,0:T(8,128)S(1)}, f32[736,128]{1,0:T(8,128)S(1)}, u32[]{:S(2)}, u32[]{:S(2)}) collective-permute-start(f32[736,128]{1,0:T(8,128)S(1)} %get-tuple-element.240), channel_id=1, source_target_pairs={{0,6},{1,7},{2,4},{3,5},{4,2},{5,3},{6,0},{7,1},{8,14},{9,15},{10,... | collective-permute-start | bytes 1130504 | tf_op jit(solution)/shard_map/ppermute | solution.py:954
  111.5 18.0 %collective-permute-start.22 = (f32[736,128]{1,0:T(8,128)S(1)}, f32[736,128]{1,0:T(8,128)S(1)}, u32[]{:S(2)}, u32[]{:S(2)}) collective-permute-start(f32[736,128]{1,0:T(8,128)S(1)} %get-tuple-element.241), channel_id=1, source_target_pairs={{0,4},{1,5},{2,6},{3,7},{4,0},{5,1},{6,2},{7,3},{8,12},{9,13},{10,... | collective-permute-start | bytes 1130504 | tf_op jit(solution)/shard_map/ppermute | solution.py:954
  112.7 16.9 %collective-permute-start.21 = (f32[736,128]{1,0:T(8,128)S(1)}, f32[736,128]{1,0:T(8,128)S(1)}, u32[]{:S(2)}, u32[]{:S(2)}) collective-permute-start(f32[736,128]{1,0:T(8,128)S(1)} %get-tuple-element.242), channel_id=1, source_target_pairs={{0,2},{1,3},{2,0},{3,1},{4,6},{5,7},{6,4},{7,5},{8,10},{9,11},{10,... | collective-permute-start | bytes 1130504 | tf_op jit(solution)/shard_map/ppermute | solution.py:954
  129.7 11.4 %collective-permute-start.27 = (f32[16,440,128]{2,1,0:T(8,128)}, f32[16,440,128]{2,1,0:T(8,128)}, u32[]{:S(2)}, u32[]{:S(2)}) collective-permute-start(f32[16,440,128]{2,1,0:T(8,128)} %get-tuple-element.193), channel_id=1, source_target_pairs={{0,1},{1,0},{2,3},{3,2},{4,5},{5,4},{6,7},{7,6},{8,9},{9,8},{10,11... | collective-permute-start | bytes 10813448 | tf_op jit(solution)/shard_map/ppermute | solution.py:954
  129.8 7.5 %collective-permute-start.26 = (f32[184,128]{1,0:T(8,128)S(1)}, f32[184,128]{1,0:T(8,128)S(1)}, u32[]{:S(2)}, u32[]{:S(2)}) collective-permute-start(f32[184,128]{1,0:T(8,128)S(1)} %get-tuple-element.244), channel_id=1, source_target_pairs={{0,24},{1,25},{2,26},{3,27},{4,28},{5,29},{6,30},{7,31},{8,16},{9,... | collective-permute-start | bytes 282632 | tf_op jit(solution)/shard_map/ppermute | solution.py:954
  132.5 8.6 %collective-permute-start.25 = (f32[184,128]{1,0:T(8,128)S(1)}, f32[184,128]{1,0:T(8,128)S(1)}, u32[]{:S(2)}, u32[]{:S(2)}) collective-permute-start(f32[184,128]{1,0:T(8,128)S(1)} %get-tuple-element.245), channel_id=1, source_target_pairs={{0,16},{1,17},{2,18},{3,19},{4,20},{5,21},{6,22},{7,23},{8,24},{9,... | collective-permute-start | bytes 282632 | tf_op jit(solution)/shard_map/ppermute | solution.py:954
  132.5 8.6 %collective-permute-start.24 = (f32[184,128]{1,0:T(8,128)S(1)}, f32[184,128]{1,0:T(8,128)S(1)}, u32[]{:S(2)}, u32[]{:S(2)}) collective-permute-start(f32[184,128]{1,0:T(8,128)S(1)} %get-tuple-element.246), channel_id=1, source_target_pairs={{0,8},{1,9},{2,10},{3,11},{4,12},{5,13},{6,14},{7,15},{8,0},{9,1},... | collective-permute-start | bytes 282632 | tf_op jit(solution)/shard_map/ppermute | solution.py:954
  141.1 5.9 %collective-permute-start.30 = (f32[184,128]{1,0:T(8,128)S(1)}, f32[184,128]{1,0:T(8,128)S(1)}, u32[]{:S(2)}, u32[]{:S(2)}) collective-permute-start(f32[184,128]{1,0:T(8,128)S(1)} %add_add_fusion), channel_id=1, source_target_pairs={{0,8},{1,9},{2,10},{3,11},{4,12},{5,13},{6,14},{7,15},{8,0},{9,1},... | collective-permute-start | bytes 282632 | tf_op jit(solution)/shard_map/ppermute | solution.py:954
  141.8 10.4 %collective-permute-start.29 = (f32[184,128]{1,0:T(8,128)S(1)}, f32[184,128]{1,0:T(8,128)S(1)}, u32[]{:S(2)}, u32[]{:S(2)}) collective-permute-start(f32[184,128]{1,0:T(8,128)S(1)} %add_add_fusion), channel_id=1, source_target_pairs={{0,16},{1,17},{2,18},{3,19},{4,20},{5,21},{6,22},{7,23},{8,24},{9,... | collective-permute-start | bytes 282632 | tf_op jit(solution)/shard_map/ppermute | solution.py:954
  144.2 7.9 %collective-permute-start.28 = (f32[184,128]{1,0:T(8,128)S(1)}, f32[184,128]{1,0:T(8,128)S(1)}, u32[]{:S(2)}, u32[]{:S(2)}) collective-permute-start(f32[184,128]{1,0:T(8,128)S(1)} %add_add_fusion), channel_id=1, source_target_pairs={{0,24},{1,25},{2,26},{3,27},{4,28},{5,29},{6,30},{7,31},{8,16},{9,... | collective-permute-start | bytes 282632 | tf_op jit(solution)/shard_map/ppermute | solution.py:954
  152.2 24.1 %collective-permute-start.33 = (f32[736,128]{1,0:T(8,128)S(1)}, f32[736,128]{1,0:T(8,128)S(1)}, u32[]{:S(2)}, u32[]{:S(2)}) collective-permute-start(f32[736,128]{1,0:T(8,128)S(1)} %pad_maximum_fusion.2.r_1_), channel_id=1, source_target_pairs={{0,6},{1,7},{2,4},{3,5},{4,2},{5,3},{6,0},{7,1},{8,14},{9,15},{10,... | collective-permute-start | bytes 1130504 | tf_op jit(solution)/shard_map/ppermute | solution.py:954
  153.9 22.4 %collective-permute-start.32 = (f32[736,128]{1,0:T(8,128)S(1)}, f32[736,128]{1,0:T(8,128)S(1)}, u32[]{:S(2)}, u32[]{:S(2)}) collective-permute-start(f32[736,128]{1,0:T(8,128)S(1)} %pad_maximum_fusion.2.r_1_), channel_id=1, source_target_pairs={{0,4},{1,5},{2,6},{3,7},{4,0},{5,1},{6,2},{7,3},{8,12},{9,13},{10,... | collective-permute-start | bytes 1130504 | tf_op jit(solution)/shard_map/ppermute | solution.py:954
  155.1 21.2 %collective-permute-start.31 = (f32[736,128]{1,0:T(8,128)S(1)}, f32[736,128]{1,0:T(8,128)S(1)}, u32[]{:S(2)}, u32[]{:S(2)}) collective-permute-start(f32[736,128]{1,0:T(8,128)S(1)} %pad_maximum_fusion.2.r_1_), channel_id=1, source_target_pairs={{0,2},{1,3},{2,0},{3,1},{4,6},{5,7},{6,4},{7,5},{8,10},{9,11},{10,... | collective-permute-start | bytes 1130504 | tf_op jit(solution)/shard_map/ppermute | solution.py:954
  (18 other events, 75.6 us)

commit v6 on v5

--- a/solution.py
+++ b/solution.py
@@ -69,7 +69,17 @@
     return nt(eye(x.shape[1]), x.astype(BF))
 
 
-def gate_weights_kernel(gin, ghid, vec, wg, wh, vb):
+def wide_vectors(vec, vb):
+    cols = jnp.transpose(cols_to(rows_to(vec[...], 128), 256))
+    for i in range(15):
+        column = cols[:, i : i + 1]
+        if i in (8, 9):
+            column = split_rows(column[:MEM])
+        wide = jnp.broadcast_to(column[:PAD], (PAD, 128))
+        vb[i] = wide * (0.5 / math.pi) if i < 2 else wide
+
+
+def gate_weights(gin, ghid, vec, wg, wh, vb):
     full = gin[...]
     for gate in range(3):
         rows = full[gate * MEM : (gate + 1) * MEM]
@@ -79,24 +89,10 @@
     for gate in range(3):
         part = cols_to(rows_to(hid[:, gate * MEM : (gate + 1) * MEM], PAD), 256)
         wh[pl.ds(gate * PAD, PAD), :] = turned(part)[:PAD].astype(BF)
-    cols = jnp.transpose(cols_to(rows_to(vec[...], 128), 256))
-    for i in range(15):
-        column = cols[:, i : i + 1]
-        if i in (8, 9):
-            column = split_rows(column[:MEM])
-        wide = jnp.broadcast_to(column[:PAD], (PAD, 128))
-        vb[i] = wide * (0.5 / math.pi) if i < 2 else wide
-
-
-def gate_weights(gin, ghid, vec):
-    outs = [jax.ShapeDtypeStruct((528, 704), BF), jax.ShapeDtypeStruct((528, 176), BF),
-            jax.ShapeDtypeStruct((15, PAD, 128), F32)]
-    return pl.pallas_call(
-        gate_weights_kernel, out_shape=outs, compiler_params=params(), name="gate_weights", cost_estimate=cost(4),
-    )(gin.T, ghid, vec)
-
-
-def main_weights_kernel(gin, kv, tall, sq, vec, wgc, kvm, kvct, kvc, t0t, t0, t1t, t1, t2t, t2, s0t, s0, s1t, s1, steady):
+    wide_vectors(vec, vb)
+
+
+def main_weights_kernel(gin, kv, tall, sq, vec, wgc, kvm, kvct, kvc, t0t, t0, t1t, t1, t2t, t2, s0t, s0, s1t, s1, steady, vb):
     for gate in range(3):
         code = cols_to(rows_to(gin[gate * MEM : (gate + 1) * MEM, 2 * MEM : 3 * MEM], PAD), 256)
         wgc[:, gate * PAD : (gate + 1) * PAD] = turned(code)[:PAD].astype(BF)
@@ -125,13 +121,15 @@
     row_id = lax.broadcasted_iota(I32, (PAD, 128), 0)
     wide_phase = jnp.where(row_id < MEM, jnp.broadcast_to(phase_low, (PAD, 128)), 0.0).astype(BF)
     steady[...] = nn(cols_to(split_rows(query[:, MEM:]), PAD).astype(BF), wide_phase)
+    wide_vectors(vec, vb)
 
 
 def main_weights(gin, kv, tall, sq, vec):
     bf = lambda *s: jax.ShapeDtypeStruct(s, BF)
     outs = [bf(176, 528), bf(352, 256), bf(352, 176), bf(176, 352),
             bf(176, 176), bf(176, 176), bf(176, 352), bf(352, 176), bf(176, 352), bf(352, 176),
-            bf(176, 176), bf(176, 176), bf(176, 176), bf(176, 176), jax.ShapeDtypeStruct((PAD, 128), F32)]
+            bf(176, 176), bf(176, 176), bf(176, 176), bf(176, 176), jax.ShapeDtypeStruct((PAD, 128), F32),
+            jax.ShapeDtypeStruct((15, PAD, 128), F32)]
     return pl.pallas_call(
         main_weights_kernel, out_shape=outs, compiler_params=params(), name="main_weights", cost_estimate=cost(5),
     )(gin.T, kv, jnp.transpose(tall, (0, 2, 1)), jnp.transpose(sq, (1, 0, 2)), vec)
@@ -321,9 +319,21 @@
     return jnp.broadcast_to(x, (rows, x.shape[1]))
 
 
-def gru_kernel(scale, cap, rounds, nodes, sources, targets, ticks_at, latest, own, source, target, ticks, edge, types, wg, wh, vb,
-               msg, keep, ren, gap_out, packed, left, right, first, second):
+SECOND = 48
+
+
+def round_height(cap):
+    return cap + SECOND * (cap // 128) + cap % 128 // 2 + 8
+
+
+def gru_kernel(scale, own, source, target, ticks, edge, types, gin, ghid, vec,
+               msg, keep, ren, gap_out, left, right, wg, wh, vb):
     step = pl.program_id(0)
+
+    @pl.when(step == 0)
+    def _():
+        gate_weights(gin, ghid, vec, wg, wh, vb)
+
     own_t = nt(eye(256), own[...])
     seen = own_t[PAD : PAD + 1] + 128.0 * own_t[PAD + 1 : PAD + 2] + 16384.0 * own_t[PAD + 2 : PAD + 3]
     gap = (both(ticks[...].astype(F32)) - seen) * scale
@@ -362,72 +372,83 @@
     numbers = mix(source[...], target[...]).astype(F32)
     low = jnp.concatenate([ren[128:MEM, :], numbers, zeros(255 - MEM, BLOCK)], axis=0)
     for role in range(2 * TILES):
-        at = pl.multiple_of(step * BLOCK + 128 * role, 128)
-        left[pl.ds(at, 128), :] = jnp.transpose(ren[0:128, 128 * role : 128 * role + 128])
-        right[pl.ds(at, 128), :] = jnp.transpose(low[:, 128 * role : 128 * role + 128])
-
-    @pl.when(step == pl.num_programs(0) - 1)
-    def _():
-        pack_rows(cap, rounds, nodes, sources, targets, ticks_at, latest, left, right, packed, first, second)
+        left[128 * role : 128 * role + 128, :] = jnp.transpose(ren[0:128, 128 * role : 128 * role + 128])
+        right[128 * role : 128 * role + 128, :] = jnp.transpose(low[:, 128 * role : 128 * role + 128])
 
 
 def pack_rows(cap, rounds, nodes, sources, targets, ticks, latest, left, right, out, first, second):
     def chunk(b, count):
-        for role, ids in enumerate((sources, targets)):
-            def some(g, count):
-                for v in range(32):
-                    e = b * 128 + g * 32 + v
-                    i = b * 256 + role * 128 + g * 32 + v
-                    won = latest[ids[e]] == 2 * ticks[e] + role
-                    first[pl.ds(count, 1), :] = left[pl.ds(i, 1), :]
-                    second[pl.ds(count, 1), :] = right[pl.ds(i, 1), :]
-                    count = count + won.astype(I32)
-                return count
-
-            count = lax.fori_loop(0, 4, some, count)
-        return count
+        def some(g, count):
+            for v in range(16):
+                e = b * 128 + g * 16 + v
+                i = b * 256 + g * 16 + v
+                order = 2 * ticks[e]
+                for role, ids in enumerate((sources, targets)):
+                    first[pl.ds(count, 1), :] = left[pl.ds(i + 128 * role, 1), :]
+                    second[pl.ds(count, 1), :] = right[pl.ds(i + 128 * role, 1), :]
+                    count = count + (latest[ids[e]] == order + role).astype(I32)
+            return count
+
+        return lax.fori_loop(0, 8, some, count)
 
     count = lax.fori_loop(0, sources.shape[0] // 128, chunk, jnp.int32(0))
-    tail = cap // 2
+    tiles = cap // 128
+    rest = cap - 128 * tiles
     lane = lax.broadcasted_iota(I32, (1, 128), 1)
     for r in range(rounds):
         at = r * cap
         out[r, 0:cap, :] = first[at : at + cap, :]
-        out[r, cap : cap + tail, :] = jnp.concatenate(
-            [second[at : at + tail, 0:64], second[at + tail : at + cap, 0:64]], axis=1)
         here = jnp.clip(count - at, 0, cap)
         lines = []
         for q in range(-(-cap // 128)):
-            numbers = jnp.transpose(second[at + 128 * q : at + 128 * q + 128, :])[MEM - 128 : MEM - 127]
-            lines.append(jnp.where(lane + 128 * q < here, numbers, float(nodes)))
+            columns = jnp.transpose(second[at + 128 * q : at + 128 * q + 128, :])
+            if q < tiles:
+                out[r, cap + SECOND * q : cap + SECOND * q + SECOND, :] = columns[0:SECOND]
+            lines.append(jnp.where(lane + 128 * q < here, columns[MEM - 128 : MEM - 127], float(nodes)))
+        line, base = cap + SECOND * tiles, at + 128 * tiles
+        if rest:
+            out[r, line : line + rest // 2, :] = jnp.concatenate(
+                [second[base : base + rest // 2, 0:64], second[base + rest // 2 : base + rest, 0:64]], axis=1)
         lines.append(jnp.full((1, 128), here, I32).astype(F32))
         lines += [zeros(1, 128)] * (8 - len(lines))
-        out[r, cap + tail :, :] = jnp.concatenate(lines, axis=0)
-
-
-def gru(scale, cap, sources, targets, ticks, latest, own, edge_t, types, wg, wh, vb):
-    ends, nodes = own.shape[0], latest.shape[0]
-    blocks = ends // BLOCK
+        out[r, line + rest // 2 :, :] = jnp.concatenate(lines, axis=0)
+
+
+def pack(cap, sources, targets, ticks, latest, left, right):
+    ends, nodes = left.shape[0], latest.shape[0]
     rounds = ends // cap + 1
     spare = rounds * cap + 128
+    smem, vm = pl.BlockSpec(memory_space=pltpu.SMEM), pl.BlockSpec(memory_space=pltpu.VMEM)
+    return pl.pallas_call(
+        lambda *r: pack_rows(cap, rounds, nodes, *r),
+        out_shape=jax.ShapeDtypeStruct((rounds, round_height(cap), 128), F32),
+        in_specs=[smem] * 4 + [vm, vm], out_specs=vm,
+        scratch_shapes=[pltpu.VMEM((spare, 128), F32), pltpu.VMEM((spare, 128), F32)],
+        compiler_params=params(), name="pack", cost_estimate=cost(5),
+    )(sources, targets, ticks, latest, left, right)
+
+
+def gru(scale, sources, targets, ticks, own, edge_t, types, gin, ghid, vec):
+    ends = own.shape[0]
+    blocks = ends // BLOCK
     whole = lambda a: pl.BlockSpec(a.shape, lambda i: (0,) * len(a.shape))
     lanes = lambda: pl.BlockSpec((1, BLOCK // 2), lambda i: (0, i))
-    smem = pl.BlockSpec(memory_space=pltpu.SMEM)
     row = lambda x: x.reshape(1, -1)
-    packed = jax.ShapeDtypeStruct((rounds, cap + cap // 2 + 8, 128), F32)
+    gin = gin.T
+    half = jax.ShapeDtypeStruct((ends, 128), F32)
     return pl.pallas_call(
-        lambda *r: gru_kernel(scale, cap, rounds, nodes, *r),
+        lambda *r: gru_kernel(scale, *r),
         out_shape=[jax.ShapeDtypeStruct((4 * PAD, ends), BF), jax.ShapeDtypeStruct((5, PAD, ends), F32),
-                   jax.ShapeDtypeStruct((PAD, ends), F32), jax.ShapeDtypeStruct((8, ends), F32), packed],
+                   jax.ShapeDtypeStruct((PAD, ends), F32), jax.ShapeDtypeStruct((8, ends), F32), half, half],
         grid=(blocks,),
-        in_specs=[smem] * 4 + [pl.BlockSpec((BLOCK, 256), lambda i: (i, 0)), lanes(), lanes(), lanes(),
-                  pl.BlockSpec((MEM, BLOCK // 2), lambda i: (0, i)), lanes(), whole(wg), whole(wh), whole(vb)],
+        in_specs=[pl.BlockSpec((BLOCK, 256), lambda i: (i, 0)), lanes(), lanes(), lanes(),
+                  pl.BlockSpec((MEM, BLOCK // 2), lambda i: (0, i)), lanes(), whole(gin), whole(ghid), whole(vec)],
         out_specs=[pl.BlockSpec((4 * PAD, BLOCK), lambda i: (0, i)), pl.BlockSpec((5, PAD, BLOCK), lambda i: (0, 0, i)),
-                   pl.BlockSpec((PAD, BLOCK), lambda i: (0, i)), pl.BlockSpec((8, BLOCK), lambda i: (0, i)), whole(packed)],
-        scratch_shapes=[pltpu.VMEM((ends, 128), F32), pltpu.VMEM((ends, 128), F32),
-                        pltpu.VMEM((spare, 128), F32), pltpu.VMEM((spare, 128), F32)],
-        compiler_params=params(), name="gru", cost_estimate=cost(10),
-    )(sources, targets, ticks, latest, own, row(sources), row(targets), row(ticks), edge_t, types, wg, wh, vb)
+                   pl.BlockSpec((PAD, BLOCK), lambda i: (0, i)), pl.BlockSpec((8, BLOCK), lambda i: (0, i)),
+                   pl.BlockSpec((BLOCK, 128), lambda i: (i, 0)), pl.BlockSpec((BLOCK, 128), lambda i: (i, 0))],
+        scratch_shapes=[pltpu.VMEM((528, 704), BF), pltpu.VMEM((528, 176), BF), pltpu.VMEM((15, PAD, 128), F32)],
+        compiler_params=params(), name="gru", cost_estimate=cost(8),
+    )(own, row(sources), row(targets), row(ticks), edge_t, types, gin, ghid, vec)
 
 
 UNROLL = 10
@@ -682,19 +703,24 @@
 
 
 def fetch_numbers(cap, rows, whole, numbers, sem):
-    whole[...] = rows[:, cap + cap // 2 :, :].astype(I32)
+    whole[...] = rows[:, round_height(cap) - 8 :, :].astype(I32)
     copy = pltpu.make_async_copy(whole, numbers, sem)
     copy.start()
     return copy
 
 
 def lay_rows(cap, rows, numbers, left, right, second):
-    tail = cap // 2
+    tiles = cap // 128
+    line, tail = cap + SECOND * tiles, cap % 128 // 2
 
     def block(q, most):
-        half = rows[q, cap : cap + tail, :]
-        second[0:tail, :] = half
-        second[tail:cap, :] = jnp.concatenate([half[:, 64:], half[:, :64]], axis=1)
+        for t in range(tiles):
+            columns = rows[q, cap + SECOND * t : cap + SECOND * t + SECOND, :]
+            second[128 * t : 128 * t + 128, :] = jnp.transpose(rows_to(columns, 128))
+        if tail:
+            half = rows[q, line : line + tail, :]
+            second[128 * tiles : 128 * tiles + tail, :] = half
+            second[128 * tiles + tail : cap, :] = jnp.concatenate([half[:, 64:], half[:, :64]], axis=1)
         here = numbers[q, -(-cap // 128), 0]
 
         def some(g, carry):
@@ -742,16 +768,18 @@
     )(*arrays)
 
 
-def merge_kernel(cap, rows, far_left, far_right, before, mem, out, full, left, right, second, sems, whole, numbers):
+def merge_kernel(cap, far_rows, far_left, far_right, before, mem, out, full, left, right, second, sems, rows, whole, numbers):
     step = pl.program_id(0)
 
     @pl.when(step == 0)
     def _():
-        copies = [pltpu.make_async_copy(far_left, left, sems.at[0]), pltpu.make_async_copy(far_right, right, sems.at[1])]
+        copies = [pltpu.make_async_copy(far, near, sems.at[i])
+                  for i, (far, near) in enumerate(((far_rows, rows), (far_left, left), (far_right, right)))]
         for copy in copies:
             copy.start()
-        copies.append(fetch_numbers(cap, rows, whole, numbers, sems.at[2]))
-        for copy in copies:
+        copies[0].wait()
+        copies.append(fetch_numbers(cap, rows, whole, numbers, sems.at[3]))
+        for copy in copies[1:]:
             copy.wait()
         most = lay_rows(cap, rows, numbers, left, right, second)
         full[0] = (jnp.maximum(most, before[0]) == cap).astype(I32)
@@ -762,7 +790,7 @@
         at = base + 256 * c
         s = slice(256 * c, 256 * c + 256)
         top = turned_exactly(left[pl.ds(at, 256), :])
-        low = turned_exactly(right[pl.ds(at, 256), :])
+        low = turned_exactly(right[pl.ds(at, 256), :][:, :64])
         fresh = low[MEM - 128 : MEM - 127] >= 0.0
         out[0:128, s] = jnp.where(fresh, top, mem[0:128, s])
         out[128:MEM, s] = jnp.where(fresh, low[: MEM - 128], mem[128:MEM, s])
@@ -777,10 +805,11 @@
         lambda *r: merge_kernel(cap, *r),
         out_shape=[jax.ShapeDtypeStruct((MEM, nodes), F32), jax.ShapeDtypeStruct((1,), I32)],
         grid=(nodes // cols,),
-        in_specs=[pl.BlockSpec(rows.shape, lambda i: (0, 0, 0)), far, far, smem, part],
+        in_specs=[far, far, far, smem, part],
         out_specs=[part, smem],
         scratch_shapes=[pltpu.VMEM((nodes + 8, 128), F32), pltpu.VMEM((nodes + 8, 128), F32), pltpu.VMEM((cap, 128), F32),
-                        pltpu.SemaphoreType.DMA((3,))] + [kind((rows.shape[0], 8, 128), I32) for kind in (pltpu.VMEM, pltpu.SMEM)],
+                        pltpu.SemaphoreType.DMA((4,)), pltpu.VMEM(rows.shape, F32)]
+        + [kind((rows.shape[0], 8, 128), I32) for kind in (pltpu.VMEM, pltpu.SMEM)],
         compiler_params=params(), name="merge", cost_estimate=cost(18),
     )(rows, *laid, mem_t)
     return new, full[0] > 0
@@ -987,12 +1016,14 @@
     return jnp.concatenate(lines, axis=0)
 
 
-def spread_latest(x, d):
-    nodes = lax.broadcasted_iota(I32, x.shape, 0) < x.shape[0] - 1
-    join = lambda p, q: jnp.where(nodes, jnp.maximum(p, q), p + q)
-    x = join(x, send(x, twin()))
-    for stride, n in levels(lax.axis_size("dp")):
-        x = tree(gather_level(x, d, stride, n), join)
+def join_latest(p, q):
+    nodes = lax.broadcasted_iota(I32, p.shape, 0) < p.shape[0] - 1
+    return jnp.where(nodes, jnp.maximum(p, q), p + q)
+
+
+def spread_latest(x, d, found):
+    for level in found:
+        x = tree(gather_level(x, d, *level), join_latest)
     return x
 
 
@@ -1021,15 +1052,18 @@
     lines = lambda x: x.reshape(tiles, 128)
     mem_t = memory.T
     spread = first_latest(nodes, lines(source), lines(target), lines(event_ticks), lines(weights))
-    spread = spread_latest(spread, d)
+    low, *upper = levels(lax.axis_size("dp"))
+    spread = join_latest(spread, send(spread, twin()))
+    spread = spread_latest(spread, d, [low])
+    left, right, own = build_table(source, target, mem_t, node_ticks)
+    spread, left = tie(spread, left)
+    spread = spread_latest(spread, d, upper)
     latest = spread[:-1].reshape(-1).astype(I32)
-    wg, wh, vb = gate_weights(gru_in, gru_hid, vectors)
-    left, right, own = build_table(source, target, mem_t, node_ticks)
     cap = room(nodes, devices)
-    msg, keep, ren, gap_own, packed = gru(
-        scale, cap, source, target, event_ticks, latest, own, edge_feats.T, row(event_types), wg, wh, vb)
+    msg, keep, ren, gap_own, ren_left, ren_right = gru(
+        scale, source, target, event_ticks, own, edge_feats.T, row(event_types), gru_in, gru_hid, vectors)
+    packed = pack(cap, source, target, event_ticks, latest, ren_left, ren_right)
     height = packed.shape[1]
-    low, *upper = levels(lax.axis_size("dp"))
     first_round, left, right = tie(packed[0], left, right)
     rows = spread_upper(first_round, d)
     near = gather_near(near_ids, left, right)
@@ -1037,7 +1071,7 @@
     w = main_weights(gru_in, keys_values, tall_stack, squares, vec_late)
     held = gather_level(rows, d, *low)
     mine, theirs = main(scale, near, near_ticks, row(event_ticks), msg, keep, ren, gap_own, row(labels), row(weights),
-                        spread[-1:], core.reshape(1), list(w) + [vb])
+                        spread[-1:], core.reshape(1), list(w))
     mine, theirs, *held = tie(mine, theirs, *held)
     got = send(theirs, twin())
     items = reduce_level([mine, got], d, *low)
@@ -1049,7 +1083,8 @@
     swapped = send(joined, twin())
     for level in upper:
         items = reduce_level(items, d, *level)
-    *items, swapped = tie(*items, swapped)
+    where = jnp.stack([core, place(d, *low)])
+    *items, swapped, where, weight_sum = tie(*items, swapped, where, spread[-1, 0])
     piece = tree(items, jnp.add)
     for level in upper[::-1]:
         piece = in_order(gather_level(piece, d, *level), d, *level)
@@ -1059,9 +1094,8 @@
     *blocks, new_mem = tie(*blocks, new_mem)
     other = [send(x, twin()) for x in blocks]
     grad_norm, loss_sum, news = adam(
-        jnp.stack([core, place(d, *low)]), [(0, len(blocks))], blocks, other,
+        where, [(0, len(blocks))], blocks, other,
         (gru_in, gru_hid, keys_values, tall_stack, squares, vectors) + moments)
-    weight_sum = spread[-1, 0]
 
     def again(carry):
         r, _, mem_now = carry

time: 192 us -> 189 us (0.984)
  waiting for transfers between devices: 24.6 us -> 21.4 us
    ppermute x31, waiting for transfers between devices: 24.6 us -> 21.4 us  [send(): return lax.ppermute(x, AXES, pairs)]
    pallas_call x2, Pallas kernels: 14.4 us -> 12.4 us  [the longest x1 7.31 us: gru(): pl.pallas_call(lambda *r: gru_kernel(scale, *r), out_shape=[jax.ShapeDtyp...]
  transfers between devices with their start and end apart: 31 -> 31, of which waited for: 12 -> 10; matrix products, arithmetic and copies ran while one was open for 1% -> 2% of each run, Pallas kernels for 52% -> 55%
where the time goes in v6:
time: 189 us; the launch traced here: 188 us
  Pallas kernels  122 us (65%)
  starting transfers between devices  34.7 us (18%)
  waiting for transfers between devices  21.4 us (11%)
  local copies, waits for them, and re-layouts  4.16 us (2%)
  other arithmetic  4.04 us (2%)
    ppermute x31, starting transfers between devices, send(): return lax.ppermute(x, AXES, pairs)  34.7 us
    pallas_call x1, Pallas kernels, main(): pl.pallas_call(lambda *r: main_kernel(scale, *r), out_shape=[jax.ShapeDty...  27.7 us
    ppermute x31, waiting for transfers between devices, send(): return lax.ppermute(x, AXES, pairs)  21.4 us
    pallas_call x1, Pallas kernels, merge(): pl.pallas_call(lambda *r: merge_kernel(cap, *r), out_shape=[jax.ShapeDtyp...  21.1 us
    pallas_call x1, Pallas kernels, gather_near(): pl.pallas_call(lambda *r: near_kernel(chunk, *r), out_shape=jax.ShapeDtyp...  19.1 us
    pallas_call x1, Pallas kernels, lay(): pl.pallas_call(lambda *r: lay_kernel(cap, count, *r), out_shape=[table, t...  15.4 us
    pallas_call x1, Pallas kernels, adam(): pl.pallas_call(lambda *r: adam_kernel(parts, *r), out_shape=outs, in_spec...  10.7 us
    pallas_call x1, Pallas kernels, build_table(): pl.pallas_call(table_kernel, out_shape=[half, half, jax.ShapeDtypeStruct(...  8.18 us
  transfers between devices with their start and end apart: 31, of which 10 were waited for; matrix products, arithmetic and copies ran while one was open for 2% of the time, Pallas kernels for 55%

profile of v6, /device:TPU:0, one launch (start us, length us, event | category | flops | bytes accessed | tf_op | source)
XLA Modules:
  0.0 188.1 jit_solution(12219026832272629274)
XLA Ops:
  0.7 2.8 %latest.1 = f32[65,128]{1,0:T(8,128)} custom-call(s32[4,128]{1,0:T(4,128)} %bitcast.107, s32[4,128]{1,0:T(4,128)} %bitcast.109, s32[4,128]{1,0:T(4,128)} %bitcast.111, f32[4,128]{1,0:T(4,128)} %bitcast.115), custom_call_target="tpu_custom_call" | custom-call | flops 2000000000 | bytes 6000000 | tf_op jit(solution)/shard_map/latest/pallas_call | solution.py:169
  5.9 3.9 %collective-permute-start.10 = (f32[65,128]{1,0:T(8,128)S(1)}, f32[65,128]{1,0:T(8,128)S(1)}, u32[]{:S(2)}, u32[]{:S(2)}) collective-permute-start(f32[65,128]{1,0:T(8,128)S(1)} %add_select_fusion.2), channel_id=1, source_target_pairs={{0,6},{1,7},{2,4},{3,5},{4,2},{5,3},{6,0},{7,1},{8,14},{9,15},{10,... | collective-permute-start | bytes 99848 | tf_op jit(solution)/shard_map/ppermute | solution.py:983
  10.4 8.2 %table.1 = (f32[8192,128]{1,0:T(8,128)}, f32[8192,128]{1,0:T(8,128)}, bf16[1024,256]{1,0:T(8,128)(2,1)}) custom-call(s32[512]{0:T(512)} %r_0_.1, s32[512]{0:T(512)} %r_1_.1, f32[172,8192]{1,0:T(8,128)} %bitcast.82, s32[1,8192]{1,0:T(1,128)} %bitcast.105), custom_call_target="tpu_custom_call" | custom-call | flops 8999999488 | bytes 27000000 | tf_op jit(solution)/shard_map/table/pallas_call | solution.py:235
  18.7 2.0 %collective-permute-start.11 = (f32[65,128]{1,0:T(8,128)S(1)}, f32[65,128]{1,0:T(8,128)S(1)}, u32[]{:S(2)}, u32[]{:S(2)}) collective-permute-start(f32[65,128]{1,0:T(8,128)S(1)} %add_select_fusion.1), channel_id=1, source_target_pairs={{0,8},{1,9},{2,10},{3,11},{4,12},{5,13},{6,14},{7,15},{8,0},{9,1},... | collective-permute-start | bytes 99848 | tf_op jit(solution)/shard_map/ppermute | solution.py:983
  20.7 2.6 %collective-permute-start.12 = (f32[65,128]{1,0:T(8,128)S(1)}, f32[65,128]{1,0:T(8,128)S(1)}, u32[]{:S(2)}, u32[]{:S(2)}) collective-permute-start(f32[65,128]{1,0:T(8,128)S(1)} %add_select_fusion.1), channel_id=1, source_target_pairs={{0,16},{1,17},{2,18},{3,19},{4,20},{5,21},{6,22},{7,23},{8,24},{9,... | collective-permute-start | bytes 99848 | tf_op jit(solution)/shard_map/ppermute | solution.py:983
  23.3 7.3 %gru.1 = (bf16[704,1024]{1,0:T(8,128)(2,1)}, f32[5,176,1024]{2,1,0:T(8,128)}, f32[176,1024]{1,0:T(8,128)}, f32[8,1024]{1,0:T(8,128)}, f32[1024,128]{1,0:T(8,128)}, /*index=5*/f32[1024,128]{1,0:T(8,128)}) custom-call(bf16[1024,256]{1,0:T(8,128)(2,1)} %get-tuple-element.145.r_0_, s32[1,512]{1,0:T(1,128)} %bitcast.108, s32[1,512]{1,0:T(1,128)} %bitcast.110, ...), custom_call_target="tpu_custom_call" | custom-call | flops 8000000000 | bytes 24000000 | tf_op jit(solution)/shard_map/gru/pallas_call | solution.py:439
  32.0 5.1 %pack.1 = f32[4,408,128]{2,1,0:T(8,128)S(1)} custom-call(s32[512]{0:T(512)} %r_0_.1, s32[512]{0:T(512)} %r_1_.1, s32[512]{0:T(512)} %r_2_.1, s32[8192]{0:T(1024)} %fusion.r_3_, f32[1024,128]{1,0:T(8,128)} %get-tuple-element.146.r_4_, f32[1024,128]{1,0:T(8,128)} %get-tuple-element.147.r_5_), custom_call_target="tpu_custom_call" | custom-call | flops 5000000000 | bytes 15000000 | tf_op jit(solution)/shard_map/pack/pallas_call | solution.py:422
  38.1 3.5 %collective-permute-start.15 = (f32[408,128]{1,0:T(8,128)S(1)}, f32[408,128]{1,0:T(8,128)S(1)}, u32[]{:S(2)}, u32[]{:S(2)}) collective-permute-start(f32[408,128]{1,0:T(8,128)S(1)} %slice_bitcast_fusion), channel_id=1, source_target_pairs={{0,16},{1,17},{2,18},{3,19},{4,20},{5,21},{6,22},{7,23},{8,24},{9,... | collective-permute-start | bytes 626696 | tf_op jit(solution)/shard_map/ppermute | solution.py:983
  41.6 19.1 %near.1 = bf16[10240,256]{1,0:T(8,128)(2,1)} custom-call(s32[10240]{0:T(1024)} %bitcast.104, f32[8192,128]{1,0:T(8,128)} %get-tuple-element.151.r_1_, f32[8192,128]{1,0:T(8,128)} %get-tuple-element.152.r_2_), custom_call_target="tpu_custom_call" | custom-call | flops 16000000000 | bytes 48000000 | tf_op jit(solution)/shard_map/near/pallas_call | solution.py:262
  61.3 1.8 collective-permute-start.17
  63.0 1.5 collective-permute-start.18
  64.8 4.7 %main_weights.1 = (bf16[176,528]{1,0:T(8,128)(2,1)}, bf16[352,256]{1,0:T(8,128)(2,1)}, bf16[352,176]{1,0:T(8,128)(2,1)}, bf16[176,352]{1,0:T(8,128)(2,1)}, bf16[...) custom-call(f32[516,688]{1,0:T(8,128)} %bitcast.85, ...), custom_call_target="tpu_custom_call" | custom-call | flops 5000000000 | bytes 15000000 | tf_op jit(solution)/shard_map/main_weights/pallas_call | solution.py:133
  69.5 27.7 %main.1 = (f32[2944,128]{1,0:T(8,128)}, f32[2944,128]{1,0:T(8,128)}) custom-call(s32[1]{0:T(128)} %bitcast.6.r_0_, bf16[10,1024,256]{2,1,0:T(8,128)(2,1)} %bitcast.117, s32[10,1024]{1,0:T(8,128)} %reshape.142.r_2_, s32[1,512]{1,0:T(1,128)} %bitcast.113, bf16[704,1024]{1,0:T(8,128)(2,1)} %get-tuple-element.154.r_4_, f32[5,176,1024]{2,1,0:T(8,128)} %get-tuple-element.155.r_5_, ...), custom_call_target="tpu_custom_call" | custom-call | flops 35000000512 | bytes 105000000 | tf_op jit(solution)/shard_map/main/pallas_call | solution.py:673
  97.2 1.7 collective-permute-done.18
  100.1 3.5 %collective-permute-done.20 = f32[2944,128]{1,0:T(8,128)S(1)} collective-permute-done((f32[2944,128]{1,0:T(8,128)}, f32[2944,128]{1,0:T(8,128)S(1)}, u32[]{:S(2)}, u32[]{:S(2)}) %collective-permute-start.20) | collective-permute-done | bytes 1507360 | tf_op jit(solution)/shard_map/ppermute | solution.py:983
  108.6 15.4 %lay.2 = (f32[8200,128]{1,0:T(8,128)}, f32[8200,128]{1,0:T(8,128)}, s32[1]{0:T(128)}, f32[16,408,128]{2,1,0:T(8,128)}) custom-call(f32[4,408,128]{2,1,0:T(8,128)} %bitcast.80, f32[4,408,128]{2,1,0:T(8,128)} %bitcast.89, f32[4,408,128]{2,1,0:T(8,128)} %bitcast.90, f32[4,408,128]{2,1,0:T(8,128)} %bitcast.91), custom_call_target="tpu_custom_call" | custom-call | flops 14000000000 | bytes 42000000 | tf_op jit(solution)/shard_map/lay/pallas_call | solution.py:761
  125.7 3.5 %collective-permute-start.25 = (f32[184,128]{1,0:T(8,128)S(1)}, f32[184,128]{1,0:T(8,128)S(1)}, u32[]{:S(2)}, u32[]{:S(2)}) collective-permute-start(f32[184,128]{1,0:T(8,128)S(1)} %get-tuple-element.251), channel_id=1, source_target_pairs={{0,16},{1,17},{2,18},{3,19},{4,20},{5,21},{6,22},{7,23},{8,24},{9,... | collective-permute-start | bytes 282632 | tf_op jit(solution)/shard_map/ppermute | solution.py:983
  131.4 5.4 %collective-permute-done.25 = f32[184,128]{1,0:T(8,128)S(1)} collective-permute-done((f32[184,128]{1,0:T(8,128)S(1)}, f32[184,128]{1,0:T(8,128)S(1)}, u32[]{:S(2)}, u32[]{:S(2)}) %collective-permute-start.25) | collective-permute-done | bytes 94240 | tf_op jit(solution)/shard_map/ppermute | solution.py:983
  136.8 2.5 %collective-permute-start.28 = (f32[184,128]{1,0:T(8,128)S(1)}, f32[184,128]{1,0:T(8,128)S(1)}, u32[]{:S(2)}, u32[]{:S(2)}) collective-permute-start(f32[184,128]{1,0:T(8,128)S(1)} %add_add_fusion), channel_id=1, source_target_pairs={{0,24},{1,25},{2,26},{3,27},{4,28},{5,29},{6,30},{7,31},{8,16},{9,... | collective-permute-start | bytes 282632 | tf_op jit(solution)/shard_map/ppermute | solution.py:983
  141.2 2.3 %collective-permute-done.28 = f32[184,128]{1,0:T(8,128)S(1)} collective-permute-done((f32[184,128]{1,0:T(8,128)S(1)}, f32[184,128]{1,0:T(8,128)S(1)}, u32[]{:S(2)}, u32[]{:S(2)}) %collective-permute-start.28) | collective-permute-done | bytes 94240 | tf_op jit(solution)/shard_map/ppermute | solution.py:983
  143.6 4.7 %collective-permute-done.29 = f32[184,128]{1,0:T(8,128)S(1)} collective-permute-done((f32[184,128]{1,0:T(8,128)S(1)}, f32[184,128]{1,0:T(8,128)S(1)}, u32[]{:S(2)}, u32[]{:S(2)}) %collective-permute-start.29) | collective-permute-done | bytes 94240 | tf_op jit(solution)/shard_map/ppermute | solution.py:983
  149.2 1.5 collective-permute-start.32
  151.9 21.1 %merge.2 = (f32[172,8192]{1,0:T(8,128)}, s32[1]{0:T(128)}) custom-call(f32[16,408,128]{2,1,0:T(8,128)} %collective-permute-done.27.r_0_, f32[8200,128]{1,0:T(8,128)} %get-tuple-element.206.r_1_, f32[8200,128]{1,0:T(8,128)} %get-tuple-element.207.r_2_, s32[1]{0:T(128)} %get-tuple-element.208.r_3_, f32[172,8192]{1,0:T(8,128)} %bitcast.83), custom_call_target="tpu_custom_call" | custom-call | flops 17999998976 | bytes 54000000 | tf_op jit(solution)/shard_map/merge/pallas_call | solution.py:804
  177.2 10.7 %adam.1 = (f32[516,688]{1,0:T(8,128)}, f32[172,516]{1,0:T(8,128)}, f32[344,344]{1,0:T(8,128)}, f32[3,172,344]{2,1,0:T(8,128)}, f32[172,2,172]{2,1,0:T(2,128)}, /...) custom-call(s32[2]{0:T(128)} %pad_add_fusion.r_0_, ...), custom_call_target="tpu_custom_call" | custom-call | flops 14000000000 | bytes 42000000 | tf_op jit(solution)/shard_map/adam/pallas_call | solution.py:947
  (91 shorter events, 23.8 us)
Async XLA Ops:
  5.9 12.7 %collective-permute-start.10 = (f32[65,128]{1,0:T(8,128)S(1)}, f32[65,128]{1,0:T(8,128)S(1)}, u32[]{:S(2)}, u32[]{:S(2)}) collective-permute-start(f32[65,128]{1,0:T(8,128)S(1)} %add_select_fusion.2), channel_id=1, source_target_pairs={{0,6},{1,7},{2,4},{3,5},{4,2},{5,3},{6,0},{7,1},{8,14},{9,15},{10,... | collective-permute-start | bytes 99848 | tf_op jit(solution)/shard_map/ppermute | solution.py:983
  9.7 8.8 %collective-permute-start.8 = (f32[65,128]{1,0:T(8,128)S(1)}, f32[65,128]{1,0:T(8,128)S(1)}, u32[]{:S(2)}, u32[]{:S(2)}) collective-permute-start(f32[65,128]{1,0:T(8,128)S(1)} %add_select_fusion.2), channel_id=1, source_target_pairs={{0,2},{1,3},{2,0},{3,1},{4,6},{5,7},{6,4},{7,5},{8,10},{9,11},{10,... | collective-permute-start | bytes 99848 | tf_op jit(solution)/shard_map/ppermute | solution.py:983
  10.2 8.3 %collective-permute-start.9 = (f32[65,128]{1,0:T(8,128)S(1)}, f32[65,128]{1,0:T(8,128)S(1)}, u32[]{:S(2)}, u32[]{:S(2)}) collective-permute-start(f32[65,128]{1,0:T(8,128)S(1)} %add_select_fusion.2), channel_id=1, source_target_pairs={{0,4},{1,5},{2,6},{3,7},{4,0},{5,1},{6,2},{7,3},{8,12},{9,13},{10,... | collective-permute-start | bytes 99848 | tf_op jit(solution)/shard_map/ppermute | solution.py:983
  18.7 12.6 %collective-permute-start.11 = (f32[65,128]{1,0:T(8,128)S(1)}, f32[65,128]{1,0:T(8,128)S(1)}, u32[]{:S(2)}, u32[]{:S(2)}) collective-permute-start(f32[65,128]{1,0:T(8,128)S(1)} %add_select_fusion.1), channel_id=1, source_target_pairs={{0,8},{1,9},{2,10},{3,11},{4,12},{5,13},{6,14},{7,15},{8,0},{9,1},... | collective-permute-start | bytes 99848 | tf_op jit(solution)/shard_map/ppermute | solution.py:983
  20.7 10.6 %collective-permute-start.12 = (f32[65,128]{1,0:T(8,128)S(1)}, f32[65,128]{1,0:T(8,128)S(1)}, u32[]{:S(2)}, u32[]{:S(2)}) collective-permute-start(f32[65,128]{1,0:T(8,128)S(1)} %add_select_fusion.1), channel_id=1, source_target_pairs={{0,16},{1,17},{2,18},{3,19},{4,20},{5,21},{6,22},{7,23},{8,24},{9,... | collective-permute-start | bytes 99848 | tf_op jit(solution)/shard_map/ppermute | solution.py:983
  23.3 8.0 %collective-permute-start.13 = (f32[65,128]{1,0:T(8,128)S(1)}, f32[65,128]{1,0:T(8,128)S(1)}, u32[]{:S(2)}, u32[]{:S(2)}) collective-permute-start(f32[65,128]{1,0:T(8,128)S(1)} %add_select_fusion.1), channel_id=1, source_target_pairs={{0,24},{1,25},{2,26},{3,27},{4,28},{5,29},{6,30},{7,31},{8,16},{9,... | collective-permute-start | bytes 99848 | tf_op jit(solution)/shard_map/ppermute | solution.py:983
  37.2 24.0 %collective-permute-start.14 = (f32[408,128]{1,0:T(8,128)S(1)}, f32[408,128]{1,0:T(8,128)S(1)}, u32[]{:S(2)}, u32[]{:S(2)}) collective-permute-start(f32[408,128]{1,0:T(8,128)S(1)} %slice_bitcast_fusion), channel_id=1, source_target_pairs={{0,8},{1,9},{2,10},{3,11},{4,12},{5,13},{6,14},{7,15},{8,0},{9,1},... | collective-permute-start | bytes 626696 | tf_op jit(solution)/shard_map/ppermute | solution.py:983
  38.1 23.1 %collective-permute-start.15 = (f32[408,128]{1,0:T(8,128)S(1)}, f32[408,128]{1,0:T(8,128)S(1)}, u32[]{:S(2)}, u32[]{:S(2)}) collective-permute-start(f32[408,128]{1,0:T(8,128)S(1)} %slice_bitcast_fusion), channel_id=1, source_target_pairs={{0,16},{1,17},{2,18},{3,19},{4,20},{5,21},{6,22},{7,23},{8,24},{9,... | collective-permute-start | bytes 626696 | tf_op jit(solution)/shard_map/ppermute | solution.py:983
  41.6 19.6 %collective-permute-start.16 = (f32[408,128]{1,0:T(8,128)S(1)}, f32[408,128]{1,0:T(8,128)S(1)}, u32[]{:S(2)}, u32[]{:S(2)}) collective-permute-start(f32[408,128]{1,0:T(8,128)S(1)} %slice_bitcast_fusion), channel_id=1, source_target_pairs={{0,24},{1,25},{2,26},{3,27},{4,28},{5,29},{6,30},{7,31},{8,16},{9,... | collective-permute-start | bytes 626696 | tf_op jit(solution)/shard_map/ppermute | solution.py:983
  61.3 35.9 %collective-permute-start.17 = (f32[1632,128]{1,0:T(8,128)S(1)}, f32[1632,128]{1,0:T(8,128)S(1)}, u32[]{:S(2)}, u32[]{:S(2)}) collective-permute-start(f32[1632,128]{1,0:T(8,128)S(1)} %pad_maximum_fusion.1), channel_id=1, source_target_pairs={{0,2},{1,3},{2,0},{3,1},{4,6},{5,7},{6,4},{7,5},{8,10},{9,11},{10,... | collective-permute-start | bytes 2506760 | tf_op jit(solution)/shard_map/ppermute | solution.py:983
  63.0 35.8 %collective-permute-start.18 = (f32[1632,128]{1,0:T(8,128)S(1)}, f32[1632,128]{1,0:T(8,128)S(1)}, u32[]{:S(2)}, u32[]{:S(2)}) collective-permute-start(f32[1632,128]{1,0:T(8,128)S(1)} %pad_maximum_fusion.1), channel_id=1, source_target_pairs={{0,4},{1,5},{2,6},{3,7},{4,0},{5,1},{6,2},{7,3},{8,12},{9,13},{10,... | collective-permute-start | bytes 2506760 | tf_op jit(solution)/shard_map/ppermute | solution.py:983
  64.6 34.3 %collective-permute-start.19 = (f32[1632,128]{1,0:T(8,128)S(1)}, f32[1632,128]{1,0:T(8,128)S(1)}, u32[]{:S(2)}, u32[]{:S(2)}) collective-permute-start(f32[1632,128]{1,0:T(8,128)S(1)} %pad_maximum_fusion.1), channel_id=1, source_target_pairs={{0,6},{1,7},{2,4},{3,5},{4,2},{5,3},{6,0},{7,1},{8,14},{9,15},{10,... | collective-permute-start | bytes 2506760 | tf_op jit(solution)/shard_map/ppermute | solution.py:983
  105.1 18.9 %collective-permute-start.21 = (f32[736,128]{1,0:T(8,128)S(1)}, f32[736,128]{1,0:T(8,128)S(1)}, u32[]{:S(2)}, u32[]{:S(2)}) collective-permute-start(f32[736,128]{1,0:T(8,128)S(1)} %get-tuple-element.248), channel_id=1, source_target_pairs={{0,2},{1,3},{2,0},{3,1},{4,6},{5,7},{6,4},{7,5},{8,10},{9,11},{10,... | collective-permute-start | bytes 1130504 | tf_op jit(solution)/shard_map/ppermute | solution.py:983
  106.1 17.9 %collective-permute-start.22 = (f32[736,128]{1,0:T(8,128)S(1)}, f32[736,128]{1,0:T(8,128)S(1)}, u32[]{:S(2)}, u32[]{:S(2)}) collective-permute-start(f32[736,128]{1,0:T(8,128)S(1)} %get-tuple-element.247), channel_id=1, source_target_pairs={{0,4},{1,5},{2,6},{3,7},{4,0},{5,1},{6,2},{7,3},{8,12},{9,13},{10,... | collective-permute-start | bytes 1130504 | tf_op jit(solution)/shard_map/ppermute | solution.py:983
  107.2 17.8 %collective-permute-start.23 = (f32[736,128]{1,0:T(8,128)S(1)}, f32[736,128]{1,0:T(8,128)S(1)}, u32[]{:S(2)}, u32[]{:S(2)}) collective-permute-start(f32[736,128]{1,0:T(8,128)S(1)} %get-tuple-element.246), channel_id=1, source_target_pairs={{0,6},{1,7},{2,4},{3,5},{4,2},{5,3},{6,0},{7,1},{8,14},{9,15},{10,... | collective-permute-start | bytes 1130504 | tf_op jit(solution)/shard_map/ppermute | solution.py:983
  125.0 11.8 %collective-permute-start.27 = (f32[16,408,128]{2,1,0:T(8,128)}, f32[16,408,128]{2,1,0:T(8,128)}, u32[]{:S(2)}, u32[]{:S(2)}) collective-permute-start(f32[16,408,128]{2,1,0:T(8,128)} %get-tuple-element.197), channel_id=1, source_target_pairs={{0,1},{1,0},{2,3},{3,2},{4,5},{5,4},{6,7},{7,6},{8,9},{9,8},{10,11... | collective-permute-start | bytes 10027016 | tf_op jit(solution)/shard_map/ppermute | solution.py:983
  125.7 11.1 %collective-permute-start.25 = (f32[184,128]{1,0:T(8,128)S(1)}, f32[184,128]{1,0:T(8,128)S(1)}, u32[]{:S(2)}, u32[]{:S(2)}) collective-permute-start(f32[184,128]{1,0:T(8,128)S(1)} %get-tuple-element.251), channel_id=1, source_target_pairs={{0,16},{1,17},{2,18},{3,19},{4,20},{5,21},{6,22},{7,23},{8,24},{9,... | collective-permute-start | bytes 282632 | tf_op jit(solution)/shard_map/ppermute | solution.py:983
  129.2 7.5 %collective-permute-start.26 = (f32[184,128]{1,0:T(8,128)S(1)}, f32[184,128]{1,0:T(8,128)S(1)}, u32[]{:S(2)}, u32[]{:S(2)}) collective-permute-start(f32[184,128]{1,0:T(8,128)S(1)} %get-tuple-element.250), channel_id=1, source_target_pairs={{0,24},{1,25},{2,26},{3,27},{4,28},{5,29},{6,30},{7,31},{8,16},{9,... | collective-permute-start | bytes 282632 | tf_op jit(solution)/shard_map/ppermute | solution.py:983
  136.8 6.8 %collective-permute-start.28 = (f32[184,128]{1,0:T(8,128)S(1)}, f32[184,128]{1,0:T(8,128)S(1)}, u32[]{:S(2)}, u32[]{:S(2)}) collective-permute-start(f32[184,128]{1,0:T(8,128)S(1)} %add_add_fusion), channel_id=1, source_target_pairs={{0,24},{1,25},{2,26},{3,27},{4,28},{5,29},{6,30},{7,31},{8,16},{9,... | collective-permute-start | bytes 282632 | tf_op jit(solution)/shard_map/ppermute | solution.py:983
  139.3 8.9 %collective-permute-start.29 = (f32[184,128]{1,0:T(8,128)S(1)}, f32[184,128]{1,0:T(8,128)S(1)}, u32[]{:S(2)}, u32[]{:S(2)}) collective-permute-start(f32[184,128]{1,0:T(8,128)S(1)} %add_add_fusion), channel_id=1, source_target_pairs={{0,16},{1,17},{2,18},{3,19},{4,20},{5,21},{6,22},{7,23},{8,24},{9,... | collective-permute-start | bytes 282632 | tf_op jit(solution)/shard_map/ppermute | solution.py:983
  140.5 7.7 %collective-permute-start.30 = (f32[184,128]{1,0:T(8,128)S(1)}, f32[184,128]{1,0:T(8,128)S(1)}, u32[]{:S(2)}, u32[]{:S(2)}) collective-permute-start(f32[184,128]{1,0:T(8,128)S(1)} %add_add_fusion), channel_id=1, source_target_pairs={{0,8},{1,9},{2,10},{3,11},{4,12},{5,13},{6,14},{7,15},{8,0},{9,1},... | collective-permute-start | bytes 282632 | tf_op jit(solution)/shard_map/ppermute | solution.py:983
  148.4 24.6 %collective-permute-start.31 = (f32[736,128]{1,0:T(8,128)S(1)}, f32[736,128]{1,0:T(8,128)S(1)}, u32[]{:S(2)}, u32[]{:S(2)}) collective-permute-start(f32[736,128]{1,0:T(8,128)S(1)} %pad_maximum_fusion.2.r_1_), channel_id=1, source_target_pairs={{0,2},{1,3},{2,0},{3,1},{4,6},{5,7},{6,4},{7,5},{8,10},{9,11},{10,... | collective-permute-start | bytes 1130504 | tf_op jit(solution)/shard_map/ppermute | solution.py:983
  149.2 23.8 %collective-permute-start.32 = (f32[736,128]{1,0:T(8,128)S(1)}, f32[736,128]{1,0:T(8,128)S(1)}, u32[]{:S(2)}, u32[]{:S(2)}) collective-permute-start(f32[736,128]{1,0:T(8,128)S(1)} %pad_maximum_fusion.2.r_1_), channel_id=1, source_target_pairs={{0,4},{1,5},{2,6},{3,7},{4,0},{5,1},{6,2},{7,3},{8,12},{9,13},{10,... | collective-permute-start | bytes 1130504 | tf_op jit(solution)/shard_map/ppermute | solution.py:983
  150.7 22.3 %collective-permute-start.33 = (f32[736,128]{1,0:T(8,128)S(1)}, f32[736,128]{1,0:T(8,128)S(1)}, u32[]{:S(2)}, u32[]{:S(2)}) collective-permute-start(f32[736,128]{1,0:T(8,128)S(1)} %pad_maximum_fusion.2.r_1_), channel_id=1, source_target_pairs={{0,6},{1,7},{2,4},{3,5},{4,2},{5,3},{6,0},{7,1},{8,14},{9,15},{10,... | collective-permute-start | bytes 1130504 | tf_op jit(solution)/shard_map/ppermute | solution.py:983
  (20 other events, 118.4 us)

commit v7 on v6

--- a/solution.py
+++ b/solution.py
@@ -228,7 +228,7 @@
 def build_table(source, target, mem_t, ticks):
     nodes = mem_t.shape[1]
     ends = 2 * source.shape[0]
-    cols = 2048
+    cols = 4096
     smem = pl.BlockSpec(memory_space=pltpu.SMEM)
     half = jax.ShapeDtypeStruct((nodes, 128), F32)
     fixed = lambda i: (0, 0)

time: 189 us -> 187 us (0.989)
  no operation moved by 1% of the time
where the time goes in v7:
time: 187 us
  Pallas kernels  121 us (65%)
  starting transfers between devices  34.7 us (19%)
  waiting for transfers between devices  21.6 us (12%)
  local copies, waits for them, and re-layouts  4.16 us (2%)
  other arithmetic  4.04 us (2%)
    ppermute x31, starting transfers between devices, send(): return lax.ppermute(x, AXES, pairs)  34.7 us
    pallas_call x1, Pallas kernels, main(): pl.pallas_call(lambda *r: main_kernel(scale, *r), out_shape=[jax.ShapeDty...  27.7 us
    ppermute x31, waiting for transfers between devices, send(): return lax.ppermute(x, AXES, pairs)  21.6 us
    pallas_call x1, Pallas kernels, merge(): pl.pallas_call(lambda *r: merge_kernel(cap, *r), out_shape=[jax.ShapeDtyp...  21.3 us
    pallas_call x1, Pallas kernels, gather_near(): pl.pallas_call(lambda *r: near_kernel(chunk, *r), out_shape=jax.ShapeDtyp...  19.1 us
    pallas_call x1, Pallas kernels, lay(): pl.pallas_call(lambda *r: lay_kernel(cap, count, *r), out_shape=[table, t...  15.2 us
    pallas_call x1, Pallas kernels, adam(): pl.pallas_call(lambda *r: adam_kernel(parts, *r), out_shape=outs, in_spec...  10.7 us
    pallas_call x1, Pallas kernels, gru(): pl.pallas_call(lambda *r: gru_kernel(scale, *r), out_shape=[jax.ShapeDtyp...  7.31 us
  transfers between devices with their start and end apart: 31, of which 10 were waited for; matrix products, arithmetic and copies ran while one was open for 2% of the time, Pallas kernels for 55%

profile of v7, /device:TPU:0, one launch (start us, length us, event | category | flops | bytes accessed | tf_op | source)
XLA Modules:
  0.0 187.0 jit_solution(15071055570030423852)
XLA Ops:
  0.7 2.8 %latest.1 = f32[65,128]{1,0:T(8,128)} custom-call(s32[4,128]{1,0:T(4,128)} %bitcast.107, s32[4,128]{1,0:T(4,128)} %bitcast.109, s32[4,128]{1,0:T(4,128)} %bitcast.111, f32[4,128]{1,0:T(4,128)} %bitcast.115), custom_call_target="tpu_custom_call" | custom-call | flops 2000000000 | bytes 6000000 | tf_op jit(solution)/shard_map/latest/pallas_call | solution.py:169
  5.9 3.9 %collective-permute-start.10 = (f32[65,128]{1,0:T(8,128)S(1)}, f32[65,128]{1,0:T(8,128)S(1)}, u32[]{:S(2)}, u32[]{:S(2)}) collective-permute-start(f32[65,128]{1,0:T(8,128)S(1)} %add_select_fusion.2), channel_id=1, source_target_pairs={{0,6},{1,7},{2,4},{3,5},{4,2},{5,3},{6,0},{7,1},{8,14},{9,15},{10,... | collective-permute-start | bytes 99848 | tf_op jit(solution)/shard_map/ppermute | solution.py:983
  10.4 6.9 %table.1 = (f32[8192,128]{1,0:T(8,128)}, f32[8192,128]{1,0:T(8,128)}, bf16[1024,256]{1,0:T(8,128)(2,1)}) custom-call(s32[512]{0:T(512)} %r_0_.1, s32[512]{0:T(512)} %r_1_.1, f32[172,8192]{1,0:T(8,128)} %bitcast.82, s32[1,8192]{1,0:T(1,128)} %bitcast.105), custom_call_target="tpu_custom_call" | custom-call | flops 8999999488 | bytes 27000000 | tf_op jit(solution)/shard_map/table/pallas_call | solution.py:235
  17.3 2.0 %collective-permute-start.11 = (f32[65,128]{1,0:T(8,128)S(1)}, f32[65,128]{1,0:T(8,128)S(1)}, u32[]{:S(2)}, u32[]{:S(2)}) collective-permute-start(f32[65,128]{1,0:T(8,128)S(1)} %add_select_fusion.1), channel_id=1, source_target_pairs={{0,8},{1,9},{2,10},{3,11},{4,12},{5,13},{6,14},{7,15},{8,0},{9,1},... | collective-permute-start | bytes 99848 | tf_op jit(solution)/shard_map/ppermute | solution.py:983
  19.4 2.6 %collective-permute-start.12 = (f32[65,128]{1,0:T(8,128)S(1)}, f32[65,128]{1,0:T(8,128)S(1)}, u32[]{:S(2)}, u32[]{:S(2)}) collective-permute-start(f32[65,128]{1,0:T(8,128)S(1)} %add_select_fusion.1), channel_id=1, source_target_pairs={{0,16},{1,17},{2,18},{3,19},{4,20},{5,21},{6,22},{7,23},{8,24},{9,... | collective-permute-start | bytes 99848 | tf_op jit(solution)/shard_map/ppermute | solution.py:983
  22.0 7.3 %gru.1 = (bf16[704,1024]{1,0:T(8,128)(2,1)}, f32[5,176,1024]{2,1,0:T(8,128)}, f32[176,1024]{1,0:T(8,128)}, f32[8,1024]{1,0:T(8,128)}, f32[1024,128]{1,0:T(8,128)}, /*index=5*/f32[1024,128]{1,0:T(8,128)}) custom-call(bf16[1024,256]{1,0:T(8,128)(2,1)} %get-tuple-element.145.r_0_, s32[1,512]{1,0:T(1,128)} %bitcast.108, s32[1,512]{1,0:T(1,128)} %bitcast.110, ...), custom_call_target="tpu_custom_call" | custom-call | flops 8000000000 | bytes 24000000 | tf_op jit(solution)/shard_map/gru/pallas_call | solution.py:439
  30.7 5.1 %pack.1 = f32[4,408,128]{2,1,0:T(8,128)S(1)} custom-call(s32[512]{0:T(512)} %r_0_.1, s32[512]{0:T(512)} %r_1_.1, s32[512]{0:T(512)} %r_2_.1, s32[8192]{0:T(1024)} %fusion.r_3_, f32[1024,128]{1,0:T(8,128)} %get-tuple-element.146.r_4_, f32[1024,128]{1,0:T(8,128)} %get-tuple-element.147.r_5_), custom_call_target="tpu_custom_call" | custom-call | flops 5000000000 | bytes 15000000 | tf_op jit(solution)/shard_map/pack/pallas_call | solution.py:422
  36.8 3.5 %collective-permute-start.15 = (f32[408,128]{1,0:T(8,128)S(1)}, f32[408,128]{1,0:T(8,128)S(1)}, u32[]{:S(2)}, u32[]{:S(2)}) collective-permute-start(f32[408,128]{1,0:T(8,128)S(1)} %slice_bitcast_fusion), channel_id=1, source_target_pairs={{0,16},{1,17},{2,18},{3,19},{4,20},{5,21},{6,22},{7,23},{8,24},{9,... | collective-permute-start | bytes 626696 | tf_op jit(solution)/shard_map/ppermute | solution.py:983
  40.3 19.1 %near.1 = bf16[10240,256]{1,0:T(8,128)(2,1)} custom-call(s32[10240]{0:T(1024)} %bitcast.104, f32[8192,128]{1,0:T(8,128)} %get-tuple-element.151.r_1_, f32[8192,128]{1,0:T(8,128)} %get-tuple-element.152.r_2_), custom_call_target="tpu_custom_call" | custom-call | flops 16000000000 | bytes 48000000 | tf_op jit(solution)/shard_map/near/pallas_call | solution.py:262
  60.0 1.8 collective-permute-start.17
  61.7 1.5 collective-permute-start.18
  63.5 4.7 %main_weights.1 = (bf16[176,528]{1,0:T(8,128)(2,1)}, bf16[352,256]{1,0:T(8,128)(2,1)}, bf16[352,176]{1,0:T(8,128)(2,1)}, bf16[176,352]{1,0:T(8,128)(2,1)}, bf16[...) custom-call(f32[516,688]{1,0:T(8,128)} %bitcast.85, ...), custom_call_target="tpu_custom_call" | custom-call | flops 5000000000 | bytes 15000000 | tf_op jit(solution)/shard_map/main_weights/pallas_call | solution.py:133
  68.2 27.7 %main.1 = (f32[2944,128]{1,0:T(8,128)}, f32[2944,128]{1,0:T(8,128)}) custom-call(s32[1]{0:T(128)} %bitcast.6.r_0_, bf16[10,1024,256]{2,1,0:T(8,128)(2,1)} %bitcast.117, s32[10,1024]{1,0:T(8,128)} %reshape.142.r_2_, s32[1,512]{1,0:T(1,128)} %bitcast.113, bf16[704,1024]{1,0:T(8,128)(2,1)} %get-tuple-element.154.r_4_, f32[5,176,1024]{2,1,0:T(8,128)} %get-tuple-element.155.r_5_, ...), custom_call_target="tpu_custom_call" | custom-call | flops 35000000512 | bytes 105000000 | tf_op jit(solution)/shard_map/main/pallas_call | solution.py:673
  95.9 1.7 collective-permute-done.18
  98.7 3.5 %collective-permute-done.20 = f32[2944,128]{1,0:T(8,128)S(1)} collective-permute-done((f32[2944,128]{1,0:T(8,128)}, f32[2944,128]{1,0:T(8,128)S(1)}, u32[]{:S(2)}, u32[]{:S(2)}) %collective-permute-start.20) | collective-permute-done | bytes 1507360 | tf_op jit(solution)/shard_map/ppermute | solution.py:983
  107.3 15.2 %lay.2 = (f32[8200,128]{1,0:T(8,128)}, f32[8200,128]{1,0:T(8,128)}, s32[1]{0:T(128)}, f32[16,408,128]{2,1,0:T(8,128)}) custom-call(f32[4,408,128]{2,1,0:T(8,128)} %bitcast.80, f32[4,408,128]{2,1,0:T(8,128)} %bitcast.89, f32[4,408,128]{2,1,0:T(8,128)} %bitcast.90, f32[4,408,128]{2,1,0:T(8,128)} %bitcast.91), custom_call_target="tpu_custom_call" | custom-call | flops 14000000000 | bytes 42000000 | tf_op jit(solution)/shard_map/lay/pallas_call | solution.py:761
  124.4 3.5 %collective-permute-start.25 = (f32[184,128]{1,0:T(8,128)S(1)}, f32[184,128]{1,0:T(8,128)S(1)}, u32[]{:S(2)}, u32[]{:S(2)}) collective-permute-start(f32[184,128]{1,0:T(8,128)S(1)} %get-tuple-element.251), channel_id=1, source_target_pairs={{0,16},{1,17},{2,18},{3,19},{4,20},{5,21},{6,22},{7,23},{8,24},{9,... | collective-permute-start | bytes 282632 | tf_op jit(solution)/shard_map/ppermute | solution.py:983
  130.1 5.4 %collective-permute-done.25 = f32[184,128]{1,0:T(8,128)S(1)} collective-permute-done((f32[184,128]{1,0:T(8,128)S(1)}, f32[184,128]{1,0:T(8,128)S(1)}, u32[]{:S(2)}, u32[]{:S(2)}) %collective-permute-start.25) | collective-permute-done | bytes 94240 | tf_op jit(solution)/shard_map/ppermute | solution.py:983
  135.5 2.5 %collective-permute-start.28 = (f32[184,128]{1,0:T(8,128)S(1)}, f32[184,128]{1,0:T(8,128)S(1)}, u32[]{:S(2)}, u32[]{:S(2)}) collective-permute-start(f32[184,128]{1,0:T(8,128)S(1)} %add_add_fusion), channel_id=1, source_target_pairs={{0,24},{1,25},{2,26},{3,27},{4,28},{5,29},{6,30},{7,31},{8,16},{9,... | collective-permute-start | bytes 282632 | tf_op jit(solution)/shard_map/ppermute | solution.py:983
  139.9 2.3 %collective-permute-done.28 = f32[184,128]{1,0:T(8,128)S(1)} collective-permute-done((f32[184,128]{1,0:T(8,128)S(1)}, f32[184,128]{1,0:T(8,128)S(1)}, u32[]{:S(2)}, u32[]{:S(2)}) %collective-permute-start.28) | collective-permute-done | bytes 94240 | tf_op jit(solution)/shard_map/ppermute | solution.py:983
  142.3 4.7 %collective-permute-done.29 = f32[184,128]{1,0:T(8,128)S(1)} collective-permute-done((f32[184,128]{1,0:T(8,128)S(1)}, f32[184,128]{1,0:T(8,128)S(1)}, u32[]{:S(2)}, u32[]{:S(2)}) %collective-permute-start.29) | collective-permute-done | bytes 94240 | tf_op jit(solution)/shard_map/ppermute | solution.py:983
  147.9 1.5 collective-permute-start.32
  150.6 21.3 %merge.2 = (f32[172,8192]{1,0:T(8,128)}, s32[1]{0:T(128)}) custom-call(f32[16,408,128]{2,1,0:T(8,128)} %collective-permute-done.27.r_0_, f32[8200,128]{1,0:T(8,128)} %get-tuple-element.206.r_1_, f32[8200,128]{1,0:T(8,128)} %get-tuple-element.207.r_2_, s32[1]{0:T(128)} %get-tuple-element.208.r_3_, f32[172,8192]{1,0:T(8,128)} %bitcast.83), custom_call_target="tpu_custom_call" | custom-call | flops 17999998976 | bytes 54000000 | tf_op jit(solution)/shard_map/merge/pallas_call | solution.py:804
  176.1 10.7 %adam.1 = (f32[516,688]{1,0:T(8,128)}, f32[172,516]{1,0:T(8,128)}, f32[344,344]{1,0:T(8,128)}, f32[3,172,344]{2,1,0:T(8,128)}, f32[172,2,172]{2,1,0:T(2,128)}, /...) custom-call(s32[2]{0:T(128)} %pad_add_fusion.r_0_, ...), custom_call_target="tpu_custom_call" | custom-call | flops 14000000000 | bytes 42000000 | tf_op jit(solution)/shard_map/adam/pallas_call | solution.py:947
  (91 shorter events, 24.0 us)
Async XLA Ops:
  5.9 11.4 %collective-permute-start.10 = (f32[65,128]{1,0:T(8,128)S(1)}, f32[65,128]{1,0:T(8,128)S(1)}, u32[]{:S(2)}, u32[]{:S(2)}) collective-permute-start(f32[65,128]{1,0:T(8,128)S(1)} %add_select_fusion.2), channel_id=1, source_target_pairs={{0,6},{1,7},{2,4},{3,5},{4,2},{5,3},{6,0},{7,1},{8,14},{9,15},{10,... | collective-permute-start | bytes 99848 | tf_op jit(solution)/shard_map/ppermute | solution.py:983
  9.7 7.5 %collective-permute-start.8 = (f32[65,128]{1,0:T(8,128)S(1)}, f32[65,128]{1,0:T(8,128)S(1)}, u32[]{:S(2)}, u32[]{:S(2)}) collective-permute-start(f32[65,128]{1,0:T(8,128)S(1)} %add_select_fusion.2), channel_id=1, source_target_pairs={{0,2},{1,3},{2,0},{3,1},{4,6},{5,7},{6,4},{7,5},{8,10},{9,11},{10,... | collective-permute-start | bytes 99848 | tf_op jit(solution)/shard_map/ppermute | solution.py:983
  10.2 7.0 %collective-permute-start.9 = (f32[65,128]{1,0:T(8,128)S(1)}, f32[65,128]{1,0:T(8,128)S(1)}, u32[]{:S(2)}, u32[]{:S(2)}) collective-permute-start(f32[65,128]{1,0:T(8,128)S(1)} %add_select_fusion.2), channel_id=1, source_target_pairs={{0,4},{1,5},{2,6},{3,7},{4,0},{5,1},{6,2},{7,3},{8,12},{9,13},{10,... | collective-permute-start | bytes 99848 | tf_op jit(solution)/shard_map/ppermute | solution.py:983
  17.3 12.6 %collective-permute-start.11 = (f32[65,128]{1,0:T(8,128)S(1)}, f32[65,128]{1,0:T(8,128)S(1)}, u32[]{:S(2)}, u32[]{:S(2)}) collective-permute-start(f32[65,128]{1,0:T(8,128)S(1)} %add_select_fusion.1), channel_id=1, source_target_pairs={{0,8},{1,9},{2,10},{3,11},{4,12},{5,13},{6,14},{7,15},{8,0},{9,1},... | collective-permute-start | bytes 99848 | tf_op jit(solution)/shard_map/ppermute | solution.py:983
  19.4 10.6 %collective-permute-start.12 = (f32[65,128]{1,0:T(8,128)S(1)}, f32[65,128]{1,0:T(8,128)S(1)}, u32[]{:S(2)}, u32[]{:S(2)}) collective-permute-start(f32[65,128]{1,0:T(8,128)S(1)} %add_select_fusion.1), channel_id=1, source_target_pairs={{0,16},{1,17},{2,18},{3,19},{4,20},{5,21},{6,22},{7,23},{8,24},{9,... | collective-permute-start | bytes 99848 | tf_op jit(solution)/shard_map/ppermute | solution.py:983
  22.0 8.0 %collective-permute-start.13 = (f32[65,128]{1,0:T(8,128)S(1)}, f32[65,128]{1,0:T(8,128)S(1)}, u32[]{:S(2)}, u32[]{:S(2)}) collective-permute-start(f32[65,128]{1,0:T(8,128)S(1)} %add_select_fusion.1), channel_id=1, source_target_pairs={{0,24},{1,25},{2,26},{3,27},{4,28},{5,29},{6,30},{7,31},{8,16},{9,... | collective-permute-start | bytes 99848 | tf_op jit(solution)/shard_map/ppermute | solution.py:983
  35.9 24.0 %collective-permute-start.14 = (f32[408,128]{1,0:T(8,128)S(1)}, f32[408,128]{1,0:T(8,128)S(1)}, u32[]{:S(2)}, u32[]{:S(2)}) collective-permute-start(f32[408,128]{1,0:T(8,128)S(1)} %slice_bitcast_fusion), channel_id=1, source_target_pairs={{0,8},{1,9},{2,10},{3,11},{4,12},{5,13},{6,14},{7,15},{8,0},{9,1},... | collective-permute-start | bytes 626696 | tf_op jit(solution)/shard_map/ppermute | solution.py:983
  36.8 23.1 %collective-permute-start.15 = (f32[408,128]{1,0:T(8,128)S(1)}, f32[408,128]{1,0:T(8,128)S(1)}, u32[]{:S(2)}, u32[]{:S(2)}) collective-permute-start(f32[408,128]{1,0:T(8,128)S(1)} %slice_bitcast_fusion), channel_id=1, source_target_pairs={{0,16},{1,17},{2,18},{3,19},{4,20},{5,21},{6,22},{7,23},{8,24},{9,... | collective-permute-start | bytes 626696 | tf_op jit(solution)/shard_map/ppermute | solution.py:983
  40.3 19.6 %collective-permute-start.16 = (f32[408,128]{1,0:T(8,128)S(1)}, f32[408,128]{1,0:T(8,128)S(1)}, u32[]{:S(2)}, u32[]{:S(2)}) collective-permute-start(f32[408,128]{1,0:T(8,128)S(1)} %slice_bitcast_fusion), channel_id=1, source_target_pairs={{0,24},{1,25},{2,26},{3,27},{4,28},{5,29},{6,30},{7,31},{8,16},{9,... | collective-permute-start | bytes 626696 | tf_op jit(solution)/shard_map/ppermute | solution.py:983
  60.0 35.9 %collective-permute-start.17 = (f32[1632,128]{1,0:T(8,128)S(1)}, f32[1632,128]{1,0:T(8,128)S(1)}, u32[]{:S(2)}, u32[]{:S(2)}) collective-permute-start(f32[1632,128]{1,0:T(8,128)S(1)} %pad_maximum_fusion.1), channel_id=1, source_target_pairs={{0,2},{1,3},{2,0},{3,1},{4,6},{5,7},{6,4},{7,5},{8,10},{9,11},{10,... | collective-permute-start | bytes 2506760 | tf_op jit(solution)/shard_map/ppermute | solution.py:983
  61.7 35.8 %collective-permute-start.18 = (f32[1632,128]{1,0:T(8,128)S(1)}, f32[1632,128]{1,0:T(8,128)S(1)}, u32[]{:S(2)}, u32[]{:S(2)}) collective-permute-start(f32[1632,128]{1,0:T(8,128)S(1)} %pad_maximum_fusion.1), channel_id=1, source_target_pairs={{0,4},{1,5},{2,6},{3,7},{4,0},{5,1},{6,2},{7,3},{8,12},{9,13},{10,... | collective-permute-start | bytes 2506760 | tf_op jit(solution)/shard_map/ppermute | solution.py:983
  63.3 34.3 %collective-permute-start.19 = (f32[1632,128]{1,0:T(8,128)S(1)}, f32[1632,128]{1,0:T(8,128)S(1)}, u32[]{:S(2)}, u32[]{:S(2)}) collective-permute-start(f32[1632,128]{1,0:T(8,128)S(1)} %pad_maximum_fusion.1), channel_id=1, source_target_pairs={{0,6},{1,7},{2,4},{3,5},{4,2},{5,3},{6,0},{7,1},{8,14},{9,15},{10,... | collective-permute-start | bytes 2506760 | tf_op jit(solution)/shard_map/ppermute | solution.py:983
  103.8 18.8 %collective-permute-start.21 = (f32[736,128]{1,0:T(8,128)S(1)}, f32[736,128]{1,0:T(8,128)S(1)}, u32[]{:S(2)}, u32[]{:S(2)}) collective-permute-start(f32[736,128]{1,0:T(8,128)S(1)} %get-tuple-element.248), channel_id=1, source_target_pairs={{0,2},{1,3},{2,0},{3,1},{4,6},{5,7},{6,4},{7,5},{8,10},{9,11},{10,... | collective-permute-start | bytes 1130504 | tf_op jit(solution)/shard_map/ppermute | solution.py:983
  104.8 17.8 %collective-permute-start.22 = (f32[736,128]{1,0:T(8,128)S(1)}, f32[736,128]{1,0:T(8,128)S(1)}, u32[]{:S(2)}, u32[]{:S(2)}) collective-permute-start(f32[736,128]{1,0:T(8,128)S(1)} %get-tuple-element.247), channel_id=1, source_target_pairs={{0,4},{1,5},{2,6},{3,7},{4,0},{5,1},{6,2},{7,3},{8,12},{9,13},{10,... | collective-permute-start | bytes 1130504 | tf_op jit(solution)/shard_map/ppermute | solution.py:983
  105.9 17.8 %collective-permute-start.23 = (f32[736,128]{1,0:T(8,128)S(1)}, f32[736,128]{1,0:T(8,128)S(1)}, u32[]{:S(2)}, u32[]{:S(2)}) collective-permute-start(f32[736,128]{1,0:T(8,128)S(1)} %get-tuple-element.246), channel_id=1, source_target_pairs={{0,6},{1,7},{2,4},{3,5},{4,2},{5,3},{6,0},{7,1},{8,14},{9,15},{10,... | collective-permute-start | bytes 1130504 | tf_op jit(solution)/shard_map/ppermute | solution.py:983
  123.7 11.8 %collective-permute-start.27 = (f32[16,408,128]{2,1,0:T(8,128)}, f32[16,408,128]{2,1,0:T(8,128)}, u32[]{:S(2)}, u32[]{:S(2)}) collective-permute-start(f32[16,408,128]{2,1,0:T(8,128)} %get-tuple-element.197), channel_id=1, source_target_pairs={{0,1},{1,0},{2,3},{3,2},{4,5},{5,4},{6,7},{7,6},{8,9},{9,8},{10,11... | collective-permute-start | bytes 10027016 | tf_op jit(solution)/shard_map/ppermute | solution.py:983
  124.4 11.1 %collective-permute-start.25 = (f32[184,128]{1,0:T(8,128)S(1)}, f32[184,128]{1,0:T(8,128)S(1)}, u32[]{:S(2)}, u32[]{:S(2)}) collective-permute-start(f32[184,128]{1,0:T(8,128)S(1)} %get-tuple-element.251), channel_id=1, source_target_pairs={{0,16},{1,17},{2,18},{3,19},{4,20},{5,21},{6,22},{7,23},{8,24},{9,... | collective-permute-start | bytes 282632 | tf_op jit(solution)/shard_map/ppermute | solution.py:983
  127.9 7.5 %collective-permute-start.26 = (f32[184,128]{1,0:T(8,128)S(1)}, f32[184,128]{1,0:T(8,128)S(1)}, u32[]{:S(2)}, u32[]{:S(2)}) collective-permute-start(f32[184,128]{1,0:T(8,128)S(1)} %get-tuple-element.250), channel_id=1, source_target_pairs={{0,24},{1,25},{2,26},{3,27},{4,28},{5,29},{6,30},{7,31},{8,16},{9,... | collective-permute-start | bytes 282632 | tf_op jit(solution)/shard_map/ppermute | solution.py:983
  135.5 6.8 %collective-permute-start.28 = (f32[184,128]{1,0:T(8,128)S(1)}, f32[184,128]{1,0:T(8,128)S(1)}, u32[]{:S(2)}, u32[]{:S(2)}) collective-permute-start(f32[184,128]{1,0:T(8,128)S(1)} %add_add_fusion), channel_id=1, source_target_pairs={{0,24},{1,25},{2,26},{3,27},{4,28},{5,29},{6,30},{7,31},{8,16},{9,... | collective-permute-start | bytes 282632 | tf_op jit(solution)/shard_map/ppermute | solution.py:983
  138.0 8.9 %collective-permute-start.29 = (f32[184,128]{1,0:T(8,128)S(1)}, f32[184,128]{1,0:T(8,128)S(1)}, u32[]{:S(2)}, u32[]{:S(2)}) collective-permute-start(f32[184,128]{1,0:T(8,128)S(1)} %add_add_fusion), channel_id=1, source_target_pairs={{0,16},{1,17},{2,18},{3,19},{4,20},{5,21},{6,22},{7,23},{8,24},{9,... | collective-permute-start | bytes 282632 | tf_op jit(solution)/shard_map/ppermute | solution.py:983
  139.2 7.7 %collective-permute-start.30 = (f32[184,128]{1,0:T(8,128)S(1)}, f32[184,128]{1,0:T(8,128)S(1)}, u32[]{:S(2)}, u32[]{:S(2)}) collective-permute-start(f32[184,128]{1,0:T(8,128)S(1)} %add_add_fusion), channel_id=1, source_target_pairs={{0,8},{1,9},{2,10},{3,11},{4,12},{5,13},{6,14},{7,15},{8,0},{9,1},... | collective-permute-start | bytes 282632 | tf_op jit(solution)/shard_map/ppermute | solution.py:983
  147.1 24.9 %collective-permute-start.31 = (f32[736,128]{1,0:T(8,128)S(1)}, f32[736,128]{1,0:T(8,128)S(1)}, u32[]{:S(2)}, u32[]{:S(2)}) collective-permute-start(f32[736,128]{1,0:T(8,128)S(1)} %pad_maximum_fusion.2.r_1_), channel_id=1, source_target_pairs={{0,2},{1,3},{2,0},{3,1},{4,6},{5,7},{6,4},{7,5},{8,10},{9,11},{10,... | collective-permute-start | bytes 1130504 | tf_op jit(solution)/shard_map/ppermute | solution.py:983
  147.9 24.0 %collective-permute-start.32 = (f32[736,128]{1,0:T(8,128)S(1)}, f32[736,128]{1,0:T(8,128)S(1)}, u32[]{:S(2)}, u32[]{:S(2)}) collective-permute-start(f32[736,128]{1,0:T(8,128)S(1)} %pad_maximum_fusion.2.r_1_), channel_id=1, source_target_pairs={{0,4},{1,5},{2,6},{3,7},{4,0},{5,1},{6,2},{7,3},{8,12},{9,13},{10,... | collective-permute-start | bytes 1130504 | tf_op jit(solution)/shard_map/ppermute | solution.py:983
  149.4 22.5 %collective-permute-start.33 = (f32[736,128]{1,0:T(8,128)S(1)}, f32[736,128]{1,0:T(8,128)S(1)}, u32[]{:S(2)}, u32[]{:S(2)}) collective-permute-start(f32[736,128]{1,0:T(8,128)S(1)} %pad_maximum_fusion.2.r_1_), channel_id=1, source_target_pairs={{0,6},{1,7},{2,4},{3,5},{4,2},{5,3},{6,0},{7,1},{8,14},{9,15},{10,... | collective-permute-start | bytes 1130504 | tf_op jit(solution)/shard_map/ppermute | solution.py:983
  (20 other events, 118.7 us)
